TPU v7x, 32 devices: a whole 2x2x4 slice. The times are simulated.
32 devices in a mesh: dp: 8 (over z, x), head: 4 (over y, core).
Axes of the slice: x: 2, y: 2, z: 4, core: 2. Of those that a mesh axis runs over, the one named last changes fastest.
Arguments:
- clean_latents: float32 [24, 832, 20], P('dp', 'head'), may hold values from -6 to 6
- noise_draw: float32 [24, 832, 20], P('dp', 'head'), may hold values from -6 to 6
- timesteps: float32 [24], P('dp'), may hold values from 0.02 to 0.98
- captions: bfloat16 [24, 256, 768], P('dp'), may hold values from -6 to 6
- cap_len: int32 [24], P('dp'), may hold values from 5 to 256, as said below
- pairing: int32 [24], P('dp'), may hold values from 0 to 23, each once
- adam_step: int32 [1], replicated, may hold values from 2 to 20
- qkv_weight: float32 [2, 768, 2304], P(None, 'dp', 'head'), may hold values from -0.21875 to 0.21875
- out_weight: float32 [2, 768, 768], P(None, 'dp', 'head'), may hold values from -1.25 to 1.25
- up_weight: float32 [2, 768, 3072], P(None, 'dp', 'head'), may hold values from -0.21875 to 0.21875
- down_weight: float32 [2, 768, 3072], P(None, 'dp', 'head'), may hold values from -0.109375 to 0.109375
- ada_weight: float32 [2, 768, 4608], P(None, 'dp', 'head'), may hold values from -0.4375 to 0.4375
- time_weight: float32 [768, 768], P('dp', 'head'), may hold values from -0.21875 to 0.21875
- io_weight: float32 [2, 768, 20], P(None, 'dp', 'head'), may hold values from -0.6 to 0.6
- qkv_moment: float32 [2, 768, 2304], P(None, 'dp', 'head'), may hold values from -0.0012207031 to 0.0012207031
- out_moment: float32 [2, 768, 768], P(None, 'dp', 'head'), may hold values from -0.0012207031 to 0.0012207031
- up_moment: float32 [2, 768, 3072], P(None, 'dp', 'head'), may hold values from -0.0012207031 to 0.0012207031
- down_moment: float32 [2, 768, 3072], P(None, 'dp', 'head'), may hold values from -0.0012207031 to 0.0012207031
- ada_first: float32 [2, 768, 4608], P(None, 'dp', 'head'), may hold values from -0.00015258789 to 0.00015258789
- ada_second: float32 [2, 768, 4608], P(None, 'dp', 'head'), may hold values from 4.575778e-11 to 1.8303112e-10
- time_first: float32 [768, 768], P('dp', 'head'), may hold values from -0.00015258789 to 0.00015258789
- time_second: float32 [768, 768], P('dp', 'head'), may hold values from 4.575778e-11 to 1.8303112e-10
- io_first: float32 [2, 768, 20], P(None, 'dp', 'head'), may hold values from -0.00015258789 to 0.00015258789
- io_second: float32 [2, 768, 20], P(None, 'dp', 'head'), may hold values from 4.575778e-11 to 1.8303112e-10
Outputs:
- total_loss: float32 [], replicated
- grad_norm: float32 [], replicated
- pooled: float32 [24, 768], P('dp')
- qkv_new: float32 [2, 768, 2304], P(None, 'dp', 'head')
- qkv_moment_new: float32 [2, 768, 2304], P(None, 'dp', 'head')
- out_new: float32 [2, 768, 768], P(None, 'dp', 'head')
- out_moment_new: float32 [2, 768, 768], P(None, 'dp', 'head')
- up_new: float32 [2, 768, 3072], P(None, 'dp', 'head')
- up_moment_new: float32 [2, 768, 3072], P(None, 'dp', 'head')
- down_new: float32 [2, 768, 3072], P(None, 'dp', 'head')
- down_moment_new: float32 [2, 768, 3072], P(None, 'dp', 'head')
- ada_new: float32 [2, 768, 4608], P(None, 'dp', 'head')
- ada_first_new: float32 [2, 768, 4608], P(None, 'dp', 'head')
- ada_second_new: float32 [2, 768, 4608], P(None, 'dp', 'head')
- time_new: float32 [768, 768], P('dp', 'head')
- time_first_new: float32 [768, 768], P('dp', 'head')
- time_second_new: float32 [768, 768], P('dp', 'head')
- io_new: float32 [2, 768, 20], P(None, 'dp', 'head')
- io_first_new: float32 [2, 768, 20], P(None, 'dp', 'head')
- io_second_new: float32 [2, 768, 20], P(None, 'dp', 'head')
Inputs may be any that keep to these rules, and one draw needn't show every extreme that they name: `cap_len`: some clip's caption has all 256 tokens. `pairing`: every caption index is named by exactly one clip.
All inputs are finite; a program needn't handle non-finite values.
Results may differ from a plain program's by a relative error of at most 0.0045.
The roundings to bfloat16 on the way count: a program that leaves them out, or rounds other values in their place, can miss the bound.
Values may be sent and summed in bfloat16 or wider, within the bound.
A program may use at most 384 MiB of HBM per device.

v0:
```python
import math

import jax
import jax.numpy as jnp
from jax import lax
from jax.sharding import PartitionSpec as P

D = 768
HEADS = 12
HDIM = 64
CAP = 256
NS_STEPS = 5


HIGHEST_PRECISION = lax.Precision.HIGHEST
NEWTON_COEFFS = (3.4445, -4.775, 2.0315)
CLIP_NORM = 1.0
MUON_RATE = 0.2
MUON_DECAY = 0.1
MUON_BETA = 0.95
ADAM_RATE = 0.02
ADAM_DECAY = 0.01
ADAM_FIRST = 0.9
ADAM_SECOND = 0.999


def to_bf16(values):
    return values.astype(jnp.bfloat16)


def sigmoid_unit(values):
    return values * jax.nn.sigmoid(values)


def double_silu(values):
    return sigmoid_unit(sigmoid_unit(values))


def soft_gelu(values):
    return (
        0.5
        * values
        * (1.0 + jnp.tanh(0.7978845608 * (values + 0.044715 * values * values * values)))
    )


def norm_rows(values):
    centre = values - jnp.mean(values, -1, keepdims=True)
    return centre * lax.rsqrt(jnp.mean(centre * centre, -1, keepdims=True) + 1e-06)


def modulate(hidden, shift, stretch):
    return norm_rows(hidden) * (1.0 + stretch) + shift


def time_table(timesteps, width):
    half_width = width // 2
    frequency = jnp.exp(
        -math.log(10000.0) * jnp.arange(half_width).astype(timesteps.dtype) / half_width
    )
    angles = 1000.0 * timesteps[:, None] * frequency[None, :]
    return jnp.concatenate([jnp.cos(angles), jnp.sin(angles)], axis=-1)


def product(form, left, right):
    return jnp.einsum(form, left, right, preferred_element_type=jnp.float32)


def exact_product(form, left, right):
    return jnp.einsum(form, left, right, precision=HIGHEST_PRECISION)


def to_heads(frames):
    return lax.all_to_all(frames, "head", split_axis=3, concat_axis=1, tiled=True)


def to_frames(heads):
    return lax.all_to_all(heads, "head", split_axis=1, concat_axis=3, tiled=True)


def to_blocks(full_grad, data_count, head_count):
    layers, rows_all, cols_all = full_grad.shape
    grouped = full_grad.reshape(
        layers, data_count, rows_all // data_count, head_count, cols_all // head_count
    )
    return grouped.transpose(0, 1, 3, 2, 4).reshape(
        layers, data_count * head_count, rows_all // data_count, cols_all // head_count
    )


def from_blocks(blocks, data_count, head_count):
    layers, total_blocks, block_rows, block_cols = blocks.shape
    grouped = blocks.reshape(layers, data_count, head_count, block_rows, block_cols)
    return grouped.transpose(0, 1, 3, 2, 4).reshape(
        layers, data_count * block_rows, head_count * block_cols
    )


def scores_of(query, keys, key_mask):
    raw_scores = product("qhe,khe->hqk", query, keys) * query.shape[-1] ** (-0.5)
    return jnp.where(key_mask[None, None, :], raw_scores, -1e30)


def attend_forward(pieces):
    query, keys, values, key_mask = pieces
    scores = scores_of(query, keys, key_mask)
    row_top = jnp.max(scores, -1, keepdims=True)
    exponent = jnp.exp(scores - row_top)
    row_total = jnp.sum(exponent, -1, keepdims=True)
    probability = to_bf16(exponent / row_total)
    mixed = product("hqk,khe->qhe", probability, values)
    return (to_bf16(mixed), row_top + jnp.log(row_total))


def attend_backward(pieces):
    query, keys, values, key_mask, log_total, grad_mixed = pieces
    scores = scores_of(query, keys, key_mask)
    probability = jnp.exp(scores - log_total)
    grad_prob = product("qhe,khe->hqk", grad_mixed, values)
    grad_scores = to_bf16(
        probability * (grad_prob - jnp.sum(probability * grad_prob, -1, keepdims=True))
    )
    factor = query.shape[-1] ** (-0.5)
    grad_query = product("hqk,khe->qhe", grad_scores, keys) * factor
    grad_keys = product("hqk,qhe->khe", grad_scores, query) * factor
    grad_values = product("hqk,qhe->khe", to_bf16(probability), grad_mixed)
    return (to_bf16(grad_query), to_bf16(grad_keys), to_bf16(grad_values))


def adam_update(weight, grad_part, first_moment, second_moment, step_count):
    first_moment = ADAM_FIRST * first_moment + (1.0 - ADAM_FIRST) * grad_part
    second_moment = ADAM_SECOND * second_moment + (1.0 - ADAM_SECOND) * grad_part * grad_part
    first_fix = 1.0 - jnp.power(ADAM_FIRST, step_count)
    second_fix = 1.0 - jnp.power(ADAM_SECOND, step_count)
    direction = first_moment / first_fix / (jnp.sqrt(second_moment / second_fix) + 1e-08)
    return (weight - ADAM_RATE * (direction + ADAM_DECAY * weight), first_moment, second_moment)


def body(
    clean_latents,
    noise_draw,
    timesteps,
    captions,
    cap_len,
    pairing,
    adam_step,
    qkv_weight,
    out_weight,
    up_weight,
    down_weight,
    ada_weight,
    time_weight,
    io_weight,
    qkv_moment,
    out_moment,
    up_moment,
    down_moment,
    ada_first,
    ada_second,
    time_first,
    time_second,
    io_first,
    io_second,
):
    data_count = lax.axis_size("dp")
    head_count = lax.axis_size("head")
    clip_count = clean_latents.shape[0]
    frame_rows = clean_latents.shape[1]
    length = frame_rows * head_count
    head_share = D // head_count
    local_heads = head_share // HDIM
    gathered = (
        lax.all_gather(to_bf16(qkv_weight)[:, None], ("dp", "head"), axis=1, tiled=True),
        lax.all_gather(to_bf16(out_weight)[:, None], ("dp", "head"), axis=1, tiled=True),
        lax.all_gather(to_bf16(up_weight)[:, None], ("dp", "head"), axis=1, tiled=True),
        lax.all_gather(to_bf16(down_weight)[:, None], ("dp", "head"), axis=1, tiled=True),
        lax.all_gather(to_bf16(ada_weight)[:, None], ("dp", "head"), axis=1, tiled=True),
        lax.all_gather(to_bf16(time_weight)[None, None], ("dp", "head"), axis=1, tiled=True),
        lax.all_gather(to_bf16(io_weight)[:, None], ("dp", "head"), axis=1, tiled=True),
    )
    qkv_full, out_full, up_full, down_full, ada_full, time_full, io_full = tuple(
        (from_blocks(blocks, data_count, head_count) for blocks in gathered)
    )
    time_full = time_full[0]
    keep_mask = jnp.arange(CAP)[None, :] < cap_len[:, None]
    cap_mean = product("ft,ftd->fd", keep_mask.astype(jnp.bfloat16), captions) / cap_len[
        :, None
    ].astype(jnp.float32)
    cap_unit = cap_mean * lax.rsqrt(jnp.mean(cap_mean * cap_mean, -1, keepdims=True) + 1e-06)
    cap_all = lax.all_gather(cap_unit, "dp", axis=0, tiled=True)
    table_bf = to_bf16(time_table(timesteps, D))
    time_hidden = jnp.dot(table_bf, time_full, preferred_element_type=jnp.float32)
    signal, signal_back = jax.vjp(double_silu, time_hidden)
    signal_bf = to_bf16(signal)
    blended = (1.0 - timesteps)[:, None, None] * clean_latents + timesteps[
        :, None, None
    ] * noise_draw
    input_bf = to_bf16(blended)
    hidden = product("flc,dc->fld", input_bf, io_full[0])

    def split_heads(values, rows_count):
        return values.reshape(clip_count, rows_count, local_heads, HDIM)

    def layer_forward(layer_index, hidden):
        modulation = jnp.dot(
            signal_bf, ada_full[layer_index], preferred_element_type=jnp.float32
        ).reshape(clip_count, 1, 6, D)
        mod_parts = [modulation[:, :, member] for member in range(6)]
        normed = to_bf16(modulate(hidden, mod_parts[0], mod_parts[1]))
        weight = qkv_full[layer_index]
        in_frames = layer_index == 1
        if layer_index == 0:
            projected = to_bf16(product("fld,dn->fln", normed, weight))
            head_rows = to_heads(projected.reshape(clip_count, frame_rows, 3, D))
            query = split_heads(head_rows[:, :, 0], length)
            keys = split_heads(head_rows[:, :, 1], length)
            values = split_heads(head_rows[:, :, 2], length)
            key_mask = jnp.ones((clip_count, length), dtype=bool)
        else:
            projected = to_bf16(product("fld,dn->fln", normed, weight[:, :D]))
            query = projected.reshape(clip_count, frame_rows, HEADS, HDIM)
            pair_kv = to_bf16(product("ftd,dn->ftn", captions, weight[:, D:]))
            keys = pair_kv[..., :D].reshape(clip_count, CAP, HEADS, HDIM)
            values = pair_kv[..., D:].reshape(clip_count, CAP, HEADS, HDIM)
            key_mask = keep_mask
        mixed, log_total = lax.map(attend_forward, (query, keys, values, key_mask))
        if in_frames:
            mixed_frames = mixed.reshape(clip_count, frame_rows, D)
        else:
            mixed_frames = to_frames(mixed.reshape(clip_count, length, 1, head_share)).reshape(
                clip_count, frame_rows, D
            )
        branch = product("fle,de->fld", mixed_frames, out_full[layer_index])
        middle = hidden + mod_parts[2] * branch
        normed2 = to_bf16(modulate(middle, mod_parts[3], mod_parts[4]))
        upper = product("fld,dn->fln", normed2, up_full[layer_index])
        active = to_bf16(soft_gelu(upper))
        down_out = product("fln,dn->fld", active, down_full[layer_index])
        kept = (
            hidden,
            mod_parts,
            normed,
            query,
            keys,
            values,
            key_mask,
            log_total,
            mixed_frames,
            branch,
            middle,
            normed2,
            upper,
            active,
            down_out,
        )
        return (middle + mod_parts[5] * down_out, kept)

    saved_layers = []
    for layer_index in range(2):
        hidden, kept = layer_forward(layer_index, hidden)
        saved_layers.append(kept)
    final = norm_rows(hidden)
    final_bf = to_bf16(final)
    predicted = product("fld,dc->flc", final_bf, io_full[1])
    errors = predicted - (noise_draw - clean_latents)
    flow_part = jnp.sum(jnp.mean(errors * errors, -1))
    grad_pred = to_bf16(2.0 * errors / errors.shape[-1])
    pool_sum = lax.psum(jnp.sum(final, 1), "head")
    pooled_out = pool_sum / length

    def contrast_of(pool_total):
        pooled = pool_total / length
        unit_rows = pooled * lax.rsqrt(jnp.mean(pooled * pooled, -1, keepdims=True) + 1e-06)
        logits = exact_product("id,jd->ij", unit_rows, cap_all) * (2.0 / math.sqrt(D))
        row_top = jnp.max(logits, -1, keepdims=True)
        log_total = row_top[:, 0] + jnp.log(jnp.sum(jnp.exp(logits - row_top), -1))
        picked = jnp.sum(
            jnp.where(jnp.arange(logits.shape[1])[None, :] == pairing[:, None], logits, 0.0), -1
        )
        return length * jnp.sum(log_total - picked)

    contrast_value, contrast_back = jax.vjp(contrast_of, pool_sum)
    grad_pool = contrast_back(jnp.ones_like(contrast_value))[0]
    loss_part = flow_part + contrast_value / head_count
    grad_final = product("flc,dc->fld", grad_pred, io_full[1]) + grad_pool[:, None, :]
    final_value, final_back = jax.vjp(norm_rows, hidden)
    grad_hidden = final_back(grad_final)[0]
    fin_grad = product("flc,fld->dc", grad_pred, final_bf)
    layer_grads = [None, None]
    ada_grads = [None, None]
    grad_signal = jnp.zeros_like(signal)
    for layer_index in (1, 0):
        layer_kept = saved_layers[layer_index]
        (
            layer_hidden,
            layer_mod_parts,
            layer_normed,
            layer_query,
            layer_keys,
            layer_values,
            layer_key_mask,
            layer_log_total,
            layer_mixed_frames,
            layer_branch,
            layer_middle,
            layer_normed2,
            layer_upper,
            layer_active,
            layer_down_out,
        ) = layer_kept
        layer_in_frames = layer_index == 1
        d_gate2 = jnp.sum(layer_down_out * grad_hidden, axis=1, keepdims=True)
        grad_down = to_bf16(layer_mod_parts[5] * grad_hidden)
        grad_active = product("fld,dn->fln", grad_down, down_full[layer_index])
        gelu_value, gelu_back = jax.vjp(soft_gelu, layer_upper)
        grad_upper = to_bf16(gelu_back(grad_active)[0])
        down_grad = product("fld,fln->dn", grad_down, layer_active)
        up_grad = product("fld,fln->dn", layer_normed2, grad_upper)
        grad_normed2 = product("fln,dn->fld", grad_upper, up_full[layer_index])
        mod_value, mod_back = jax.vjp(
            modulate, layer_middle, layer_mod_parts[3], layer_mod_parts[4]
        )
        grad_middle, d_shift2, d_scale2 = mod_back(grad_normed2)
        grad_middle = grad_middle + grad_hidden
        d_gate1 = jnp.sum(layer_branch * grad_middle, axis=1, keepdims=True)
        grad_branch = to_bf16(layer_mod_parts[2] * grad_middle)
        out_grad = product("fld,fle->de", grad_branch, layer_mixed_frames)
        grad_mixed = to_bf16(product("fld,de->fle", grad_branch, out_full[layer_index]))
        if layer_in_frames:
            grad_heads = grad_mixed.reshape(clip_count, frame_rows, HEADS, HDIM)
        else:
            grad_heads = split_heads(
                to_heads(grad_mixed.reshape(clip_count, frame_rows, 1, D))[:, :, 0], length
            )
        grad_query, grad_keys, grad_values = lax.map(
            attend_backward,
            (layer_query, layer_keys, layer_values, layer_key_mask, layer_log_total, grad_heads),
        )
        layer_weight = qkv_full[layer_index]
        if layer_index == 0:
            stacked = jnp.stack([grad_query, grad_keys, grad_values], 2).reshape(
                clip_count, length, 3, head_share
            )
            grad_proj = to_frames(stacked).reshape(clip_count, frame_rows, 3 * D)
            qkv_grad = product("fld,fln->dn", layer_normed, grad_proj)
            grad_normed = product("fln,dn->fld", grad_proj, layer_weight)
        else:
            grad_proj = grad_query.reshape(clip_count, frame_rows, D)
            query_grad = product("fld,fln->dn", layer_normed, grad_proj)
            key_grad = product("ftd,ftn->dn", captions, grad_keys.reshape(clip_count, CAP, D))
            value_grad = product("ftd,ftn->dn", captions, grad_values.reshape(clip_count, CAP, D))
            qkv_grad = jnp.concatenate([query_grad, key_grad, value_grad], 1)
            grad_normed = product("fln,dn->fld", grad_proj, layer_weight[:, :D])
        first_value, first_back = jax.vjp(
            modulate, layer_hidden, layer_mod_parts[0], layer_mod_parts[1]
        )
        grad_in, d_shift1, d_scale1 = first_back(grad_normed)
        d_mod = jnp.concatenate([d_shift1, d_scale1, d_gate1, d_shift2, d_scale2, d_gate2], -1)[
            :, 0
        ]
        grad_hidden, layer_grads[layer_index], d_mod = (
            grad_in + grad_middle,
            (qkv_grad, out_grad, up_grad, down_grad),
            d_mod,
        )
        ada_grads[layer_index] = jnp.dot(
            signal_bf.astype(jnp.float32).T, d_mod, precision=HIGHEST_PRECISION
        )
        grad_signal = grad_signal + jnp.dot(
            d_mod, ada_full[layer_index].astype(jnp.float32).T, precision=HIGHEST_PRECISION
        )
    time_grad = jnp.dot(
        table_bf.astype(jnp.float32).T, signal_back(grad_signal)[0], precision=HIGHEST_PRECISION
    )
    in_grad = product("fld,flc->dc", to_bf16(grad_hidden), input_bf)
    grads_full = tuple(
        (jnp.stack([layer_grads[0][member], layer_grads[1][member]]) for member in range(4))
    ) + (jnp.stack(ada_grads), time_grad[None], jnp.stack([in_grad, fin_grad]))
    blocks = tuple((to_blocks(grad_part, data_count, head_count) for grad_part in grads_full))
    summed = (
        lax.psum_scatter(blocks[0], ("dp", "head"), scatter_dimension=1, tiled=True),
        lax.psum_scatter(blocks[1], ("dp", "head"), scatter_dimension=1, tiled=True),
        lax.psum_scatter(blocks[2], ("dp", "head"), scatter_dimension=1, tiled=True),
        lax.psum_scatter(blocks[3], ("dp", "head"), scatter_dimension=1, tiled=True),
        lax.psum_scatter(blocks[4], ("dp", "head"), scatter_dimension=1, tiled=True),
        lax.psum_scatter(blocks[5], ("dp", "head"), scatter_dimension=1, tiled=True),
        lax.psum_scatter(blocks[6], ("dp", "head"), scatter_dimension=1, tiled=True),
    )
    shards = tuple((block[:, 0] for block in summed))
    square = sum((jnp.sum(shard * shard) for shard in shards))
    old_moments = (qkv_moment, out_moment, up_moment, down_moment)
    total_square, total_loss = lax.psum((square, loss_part), ("dp", "head"))
    grad_norm = jnp.sqrt(total_square)
    clip_scale = jnp.minimum(1.0, CLIP_NORM / (grad_norm + 1e-06))
    moments = tuple(
        (MUON_BETA * old_moments[member] + clip_scale * shards[member] for member in range(4))
    )
    moment_sizes = lax.psum(
        jnp.stack([jnp.sum(moment * moment, axis=(1, 2)) for moment in moments]), ("dp", "head")
    )
    coeff_a, coeff_b, coeff_c = NEWTON_COEFFS
    ortho_rows = tuple(
        (
            moments[member] / (jnp.sqrt(moment_sizes[member])[:, None, None] + 1e-07)
            for member in range(4)
        )
    )
    for ns_step in range(NS_STEPS):
        whole_rows = (
            lax.all_gather(ortho_rows[0], "dp", axis=1, tiled=True),
            lax.all_gather(ortho_rows[1], "dp", axis=1, tiled=True),
            lax.all_gather(ortho_rows[2], "dp", axis=1, tiled=True),
            lax.all_gather(ortho_rows[3], "dp", axis=1, tiled=True),
        )
        gram_parts = tuple(
            (
                exact_product("lrc,lkc->lrk", ortho_rows[member], whole_rows[member])
                for member in range(4)
            )
        )
        gram_rows = lax.psum((gram_parts[0], gram_parts[1], gram_parts[2], gram_parts[3]), "head")
        gram_once = tuple(
            (
                exact_product("lrk,lkc->lrc", gram_rows[member], whole_rows[member])
                for member in range(4)
            )
        )
        once_whole = (
            lax.all_gather(gram_once[0], "dp", axis=1, tiled=True),
            lax.all_gather(gram_once[1], "dp", axis=1, tiled=True),
            lax.all_gather(gram_once[2], "dp", axis=1, tiled=True),
            lax.all_gather(gram_once[3], "dp", axis=1, tiled=True),
        )
        gram_twice = tuple(
            (
                exact_product("lrk,lkc->lrc", gram_rows[member], once_whole[member])
                for member in range(4)
            )
        )
        ortho_rows = tuple(
            (
                coeff_a * ortho_rows[member]
                + coeff_b * gram_once[member]
                + coeff_c * gram_twice[member]
                for member in range(4)
            )
        )
    muon_weights = (qkv_weight, out_weight, up_weight, down_weight)
    muon_new = tuple(
        (
            muon_weights[member] * (1.0 - MUON_RATE * MUON_DECAY)
            - MUON_RATE
            * 0.2
            * math.sqrt(max(D, muon_weights[member].shape[2] * head_count))
            * ortho_rows[member]
            for member in range(4)
        )
    )
    step_count = adam_step[0].astype(jnp.float32)
    ada_new, ada_first_new, ada_second_new = adam_update(
        ada_weight, clip_scale * shards[4], ada_first, ada_second, step_count
    )
    time_new, time_first_new, time_second_new = adam_update(
        time_weight, clip_scale * shards[5][0], time_first, time_second, step_count
    )
    io_new, io_first_new, io_second_new = adam_update(
        io_weight, clip_scale * shards[6], io_first, io_second, step_count
    )
    return (
        total_loss,
        grad_norm,
        pooled_out,
        muon_new[0],
        moments[0],
        muon_new[1],
        moments[1],
        muon_new[2],
        moments[2],
        muon_new[3],
        moments[3],
        ada_new,
        ada_first_new,
        ada_second_new,
        time_new,
        time_first_new,
        time_second_new,
        io_new,
        io_first_new,
        io_second_new,
    )


def solution(mesh):
    placed = (
        P("dp", "head", None),
        P("dp", "head", None),
        P("dp"),
        P("dp", None, None),
        P("dp"),
        P("dp"),
        P(),
        P(None, "dp", "head"),
        P(None, "dp", "head"),
        P(None, "dp", "head"),
        P(None, "dp", "head"),
        P(None, "dp", "head"),
        P("dp", "head"),
        P(None, "dp", "head"),
        P(None, "dp", "head"),
        P(None, "dp", "head"),
        P(None, "dp", "head"),
        P(None, "dp", "head"),
        P(None, "dp", "head"),
        P(None, "dp", "head"),
        P("dp", "head"),
        P("dp", "head"),
        P(None, "dp", "head"),
        P(None, "dp", "head"),
    )
    return jax.shard_map(
        body,
        mesh=mesh,
        in_specs=placed,
        out_specs=(
            P(),
            P(),
            P("dp", None),
            P(None, "dp", "head"),
            P(None, "dp", "head"),
            P(None, "dp", "head"),
            P(None, "dp", "head"),
            P(None, "dp", "head"),
            P(None, "dp", "head"),
            P(None, "dp", "head"),
            P(None, "dp", "head"),
            P(None, "dp", "head"),
            P(None, "dp", "head"),
            P(None, "dp", "head"),
            P("dp", "head"),
            P("dp", "head"),
            P("dp", "head"),
            P(None, "dp", "head"),
            P(None, "dp", "head"),
            P(None, "dp", "head"),
        ),
        check_vma=False,
    )
```

profile of v0, /device:TPU:11, one launch (start us, length us, event | category | flops | bytes accessed | tf_op | source)
XLA Modules:
  0.0 5443.6 jit_solution(9667576644979574312)
XLA Ops:
  77.0 69.8 %all-gather.139.cloned.1.call-done = bf16[2,3072,576]{2,1,0:T(8,128)(2,1)} async-done(((bf16[2,96,576]{2,1,0:T(8,128)(2,1)}), bf16[2,3072,576]{2,1,0:T(8,128)(2,1)}) %all-gather.139.cloned.1.call-update) | async-done | bytes 7077904 | tf_op jit(solution)/shard_map/all_gather | solution.py:173
  173.0 78.2 %all-gather.137.cloned.1.call-done = bf16[2,3072,1152]{2,1,0:T(8,128)(2,1)} async-done(((bf16[2,96,1152]{2,1,0:T(8,128)(2,1)}), bf16[2,3072,1152]{2,1,0:T(8,128)(2,1)}) %all-gather.137.cloned.1.call-update) | async-done | bytes 14155792 | tf_op jit(solution)/shard_map/all_gather | solution.py:177
  415.1 72.6 %all-gather.145.cloned.1.call-done = bf16[2,3072,768]{2,1,0:T(8,128)(2,1)} async-done(((bf16[2,96,768]{2,1,0:T(8,128)(2,1)}), bf16[2,3072,768]{2,1,0:T(8,128)(2,1)}) %all-gather.145.cloned.1.call-update) | async-done | bytes 9437200 | tf_op jit(solution)/shard_map/all_gather | solution.py:176
  823.1 85.0 %while.55 = (s32[]{:T(128)}, bf16[3,832,3,64]{1,3,2,0:T(8,128)(2,1)}, bf16[3,832,3,64]{1,3,2,0:T(8,128)(2,1)}, bf16[3,832,3,64]{1,3,2,0:T(8,128)(2,1)}, bf16[3,8...) while((s32[]{:T(128)}, ...), condition=%wide.region_45.46_spmd, body=%wide.region_43.45_spmd.sunk | while | flops 1354786304 | bytes 121415616 | solution.py:335
  1353.1 175.0 %reduce-scatter.7.cloned.1.call-done = f32[2,1,96,576]{3,2,0,1:T(8,128)} async-done(((f32[2,32,96,576]{3,2,0,1:T(8,128)}), f32[2,1,96,576]{3,2,0,1:T(8,128)}) %reduce-scatter.7.cloned.1.call-update) | async-done | bytes 442384 | tf_op jit(solution)/shard_map/reduce_scatter | solution.py:381
  1531.2 210.7 %reduce-scatter.11.cloned.1.call-done = f32[2,1,96,768]{3,2,0,1:T(8,128)} async-done(((f32[2,32,96,768]{3,2,0,1:T(8,128)}), f32[2,1,96,768]{3,2,0,1:T(8,128)}) %reduce-scatter.11.cloned.1.call-update) | async-done | bytes 589840 | tf_op jit(solution)/shard_map/reduce_scatter | solution.py:383
  1744.5 210.5 %reduce-scatter.13.cloned.1.call-done = f32[2,1,96,768]{3,2,0,1:T(8,128)} async-done(((f32[2,32,96,768]{3,2,0,1:T(8,128)}), f32[2,1,96,768]{3,2,0,1:T(8,128)}) %reduce-scatter.13.cloned.1.call-update) | async-done | bytes 589840 | tf_op jit(solution)/shard_map/reduce_scatter | solution.py:384
  1957.4 268.8 %reduce-scatter.15.cloned.1.call-done = f32[2,1,96,1152]{3,2,0,1:T(8,128)} async-done(((f32[2,32,96,1152]{3,2,0,1:T(8,128)}), f32[2,1,96,1152]{3,2,0,1:T(8,128)}) %reduce-scatter.15.cloned.1.call-update) | async-done | bytes 884752 | tf_op jit(solution)/shard_map/reduce_scatter | solution.py:385
  2436.2 74.1 %all-gather.95.cloned.1.call-done = f32[2,768,768]{2,1,0:T(8,128)} async-done(((f32[2,96,768]{2,1,0:T(8,128)}), f32[2,768,768]{2,1,0:T(8,128)}) %all-gather.95.cloned.1.call-update) | async-done | bytes 4718608 | tf_op jit(solution)/shard_map/all_gather | solution.py:412
  2518.1 73.2 %all-gather.115.cloned.1.call-done = f32[2,768,768]{2,1,0:T(8,128)} async-done(((f32[2,96,768]{2,1,0:T(8,128)}), f32[2,768,768]{2,1,0:T(8,128)}) %all-gather.115.cloned.1.call-update) | async-done | bytes 4718608 | tf_op jit(solution)/shard_map/all_gather | solution.py:413
  2779.0 75.4 %all-gather.117.cloned.1.call-done = f32[2,768,768]{2,1,0:T(8,128)} async-done(((f32[2,96,768]{2,1,0:T(8,128)}), f32[2,768,768]{2,1,0:T(8,128)}) %all-gather.117.cloned.1.call-update) | async-done | bytes 4718608 | tf_op jit(solution)/shard_map/all_gather | solution.py:432
  2860.7 74.7 %all-gather.97.cloned.1.call-done = f32[2,768,768]{2,1,0:T(8,128)} async-done(((f32[2,96,768]{2,1,0:T(8,128)}), f32[2,768,768]{2,1,0:T(8,128)}) %all-gather.97.cloned.1.call-update) | async-done | bytes 4718608 | tf_op jit(solution)/shard_map/all_gather | solution.py:431
  3059.6 74.2 %all-gather.119.cloned.1.call-done = f32[2,768,768]{2,1,0:T(8,128)} async-done(((f32[2,96,768]{2,1,0:T(8,128)}), f32[2,768,768]{2,1,0:T(8,128)}) %all-gather.119.cloned.1.call-update) | async-done | bytes 4718608 | tf_op jit(solution)/shard_map/all_gather | solution.py:413
  3141.7 73.2 %all-gather.99.cloned.1.call-done = f32[2,768,768]{2,1,0:T(8,128)} async-done(((f32[2,96,768]{2,1,0:T(8,128)}), f32[2,768,768]{2,1,0:T(8,128)}) %all-gather.99.cloned.1.call-update) | async-done | bytes 4718608 | tf_op jit(solution)/shard_map/all_gather | solution.py:412
  3330.5 66.6 %all-gather.61.cloned.1.call-done = f32[2,768,576]{2,1,0:T(8,128)} async-done(((f32[2,96,576]{2,1,0:T(8,128)}), f32[2,768,576]{2,1,0:T(8,128)}) %all-gather.61.cloned.1.call-update) | async-done | bytes 3538960 | tf_op jit(solution)/shard_map/all_gather | solution.py:429
  3402.8 75.3 %all-gather.121.cloned.1.call-done = f32[2,768,768]{2,1,0:T(8,128)} async-done(((f32[2,96,768]{2,1,0:T(8,128)}), f32[2,768,768]{2,1,0:T(8,128)}) %all-gather.121.cloned.1.call-update) | async-done | bytes 4718608 | tf_op jit(solution)/shard_map/all_gather | solution.py:432
  3484.4 74.7 %all-gather.101.cloned.1.call-done = f32[2,768,768]{2,1,0:T(8,128)} async-done(((f32[2,96,768]{2,1,0:T(8,128)}), f32[2,768,768]{2,1,0:T(8,128)}) %all-gather.101.cloned.1.call-update) | async-done | bytes 4718608 | tf_op jit(solution)/shard_map/all_gather | solution.py:431
  3683.3 74.2 %all-gather.123.cloned.1.call-done = f32[2,768,768]{2,1,0:T(8,128)} async-done(((f32[2,96,768]{2,1,0:T(8,128)}), f32[2,768,768]{2,1,0:T(8,128)}) %all-gather.123.cloned.1.call-update) | async-done | bytes 4718608 | tf_op jit(solution)/shard_map/all_gather | solution.py:413
  3765.3 73.3 %all-gather.103.cloned.1.call-done = f32[2,768,768]{2,1,0:T(8,128)} async-done(((f32[2,96,768]{2,1,0:T(8,128)}), f32[2,768,768]{2,1,0:T(8,128)}) %all-gather.103.cloned.1.call-update) | async-done | bytes 4718608 | tf_op jit(solution)/shard_map/all_gather | solution.py:412
  3954.0 66.6 %all-gather.65.cloned.1.call-done = f32[2,768,576]{2,1,0:T(8,128)} async-done(((f32[2,96,576]{2,1,0:T(8,128)}), f32[2,768,576]{2,1,0:T(8,128)}) %all-gather.65.cloned.1.call-update) | async-done | bytes 3538960 | tf_op jit(solution)/shard_map/all_gather | solution.py:429
  4026.3 75.3 %all-gather.125.cloned.1.call-done = f32[2,768,768]{2,1,0:T(8,128)} async-done(((f32[2,96,768]{2,1,0:T(8,128)}), f32[2,768,768]{2,1,0:T(8,128)}) %all-gather.125.cloned.1.call-update) | async-done | bytes 4718608 | tf_op jit(solution)/shard_map/all_gather | solution.py:432
  4107.8 74.7 %all-gather.105.cloned.1.call-done = f32[2,768,768]{2,1,0:T(8,128)} async-done(((f32[2,96,768]{2,1,0:T(8,128)}), f32[2,768,768]{2,1,0:T(8,128)}) %all-gather.105.cloned.1.call-update) | async-done | bytes 4718608 | tf_op jit(solution)/shard_map/all_gather | solution.py:431
  4233.5 66.6 %all-gather.67.cloned.1.call-done = f32[2,768,576]{2,1,0:T(8,128)} async-done(((f32[2,96,576]{2,1,0:T(8,128)}), f32[2,768,576]{2,1,0:T(8,128)}) %all-gather.67.cloned.1.call-update) | async-done | bytes 3538960 | tf_op jit(solution)/shard_map/all_gather | solution.py:410
  4306.9 74.1 %all-gather.127.cloned.1.call-done = f32[2,768,768]{2,1,0:T(8,128)} async-done(((f32[2,96,768]{2,1,0:T(8,128)}), f32[2,768,768]{2,1,0:T(8,128)}) %all-gather.127.cloned.1.call-update) | async-done | bytes 4718608 | tf_op jit(solution)/shard_map/all_gather | solution.py:413
  4388.8 73.3 %all-gather.107.cloned.1.call-done = f32[2,768,768]{2,1,0:T(8,128)} async-done(((f32[2,96,768]{2,1,0:T(8,128)}), f32[2,768,768]{2,1,0:T(8,128)}) %all-gather.107.cloned.1.call-update) | async-done | bytes 4718608 | tf_op jit(solution)/shard_map/all_gather | solution.py:412
  4649.8 75.3 %all-gather.129.cloned.1.call-done = f32[2,768,768]{2,1,0:T(8,128)} async-done(((f32[2,96,768]{2,1,0:T(8,128)}), f32[2,768,768]{2,1,0:T(8,128)}) %all-gather.129.cloned.1.call-update) | async-done | bytes 4718608 | tf_op jit(solution)/shard_map/all_gather | solution.py:432
  4731.4 74.6 %all-gather.109.cloned.1.call-done = f32[2,768,768]{2,1,0:T(8,128)} async-done(((f32[2,96,768]{2,1,0:T(8,128)}), f32[2,768,768]{2,1,0:T(8,128)}) %all-gather.109.cloned.1.call-update) | async-done | bytes 4718608 | tf_op jit(solution)/shard_map/all_gather | solution.py:431
  4930.2 74.3 %all-gather.131.cloned.1.call-done = f32[2,768,768]{2,1,0:T(8,128)} async-done(((f32[2,96,768]{2,1,0:T(8,128)}), f32[2,768,768]{2,1,0:T(8,128)}) %all-gather.131.cloned.1.call-update) | async-done | bytes 4718608 | tf_op jit(solution)/shard_map/all_gather | solution.py:413
  5012.2 73.2 %all-gather.111.cloned.1.call-done = f32[2,768,768]{2,1,0:T(8,128)} async-done(((f32[2,96,768]{2,1,0:T(8,128)}), f32[2,768,768]{2,1,0:T(8,128)}) %all-gather.111.cloned.1.call-update) | async-done | bytes 4718608 | tf_op jit(solution)/shard_map/all_gather | solution.py:412
  5200.6 67.0 %all-gather.73.cloned.1.call-done = f32[2,768,576]{2,1,0:T(8,128)} async-done(((f32[2,96,576]{2,1,0:T(8,128)}), f32[2,768,576]{2,1,0:T(8,128)}) %all-gather.73.cloned.1.call-update) | async-done | bytes 3538960 | tf_op jit(solution)/shard_map/all_gather | solution.py:429
  5273.4 75.3 %all-gather.113.cloned.1.call-done = f32[2,768,768]{2,1,0:T(8,128)} async-done(((f32[2,96,768]{2,1,0:T(8,128)}), f32[2,768,768]{2,1,0:T(8,128)}) %all-gather.113.cloned.1.call-update) | async-done | bytes 4718608 | tf_op jit(solution)/shard_map/all_gather | solution.py:431
  5355.1 73.9 %all-gather.133.cloned.1.call-done = f32[2,768,768]{2,1,0:T(8,128)} async-done(((f32[2,96,768]{2,1,0:T(8,128)}), f32[2,768,768]{2,1,0:T(8,128)}) %all-gather.133.cloned.1.call-update) | async-done | bytes 4718608 | tf_op jit(solution)/shard_map/all_gather | solution.py:432
  (976 shorter events, 2647.9 us)
Async XLA Ops:
  12.9 322.9 %all-gather.141.cloned.1.call-start = ((), (), s32[]{:S(2)}) async-start(), calls=%async_computation.59 | async-start | bytes 3244032 | tf_op jit(solution)/shard_map/all_gather | solution.py:174
  13.6 389.1 %all-gather.143.cloned.1.call-start = ((), (), s32[]{:S(2)}) async-start(), calls=%async_computation.60 | async-start | bytes 9732096 | tf_op jit(solution)/shard_map/all_gather | solution.py:175
  14.4 473.3 %all-gather.145.cloned.1.call-start = ((), (), s32[]{:S(2)}) async-start(), calls=%async_computation.61 | async-start | bytes 9732096 | tf_op jit(solution)/shard_map/all_gather | solution.py:176
  927.9 370.1 %all-reduce.14.cloned.1.call-start = ((), (), s32[]{:S(2)}) async-start(), calls=%async_computation.62 | async-start | bytes 327680
  1004.5 294.9 %reduce-scatter.17.cloned.1.call-start = ((), (), s32[]{:S(2)}) async-start(), calls=%async_computation.15 | async-start | bytes 3244032 | tf_op jit(solution)/shard_map/reduce_scatter | solution.py:386
  1024.2 327.3 %reduce-scatter.9.cloned.1.call-start = ((), (), s32[]{:S(2)}) async-start(), calls=%async_computation.11 | async-start | bytes 6488064 | tf_op jit(solution)/shard_map/reduce_scatter | solution.py:382
  1052.6 475.5 %reduce-scatter.7.cloned.1.call-start = ((), (), s32[]{:S(2)}) async-start(), calls=%async_computation.10 | async-start | bytes 16220160 | tf_op jit(solution)/shard_map/reduce_scatter | solution.py:381
  1126.2 615.8 %reduce-scatter.11.cloned.1.call-start = ((), (), s32[]{:S(2)}) async-start(), calls=%async_computation.12 | async-start | bytes 19464192 | tf_op jit(solution)/shard_map/reduce_scatter | solution.py:383
  1189.3 765.7 %reduce-scatter.13.cloned.1.call-start = ((), (), s32[]{:S(2)}) async-start(), calls=%async_computation.13 | async-start | bytes 19464192 | tf_op jit(solution)/shard_map/reduce_scatter | solution.py:384
  1256.8 969.4 %reduce-scatter.15.cloned.1.call-start = ((), (), s32[]{:S(2)}) async-start(), calls=%async_computation.14 | async-start | bytes 29196288 | tf_op jit(solution)/shard_map/reduce_scatter | solution.py:385
  1296.7 1062.4 %all-gather.75.cloned.1.call-start = ((), (), s32[]{:S(2)}) async-start(), calls=%async_computation.26 | async-start | bytes 1769472 | tf_op jit(solution)/shard_map/all_gather | solution.py:411
  2318.5 337.8 %all-reduce.24.cloned.1.call-start = ((), (), s32[]{:S(2)}) async-start(), calls=%async_computation.67 | async-start | bytes 4718592 | tf_op jit(solution)/shard_map/psum | solution.py:421
  2677.9 304.6 %all-gather.79.cloned.1.call-start = ((), (), s32[]{:S(2)}) async-start(), calls=%async_computation.28 | async-start | bytes 1769472 | tf_op jit(solution)/shard_map/all_gather | solution.py:411
  2706.5 346.4 %all-gather.59.cloned.1.call-start = ((), (), s32[]{:S(2)}) async-start(), calls=%async_computation.18 | async-start | bytes 4423680 | tf_op jit(solution)/shard_map/all_gather | solution.py:410
  2778.9 355.0 %all-gather.119.cloned.1.call-start = ((), (), s32[]{:S(2)}) async-start(), calls=%async_computation.48 | async-start | bytes 5308416 | tf_op jit(solution)/shard_map/all_gather | solution.py:413
  2860.7 354.2 %all-gather.99.cloned.1.call-start = ((), (), s32[]{:S(2)}) async-start(), calls=%async_computation.38 | async-start | bytes 5308416 | tf_op jit(solution)/shard_map/all_gather | solution.py:412
  2941.7 338.2 %all-reduce.22.cloned.1.call-start = ((), (), s32[]{:S(2)}) async-start(), calls=%async_computation.66 | async-start | bytes 4718592 | tf_op jit(solution)/shard_map/psum | solution.py:421
  3301.5 304.6 %all-gather.83.cloned.1.call-start = ((), (), s32[]{:S(2)}) async-start(), calls=%async_computation.30 | async-start | bytes 1769472 | tf_op jit(solution)/shard_map/all_gather | solution.py:411
  3330.1 346.4 %all-gather.63.cloned.1.call-start = ((), (), s32[]{:S(2)}) async-start(), calls=%async_computation.20 | async-start | bytes 4423680 | tf_op jit(solution)/shard_map/all_gather | solution.py:410
  3402.7 354.8 %all-gather.123.cloned.1.call-start = ((), (), s32[]{:S(2)}) async-start(), calls=%async_computation.50 | async-start | bytes 5308416 | tf_op jit(solution)/shard_map/all_gather | solution.py:413
  3484.3 354.3 %all-gather.103.cloned.1.call-start = ((), (), s32[]{:S(2)}) async-start(), calls=%async_computation.40 | async-start | bytes 5308416 | tf_op jit(solution)/shard_map/all_gather | solution.py:412
  3565.4 338.3 %all-reduce.20.cloned.1.call-start = ((), (), s32[]{:S(2)}) async-start(), calls=%async_computation.65 | async-start | bytes 4718592 | tf_op jit(solution)/shard_map/psum | solution.py:421
  3925.3 304.4 %all-gather.87.cloned.1.call-start = ((), (), s32[]{:S(2)}) async-start(), calls=%async_computation.32 | async-start | bytes 1769472 | tf_op jit(solution)/shard_map/all_gather | solution.py:411
  3953.6 346.5 %all-gather.67.cloned.1.call-start = ((), (), s32[]{:S(2)}) async-start(), calls=%async_computation.22 | async-start | bytes 4423680 | tf_op jit(solution)/shard_map/all_gather | solution.py:410
  4026.2 354.8 %all-gather.127.cloned.1.call-start = ((), (), s32[]{:S(2)}) async-start(), calls=%async_computation.52 | async-start | bytes 5308416 | tf_op jit(solution)/shard_map/all_gather | solution.py:413
  4107.8 354.3 %all-gather.107.cloned.1.call-start = ((), (), s32[]{:S(2)}) async-start(), calls=%async_computation.42 | async-start | bytes 5308416 | tf_op jit(solution)/shard_map/all_gather | solution.py:412
  4188.8 338.3 %all-reduce.18.cloned.1.call-start = ((), (), s32[]{:S(2)}) async-start(), calls=%async_computation.64 | async-start | bytes 4718592 | tf_op jit(solution)/shard_map/psum | solution.py:421
  4548.7 304.3 %all-gather.91.cloned.1.call-start = ((), (), s32[]{:S(2)}) async-start(), calls=%async_computation.34 | async-start | bytes 1769472 | tf_op jit(solution)/shard_map/all_gather | solution.py:411
  4577.3 346.1 %all-gather.71.cloned.1.call-start = ((), (), s32[]{:S(2)}) async-start(), calls=%async_computation.24 | async-start | bytes 4423680 | tf_op jit(solution)/shard_map/all_gather | solution.py:410
  4649.7 354.7 %all-gather.131.cloned.1.call-start = ((), (), s32[]{:S(2)}) async-start(), calls=%async_computation.54 | async-start | bytes 5308416 | tf_op jit(solution)/shard_map/all_gather | solution.py:413
  4731.4 354.0 %all-gather.111.cloned.1.call-start = ((), (), s32[]{:S(2)}) async-start(), calls=%async_computation.44 | async-start | bytes 5308416 | tf_op jit(solution)/shard_map/all_gather | solution.py:412
  4812.2 338.2 %all-reduce.16.cloned.1.call-start = ((), (), s32[]{:S(2)}) async-start(), calls=%async_computation.63 | async-start | bytes 4718592 | tf_op jit(solution)/shard_map/psum | solution.py:421
  (255 other events, 13214.7 us)
Sparse Core Ops, SparseCore 0:
  71.5 75.2 all-gather.138
  150.2 100.8 all-gather.136
  314.9 87.6 all-gather.142
  406.0 81.7 all-gather.144
  1004.6 120.2 all-reduce.13
  1130.3 102.1 reduce-scatter.16
  1238.1 113.3 reduce-scatter.8
  1358.4 169.6 reduce-scatter.6
  1535.7 206.2 reduce-scatter.10
  1749.3 205.6 reduce-scatter.12
  1962.5 263.6 reduce-scatter.14
  2432.2 78.0 all-gather.94
  2513.1 78.0 all-gather.114
  2776.3 78.0 all-gather.116
  2857.4 78.0 all-gather.96
  3055.8 78.0 all-gather.118
  3136.8 78.0 all-gather.98
  3329.7 67.3 all-gather.60
  3399.9 78.0 all-gather.120
  3481.0 78.0 all-gather.100
  3679.4 78.0 all-gather.122
  3760.5 78.0 all-gather.102
  4023.4 78.0 all-gather.124
  4104.5 78.0 all-gather.104
  4302.9 78.0 all-gather.126
  4384.0 78.0 all-gather.106
  4647.0 78.0 all-gather.128
  4727.9 78.0 all-gather.108
  4926.3 78.0 all-gather.130
  5007.3 78.0 all-gather.110
  5270.6 78.0 all-gather.112
  5351.0 78.0 all-gather.132
  (26 shorter events, 1439.4 us)
where the time goes:
time: 5470 us; the launch traced here: 5440 us
  waiting for transfers between devices  3990 us (73%)
  matrix products  643 us (12%)
  local copies, waits for them, and re-layouts  430 us (8%)
  blocking collectives  174 us (3%)
  other arithmetic  156 us (3%)
    all_gather x5, waiting for transfers between devices, body(): lax.all_gather(gram_once[3], 'dp', axis=1, tiled=True)  375 us
    all_gather x5, waiting for transfers between devices, body(): lax.all_gather(gram_once[2], 'dp', axis=1, tiled=True)  374 us
    all_gather x5, waiting for transfers between devices, body(): lax.all_gather(ortho_rows[3], 'dp', axis=1, tiled=True)  370 us
    all_gather x5, waiting for transfers between devices, body(): lax.all_gather(ortho_rows[2], 'dp', axis=1, tiled=True)  367 us
    dot_general x62, matrix products, exact_product(): return jnp.einsum(form, left, right, precision=HIGHEST_PRECISION)  346 us
    all_gather x5, waiting for transfers between devices, body(): lax.all_gather(gram_once[0], 'dp', axis=1, tiled=True)  333 us
    all_gather x5, waiting for transfers between devices, body(): lax.all_gather(ortho_rows[0], 'dp', axis=1, tiled=True)  332 us
    psum x5, waiting for transfers between devices, body(): lax.psum((gram_parts[0], gram_parts[1], gram_parts[2], gram_parts[3]), 'h...  285 us
  transfers between devices with their start and end apart: 61, of which 56 were waited for; matrix products, arithmetic and copies ran while one was open for 15% of the time, Pallas kernels for 0%

commit v1 on v0

--- a/solution.py
+++ b/solution.py
@@ -76,24 +76,6 @@
 
 def to_frames(heads):
     return lax.all_to_all(heads, "head", split_axis=1, concat_axis=3, tiled=True)
-
-
-def to_blocks(full_grad, data_count, head_count):
-    layers, rows_all, cols_all = full_grad.shape
-    grouped = full_grad.reshape(
-        layers, data_count, rows_all // data_count, head_count, cols_all // head_count
-    )
-    return grouped.transpose(0, 1, 3, 2, 4).reshape(
-        layers, data_count * head_count, rows_all // data_count, cols_all // head_count
-    )
-
-
-def from_blocks(blocks, data_count, head_count):
-    layers, total_blocks, block_rows, block_cols = blocks.shape
-    grouped = blocks.reshape(layers, data_count, head_count, block_rows, block_cols)
-    return grouped.transpose(0, 1, 3, 2, 4).reshape(
-        layers, data_count * block_rows, head_count * block_cols
-    )
 
 
 def scores_of(query, keys, key_mask):
@@ -169,29 +151,59 @@
     length = frame_rows * head_count
     head_share = D // head_count
     local_heads = head_share // HDIM
+    rows_own = qkv_weight.shape[1]
+    own_row = lax.axis_index("dp") * rows_own
+
+    def whole_weight(shard):
+        layers, rows, cols = shard.shape
+        blocks = lax.all_gather(to_bf16(shard), ("head", "dp"), axis=0, tiled=False)
+        blocks = blocks.reshape(head_count, data_count, layers, rows, cols)
+        return blocks.transpose(2, 1, 3, 0, 4).reshape(layers, D, head_count * cols)
+
+    small = jnp.concatenate(
+        [time_weight.reshape(-1), io_weight.reshape(-1), jnp.pad(timesteps, (0, 125))]
+    )
+    small_all = lax.all_gather(small, ("dp", "head"), axis=0, tiled=False)
+    small_all = small_all.reshape(data_count, head_count, -1)
+    time_size = time_weight.size
+    io_size = io_weight.size
+    time_full = to_bf16(
+        small_all[:, :, :time_size]
+        .reshape(data_count, head_count, rows_own, -1)
+        .transpose(0, 2, 1, 3)
+        .reshape(D, D)
+    )
+    io_full = to_bf16(
+        small_all[:, :, time_size : time_size + io_size]
+        .reshape(data_count, head_count, 2, rows_own, -1)
+        .transpose(2, 0, 3, 1, 4)
+        .reshape(2, D, -1)
+    )
+    times_all = small_all[:, 0, time_size + io_size : time_size + io_size + clip_count].reshape(-1)
     gathered = (
-        lax.all_gather(to_bf16(qkv_weight)[:, None], ("dp", "head"), axis=1, tiled=True),
-        lax.all_gather(to_bf16(out_weight)[:, None], ("dp", "head"), axis=1, tiled=True),
-        lax.all_gather(to_bf16(up_weight)[:, None], ("dp", "head"), axis=1, tiled=True),
-        lax.all_gather(to_bf16(down_weight)[:, None], ("dp", "head"), axis=1, tiled=True),
-        lax.all_gather(to_bf16(ada_weight)[:, None], ("dp", "head"), axis=1, tiled=True),
-        lax.all_gather(to_bf16(time_weight)[None, None], ("dp", "head"), axis=1, tiled=True),
-        lax.all_gather(to_bf16(io_weight)[:, None], ("dp", "head"), axis=1, tiled=True),
-    )
-    qkv_full, out_full, up_full, down_full, ada_full, time_full, io_full = tuple(
-        (from_blocks(blocks, data_count, head_count) for blocks in gathered)
-    )
-    time_full = time_full[0]
+        [whole_weight(qkv_weight[layer : layer + 1])[0] for layer in range(2)],
+        [whole_weight(out_weight[layer : layer + 1])[0] for layer in range(2)],
+    )
+    qkv_full, out_full = gathered
+    up_full, down_full = [None, None], [None, None]
+    for layer in range(2):
+        pair = whole_weight(jnp.stack([up_weight[layer], down_weight[layer]]))
+        up_full[layer], down_full[layer] = pair[0], pair[1]
     keep_mask = jnp.arange(CAP)[None, :] < cap_len[:, None]
     cap_mean = product("ft,ftd->fd", keep_mask.astype(jnp.bfloat16), captions) / cap_len[
         :, None
     ].astype(jnp.float32)
     cap_unit = cap_mean * lax.rsqrt(jnp.mean(cap_mean * cap_mean, -1, keepdims=True) + 1e-06)
     cap_all = lax.all_gather(cap_unit, "dp", axis=0, tiled=True)
-    table_bf = to_bf16(time_table(timesteps, D))
+    table_bf = to_bf16(time_table(times_all, D))
     time_hidden = jnp.dot(table_bf, time_full, preferred_element_type=jnp.float32)
-    signal, signal_back = jax.vjp(double_silu, time_hidden)
-    signal_bf = to_bf16(signal)
+    signal_bf = to_bf16(double_silu(time_hidden))
+    signal_own = lax.dynamic_slice_in_dim(signal_bf, own_row, rows_own, 1)
+    table_own = lax.dynamic_slice_in_dim(table_bf, own_row, rows_own, 1)
+    ada_bf = to_bf16(ada_weight)
+    mod_part = product("fd,ldn->fln", signal_own, ada_bf)
+    mod_own = lax.psum_scatter(mod_part, "dp", scatter_dimension=0, tiled=True)
+    mod_all = lax.all_gather(mod_own, "head", axis=2, tiled=True)
     blended = (1.0 - timesteps)[:, None, None] * clean_latents + timesteps[
         :, None, None
     ] * noise_draw
@@ -202,9 +214,7 @@
         return values.reshape(clip_count, rows_count, local_heads, HDIM)
 
     def layer_forward(layer_index, hidden):
-        modulation = jnp.dot(
-            signal_bf, ada_full[layer_index], preferred_element_type=jnp.float32
-        ).reshape(clip_count, 1, 6, D)
+        modulation = mod_all[:, layer_index].reshape(clip_count, 1, 6, D)
         mod_parts = [modulation[:, :, member] for member in range(6)]
         normed = to_bf16(modulate(hidden, mod_parts[0], mod_parts[1]))
         weight = qkv_full[layer_index]
@@ -288,7 +298,6 @@
     fin_grad = product("flc,fld->dc", grad_pred, final_bf)
     layer_grads = [None, None]
     ada_grads = [None, None]
-    grad_signal = jnp.zeros_like(signal)
     for layer_index in (1, 0):
         layer_kept = saved_layers[layer_index]
         (
@@ -363,30 +372,52 @@
             (qkv_grad, out_grad, up_grad, down_grad),
             d_mod,
         )
-        ada_grads[layer_index] = jnp.dot(
-            signal_bf.astype(jnp.float32).T, d_mod, precision=HIGHEST_PRECISION
-        )
-        grad_signal = grad_signal + jnp.dot(
-            d_mod, ada_full[layer_index].astype(jnp.float32).T, precision=HIGHEST_PRECISION
-        )
-    time_grad = jnp.dot(
-        table_bf.astype(jnp.float32).T, signal_back(grad_signal)[0], precision=HIGHEST_PRECISION
-    )
+        ada_grads[layer_index] = d_mod
     in_grad = product("fld,flc->dc", to_bf16(grad_hidden), input_bf)
-    grads_full = tuple(
-        (jnp.stack([layer_grads[0][member], layer_grads[1][member]]) for member in range(4))
-    ) + (jnp.stack(ada_grads), time_grad[None], jnp.stack([in_grad, fin_grad]))
-    blocks = tuple((to_blocks(grad_part, data_count, head_count) for grad_part in grads_full))
-    summed = (
-        lax.psum_scatter(blocks[0], ("dp", "head"), scatter_dimension=1, tiled=True),
-        lax.psum_scatter(blocks[1], ("dp", "head"), scatter_dimension=1, tiled=True),
-        lax.psum_scatter(blocks[2], ("dp", "head"), scatter_dimension=1, tiled=True),
-        lax.psum_scatter(blocks[3], ("dp", "head"), scatter_dimension=1, tiled=True),
-        lax.psum_scatter(blocks[4], ("dp", "head"), scatter_dimension=1, tiled=True),
-        lax.psum_scatter(blocks[5], ("dp", "head"), scatter_dimension=1, tiled=True),
-        lax.psum_scatter(blocks[6], ("dp", "head"), scatter_dimension=1, tiled=True),
-    )
-    shards = tuple((block[:, 0] for block in summed))
+    d_mod_own = lax.psum_scatter(
+        jnp.stack(ada_grads, 1), "head", scatter_dimension=2, tiled=True
+    )
+    d_mod_all = lax.all_gather(d_mod_own, "dp", axis=0, tiled=True)
+    ada_grad = exact_product("fd,fln->ldn", signal_own.astype(jnp.float32), d_mod_all)
+    grad_signal = lax.psum(
+        exact_product("fln,ldn->fd", d_mod_all, ada_bf.astype(jnp.float32)), "head"
+    )
+    hidden_own = lax.dynamic_slice_in_dim(time_hidden, own_row, rows_own, 1)
+    signal_own_value, signal_back = jax.vjp(double_silu, hidden_own)
+    grad_cond = lax.all_gather(signal_back(grad_signal)[0], "dp", axis=1, tiled=True)
+    time_cols = time_weight.shape[1]
+    time_grad = exact_product(
+        "fd,fn->dn",
+        table_own.astype(jnp.float32),
+        lax.dynamic_slice_in_dim(grad_cond, lax.axis_index("head") * time_cols, time_cols, 1),
+    )
+
+    def scatter(parts):
+        stacked = jnp.stack(parts)
+        layers, rows_all, cols_all = stacked.shape
+        blocks = stacked.reshape(
+            layers, data_count, rows_all // data_count, head_count, cols_all // head_count
+        ).transpose(3, 1, 0, 2, 4)
+        blocks = blocks.reshape((head_count * data_count,) + blocks.shape[2:])
+        return lax.psum_scatter(blocks, ("head", "dp"), scatter_dimension=0, tiled=True)[0]
+
+    per_layer = [
+        (
+            scatter([layer_grads[layer][0]])[0],
+            scatter([layer_grads[layer][1]])[0],
+            scatter([layer_grads[layer][2], layer_grads[layer][3]]),
+        )
+        for layer in range(2)
+    ]
+    shards = (
+        jnp.stack([per_layer[0][0], per_layer[1][0]]),
+        jnp.stack([per_layer[0][1], per_layer[1][1]]),
+        jnp.stack([per_layer[0][2][0], per_layer[1][2][0]]),
+        jnp.stack([per_layer[0][2][1], per_layer[1][2][1]]),
+        ada_grad,
+        time_grad[None],
+        scatter([in_grad, fin_grad]),
+    )
     square = sum((jnp.sum(shard * shard) for shard in shards))
     old_moments = (qkv_moment, out_moment, up_moment, down_moment)
     total_square, total_loss = lax.psum((square, loss_part), ("dp", "head"))
@@ -395,56 +426,43 @@
     moments = tuple(
         (MUON_BETA * old_moments[member] + clip_scale * shards[member] for member in range(4))
     )
-    moment_sizes = lax.psum(
-        jnp.stack([jnp.sum(moment * moment, axis=(1, 2)) for moment in moments]), ("dp", "head")
-    )
     coeff_a, coeff_b, coeff_c = NEWTON_COEFFS
+    wide = max(moment.shape[2] for moment in moments)
+    sent = jnp.concatenate(
+        [jnp.pad(moment, ((0, 0), (0, 0), (0, wide - moment.shape[2]))) for moment in moments]
+    )
+    matrices = sent.shape[0]
+    sent = jnp.pad(sent, ((0, data_count - matrices), (0, 0), (0, 0)))
+    own_matrix = lax.all_to_all(sent, "dp", split_axis=0, concat_axis=0, tiled=True)
+    own_matrix = own_matrix.reshape(D, wide)
+
+    def near_product(form, left, right):
+        return jnp.einsum(form, left, right, precision=lax.Precision.HIGH)
+
+    gram = lax.psum(near_product("rc,kc->rk", own_matrix, own_matrix), "head")
+    unit = jnp.eye(D, dtype=jnp.float32)
+    size_frob = jnp.sqrt(jnp.sum(gram * unit)) + 1e-07
+    gram = gram / (size_frob * size_frob)
+    factor = None
+    for ns_step in range(NS_STEPS):
+        poly = coeff_a * unit + coeff_b * gram + coeff_c * near_product("rk,kj->rj", gram, gram)
+        factor = poly if factor is None else near_product("rk,kj->rj", poly, factor)
+        if ns_step < NS_STEPS - 1:
+            gram = near_product("rk,kj->rj", near_product("rk,kj->rj", poly, gram), poly)
+    ortho_matrix = near_product("rk,kc->rc", factor, own_matrix) / size_frob
+    ortho_back = lax.all_to_all(
+        ortho_matrix.reshape(data_count, rows_own, wide),
+        "dp",
+        split_axis=0,
+        concat_axis=0,
+        tiled=True,
+    )
     ortho_rows = tuple(
         (
-            moments[member] / (jnp.sqrt(moment_sizes[member])[:, None, None] + 1e-07)
+            ortho_back[2 * member : 2 * member + 2, :, : moments[member].shape[2]]
             for member in range(4)
         )
     )
-    for ns_step in range(NS_STEPS):
-        whole_rows = (
-            lax.all_gather(ortho_rows[0], "dp", axis=1, tiled=True),
-            lax.all_gather(ortho_rows[1], "dp", axis=1, tiled=True),
-            lax.all_gather(ortho_rows[2], "dp", axis=1, tiled=True),
-            lax.all_gather(ortho_rows[3], "dp", axis=1, tiled=True),
-        )
-        gram_parts = tuple(
-            (
-                exact_product("lrc,lkc->lrk", ortho_rows[member], whole_rows[member])
-                for member in range(4)
-            )
-        )
-        gram_rows = lax.psum((gram_parts[0], gram_parts[1], gram_parts[2], gram_parts[3]), "head")
-        gram_once = tuple(
-            (
-                exact_product("lrk,lkc->lrc", gram_rows[member], whole_rows[member])
-                for member in range(4)
-            )
-        )
-        once_whole = (
-            lax.all_gather(gram_once[0], "dp", axis=1, tiled=True),
-            lax.all_gather(gram_once[1], "dp", axis=1, tiled=True),
-            lax.all_gather(gram_once[2], "dp", axis=1, tiled=True),
-            lax.all_gather(gram_once[3], "dp", axis=1, tiled=True),
-        )
-        gram_twice = tuple(
-            (
-                exact_product("lrk,lkc->lrc", gram_rows[member], once_whole[member])
-                for member in range(4)
-            )
-        )
-        ortho_rows = tuple(
-            (
-                coeff_a * ortho_rows[member]
-                + coeff_b * gram_once[member]
-                + coeff_c * gram_twice[member]
-                for member in range(4)
-            )
-        )
     muon_weights = (qkv_weight, out_weight, up_weight, down_weight)
     muon_new = tuple(
         (

time: 5470 us -> 2450 us (0.45)
  waiting for transfers between devices: 3990 us -> 1320 us
  matrix products: 643 us -> 328 us
    all_gather x46 -> x6, waiting for transfers between devices: 2740 us -> 192 us  [whole_weight(): blocks = lax.all_gather(to_bf16(shard), ('head', 'dp'), axis=0, tiled=False)]
    dot_general x62 -> x5, matrix products: 346 us -> 5.6 us  [exact_product(): return jnp.einsum(form, left, right, precision=HIGHEST_PRECISION)]
    psum x5 -> x1, waiting for transfers between devices: 285 us -> 57.8 us  [body(): gram = lax.psum(near_product('rc,kc->rk', own_matrix, own_matrix), 'head')]
    unnamed x59 -> x21, waiting for transfers between devices: 0.95 us -> 190 us
    reduce_scatter x6, waiting for transfers between devices: 916 us -> 757 us  [scatter(): lax.psum_scatter(blocks, ('head', 'dp'), scatter_dimension=0, tiled=True)[0]]
    dot_general x75 -> x76, matrix products: 249 us -> 254 us  [product(): return jnp.einsum(form, left, right, preferred_element_type=jnp.float32)]
  transfers between devices with their start and end apart: 61 -> 22, of which waited for: 56 -> 16; matrix products, arithmetic and copies ran while one was open for 15% -> 17% of each run, Pallas kernels for 0% -> 0%
where the time goes in v1:
time: 2450 us; the launch traced here: 2430 us
  waiting for transfers between devices  1320 us (54%)
  local copies, waits for them, and re-layouts  408 us (17%)
  matrix products  328 us (13%)
  blocking collectives  194 us (8%)
  other arithmetic  131 us (5%)
  starting transfers between devices  29 us (1%)
  between operations  26.4 us (1%)
    reduce_scatter x6, waiting for transfers between devices, scatter(): lax.psum_scatter(blocks, ('head', 'dp'), scatter_dimension=0, tiled=True)[0]  757 us
    dot_general x76, matrix products, product(): return jnp.einsum(form, left, right, preferred_element_type=jnp.float32)  254 us
    all_gather x6, waiting for transfers between devices, whole_weight(): blocks = lax.all_gather(to_bf16(shard), ('head', 'dp'), axis=0, tiled=False)  192 us
    unnamed x21, waiting for transfers between devices  190 us
    dot_general x19, matrix products, near_product(): return jnp.einsum(form, left, right, precision=lax.Precision.HIGH)  67 us
    psum x1, waiting for transfers between devices, body(): gram = lax.psum(near_product('rc,kc->rk', own_matrix, own_matrix), 'head')  57.8 us
    all_to_all x2, waiting for transfers between devices, to_frames(): lax.all_to_all(heads, 'head', split_axis=1, concat_axis=3, tiled=True)  55.4 us
    all_to_all x1, blocking collectives, body(): lax.all_to_all(sent, 'dp', split_axis=0, concat_axis=0, tiled=True)  54.5 us
  transfers between devices with their start and end apart: 22, of which 16 were waited for; matrix products, arithmetic and copies ran while one was open for 17% of the time, Pallas kernels for 0%

profile of v1, /device:TPU:11, one launch (start us, length us, event | category | flops | bytes accessed | tf_op | source)
XLA Modules:
  0.0 2432.5 jit_solution(8028662096897967259)
XLA Ops:
  13.5 135.5 %all-reduce.14.cloned.1.call-done = f32[624640]{0:T(1024)} async-done(((f32[624640]{0:T(1024)}), f32[624640]{0:T(1024)}) %all-reduce.14.cloned.1.call-update) | async-done | bytes 2498576
  184.3 53.6 %all-reduce.16.cloned.1.call-done = f32[24,2,1152]{2,1,0:T(2,128)} async-done(((f32[24,2,1152]{2,1,0:T(2,128)}), f32[24,2,1152]{2,1,0:T(2,128)}) %all-reduce.16.cloned.1.call-update) | async-done | bytes 221200
  247.8 57.0 %all-gather.18.cloned.1.call-done = bf16[32,96,576]{2,1,0:T(8,128)(2,1)} async-done(((bf16[1,96,576]{2,1,0:T(8,128)(2,1)}), bf16[32,96,576]{2,1,0:T(8,128)(2,1)}) %all-gather.18.cloned.1.call-update) | async-done | bytes 3538960 | tf_op jit(solution)/shard_map/all_gather | solution.py:159
  344.1 21.6 all-gather.5
  379.9 41.0 %all-gather.20.cloned.1.call-done = bf16[32,96,192]{2,1,0:T(8,128)(2,1)} async-done(((bf16[1,96,192]{2,1,0:T(8,128)(2,1)}), bf16[32,96,192]{2,1,0:T(8,128)(2,1)}) %all-gather.20.cloned.1.call-update) | async-done | bytes 1179664 | tf_op jit(solution)/shard_map/all_gather | solution.py:159
  428.8 56.5 %all-gather.22.cloned.1.call-done = bf16[32,96,576]{2,1,0:T(8,128)(2,1)} async-done(((bf16[1,96,576]{2,1,0:T(8,128)(2,1)}), bf16[32,96,576]{2,1,0:T(8,128)(2,1)}) %all-gather.22.cloned.1.call-update) | async-done | bytes 3538960 | tf_op jit(solution)/shard_map/all_gather | solution.py:159
  520.0 25.1 %while.52 = (s32[]{:T(128)}, bf16[3,832,3,64]{1,3,2,0:T(8,128)(2,1)}, f32[3,3,832,1]{2,1,3,0:T(4,128)}, bf16[3,832,3,64]{1,3,2,0:T(8,128)(2,1)}, bf16[3,832,3,64...) while((s32[]{:T(128)}, bf16[3,832,3,64]{1,3,2,0:T(8,128)(2,1)}, ...), condition=%wide.region_6.7_spmd, body=%wide.region_3.6_spmd.sunk | while | flops 550475328 | bytes 26382680 | solution.py:236
  584.4 12.4 copy.461
  617.2 37.0 %all-gather.14.cloned.1.call-done = bf16[32,2,96,768]{3,2,1,0:T(8,128)(2,1)} async-done(((bf16[1,2,96,768]{3,2,1,0:T(8,128)(2,1)}), bf16[32,2,96,768]{3,2,1,0:T(8,128)(2,1)}) %all-gather.14.cloned.1.call-update) | async-done | bytes 9437200 | tf_op jit(solution)/shard_map/all_gather | solution.py:159
  654.3 12.5 copy.462
  723.8 17.2 while.53
  772.5 12.1 fusion.116
  799.5 25.0 %while.54 = (s32[]{:T(128)}, bf16[3,208,12,64]{1,3,2,0:T(8,128)(2,1)}, bf16[3,256,12,64]{1,3,2,0:T(8,128)(2,1)}, bf16[3,256,12,64]{1,3,2,0:T(8,128)(2,1)}, bf16[...) while((s32[]{:T(128)}, ...), condition=%wide.region_39.40_spmd, body=%wide.region_37.39_spmd.sunk | while | flops 415602240 | bytes 31716532 | solution.py:344
  866.3 18.8 all-to-all-done.2
  895.4 85.0 %while.55 = (s32[]{:T(128)}, bf16[3,832,3,64]{1,3,2,0:T(8,128)(2,1)}, bf16[3,832,3,64]{1,3,2,0:T(8,128)(2,1)}, bf16[3,832,3,64]{1,3,2,0:T(8,128)(2,1)}, bf16[3,8...) while((s32[]{:T(128)}, ...), condition=%wide.region_46.47_spmd, body=%wide.region_44.46_spmd.sunk | while | flops 1354786304 | bytes 121415616 | solution.py:344
  1012.8 44.7 %all-to-all-done.3 = bf16[3,832,3,192]{3,2,0,1:T(4,128)(2,1)} async-done(((bf16[3,832,3,192]{3,2,0,1:T(4,128)(2,1)}), bf16[3,832,3,192]{3,2,0,1:T(4,128)(2,1)}, u32[]{:S(2)}, u32[]{:S(2)}) %all-to-all-start.3) | async-done | bytes 2875424 | tf_op jit(solution)/shard_map/all_to_all | solution.py:78
  1170.8 12.6 stack.81
  1192.0 12.5 stack.80
  1237.7 12.6 stack.84
  1259.0 12.6 stack.83
  1300.2 20.8 all_gather.64
  1321.5 14.8 psum.37
  1337.2 25.0 %all-gather.6 = f32[8,96,24]{1,2,0:T(8,128)S(1)} all-gather(f32[1,96,24]{1,2,0:T(8,128)S(1)} %fusion.276), channel_id=1, replica_groups=mesh['dp'=8,'head'=4] {'dp'}, dimensions={0}, use_global_device_ids=true | all-gather | bytes 82944 | tf_op jit(solution)/shard_map/all_gather | solution.py:387
  1366.8 81.1 %reduce-scatter.16.cloned.1.call-done = f32[1,1,96,192]{3,2,1,0:T(8,128)} async-done(((f32[32,1,96,192]{3,2,1,0:T(8,128)}), f32[1,1,96,192]{3,2,1,0:T(8,128)}) %reduce-scatter.16.cloned.1.call-update) | async-done | bytes 73744 | tf_op jit(solution)/shard_map/reduce_scatter | solution.py:402
  1449.5 126.6 %reduce-scatter.12.cloned.1.call-done = f32[1,1,96,576]{3,2,1,0:T(8,128)} async-done(((f32[32,1,96,576]{3,2,1,0:T(8,128)}), f32[1,1,96,576]{3,2,1,0:T(8,128)}) %reduce-scatter.12.cloned.1.call-update) | async-done | bytes 221200 | tf_op jit(solution)/shard_map/reduce_scatter | solution.py:402
  1576.1 127.2 %reduce-scatter.10.cloned.1.call-done = f32[1,1,96,576]{3,2,0,1:T(8,128)} async-done(((f32[32,1,96,576]{3,2,0,1:T(8,128)}), f32[1,1,96,576]{3,2,0,1:T(8,128)}) %reduce-scatter.10.cloned.1.call-update) | async-done | bytes 221200 | tf_op jit(solution)/shard_map/reduce_scatter | solution.py:402
  1706.4 210.7 %reduce-scatter.18.cloned.1.call-done = f32[1,2,96,768]{3,2,1,0:T(8,128)} async-done(((f32[32,2,96,768]{3,2,1,0:T(8,128)}), f32[1,2,96,768]{3,2,1,0:T(8,128)}) %reduce-scatter.18.cloned.1.call-update) | async-done | bytes 589840 | tf_op jit(solution)/shard_map/reduce_scatter | solution.py:402
  1918.2 211.9 %reduce-scatter.20.cloned.1.call-done = f32[1,2,96,768]{3,2,1,0:T(8,128)} async-done(((f32[32,2,96,768]{3,2,1,0:T(8,128)}), f32[1,2,96,768]{3,2,1,0:T(8,128)}) %reduce-scatter.20.cloned.1.call-update) | async-done | bytes 589840 | tf_op jit(solution)/shard_map/reduce_scatter | solution.py:402
  2135.9 39.9 %all-reduce.6 = (f32[]{:T(128)}, f32[]{:T(128)}) all-reduce(f32[]{:T(128)S(6)} %add.508, f32[]{:T(128)S(6)} %add.536), channel_id=1, replica_groups=mesh['dp'=8,'head'=4] {'dp','head'}, use_global_device_ids=true, to_apply=%region_29.30 | all-reduce | flops 2 | bytes 16 | tf_op jit(solution)/shard_map/psum | solution.py:423
  2179.0 54.5 %all_to_all.73 = f32[8,96,768]{2,1,0:T(8,128)S(1)} all-to-all(f32[8,96,768]{2,1,0:T(8,128)S(1)} %fusion.134), channel_id=1, replica_groups=mesh['dp'=8,'head'=4] {'dp'}, dimensions={0} | all-to-all | bytes 4718592 | tf_op jit(solution)/shard_map/all_to_all | solution.py:436
  2238.0 57.8 %all-reduce.12.cloned.1.call-done = f32[768,768]{1,0:T(8,128)} async-done(((f32[768,768]{1,0:T(8,128)}), f32[768,768]{1,0:T(8,128)}) %all-reduce.12.cloned.1.call-update) | async-done | bytes 2359312 | tf_op jit(solution)/shard_map/psum | solution.py:442
  2374.1 44.4 %all-to-all-done.5 = f32[8,96,768]{2,1,0:T(8,128)} async-done(((f32[8,96,768]{2,1,0:T(8,128)}), f32[8,96,768]{2,1,0:T(8,128)}, u32[]{:S(2)}, u32[]{:S(2)}) %all-to-all-start.5) | async-done | bytes 2359328 | tf_op jit(solution)/shard_map/all_to_all | solution.py:453
  (758 shorter events, 837.6 us)
Async XLA Ops:
  7.2 336.4 %copy-start = (bf16[3,256,768]{2,1,0:T(8,128)(2,1)S(1)}, bf16[3,256,768]{2,1,0:T(8,128)(2,1)}, u32[]{:S(2)}) copy-start(bf16[3,256,768]{2,1,0:T(8,128)(2,1)} %param.35) | copy-start | bytes 3538948
  7.2 141.8 %all-reduce.14.cloned.1.call-start = ((), (), s32[]{:S(2)}) async-start(), calls=%async_computation.26 | async-start | bytes 4997120
  13.4 224.5 %all-reduce.16.cloned.1.call-start = ((), (), s32[]{:S(2)}) async-start(), calls=%async_computation.28 | async-start | bytes 442368
  169.7 135.1 %all-gather.18.cloned.1.call-start = ((), (), s32[]{:S(2)}) async-start(), calls=%async_computation.22 | async-start | bytes 4055040 | tf_op jit(solution)/shard_map/all_gather | solution.py:159
  170.5 201.4 %all-gather.24.cloned.1.call-start = ((), (), s32[]{:S(2)}) async-start(), calls=%async_computation.25 | async-start | bytes 1622016 | tf_op jit(solution)/shard_map/all_gather | solution.py:159
  172.1 248.8 %all-gather.20.cloned.1.call-start = ((), (), s32[]{:S(2)}) async-start(), calls=%async_computation.23 | async-start | bytes 1622016 | tf_op jit(solution)/shard_map/all_gather | solution.py:159
  172.7 312.5 %all-gather.22.cloned.1.call-start = ((), (), s32[]{:S(2)}) async-start(), calls=%async_computation.24 | async-start | bytes 4055040 | tf_op jit(solution)/shard_map/all_gather | solution.py:159
  173.4 411.1 %all-gather.16.cloned.1.call-start = ((), (), s32[]{:S(2)}) async-start(), calls=%async_computation.14 | async-start | bytes 9732096 | tf_op jit(solution)/shard_map/all_gather | solution.py:159
  174.3 479.9 %all-gather.14.cloned.1.call-start = ((), (), s32[]{:S(2)}) async-start(), calls=%async_computation.13 | async-start | bytes 9732096 | tf_op jit(solution)/shard_map/all_gather | solution.py:159
  183.9 396.3 %copy-start.3 = (f32[3,208,768]{2,1,0:T(8,128)}, f32[3,208,768]{2,1,0:T(8,128)S(1)}, u32[]{:S(2)}) copy-start(f32[3,208,768]{2,1,0:T(8,128)S(1)} %get-tuple-element.408) | copy-start | bytes 5750788
  183.9 135.7 %copy-start.100 = (f32[3,208]{1,0:T(4,128)}, f32[3,208]{1,0:T(4,128)S(1)}, u32[]{:S(2)}) copy-start(f32[3,208]{1,0:T(4,128)S(1)} %broadcast_multiply_fusion.5) | copy-start | bytes 7492
  184.3 135.4 %copy-start.106 = (f32[3,208]{1,0:T(4,128)}, f32[3,208]{1,0:T(4,128)S(1)}, u32[]{:S(2)}) copy-start(f32[3,208]{1,0:T(4,128)S(1)} %fusion.290) | copy-start | bytes 7492
  247.8 71.9 %copy-start.98 = (f32[3,768]{1,0:T(4,128)}, f32[3,768]{1,0:T(4,128)S(1)}, u32[]{:S(2)}) copy-start(f32[3,768]{1,0:T(4,128)S(1)} %get-tuple-element.435) | copy-start | bytes 27652
  338.4 161.7 %all-to-all-start = ((bf16[3,208,3,768]{1,2,0,3:T(4,128)(2,1)}), bf16[3,208,3,768]{1,2,0,3:T(4,128)(2,1)}, u32[]{:S(2)}, u32[]{:S(2)}) async-start(bf16[3,208,3,768]{1,2,0,3:T(4,128)(2,1)} %copy.318), calls=%async_computation | async-start | bytes 9437184 | tf_op jit(solution)/shard_map/all_to_all | solution.py:74
  370.0 210.2 %copy-start.126 = (f32[3,768]{1,0:T(4,128)}, f32[3,768]{1,0:T(4,128)S(1)}, u32[]{:S(2)}) copy-start(f32[3,768]{1,0:T(4,128)S(1)} %get-tuple-element.388) | copy-start | bytes 27652
  370.0 335.6 %copy-start.108 = (f32[3,768]{1,0:T(4,128)}, f32[3,768]{1,0:T(4,128)S(1)}, u32[]{:S(2)}) copy-start(f32[3,768]{1,0:T(4,128)S(1)} %get-tuple-element.437) | copy-start | bytes 27652
  371.9 479.0 %copy-start.86 = (f32[3,768]{1,0:T(4,128)}, f32[3,768]{1,0:T(4,128)S(1)}, u32[]{:S(2)}) copy-start(f32[3,768]{1,0:T(4,128)S(1)} %get-tuple-element.390) | copy-start | bytes 27652
  549.0 25.4 %all-to-all-start.1 = ((bf16[3,832,1,192]{3,0,2,1:T(4,128)(2,1)}), bf16[3,832,1,192]{3,0,2,1:T(4,128)(2,1)}, u32[]{:S(2)}, u32[]{:S(2)}) async-start(bf16[3,832,1,192]{3,0,2,1:T(4,128)(2,1)} %copy.321), calls=%async_computation.1 | async-start | bytes 3407872 | tf_op jit(solution)/shard_map/all_to_all | solution.py:78
  584.4 121.2 %copy-start.68 = (f32[3,208]{1,0:T(4,128)}, f32[3,208]{1,0:T(4,128)S(1)}, u32[]{:S(2)}) copy-start(f32[3,208]{1,0:T(4,128)S(1)} %fusion.291) | copy-start | bytes 7492
  860.1 25.0 %all-to-all-start.2 = ((bf16[3,208,1,768]{1,0,2,3:T(4,128)(2,1)}), bf16[3,208,1,768]{1,0,2,3:T(4,128)(2,1)}, u32[]{:S(2)}, u32[]{:S(2)}) async-start(bf16[3,208,1,768]{1,0,2,3:T(4,128)(2,1)} %copy.337), calls=%async_computation.2 | async-start | bytes 3145728 | tf_op jit(solution)/shard_map/all_to_all | solution.py:74
  994.2 63.2 %all-to-all-start.3 = ((bf16[3,832,3,192]{3,2,0,1:T(4,128)(2,1)}), bf16[3,832,3,192]{3,2,0,1:T(4,128)(2,1)}, u32[]{:S(2)}, u32[]{:S(2)}) async-start(bf16[3,832,3,192]{3,2,0,1:T(4,128)(2,1)} %copy.340), calls=%async_computation.3 | async-start | bytes 10223616 | tf_op jit(solution)/shard_map/all_to_all | solution.py:78
  1000.2 295.2 %all-reduce.18.cloned.1.call-start = ((), (), s32[]{:S(2)}) async-start(), calls=%async_computation.29 | async-start | bytes 327680
  1076.6 220.8 %reduce-scatter.22.cloned.1.call-start = ((), (), s32[]{:S(2)}) async-start(), calls=%async_computation.27 | async-start | bytes 2949120
  1087.1 279.7 %reduce-scatter.14.cloned.1.call-start = ((), (), s32[]{:S(2)}) async-start(), calls=%async_computation.17 | async-start | bytes 3244032 | tf_op jit(solution)/shard_map/reduce_scatter | solution.py:402
  1092.6 355.3 %reduce-scatter.16.cloned.1.call-start = ((), (), s32[]{:S(2)}) async-start(), calls=%async_computation.18 | async-start | bytes 3244032 | tf_op jit(solution)/shard_map/reduce_scatter | solution.py:402
  1104.3 471.7 %reduce-scatter.12.cloned.1.call-start = ((), (), s32[]{:S(2)}) async-start(), calls=%async_computation.16 | async-start | bytes 8110080 | tf_op jit(solution)/shard_map/reduce_scatter | solution.py:402
  1138.9 564.4 %reduce-scatter.10.cloned.1.call-start = ((), (), s32[]{:S(2)}) async-start(), calls=%async_computation.15 | async-start | bytes 8110080 | tf_op jit(solution)/shard_map/reduce_scatter | solution.py:402
  1158.4 758.6 %reduce-scatter.18.cloned.1.call-start = ((), (), s32[]{:S(2)}) async-start(), calls=%async_computation.19 | async-start | bytes 19464192 | tf_op jit(solution)/shard_map/reduce_scatter | solution.py:402
  1225.2 904.9 %reduce-scatter.20.cloned.1.call-start = ((), (), s32[]{:S(2)}) async-start(), calls=%async_computation.20 | async-start | bytes 19464192 | tf_op jit(solution)/shard_map/reduce_scatter | solution.py:402
  1291.7 1004.1 %all-reduce.12.cloned.1.call-start = ((), (), s32[]{:S(2)}) async-start(), calls=%async_computation.21 | async-start | bytes 4718592 | tf_op jit(solution)/shard_map/psum | solution.py:442
  1366.8 809.7 %copy-start.62 = (f32[2,96,768]{2,1,0:T(8,128)S(1)}, f32[2,96,768]{2,1,0:T(8,128)}, u32[]{:S(2)}) copy-start(f32[2,96,768]{2,1,0:T(8,128)} %param.49) | copy-start | bytes 1769476
  2361.6 57.0 %all-to-all-start.5 = ((f32[8,96,768]{2,1,0:T(8,128)}), f32[8,96,768]{2,1,0:T(8,128)}, u32[]{:S(2)}, u32[]{:S(2)}) async-start(f32[8,96,768]{2,1,0:T(8,128)} %bitcast.714), calls=%async_computation.11 | async-start | bytes 4718592 | tf_op jit(solution)/shard_map/all_to_all | solution.py:453
  (175 other events, 1529.0 us)
Sparse Core Ops, SparseCore 0:
  13.5 135.4 all-reduce.13
  169.8 68.0 all-reduce.15
  241.5 63.2 all-gather.17
  308.2 54.9 all-gather.23
  366.6 54.2 all-gather.19
  424.3 60.8 all-gather.21
  488.8 81.0 all-gather.15
  573.5 80.7 all-gather.13
  1076.7 120.1 all-reduce.17
  1199.3 35.5 reduce-scatter.21
  1241.2 99.9 reduce-scatter.13
  1347.4 100.4 reduce-scatter.15
  1454.5 121.5 reduce-scatter.11
  1581.6 121.6 reduce-scatter.9
  1710.7 206.3 reduce-scatter.17
  1924.5 205.5 reduce-scatter.19
  2238.1 57.6 all-reduce.11

commit v2 on v1

v2 whole, which is shorter than its diff:
```python
import functools
import math

import jax
import jax.numpy as jnp
from jax import lax
from jax.experimental import pallas as pl
from jax.experimental.pallas import tpu as pltpu
from jax.sharding import PartitionSpec as P

D = 768
HEADS = 12
HDIM = 64
CAP = 256
NS_STEPS = 5


HIGHEST_PRECISION = lax.Precision.HIGHEST
NEWTON_COEFFS = (3.4445, -4.775, 2.0315)
CLIP_NORM = 1.0
MUON_RATE = 0.2
MUON_DECAY = 0.1
MUON_BETA = 0.95
ADAM_RATE = 0.02
ADAM_DECAY = 0.01
ADAM_FIRST = 0.9
ADAM_SECOND = 0.999


def to_bf16(values):
    return values.astype(jnp.bfloat16)


def sigmoid_unit(values):
    return values * jax.nn.sigmoid(values)


def double_silu(values):
    return sigmoid_unit(sigmoid_unit(values))


def soft_gelu(values):
    return (
        0.5
        * values
        * (1.0 + jnp.tanh(0.7978845608 * (values + 0.044715 * values * values * values)))
    )


def norm_rows(values):
    centre = values - jnp.mean(values, -1, keepdims=True)
    return centre * lax.rsqrt(jnp.mean(centre * centre, -1, keepdims=True) + 1e-06)


def modulate(hidden, shift, stretch):
    return norm_rows(hidden) * (1.0 + stretch) + shift


def time_table(timesteps, width):
    half_width = width // 2
    frequency = jnp.exp(
        -math.log(10000.0) * jnp.arange(half_width).astype(timesteps.dtype) / half_width
    )
    angles = 1000.0 * timesteps[:, None] * frequency[None, :]
    return jnp.concatenate([jnp.cos(angles), jnp.sin(angles)], axis=-1)


def product(form, left, right):
    return jnp.einsum(form, left, right, preferred_element_type=jnp.float32)


def exact_product(form, left, right):
    return jnp.einsum(form, left, right, precision=HIGHEST_PRECISION)


def adam_update(weight, grad_part, first_moment, second_moment, step_count):
    first_moment = ADAM_FIRST * first_moment + (1.0 - ADAM_FIRST) * grad_part
    second_moment = ADAM_SECOND * second_moment + (1.0 - ADAM_SECOND) * grad_part * grad_part
    first_fix = 1.0 - jnp.power(ADAM_FIRST, step_count)
    second_fix = 1.0 - jnp.power(ADAM_SECOND, step_count)
    direction = first_moment / first_fix / (jnp.sqrt(second_moment / second_fix) + 1e-08)
    return (weight - ADAM_RATE * (direction + ADAM_DECAY * weight), first_moment, second_moment)


MESH = pl.DeviceIdType.MESH
ROWS_A = 64
PIECE_COLS = 256
SLOTS = 4
HALF = 384
WIDE = 256
VMEM_BYTES = 56 * 1024 * 1024


def vmem():
    return pl.BlockSpec(memory_space=pltpu.VMEM)


def anywhere():
    return pl.BlockSpec(memory_space=pl.ANY)


def comm_params(collective_id):
    return pltpu.CompilerParams(
        collective_id=collective_id, has_side_effects=True, vmem_limit_bytes=VMEM_BYTES
    )


def greet(peers):
    barrier = pltpu.get_barrier_semaphore()
    for peer in peers:
        pl.semaphore_signal(barrier, inc=1, device_id=peer, device_id_type=MESH)
    pl.semaphore_wait(barrier, len(peers))


def exchange_kernel(axis, count, swapped, x_ref, out_ref, send_sem, recv_sem):
    me = lax.axis_index(axis)
    peers = [lax.rem(me + shift, count) for shift in range(1, count)]
    greet([{axis: peer} for peer in peers])
    copies = []
    for place, peer in enumerate(peers):
        copy = pltpu.make_async_remote_copy(
            src_ref=x_ref.at[peer] if swapped else x_ref,
            dst_ref=out_ref.at[me],
            send_sem=send_sem.at[place],
            recv_sem=recv_sem.at[place],
            device_id={axis: peer},
            device_id_type=MESH,
        )
        copy.start()
        copies.append(copy)
    out_ref[me] = x_ref[me] if swapped else x_ref[...]
    for copy in copies:
        copy.wait()


def exchange(x, axis, swapped, collective_id):
    count = lax.axis_size(axis)
    block = x.shape[1:] if swapped else x.shape
    return pl.pallas_call(
        functools.partial(exchange_kernel, axis, count, swapped),
        out_shape=jax.ShapeDtypeStruct((count,) + block, x.dtype),
        in_specs=[vmem()],
        out_specs=vmem(),
        scratch_shapes=[
            pltpu.SemaphoreType.DMA((count - 1,)),
            pltpu.SemaphoreType.DMA((count - 1,)),
        ],
        compiler_params=comm_params(collective_id),
        name="swap" if swapped else "spread",
    )(x)


def link_peers(d, h):
    return {
        "core": (d, h ^ 1),
        "y": (d, h ^ 2),
        "x": (d ^ 1, h),
        "zl": (d ^ 2, h),
        "zh": (d ^ 4, h),
    }


def gather_kernel(groups, *refs):
    own_refs, out_refs = refs[:groups], refs[groups : 2 * groups]
    send_sem, recv_sem, core_send, core_recv, local_sem = refs[2 * groups :]
    d = lax.axis_index("dp")
    h = lax.axis_index("head")
    peers = link_peers(d, h)
    greet(list(peers.values()))
    y, c = h // 2, h % 2
    zh, zl, x = d // 4, (d // 2) % 2, d % 2
    every = slice(None)
    pieces = [
        (group, start)
        for group in range(groups)
        for start in range(0, own_refs[group].shape[1], PIECE_COLS)
    ]
    order_a = (("zh", (zh, zl, x)), ("zl", (every, zl, x)), ("x", (every, every, x)),
               ("y", (every, every, every)))
    order_b = (("y", (zh, zl, x)), ("zh", (zh, zl, x)), ("zl", (every, zl, x)),
               ("x", (every, every, x)))

    def columns_of(piece, head):
        group, start = pieces[piece]
        width = own_refs[group].shape[1]
        return pl.ds(pl.multiple_of(head * width + start, 128), PIECE_COLS)

    def own_copy(piece):
        group, start = pieces[piece]
        return pltpu.make_async_copy(
            own_refs[group].at[:, pl.ds(start, PIECE_COLS)],
            out_refs[group].at[zh, zl, x, :, columns_of(piece, h)],
            local_sem.at[piece],
        )

    def hop(piece, step, stream):
        group, start = pieces[piece]
        rows_all = own_refs[group].shape[0]
        rows = pl.ds(0, ROWS_A) if stream == 0 else pl.ds(ROWS_A, rows_all - ROWS_A)
        head = h if stream < 2 else h ^ 2
        peer, index = (order_a if stream == 0 else order_b)[step]
        view = out_refs[group].at[index + (rows, columns_of(piece, head))]
        source = view
        if step == 0:
            source = own_refs[group].at[rows, pl.ds(start, PIECE_COLS)]
        return pltpu.make_async_remote_copy(
            src_ref=source,
            dst_ref=view,
            send_sem=send_sem.at[piece, step, stream],
            recv_sem=recv_sem.at[piece, step, stream],
            device_id=peers[peer],
            device_id_type=MESH,
        )

    def streams(step):
        return range(2) if step == 0 else range(3)

    def across(piece, side):
        group, start = pieces[piece]
        view = out_refs[group].at[:, :, :, :, columns_of(piece, h ^ (2 * side))]
        return pltpu.make_async_remote_copy(
            src_ref=view,
            dst_ref=view,
            send_sem=core_send.at[piece, side],
            recv_sem=core_recv.at[piece, side],
            device_id=peers["core"],
            device_id_type=MESH,
        )

    for piece in range(len(pieces)):
        own_copy(piece).start()
    for turn in range(len(pieces) + 4):
        for step in range(5):
            piece = turn - step
            if not 0 <= piece < len(pieces):
                continue
            if step == 1:
                own_copy(piece).wait()
            if step >= 1:
                for stream in streams(step - 1):
                    hop(piece, step - 1, stream).wait_recv()
            if step < 4:
                for stream in streams(step):
                    hop(piece, step, stream).start()
            else:
                for side in range(2):
                    across(piece, side).start()
    for piece in range(len(pieces)):
        for step in range(4):
            for stream in streams(step):
                hop(piece, step, stream).wait_send()
        for side in range(2):
            across(piece, side).wait()


def gather_whole(owns, collective_id):
    groups = len(owns)
    pieces = sum(own.shape[1] // PIECE_COLS for own in owns)
    wholes = pl.pallas_call(
        functools.partial(gather_kernel, groups),
        out_shape=[
            jax.ShapeDtypeStruct((2, 2, 2, own.shape[0], 4 * own.shape[1]), own.dtype)
            for own in owns
        ],
        in_specs=[anywhere()] * groups,
        out_specs=[anywhere()] * groups,
        scratch_shapes=[
            pltpu.SemaphoreType.DMA((pieces, 4, 3)),
            pltpu.SemaphoreType.DMA((pieces, 4, 3)),
            pltpu.SemaphoreType.DMA((pieces, 2)),
            pltpu.SemaphoreType.DMA((pieces, 2)),
            pltpu.SemaphoreType.DMA((pieces,)),
        ],
        compiler_params=pltpu.CompilerParams(collective_id=collective_id, has_side_effects=True),
        name="gather_weights",
    )(*owns)
    return [whole.reshape(8 * own.shape[0], -1) for whole, own in zip(wholes, owns)]


def gather_general(own):
    rows, columns = own.shape
    blocks = lax.all_gather(own, ("dp", "head"), axis=0, tiled=False)
    blocks = blocks.reshape(-1, lax.axis_size("head"), rows, columns)
    return blocks.transpose(0, 2, 1, 3).reshape(-1, lax.axis_size("head") * columns)


def reduce_kernel(groups, pieces, *refs):
    part_refs = refs[:groups]
    out_ref = refs[groups]
    (own, near, send_a, send_b, got_a, got_b, keep_a, keep_b, own_sem, near_send, near_recv,
     hop_send, hop_recv) = refs[groups + 1 :]
    per_group = 768 // PIECE_COLS
    d = lax.axis_index("dp")
    h = lax.axis_index("head")
    peers = link_peers(d, h)
    greet(list(peers.values()))
    y, c = h // 2, h % 2
    zh, zl, x = d // 4, (d // 2) % 2, d % 2
    order = (("y", "x"), ("x", "zl"), ("zl", "zh"), ("zh", "y"))
    bottom_rows = own.shape[-2] - ROWS_A
    top, bottom = pl.ds(0, ROWS_A), pl.ds(ROWS_A, bottom_rows)
    every = slice(None)

    def columns_of(piece, group, head):
        width = part_refs[group].shape[-1] // 4
        start = head * width + (piece % per_group) * PIECE_COLS
        return pl.ds(pl.multiple_of(start, PIECE_COLS), PIECE_COLS)

    def own_copy(piece, group, side):
        return pltpu.make_async_copy(
            part_refs[group].at[:, :, :, :, columns_of(piece, group, 2 * side + c)],
            own.at[piece % SLOTS, side],
            own_sem.at[piece % SLOTS, side],
        )

    def near_copy(piece, group, side):
        return pltpu.make_async_remote_copy(
            src_ref=part_refs[group].at[:, :, :, :, columns_of(piece, group, 2 * side + 1 - c)],
            dst_ref=near.at[piece % SLOTS, side],
            send_sem=near_send.at[piece % SLOTS, side],
            recv_sem=near_recv.at[piece % SLOTS, side],
            device_id=peers["core"],
            device_id_type=MESH,
        )

    def bring(piece):
        for group in range(groups):

            @pl.when(piece // per_group == group)
            def _():
                for side in range(2):
                    near_copy(piece, group, side).start()
                    own_copy(piece, group, side).start()

    def hop(piece, step, stream):
        slot = piece % SLOTS
        sent, got = (send_a, got_a) if stream == 0 else (send_b, got_b)
        return pltpu.make_async_remote_copy(
            src_ref=sent[step].at[slot],
            dst_ref=got[step].at[slot],
            send_sem=hop_send.at[step, stream, slot],
            recv_sem=hop_recv.at[step, stream, slot],
            device_id=peers[order[step][stream]],
            device_id_type=MESH,
        )

    def first(piece):
        slot = piece % SLOTS
        for side in range(2):
            near_copy(piece, 0, side).wait()
            own_copy(piece, 0, side).wait()

        def total(*index):
            return own[(slot,) + index] + near[(slot,) + index]

        send_a[0][slot] = to_bf16(total(1 - y, every, every, every, top))
        hop(piece, 0, 0).start()
        send_b[0][slot] = to_bf16(total(every, every, every, 1 - x, bottom))
        hop(piece, 0, 1).start()
        keep_a[0][slot] = total(y, every, every, every, top)
        keep_b[0][slot] = total(every, every, every, x, bottom)

    cut_a = (None, (2, x), (1, zl), (0, zh))
    cut_b = (None, (2, zl), (1, zh), (0, y))

    def later(piece, step):
        slot = piece % SLOTS
        for stream in range(2):
            keep, got, sent = (keep_a, got_a, send_a) if stream == 0 else (keep_b, got_b, send_b)
            axis, mine = (cut_a if stream == 0 else cut_b)[step]
            hop(piece, step - 1, stream).wait()

            def total(which):
                index = (slot,) + (every,) * axis + (which,)
                return keep[step - 1][index] + got[step - 1][index].astype(jnp.float32)

            sent[step][slot] = to_bf16(total(1 - mine))
            hop(piece, step, stream).start()
            keep[step][slot] = total(mine)

    def last(piece):
        slot = piece % SLOTS
        for stream in range(2):
            keep, got = (keep_a, got_a) if stream == 0 else (keep_b, got_b)
            hop(piece, 3, stream).wait()
            out_ref[piece, top if stream == 0 else bottom, :] = keep[3][slot] + got[3][
                slot
            ].astype(jnp.float32)

    bring(0)

    @pl.loop(0, pieces + 4)
    def _(turn):
        @pl.when(turn + 1 < pieces)
        def _():
            bring(turn + 1)

        @pl.when(turn < pieces)
        def _():
            first(turn)

        for step in (1, 2, 3):

            @pl.when((turn >= step) & (turn - step < pieces))
            def _():
                later(turn - step, step)

        @pl.when(turn >= 4)
        def _():
            last(turn - 4)


def reduce_whole(parts, collective_id):
    groups = len(parts)
    rows = parts[0].shape[0] // 8
    widths = [part.shape[1] // 4 for part in parts]
    pieces = sum(widths) // PIECE_COLS
    views = [part.reshape(2, 2, 2, rows, part.shape[1]) for part in parts]
    leads = ((2, 2, 2), (2, 2), (2,), ())

    def buffers(count, dtype):
        return [pltpu.VMEM((SLOTS,) + lead + (count, PIECE_COLS), dtype) for lead in leads]

    bottom_rows = rows - ROWS_A
    whole = (SLOTS, 2, 2, 2, 2, rows, PIECE_COLS)
    summed = pl.pallas_call(
        functools.partial(reduce_kernel, groups, pieces),
        out_shape=jax.ShapeDtypeStruct((pieces, rows, PIECE_COLS), jnp.float32),
        in_specs=[anywhere()] * groups,
        out_specs=vmem(),
        scratch_shapes=[
            pltpu.VMEM(whole, jnp.float32),
            pltpu.VMEM(whole, jnp.float32),
            buffers(ROWS_A, jnp.bfloat16),
            buffers(bottom_rows, jnp.bfloat16),
            buffers(ROWS_A, jnp.bfloat16),
            buffers(bottom_rows, jnp.bfloat16),
            buffers(ROWS_A, jnp.float32),
            buffers(bottom_rows, jnp.float32),
            pltpu.SemaphoreType.DMA((SLOTS, 2)),
            pltpu.SemaphoreType.DMA((SLOTS, 2)),
            pltpu.SemaphoreType.DMA((SLOTS, 2)),
            pltpu.SemaphoreType.DMA((4, 2, SLOTS)),
            pltpu.SemaphoreType.DMA((4, 2, SLOTS)),
        ],
        compiler_params=comm_params(collective_id),
        name="reduce_grads",
    )(*views)
    blocks, at = [], 0
    for width in widths:
        count = width // PIECE_COLS
        blocks.append(summed[at : at + count].transpose(1, 0, 2).reshape(rows, width))
        at += count
    return blocks


def reduce_general(part):
    data_count, head_count = lax.axis_size("dp"), lax.axis_size("head")
    blocks = part.reshape(
        data_count, part.shape[0] // data_count, head_count, part.shape[1] // head_count
    ).transpose(0, 2, 1, 3)
    blocks = blocks.reshape((-1,) + blocks.shape[2:])
    return lax.psum_scatter(blocks, ("dp", "head"), scatter_dimension=0, tiled=True)[0]


def send_to(source, target, sems, place, peer):
    return pltpu.make_async_remote_copy(
        src_ref=source,
        dst_ref=target,
        send_sem=sems[0].at[place],
        recv_sem=sems[1].at[place],
        device_id={"head": peer},
        device_id_type=MESH,
    )


def half_mask(pair_half):
    lane = lax.broadcasted_iota(jnp.int32, (1, 128), 1)
    return (lane // 64) == pair_half


def dot_nt(left, right):
    return lax.dot_general(
        left, right, (((1,), (1,)), ((), ())), preferred_element_type=jnp.float32
    )


def dot_nn(left, right):
    return lax.dot_general(
        left, right, (((1,), (0,)), ((), ())), preferred_element_type=jnp.float32
    )


def dot_tn(left, right):
    return lax.dot_general(
        left, right, (((0,), (0,)), ((), ())), preferred_element_type=jnp.float32
    )


def own_exchange(h, pair_in, pair_all, quad_in, quad_all, sems, start_place):
    c = h % 2
    pair = [send_to(pair_in.at[1 - c], pair_all.at[c], sems, start_place, h ^ 1)]
    quad = [
        send_to(quad_in.at[h ^ other], quad_all.at[h], sems, start_place + other, h ^ other)
        for other in (1, 2, 3)
    ]
    return pair, quad


def attend_kernel(pair_in, quad_in, pair_mix, quad_mix, pair_all, quad_all, log_ref,
                  pair_out, quad_out, send_sem, recv_sem):
    h = lax.axis_index("head")
    c = h % 2
    sems = (send_sem, recv_sem)
    greet([{"head": h ^ other} for other in (1, 2, 3)])
    pair_copies, quad_copies = own_exchange(h, pair_in, pair_all, quad_in, quad_all, sems, 0)
    for copy in pair_copies + quad_copies:
        copy.start()
    pair_all[c] = pair_in[c]
    quad_all[h] = quad_in[h]
    tile = quad_in.shape[1]

    def one_pair(packed, starts, head_place, heads, out):
        length = packed.shape[0] * packed.shape[1]

        def cols(start):
            return packed[:, :, start : start + 128].reshape(length, 128)

        keys, values = cols(starts[1]), cols(starts[2])

        for row in range(length // tile):
            per = packed.shape[1] // tile
            query = packed[row // per, (row % per) * tile : (row % per + 1) * tile,
                           starts[0] : starts[0] + 128]
            mixed = jnp.zeros((tile, 128), jnp.float32)
            logs = log_ref[row * tile : (row + 1) * tile, :]
            lane = lax.broadcasted_iota(jnp.int32, (1, 128), 1)
            for half in range(heads):
                mask = half_mask(half)
                scores = dot_nt(jnp.where(mask, query, 0), keys) * 0.125
                top = jnp.max(scores, -1, keepdims=True)
                exponent = jnp.exp(scores - top)
                total = jnp.sum(exponent, -1, keepdims=True)
                probability = to_bf16(exponent / total)
                mixed = mixed + dot_nn(probability, jnp.where(mask, values, 0))
                logs = jnp.where(lane == head_place + half, top + jnp.log(total), logs)
            log_ref[row * tile : (row + 1) * tile, :] = logs
            out(row, to_bf16(mixed))

    log_ref[...] = jnp.zeros_like(log_ref)
    for copy in pair_copies:
        copy.wait()
    for pair in range(3):

        def put(row, value, pair=pair):
            pair_out[row // 2, (row % 2) * tile : (row % 2 + 1) * tile,
                     pair * 128 : pair * 128 + 128] = value

        one_pair(pair_all, (pair * 128, HALF + pair * 128, 2 * HALF + pair * 128),
                 2 * pair, 2, put)
    back = [send_to(pair_out.at[1 - c], pair_mix.at[c], sems, 4, h ^ 1)]
    back[0].start()
    pair_mix[c] = pair_out[c]
    for copy in quad_copies:
        copy.wait()
    for pair in range(2):

        def put(row, value, pair=pair):
            quad_out[row, :, pair * 128 : pair * 128 + 128] = value

        one_pair(quad_all, (pair * 128, WIDE + pair * 128, 2 * WIDE + pair * 128),
                 6 + 2 * pair, 2 - pair, put)
    for other in (1, 2, 3):
        back.append(send_to(quad_out.at[h ^ other], quad_mix.at[h], sems, 4 + other, h ^ other))
        back[-1].start()
    quad_mix[h] = quad_out[h]
    for copy in back:
        copy.wait()


def attend(pair_in, quad_in, collective_id):
    rows, tile = pair_in.shape[1], quad_in.shape[1]
    low = jnp.bfloat16
    return pl.pallas_call(
        attend_kernel,
        out_shape=[
            jax.ShapeDtypeStruct((2, rows, HALF), low),
            jax.ShapeDtypeStruct((4, tile, WIDE), low),
            jax.ShapeDtypeStruct(pair_in.shape, low),
            jax.ShapeDtypeStruct(quad_in.shape, low),
            jax.ShapeDtypeStruct((4 * tile, 128), jnp.float32),
        ],
        in_specs=[vmem()] * 2,
        out_specs=[vmem()] * 5,
        scratch_shapes=[
            pltpu.VMEM((2, rows, HALF), low),
            pltpu.VMEM((4, tile, WIDE), low),
            pltpu.SemaphoreType.DMA((8,)),
            pltpu.SemaphoreType.DMA((8,)),
        ],
        compiler_params=comm_params(collective_id),
        name="attend",
    )(pair_in, quad_in)


def attend_back_kernel(pair_all, quad_all, log_ref, pair_grad_in, quad_grad_in,
                       pair_grad, quad_grad, pair_mixed, quad_mixed, pair_out, quad_out,
                       grad_keys, grad_values, send_sem, recv_sem):
    h = lax.axis_index("head")
    c = h % 2
    sems = (send_sem, recv_sem)
    greet([{"head": h ^ other} for other in (1, 2, 3)])
    pair_copies, quad_copies = own_exchange(
        h, pair_grad_in, pair_mixed, quad_grad_in, quad_mixed, sems, 0
    )
    for copy in pair_copies + quad_copies:
        copy.start()
    pair_mixed[c] = pair_grad_in[c]
    quad_mixed[h] = quad_grad_in[h]
    tile = quad_all.shape[1]
    length = 4 * tile

    def one_pair(packed, grad_mixed, grad_start, starts, head_place, heads, out, wide):
        per = packed.shape[1] // tile

        def cols(start):
            return packed[:, :, start : start + 128].reshape(length, 128)

        keys, values = cols(starts[1]), cols(starts[2])
        grad_keys[...] = jnp.zeros_like(grad_keys)
        grad_values[...] = jnp.zeros_like(grad_values)
        for row in range(4):
            rows = slice((row % per) * tile, (row % per + 1) * tile)
            query = packed[row // per, rows, starts[0] : starts[0] + 128]
            grad_out = grad_mixed[row // per, rows, grad_start : grad_start + 128]
            lane = lax.broadcasted_iota(jnp.int32, (1, 128), 1)
            grad_query = jnp.zeros((tile, 128), jnp.float32)
            for half in range(heads):
                mask = half_mask(half)
                log_total = jnp.sum(
                    jnp.where(lane == head_place + half, log_ref[row * tile : (row + 1) * tile, :], 0.0),
                    -1, keepdims=True,
                )
                query_half = jnp.where(mask, query, 0)
                grad_half = jnp.where(mask, grad_out, 0)
                probability = jnp.exp(dot_nt(query_half, keys) * 0.125 - log_total)
                grad_prob = dot_nt(grad_half, values)
                mean = jnp.sum(probability * grad_prob, -1, keepdims=True)
                grad_scores = to_bf16(probability * (grad_prob - mean))
                grad_query = grad_query + dot_nn(grad_scores, jnp.where(mask, keys, 0))
                grad_keys[...] += dot_tn(grad_scores, query_half)
                grad_values[...] += dot_tn(to_bf16(probability), grad_half)
            out[row // per, rows, starts[0] : starts[0] + 128] = to_bf16(grad_query * 0.125)
        out[:, :, starts[1] : starts[1] + 128] = to_bf16(grad_keys[...] * 0.125).reshape(
            packed.shape[0], packed.shape[1], 128
        )
        out[:, :, starts[2] : starts[2] + 128] = to_bf16(grad_values[...]).reshape(
            packed.shape[0], packed.shape[1], 128
        )

    for copy in pair_copies:
        copy.wait()
    for pair in range(3):
        one_pair(pair_all, pair_mixed, pair * 128,
                 (pair * 128, HALF + pair * 128, 2 * HALF + pair * 128), 2 * pair, 2, pair_out, 3)
    back = [send_to(pair_out.at[1 - c], pair_grad.at[c], sems, 4, h ^ 1)]
    back[0].start()
    pair_grad[c] = pair_out[c]
    for copy in quad_copies:
        copy.wait()
    for pair in range(2):
        one_pair(quad_all, quad_mixed, pair * 128,
                 (pair * 128, WIDE + pair * 128, 2 * WIDE + pair * 128), 6 + 2 * pair, 2 - pair,
                 quad_out, 2)
    for other in (1, 2, 3):
        back.append(send_to(quad_out.at[h ^ other], quad_grad.at[h], sems, 4 + other, h ^ other))
        back[-1].start()
    quad_grad[h] = quad_out[h]
    for copy in back:
        copy.wait()


def attend_back(pair_all, quad_all, logs, pair_grad, quad_grad, collective_id):
    rows, tile = pair_all.shape[1], quad_all.shape[1]
    low = jnp.bfloat16
    return pl.pallas_call(
        attend_back_kernel,
        out_shape=[
            jax.ShapeDtypeStruct(pair_all.shape, low),
            jax.ShapeDtypeStruct(quad_all.shape, low),
        ],
        in_specs=[vmem()] * 5,
        out_specs=[vmem()] * 2,
        scratch_shapes=[
            pltpu.VMEM((2, rows, HALF), low),
            pltpu.VMEM((4, tile, WIDE), low),
            pltpu.VMEM(pair_all.shape, low),
            pltpu.VMEM(quad_all.shape, low),
            pltpu.VMEM((4 * tile, 128), jnp.float32),
            pltpu.VMEM((4 * tile, 128), jnp.float32),
            pltpu.SemaphoreType.DMA((8,)),
            pltpu.SemaphoreType.DMA((8,)),
        ],
        compiler_params=comm_params(collective_id),
        name="attend_back",
    )(pair_all, quad_all, logs, pair_grad, quad_grad)


def masked_scores(query_half, keys, keep):
    return jnp.where(keep, dot_nt(query_half, keys) * 0.125, -1e30)


def cross_kernel(query_ref, keys_ref, values_ref, len_ref, out_ref):
    tile = query_ref.shape[1]
    tokens = keys_ref.shape[1]
    token = lax.broadcasted_iota(jnp.int32, (1, tokens), 1)
    for row in range(3):
        clip = row // 2
        keep = token < len_ref[clip]
        keys, values = keys_ref[clip], values_ref[clip]
        mixed = jnp.zeros((tile, 128), jnp.float32)
        for half in range(2):
            mask = half_mask(half)
            scores = masked_scores(jnp.where(mask, query_ref[row], 0), keys, keep)
            exponent = jnp.exp(scores - jnp.max(scores, -1, keepdims=True))
            probability = to_bf16(exponent / jnp.sum(exponent, -1, keepdims=True))
            mixed = mixed + dot_nn(probability, jnp.where(mask, values, 0))
        out_ref[row] = to_bf16(mixed)


def cross(query, pair_kv, lengths):
    _, tile, width = query.shape
    blocks = width // 128
    tokens = pair_kv.shape[1]
    return pl.pallas_call(
        cross_kernel,
        grid=(blocks,),
        out_shape=jax.ShapeDtypeStruct(query.shape, jnp.bfloat16),
        in_specs=[
            pl.BlockSpec((3, tile, 128), lambda i: (0, 0, i)),
            pl.BlockSpec((2, tokens, 128), lambda i: (0, 0, i)),
            pl.BlockSpec((2, tokens, 128), lambda i: (0, 0, blocks + i)),
            pl.BlockSpec(memory_space=pltpu.SMEM),
        ],
        out_specs=pl.BlockSpec((3, tile, 128), lambda i: (0, 0, i)),
        compiler_params=pltpu.CompilerParams(vmem_limit_bytes=VMEM_BYTES),
        name="cross",
    )(query, pair_kv, pair_kv, lengths)


def cross_back_kernel(query_ref, keys_ref, values_ref, grad_ref, len_ref, grad_query_ref,
                      grad_keys_ref, grad_values_ref):
    tile = query_ref.shape[1]
    tokens = keys_ref.shape[1]
    token = lax.broadcasted_iota(jnp.int32, (1, tokens), 1)
    for clip in range(2):
        keep = token < len_ref[clip]
        keys, values = keys_ref[clip], values_ref[clip]
        grad_keys = jnp.zeros((tokens, 128), jnp.float32)
        grad_values = jnp.zeros((tokens, 128), jnp.float32)
        for row in range(2 * clip, 2 + clip):
            grad_query = jnp.zeros((tile, 128), jnp.float32)
            for half in range(2):
                mask = half_mask(half)
                query_half = jnp.where(mask, query_ref[row], 0)
                grad_half = jnp.where(mask, grad_ref[row], 0)
                scores = masked_scores(query_half, keys, keep)
                exponent = jnp.exp(scores - jnp.max(scores, -1, keepdims=True))
                probability = exponent / jnp.sum(exponent, -1, keepdims=True)
                grad_prob = dot_nt(grad_half, values)
                mean = jnp.sum(probability * grad_prob, -1, keepdims=True)
                grad_scores = to_bf16(probability * (grad_prob - mean))
                grad_query = grad_query + dot_nn(grad_scores, jnp.where(mask, keys, 0))
                grad_keys = grad_keys + dot_tn(grad_scores, query_half)
                grad_values = grad_values + dot_tn(to_bf16(probability), grad_half)
            grad_query_ref[row] = to_bf16(grad_query * 0.125)
        grad_keys_ref[clip] = to_bf16(grad_keys * 0.125)
        grad_values_ref[clip] = to_bf16(grad_values)


def cross_back(query, pair_kv, lengths, grad):
    _, tile, width = query.shape
    blocks = width // 128
    tokens = pair_kv.shape[1]
    rows_spec = pl.BlockSpec((3, tile, 128), lambda i: (0, 0, i))
    keys_spec = pl.BlockSpec((2, tokens, 128), lambda i: (0, 0, i))
    return pl.pallas_call(
        cross_back_kernel,
        grid=(blocks,),
        out_shape=[
            jax.ShapeDtypeStruct(query.shape, jnp.bfloat16),
            jax.ShapeDtypeStruct((2, tokens, width), jnp.bfloat16),
            jax.ShapeDtypeStruct((2, tokens, width), jnp.bfloat16),
        ],
        in_specs=[
            rows_spec,
            keys_spec,
            pl.BlockSpec((2, tokens, 128), lambda i: (0, 0, blocks + i)),
            rows_spec,
            pl.BlockSpec(memory_space=pltpu.SMEM),
        ],
        out_specs=[rows_spec, keys_spec, keys_spec],
        compiler_params=pltpu.CompilerParams(vmem_limit_bytes=VMEM_BYTES),
        name="cross_back",
    )(query, pair_kv, pair_kv, grad, lengths)


def body(
    clean_latents,
    noise_draw,
    timesteps,
    captions,
    cap_len,
    pairing,
    adam_step,
    qkv_weight,
    out_weight,
    up_weight,
    down_weight,
    ada_weight,
    time_weight,
    io_weight,
    qkv_moment,
    out_moment,
    up_moment,
    down_moment,
    ada_first,
    ada_second,
    time_first,
    time_second,
    io_first,
    io_second,
):
    data_count = lax.axis_size("dp")
    head_count = lax.axis_size("head")
    clip_count, tile, channels = clean_latents.shape
    length = tile * head_count
    rows_own = qkv_weight.shape[1]
    d, h = lax.axis_index("dp"), lax.axis_index("head")
    own_clip, core = h // 2, h % 2
    own_row = d * rows_own
    linked = data_count == 8 and rows_own == 96
    ids = iter(range(64))

    def swap(x, axis):
        return exchange(x, axis, True, next(ids))

    def spread(x, axis):
        return exchange(x, axis, False, next(ids))

    def by_tile(values):
        own = lax.dynamic_slice_in_dim(values, own_clip, 1, 0)
        return jnp.concatenate([own, own, values[2:3]])

    def by_clip(tiles):
        own = tiles[0:1] + tiles[1:2]
        none = jnp.zeros_like(own)
        return jnp.concatenate(
            [jnp.where(own_clip == 0, own, none), jnp.where(own_clip == 1, own, none), tiles[2:3]]
        )

    weight_groups = []
    for layer in range(2):
        weight_groups.append(
            to_bf16(jnp.concatenate([qkv_weight[layer], out_weight[layer]], 1))
        )
        weight_groups.append(to_bf16(up_weight[layer]))
        weight_groups.append(to_bf16(down_weight[layer]))
    time_cols = time_weight.shape[1]
    io_cols = io_weight.shape[2]
    io_flat = io_weight.transpose(1, 0, 2).reshape(rows_own, 2 * io_cols)
    table_rows = clip_count * D // WIDE
    small_rows = -(-(rows_own + table_rows) // 16) * 16
    small_own = jnp.concatenate(
        [
            jnp.pad(
                to_bf16(jnp.concatenate([time_weight, io_flat], 1)),
                ((0, 0), (0, WIDE - time_cols - 2 * io_cols)),
            ),
            to_bf16(time_table(timesteps, D)).reshape(table_rows, WIDE),
            jnp.zeros((small_rows - rows_own - table_rows, WIDE), jnp.bfloat16),
        ]
    )
    if linked:
        gathered = gather_whole([small_own] + weight_groups, next(ids))
    else:
        gathered = [gather_general(own) for own in [small_own] + weight_groups]
    small_all = gathered[0].reshape(data_count, small_rows, head_count, WIDE)
    qkv_out_full = [gathered[1], gathered[4]]
    up_full = [gathered[2], gathered[5]]
    down_full = [gathered[3], gathered[6]]
    time_full = small_all[:, :rows_own, :, :time_cols].reshape(D, D)
    io_full = (
        small_all[:, :rows_own, :, time_cols : time_cols + 2 * io_cols]
        .reshape(D, head_count, 2, io_cols)
        .transpose(2, 0, 1, 3)
        .reshape(2, D, channels)
    )
    table_bf = small_all[:, rows_own : rows_own + table_rows, 0].reshape(-1, D)
    out_full = [
        full.reshape(D, head_count, D)[:, :, 3 * D // head_count :].reshape(D, D)
        for full in qkv_out_full
    ]

    latents = jnp.concatenate([clean_latents, noise_draw], -1)
    latents_all = spread(latents.reshape(-1, 128), "head").reshape(
        head_count, clip_count, tile, 2 * channels
    )
    own_latents = lax.dynamic_slice(
        latents_all, (2 * core, own_clip, 0, 0), (2, 1, tile, 2 * channels)
    )[:, 0]
    latents = jnp.concatenate([own_latents, latents[2:3]])
    clean_rows, noise_rows = latents[..., :channels], latents[..., channels:]
    tile_times = by_tile(timesteps)[:, None, None]
    input_bf = to_bf16((1.0 - tile_times) * clean_rows + tile_times * noise_rows)
    target = noise_rows - clean_rows
    hidden = product("flc,dc->fld", input_bf, io_full[0])

    keep_mask = jnp.arange(CAP)[None, :] < cap_len[:, None]
    cap_mean = product("ft,ftd->fd", keep_mask.astype(jnp.bfloat16), captions) / cap_len[
        :, None
    ].astype(jnp.float32)
    cap_unit = cap_mean * lax.rsqrt(jnp.mean(cap_mean * cap_mean, -1, keepdims=True) + 1e-06)
    cap_all = spread(cap_unit, "dp").reshape(-1, D)
    own_captions = jnp.concatenate([lax.dynamic_slice_in_dim(captions, own_clip, 1, 0), captions[2:3]])
    own_lengths = jnp.concatenate([lax.dynamic_slice_in_dim(cap_len, own_clip, 1, 0), cap_len[2:3]])

    time_hidden = jnp.dot(table_bf, time_full, preferred_element_type=jnp.float32)
    signal_bf = to_bf16(double_silu(time_hidden))
    signal_own = lax.dynamic_slice_in_dim(signal_bf, own_row, rows_own, 1)
    table_own = lax.dynamic_slice_in_dim(table_bf, own_row, rows_own, 1)
    ada_bf = to_bf16(ada_weight)
    ada_cols = ada_weight.shape[2]
    mod_part = product("fd,ldn->fln", signal_own, ada_bf).reshape(
        data_count, clip_count, 2 * ada_cols
    )
    mod_own = jnp.sum(swap(mod_part, "dp"), 0)
    mod_all = (
        spread(mod_own, "head")
        .reshape(head_count, clip_count, 2, ada_cols)
        .transpose(1, 2, 0, 3)
        .reshape(clip_count, 2, 6 * D)
    )
    tile_mods = by_tile(mod_all)

    block = 3 * D // head_count

    def take_qkv(wide_rows):
        lead = wide_rows.shape[:-1]
        return wide_rows.reshape(lead + (head_count, D))[..., :block].reshape(lead + (3 * D,))

    def put_qkv(rows):
        blocks = rows.reshape(rows.shape[0], head_count, block)
        return jnp.pad(blocks, ((0, 0), (0, 0), (0, D - block))).reshape(rows.shape[0], -1)

    def put_out(rows):
        blocks = rows.reshape(rows.shape[0], head_count, D - block)
        return jnp.pad(blocks, ((0, 0), (0, 0), (block, 0))).reshape(rows.shape[0], -1)

    frames = clip_count * tile
    share = D // head_count

    def cut_rows(rows, parts):
        pair = rows[: 2 * tile].reshape(2 * tile, parts, 2, HALF)
        pair = pair.transpose(2, 0, 1, 3).reshape(2, 2 * tile, parts * HALF)
        quad = rows[2 * tile :].reshape(tile, parts, head_count, share)
        quad = jnp.pad(quad, ((0, 0), (0, 0), (0, 0), (0, WIDE - share)))
        return pair, quad.transpose(2, 0, 1, 3).reshape(head_count, tile, parts * WIDE)

    def join_rows(pair, quad, parts):
        pair = pair.reshape(2, 2 * tile, parts, HALF).transpose(1, 2, 0, 3)
        quad = quad.reshape(head_count, tile, parts, WIDE)[..., :share].transpose(1, 2, 0, 3)
        return jnp.concatenate(
            [pair.reshape(2 * tile, parts * D), quad.reshape(tile, parts * D)]
        )

    def layer_forward(layer_index, hidden):
        modulation = tile_mods[:, layer_index].reshape(clip_count, 1, 6, D)
        mod_parts = [modulation[:, :, member] for member in range(6)]
        normed = to_bf16(modulate(hidden, mod_parts[0], mod_parts[1]))
        weight = qkv_out_full[layer_index]
        if layer_index == 0:
            projected = take_qkv(to_bf16(product("fld,dn->fln", normed, weight)))
            pair, quad = cut_rows(projected.reshape(frames, 3 * D), 3)
            pair_mix, quad_mix, *attended = attend(pair, quad, next(ids))
            mixed = join_rows(pair_mix, quad_mix, 1).reshape(clip_count, tile, D)
        else:
            query = to_bf16(product("fld,dn->fln", normed, weight[:, : 2 * D]))
            query = jnp.concatenate([query[..., :block], query[..., D : 2 * D - block]], -1)
            pair_kv = take_qkv(to_bf16(product("ftd,dn->ftn", own_captions, weight)))[..., D:]
            attended = (query, pair_kv)
            mixed = cross(query, pair_kv, own_lengths)
        branch = product("fle,de->fld", mixed, out_full[layer_index])
        middle = hidden + mod_parts[2] * branch
        normed2 = to_bf16(modulate(middle, mod_parts[3], mod_parts[4]))
        upper = product("fld,dn->fln", normed2, up_full[layer_index])
        active = to_bf16(soft_gelu(upper))
        down_out = product("fln,dn->fld", active, down_full[layer_index])
        kept = (hidden, mod_parts, normed, attended, mixed, branch, middle, normed2, upper,
                active, down_out)
        return (middle + mod_parts[5] * down_out, kept)

    saved_layers = []
    for layer_index in range(2):
        hidden, kept = layer_forward(layer_index, hidden)
        saved_layers.append(kept)
    final = norm_rows(hidden)
    final_bf = to_bf16(final)
    predicted = product("fld,dc->flc", final_bf, io_full[1])
    errors = predicted - target
    flow_part = jnp.sum(jnp.mean(errors * errors, -1))
    grad_pred = to_bf16(2.0 * errors / errors.shape[-1])
    pool_sum = jnp.sum(spread(by_clip(jnp.sum(final, 1)), "head"), 0)
    pooled_out = pool_sum / length

    def contrast_of(pool_total):
        pooled = pool_total / length
        unit_rows = pooled * lax.rsqrt(jnp.mean(pooled * pooled, -1, keepdims=True) + 1e-06)
        logits = exact_product("id,jd->ij", unit_rows, cap_all) * (2.0 / math.sqrt(D))
        row_top = jnp.max(logits, -1, keepdims=True)
        log_total = row_top[:, 0] + jnp.log(jnp.sum(jnp.exp(logits - row_top), -1))
        picked = jnp.sum(
            jnp.where(jnp.arange(logits.shape[1])[None, :] == pairing[:, None], logits, 0.0), -1
        )
        return length * jnp.sum(log_total - picked)

    contrast_value, contrast_back = jax.vjp(contrast_of, pool_sum)
    grad_pool = by_tile(contrast_back(jnp.ones_like(contrast_value))[0])
    loss_part = flow_part + contrast_value / head_count
    grad_final = product("flc,dc->fld", grad_pred, io_full[1]) + grad_pool[:, None, :]
    final_value, final_back = jax.vjp(norm_rows, hidden)
    grad_hidden = final_back(grad_final)[0]
    fin_grad = product("flc,fld->dc", grad_pred, final_bf)
    grad_parts = [None] * 6
    mod_grads = [None, None]
    for layer_index in (1, 0):
        (
            layer_hidden,
            mod_parts,
            layer_normed,
            attended,
            layer_mixed,
            layer_branch,
            layer_middle,
            layer_normed2,
            layer_upper,
            layer_active,
            layer_down_out,
        ) = saved_layers[layer_index]
        weight = qkv_out_full[layer_index]
        d_gate2 = jnp.sum(layer_down_out * grad_hidden, axis=1, keepdims=True)
        grad_down = to_bf16(mod_parts[5] * grad_hidden)
        grad_active = product("fld,dn->fln", grad_down, down_full[layer_index])
        gelu_value, gelu_back = jax.vjp(soft_gelu, layer_upper)
        grad_upper = to_bf16(gelu_back(grad_active)[0])
        grad_parts[3 * layer_index + 2] = product("fld,fln->dn", grad_down, layer_active)
        grad_parts[3 * layer_index + 1] = product("fld,fln->dn", layer_normed2, grad_upper)
        grad_normed2 = product("fln,dn->fld", grad_upper, up_full[layer_index])
        mod_value, mod_back = jax.vjp(modulate, layer_middle, mod_parts[3], mod_parts[4])
        grad_middle, d_shift2, d_scale2 = mod_back(grad_normed2)
        grad_middle = grad_middle + grad_hidden
        d_gate1 = jnp.sum(layer_branch * grad_middle, axis=1, keepdims=True)
        grad_branch = to_bf16(mod_parts[2] * grad_middle)
        grad_mixed = to_bf16(product("fld,de->fle", grad_branch, out_full[layer_index]))
        left = [layer_normed.reshape(frames, D), grad_branch.reshape(frames, D)]
        right = [None, put_out(layer_mixed.reshape(frames, D))]
        if layer_index == 0:
            pair, quad = cut_rows(grad_mixed.reshape(frames, D), 1)
            pair_grad, quad_grad = attend_back(*attended, pair, quad, next(ids))
            grad_proj = put_qkv(join_rows(pair_grad, quad_grad, 3))
            right[0] = grad_proj
            grad_normed = product("fn,dn->fd", grad_proj, weight)
        else:
            query, pair_kv = attended
            grad_query, grad_keys, grad_values = cross_back(query, pair_kv, own_lengths, grad_mixed)
            tokens = 2 * CAP
            grad_kv = jnp.concatenate(
                [
                    jnp.zeros((tokens, D), jnp.bfloat16),
                    grad_keys.reshape(tokens, D),
                    grad_values.reshape(tokens, D),
                ],
                1,
            )
            grad_query = jnp.pad(grad_query.reshape(frames, D), ((0, 0), (0, 2 * D)))
            grad_proj = put_qkv(grad_query)
            right[0] = grad_proj
            left.append(own_captions.reshape(tokens, D))
            right.append(put_qkv(grad_kv))
            grad_normed = product("fn,dn->fd", grad_proj[:, : 2 * D], weight[:, : 2 * D])
        grad_parts[3 * layer_index] = product(
            "kd,kn->dn", jnp.concatenate(left), jnp.concatenate(right)
        )
        first_value, first_back = jax.vjp(modulate, layer_hidden, mod_parts[0], mod_parts[1])
        grad_in, d_shift1, d_scale1 = first_back(grad_normed.reshape(clip_count, tile, D))
        mod_grads[layer_index] = jnp.concatenate(
            [d_shift1, d_scale1, d_gate1, d_shift2, d_scale2, d_gate2], -1
        )[:, 0]
        grad_hidden = grad_in + grad_middle
    in_grad = product("fld,flc->dc", to_bf16(grad_hidden), input_bf)

    mod_size = clip_count * 2 * ada_cols
    io_size = rows_own * 2 * io_cols
    mod_grad = by_clip(jnp.stack(mod_grads, 1)).reshape(clip_count, 2, head_count, ada_cols)
    mod_grad = mod_grad.transpose(2, 0, 1, 3).reshape(head_count, mod_size)
    io_part = (
        jnp.stack([in_grad, fin_grad])
        .reshape(2, data_count, rows_own, head_count, io_cols)
        .transpose(3, 1, 0, 2, 4)
        .reshape(head_count, data_count * io_size)
    )
    packed = jnp.concatenate([mod_grad, io_part], 1).reshape(head_count, -1, 128)
    packed = jnp.sum(swap(packed, "head"), 0).reshape(-1)
    mod_grad = jnp.broadcast_to(packed[:mod_size], (data_count, mod_size))
    lines = -(-(mod_size + io_size) // 128)
    packed = jnp.concatenate([mod_grad, packed[mod_size:].reshape(data_count, io_size)], 1)
    packed = jnp.pad(packed, ((0, 0), (0, lines * 128 - mod_size - io_size)))
    packed = swap(packed.reshape(data_count, lines, 128), "dp").reshape(data_count, -1)
    mod_grad = packed[:, :mod_size].reshape(-1, 2, ada_cols)
    io_grad = jnp.sum(packed[:, mod_size : mod_size + io_size], 0).reshape(2, rows_own, io_cols)
    ada_grad = exact_product("fd,fln->ldn", signal_own.astype(jnp.float32), mod_grad)
    grad_signal = exact_product("fln,ldn->fd", mod_grad, ada_bf.astype(jnp.float32))
    grad_signal = jnp.sum(spread(grad_signal, "head"), 0)
    hidden_own = lax.dynamic_slice_in_dim(time_hidden, own_row, rows_own, 1)
    signal_own_value, signal_back = jax.vjp(double_silu, hidden_own)
    grad_cond = spread(signal_back(grad_signal)[0], "dp").transpose(1, 0, 2).reshape(-1, D)
    time_grad = exact_product(
        "fd,fn->dn",
        table_own.astype(jnp.float32),
        lax.dynamic_slice_in_dim(grad_cond, h * time_cols, time_cols, 1),
    )

    if linked:
        owned = reduce_whole(grad_parts, next(ids))
    else:
        owned = [reduce_general(part) for part in grad_parts]
    shards = (
        jnp.stack([owned[0][:, :block], owned[3][:, :block]]),
        jnp.stack([owned[0][:, block:], owned[3][:, block:]]),
        jnp.stack([owned[1], owned[4]]),
        jnp.stack([owned[2], owned[5]]),
        ada_grad,
        time_grad[None],
        io_grad,
    )
    square = sum((jnp.sum(shard * shard) for shard in shards))
    totals = jnp.pad(jnp.stack([square, loss_part])[None], ((0, 7), (0, 126)))
    totals = jnp.sum(spread(jnp.sum(spread(totals, "head"), 0), "dp"), 0)
    total_square, total_loss = totals[0, 0], totals[0, 1]
    old_moments = (qkv_moment, out_moment, up_moment, down_moment)
    grad_norm = jnp.sqrt(total_square)
    clip_scale = jnp.minimum(1.0, CLIP_NORM / (grad_norm + 1e-06))
    moments = tuple(
        (MUON_BETA * old_moments[member] + clip_scale * shards[member] for member in range(4))
    )
    coeff_a, coeff_b, coeff_c = NEWTON_COEFFS
    wide = max(moment.shape[2] for moment in moments)
    sent = jnp.concatenate(
        [jnp.pad(moment, ((0, 0), (0, 0), (0, wide - moment.shape[2]))) for moment in moments]
    )
    matrices = sent.shape[0]
    sent = jnp.pad(sent, ((0, data_count - matrices), (0, 0), (0, 0)))
    own_matrix = swap(sent, "dp").reshape(D, wide)

    def near_product(form, left, right):
        return jnp.einsum(form, left, right, precision=lax.Precision.HIGH)

    gram = lax.psum(near_product("rc,kc->rk", own_matrix, own_matrix), "head")
    unit = jnp.eye(D, dtype=jnp.float32)
    size_frob = jnp.sqrt(jnp.sum(gram * unit)) + 1e-07
    gram = gram / (size_frob * size_frob)
    factor = None
    for ns_step in range(NS_STEPS):
        poly = coeff_a * unit + coeff_b * gram + coeff_c * near_product("rk,kj->rj", gram, gram)
        factor = poly if factor is None else near_product("rk,kj->rj", poly, factor)
        if ns_step < NS_STEPS - 1:
            gram = near_product("rk,kj->rj", near_product("rk,kj->rj", poly, gram), poly)
    ortho_matrix = near_product("rk,kc->rc", factor, own_matrix) / size_frob
    ortho_back = swap(ortho_matrix.reshape(data_count, rows_own, wide), "dp")
    ortho_rows = tuple(
        (
            ortho_back[2 * member : 2 * member + 2, :, : moments[member].shape[2]]
            for member in range(4)
        )
    )
    muon_weights = (qkv_weight, out_weight, up_weight, down_weight)
    muon_new = tuple(
        (
            muon_weights[member] * (1.0 - MUON_RATE * MUON_DECAY)
            - MUON_RATE
            * 0.2
            * math.sqrt(max(D, muon_weights[member].shape[2] * head_count))
            * ortho_rows[member]
            for member in range(4)
        )
    )
    step_count = adam_step[0].astype(jnp.float32)
    ada_new, ada_first_new, ada_second_new = adam_update(
        ada_weight, clip_scale * shards[4], ada_first, ada_second, step_count
    )
    time_new, time_first_new, time_second_new = adam_update(
        time_weight, clip_scale * shards[5][0], time_first, time_second, step_count
    )
    io_new, io_first_new, io_second_new = adam_update(
        io_weight, clip_scale * shards[6], io_first, io_second, step_count
    )
    return (
        total_loss,
        grad_norm,
        pooled_out,
        muon_new[0],
        moments[0],
        muon_new[1],
        moments[1],
        muon_new[2],
        moments[2],
        muon_new[3],
        moments[3],
        ada_new,
        ada_first_new,
        ada_second_new,
        time_new,
        time_first_new,
        time_second_new,
        io_new,
        io_first_new,
        io_second_new,
    )


def solution(mesh):
    placed = (
        P("dp", "head", None),
        P("dp", "head", None),
        P("dp"),
        P("dp", None, None),
        P("dp"),
        P("dp"),
        P(),
        P(None, "dp", "head"),
        P(None, "dp", "head"),
        P(None, "dp", "head"),
        P(None, "dp", "head"),
        P(None, "dp", "head"),
        P("dp", "head"),
        P(None, "dp", "head"),
        P(None, "dp", "head"),
        P(None, "dp", "head"),
        P(None, "dp", "head"),
        P(None, "dp", "head"),
        P(None, "dp", "head"),
        P(None, "dp", "head"),
        P("dp", "head"),
        P("dp", "head"),
        P(None, "dp", "head"),
        P(None, "dp", "head"),
    )
    return jax.shard_map(
        body,
        mesh=mesh,
        in_specs=placed,
        out_specs=(
            P(),
            P(),
            P("dp", None),
            P(None, "dp", "head"),
            P(None, "dp", "head"),
            P(None, "dp", "head"),
            P(None, "dp", "head"),
            P(None, "dp", "head"),
            P(None, "dp", "head"),
            P(None, "dp", "head"),
            P(None, "dp", "head"),
            P(None, "dp", "head"),
            P(None, "dp", "head"),
            P(None, "dp", "head"),
            P("dp", "head"),
            P("dp", "head"),
            P("dp", "head"),
            P(None, "dp", "head"),
            P(None, "dp", "head"),
            P(None, "dp", "head"),
        ),
        check_vma=False,
    )
```

time: 2450 us -> 1190 us (0.49)
  waiting for transfers between devices: 1320 us -> 51.3 us
  Pallas kernels: 0 us -> 576 us
  local copies, waits for them, and re-layouts: 408 us -> 214 us
  blocking collectives: 194 us -> 0 us
  matrix products: 328 us -> 232 us
  other arithmetic: 131 us -> 79.7 us
  starting transfers between devices: 29 us -> 0.04 us
    reduce_scatter x6 -> x0, waiting for transfers between devices: 757 us -> none  [scatter(): lax.psum_scatter(blocks, ('head', 'dp'), scatter_dimension=0, tiled=True)[0]]
    pallas_call x0 -> x19, Pallas kernels: none -> 576 us  [the longest x13 200 us: exchange(): pl.pallas_call(functools.partial(exchange_kernel, axis, count, swapped),...]
    all_gather x6 -> x0, waiting for transfers between devices: 192 us -> none  [whole_weight(): blocks = lax.all_gather(to_bf16(shard), ('head', 'dp'), axis=0, tiled=False)]
    unnamed x21 -> x1, waiting for transfers between devices: 190 us -> 0.02 us
    all_to_all x5 -> x0, waiting for transfers between devices: 119 us -> none  [the longest x2 55.4 us: to_frames(): lax.all_to_all(heads, 'head', split_axis=1, concat_axis=3, tiled=True)]
    dot_general x76 -> x30, matrix products: 254 us -> 154 us  [product(): return jnp.einsum(form, left, right, preferred_element_type=jnp.float32)]
    another operation x25 -> x19, local copies, waits for them, and re-layouts: 114 us -> 27.3 us  [the longest x2 20 us: body(): full.reshape(D, head_count, D)[:, :, 3 * D // head_count:].reshape(D, D)]
    all_gather x4 -> x0, blocking collectives: 75.6 us -> none  [the longest x1 25 us: body(): lax.all_gather(signal_back(grad_signal)[0], 'dp', axis=1, tiled=True)]
  transfers between devices with their start and end apart: 22 -> 1, of which waited for: 16 -> 1; matrix products, arithmetic and copies ran while one was open for 17% -> 0% of each run, Pallas kernels for 0% -> 0%
where the time goes in v2:
time: 1190 us; the launch traced here: 1180 us
  Pallas kernels  576 us (48%)
  matrix products  232 us (19%)
  local copies, waits for them, and re-layouts  214 us (18%)
  other arithmetic  79.7 us (7%)
  waiting for transfers between devices  51.3 us (4%)
  between operations  26.5 us (2%)
    pallas_call x13, Pallas kernels, exchange(): pl.pallas_call(functools.partial(exchange_kernel, axis, count, swapped),...  200 us
    dot_general x30, matrix products, product(): return jnp.einsum(form, left, right, preferred_element_type=jnp.float32)  154 us
    pallas_call x1, Pallas kernels, gather_whole(): pl.pallas_call(functools.partial(gather_kernel, groups), out_shape=[jax.S...  137 us
    pallas_call x1, Pallas kernels, reduce_whole(): pl.pallas_call(functools.partial(reduce_kernel, groups, pieces), out_shap...  125 us
    dot_general x19, matrix products, near_product(): return jnp.einsum(form, left, right, precision=lax.Precision.HIGH)  69.5 us
    pallas_call x1, Pallas kernels, attend_back(): pl.pallas_call(attend_back_kernel, out_shape=[jax.ShapeDtypeStruct(pair_a...  52.6 us
    psum x1, waiting for transfers between devices, body(): gram = lax.psum(near_product('rc,kc->rk', own_matrix, own_matrix), 'head')  51.2 us
    unnamed x365, local copies, waits for them, and re-layouts  39 us
  transfers between devices with their start and end apart: 1, of which 1 were waited for; matrix products, arithmetic and copies ran while one was open for 0% of the time, Pallas kernels for 0%

profile of v2, /device:TPU:11, one launch (start us, length us, event | category | flops | bytes accessed | tf_op | source)
XLA Modules:
  0.0 1180.2 jit_solution(7787803391403577178)
XLA Ops:
  14.2 136.9 %gather_weights.1 = (bf16[2,2,2,112,1024]{4,3,2,1,0:T(8,128)(2,1)}, bf16[2,2,2,96,3072]{4,3,2,1,0:T(8,128)(2,1)}, bf16[2,2,2,96,3072]{4,3,2,1,0:T(8,128)(2,1)}, ...) custom-call(bf16[112,256]{1,0:T(8,128)(2,1)} %maximum_maximum_fusion, ...), custom_call_target="tpu_custom_call" | custom-call | tf_op jit(solution)/shard_map/gather_weights/pallas_call | solution.py:259
  158.3 8.5 spread.8
  182.0 12.1 %swap.5 = f32[8,3,2304]{2,1,0:T(4,128)} custom-call(f32[8,3,2304]{2,1,0:T(4,128)} %reshape.571.x_ref), custom_call_target="tpu_custom_call" | custom-call | tf_op jit(solution)/shard_map/swap/pallas_call | solution.py:139
  206.3 7.0 convolution_convert_fusion
  213.2 8.1 reshape.576
  227.6 10.1 reshape_reshape.14
  259.7 33.5 %attend.1 = (bf16[2,416,384]{2,1,0:T(8,128)(2,1)}, bf16[4,208,256]{2,1,0:T(8,128)(2,1)}, bf16[2,416,1152]{2,1,0:T(8,128)(2,1)}, bf16[4,208,768]{2,1,0:T(8,128)(2,1)}, f32[832,128]{1,0:T(8,128)}) custom-call(bf16[2,416,1152]{2,1,0:T(8,128)(2,1)} %copy.262.pair_in, bf16[4,208,768]{2,1,0:T(8,128)(2,1)} %copy.263.quad_in), custom_call_target="tpu_custom_call" | custom-call | tf_op jit(solution)/shard_map/attend/pallas_call | solution.py:584
  326.0 9.8 reshape_reshape.15
  362.4 9.7 cross.1
  414.8 10.7 fusion.9
  437.2 18.4 %cross_back.1 = (bf16[3,208,768]{2,1,0:T(8,128)(2,1)}, bf16[2,256,768]{2,1,0:T(8,128)(2,1)}, bf16[2,256,768]{2,1,0:T(8,128)(2,1)}) custom-call(bf16[3,208,768]{2,1,0:T(8,128)(2,1)} %pad_maximum_fusion.2.query_ref, bf16[2,256,1536]{2,1,0:T(8,128)(2,1)} %copy.334.keys_ref.values_ref, bf16[2,256,1536]{2,1,0:T(8,128)(2,1)} %copy.334.keys_ref.values_ref, ...), custom_call_target="tpu_custom_call" | custom-call | tf_op jit(solution)/shard_map/cross_back/pallas_call | solution.py:787
  466.8 11.3 fusion.5
  494.3 52.6 %attend_back.1 = (bf16[2,416,1152]{2,1,0:T(8,128)(2,1)}, bf16[4,208,768]{2,1,0:T(8,128)(2,1)}) custom-call(bf16[2,416,1152]{2,1,0:T(8,128)(2,1)} %get-tuple-element.47.pair_all, bf16[4,208,768]{2,1,0:T(8,128)(2,1)} %get-tuple-element.48.quad_all, f32[832,128]{1,0:T(8,128)} %get-tuple-element.49.log_ref, bf16[2,416,384]{2,1,0:T(8,128)(2,1)} %bitcast.358, ...), custom_call_target="tpu_custom_call" | custom-call | tf_op jit(solution)/shard_map/attend_back/pallas_call | solution.py:686
  551.0 6.8 copy.281
  557.8 7.2 concatenate.118
  569.4 9.0 fusion.21
  578.4 7.8 dot_general.197
  586.2 6.9 multiply_reduce_fusion
  606.0 6.9 swap.6
  614.8 11.8 swap.7
  631.8 11.5 fusion.127
  653.4 11.5 fusion.122
  697.6 18.5 %concatenate.127 = bf16[1760,3072]{0,1:T(8,128)(2,1)} concatenate(bf16[624,3072]{0,1:T(8,128)(2,1)} %bitcast.325, bf16[624,3072]{0,1:T(8,128)(2,1)} %bitcast.326, bf16[512,3072]{0,1:T(8,128)(2,1)} %bitcast.328), dimensions={0} | concatenate | bytes 21626880 | tf_op jit(solution)/shard_map/concatenate | solution.py:1092
  716.1 14.6 %fusion.22 = f32[768,3072]{1,0:T(8,128)} fusion(bf16[1760,3072]{0,1:T(8,128)(2,1)} %concatenate.127, bf16[512,768]{1,0:T(8,128)(2,1)} %bitcast.380, bf16[624,768]{1,0:T(8,128)(2,1)S(1)} %bitcast.375, bf16[624,768]{1,0:T(8,128)(2,1)S(1)} %bitcast.374), kind=kOutput, calls=%fused_computation.49 | convolution fusion | flops 8312832000 | bytes 22953984 | tf_op jit(solution)/shard_map/kd,kn->dn/dot_general | solution.py:69
  730.8 9.0 fusion.16
  739.8 125.4 %reduce_grads.1 = f32[18,96,256]{2,1,0:T(8,128)} custom-call(f32[2,2,2,96,3072]{4,3,2,1,0:T(8,128)} %bitcast.337, f32[2,2,2,96,3072]{4,3,2,1,0:T(8,128)} %bitcast.317, f32[2,2,2,96,3072]{4,3,2,1,0:T(8,128)} %bitcast.335, f32[2,2,2,96,3072]{4,3,2,1,0:T(8,128)} %bitcast.336, f32[2,2,2,96,3072]{4,3,2,1,0:T(8,128)} %bitcast.316, f32[2,2,2,96,3072]{4,3,2,1,0:T(8,128)} %bitcast.334), custom_call_target="tpu_custom_call" | custom-call | tf_op jit(solution)/shard_map/reduce_grads/pallas_call | solution.py:426
  867.0 8.0 spread.12
  877.3 6.8 spread.13
  920.4 57.3 %swap.8 = f32[8,96,768]{2,1,0:T(8,128)} custom-call(f32[8,96,768]{2,1,0:T(8,128)} %fusion.36.x_ref), custom_call_target="tpu_custom_call" | custom-call | tf_op jit(solution)/shard_map/swap/pallas_call | solution.py:139
  977.8 6.9 fusion.267
  990.4 51.2 %all-reduce.15.cloned.1.call-done = f32[768,768]{1,0:T(8,128)} async-done(((f32[768,768]{1,0:T(8,128)}), f32[768,768]{1,0:T(8,128)}) %all-reduce.15.cloned.1.call-update) | async-done | bytes 2359312 | tf_op jit(solution)/shard_map/psum | solution.py:1168
  1107.5 58.4 %swap.9 = f32[8,96,768]{2,1,0:T(8,128)} custom-call(f32[8,96,768]{2,1,0:T(8,128)} %bitcast.363), custom_call_target="tpu_custom_call" | custom-call | tf_op jit(solution)/shard_map/swap/pallas_call | solution.py:139
  (666 shorter events, 389.4 us)
Async XLA Ops:
  7.2 1034.4 %all-reduce.15.cloned.1.call-start = ((), (), s32[]{:S(2)}) async-start(), calls=%async_computation | async-start | bytes 4718592 | tf_op jit(solution)/shard_map/psum | solution.py:1168
  9.1 163.0 %copy-start.75 = (f32[1,208,40]{1,2,0:T(8,128)}, f32[1,208,40]{1,2,0:T(8,128)S(1)}, u32[]{:S(2)}) copy-start(f32[1,208,40]{1,2,0:T(8,128)S(1)} %fusion.141) | copy-start | bytes 99844
  173.4 30.8 %copy-start.96 = (f32[3,208]{1,0:T(4,128)}, f32[3,208]{1,0:T(4,128)S(1)}, u32[]{:S(2)}) copy-start(f32[3,208]{1,0:T(4,128)S(1)} %broadcast_multiply_fusion.7) | copy-start | bytes 7492
  174.4 29.8 %copy-start.102 = (f32[3,208]{1,0:T(4,128)}, f32[3,208]{1,0:T(4,128)S(1)}, u32[]{:S(2)}) copy-start(f32[3,208]{1,0:T(4,128)S(1)} %fusion.168) | copy-start | bytes 7492
  180.7 24.6 %copy-start.88 = (f32[24,768]{1,0:T(8,128)}, f32[24,768]{1,0:T(8,128)S(1)}, u32[]{:S(2)}) copy-start(f32[24,768]{1,0:T(8,128)S(1)} %get-tuple-element.216) | copy-start | bytes 221188
  353.4 18.7 %copy-start.92 = (f32[3,1,1,768]{3,0,1,2:T(4,128)}, f32[3,1,1,768]{3,0,1,2:T(4,128)S(1)}, u32[]{:S(2)}) copy-start(f32[3,1,1,768]{3,0,1,2:T(4,128)S(1)} %copy.373) | copy-start | bytes 27652
  376.1 36.2 %copy-start.136 = (f32[3,1,1,768]{3,0,1,2:T(4,128)}, f32[3,1,1,768]{3,0,1,2:T(4,128)S(1)}, u32[]{:S(2)}) copy-start(f32[3,1,1,768]{3,0,1,2:T(4,128)S(1)} %copy.370) | copy-start | bytes 27652
  388.5 18.4 %copy-start.147 = (s32[3]{0:T(128)S(1)}, s32[3]{0:T(128)}, u32[]{:S(2)}) copy-start(s32[3]{0:T(128)} %param.29) | copy-start | bytes 40
  388.5 19.6 %copy-start.89 = (bf16[1,768,4,5]{1,2,3,0:T(4,128)(2,1)S(1)}, bf16[1,768,4,5]{1,2,3,0:T(4,128)(2,1)}, u32[]{:S(2)}) copy-start(bf16[1,768,4,5]{1,2,3,0:T(4,128)(2,1)} %get-tuple-element.202) | copy-start | bytes 92164
  388.5 19.6 %copy-start.71 = (f32[2,1,208,40]{2,3,0,1:T(8,128)S(1)}, f32[2,1,208,40]{2,3,0,1:T(8,128)}, u32[]{:S(2)}) copy-start(f32[2,1,208,40]{2,3,0,1:T(8,128)} %copy-done.70) | copy-start | bytes 199684
  388.5 19.6 %copy-start.76 = (f32[1,208,40]{1,2,0:T(8,128)S(1)}, f32[1,208,40]{1,2,0:T(8,128)}, u32[]{:S(2)}) copy-start(f32[1,208,40]{1,2,0:T(8,128)} %copy-done.75) | copy-start | bytes 99844
  389.4 22.2 %copy-start.94 = (f32[3,208]{1,0:T(4,128)}, f32[3,208]{1,0:T(4,128)S(1)}, u32[]{:S(2)}) copy-start(f32[3,208]{1,0:T(4,128)S(1)} %fusion.172) | copy-start | bytes 7492
  396.3 14.6 %copy-start.132 = (f32[3,768]{1,0:T(4,128)}, f32[3,768]{1,0:T(4,128)S(1)}, u32[]{:S(2)}) copy-start(f32[3,768]{1,0:T(4,128)S(1)} %get-tuple-element.151) | copy-start | bytes 27652
  411.6 13.9 %slice-start.11 = ((s8[4718592]{0:T(1024)(128)(4,1)}), s8[4194304]{0:T(1024)(128)(4,1)S(1)}, s32[]{:S(2)}) async-start(s8[4718592]{0:T(1024)(128)(4,1)} %bitcast.437), calls=%async_computation.12 | async-start | bytes 8388608
  412.3 18.2 %copy-start.22 = (f32[3,208,768]{2,1,0:T(8,128)}, f32[3,208,768]{2,1,0:T(8,128)S(1)}, u32[]{:S(2)}) copy-start(f32[3,208,768]{2,1,0:T(8,128)S(1)} %get-tuple-element.149) | copy-start | bytes 5750788
  412.3 18.2 %copy-start.129 = (f32[3,208]{1,0:T(4,128)}, f32[3,208]{1,0:T(4,128)S(1)}, u32[]{:S(2)}) copy-start(f32[3,208]{1,0:T(4,128)S(1)} %negate_multiply_fusion.4) | copy-start | bytes 7492
  437.2 20.5 %slice-start = ((s8[4718592]{0:T(1024)(128)(4,1)}), s8[524288]{0:T(1024)(128)(4,1)S(1)}, s32[]{:S(2)}) async-start(s8[4718592]{0:T(1024)(128)(4,1)} %bitcast.346), calls=%async_computation.1 | async-start | bytes 1048576
  465.3 14.7 %slice-start.5 = ((s8[4718592]{0:T(1024)(128)(4,1)}), s8[4194304]{0:T(1024)(128)(4,1)S(1)}, s32[]{:S(2)}) async-start(s8[4718592]{0:T(1024)(128)(4,1)} %bitcast.427), calls=%async_computation.6 | async-start | bytes 8388608
  466.8 18.2 %copy-start.26 = (f32[3,208,768]{2,1,0:T(8,128)}, f32[3,208,768]{2,1,0:T(8,128)S(1)}, u32[]{:S(2)}) copy-start(f32[3,208,768]{2,1,0:T(8,128)S(1)} %get-tuple-element.145) | copy-start | bytes 5750788
  605.2 22.7 %copy-start.20 = (f32[2,96,1152]{2,1,0:T(8,128)S(1)}, f32[2,96,1152]{2,1,0:T(8,128)}, u32[]{:S(2)}) copy-start(f32[2,96,1152]{2,1,0:T(8,128)} %param.35) | copy-start | bytes 2654212
  614.0 17.8 %copy-start.130 = (f32[3,208]{1,0:T(4,128)S(1)}, f32[3,208]{1,0:T(4,128)}, u32[]{:S(2)}) copy-start(f32[3,208]{1,0:T(4,128)} %copy-done.129) | copy-start | bytes 7492
  614.0 17.8 %copy-start.137 = (f32[3,1,1,768]{3,0,1,2:T(4,128)S(1)}, f32[3,1,1,768]{3,0,1,2:T(4,128)}, u32[]{:S(2)}) copy-start(f32[3,1,1,768]{3,0,1,2:T(4,128)} %copy-done.136) | copy-start | bytes 27652
  697.6 18.5 %copy-start.62 = (bf16[3,208,768]{2,1,0:T(8,128)(2,1)S(1)}, bf16[3,208,768]{2,1,0:T(8,128)(2,1)}, u32[]{:S(2)}) copy-start(bf16[3,208,768]{2,1,0:T(8,128)(2,1)} %copy-done.61) | copy-start | bytes 2875396
  697.6 18.5 %copy-start.64 = (bf16[3,208,768]{2,1,0:T(8,128)(2,1)S(1)}, bf16[3,208,768]{2,1,0:T(8,128)(2,1)}, u32[]{:S(2)}) copy-start(bf16[3,208,768]{2,1,0:T(8,128)(2,1)} %copy-done.63) | copy-start | bytes 2875396
  716.1 14.7 %copy-start.35 = (bf16[78,8,4,768]{3,1,2,0:T(8,128)(2,1)S(1)}, bf16[78,8,4,768]{3,1,2,0:T(8,128)(2,1)}, u32[]{:S(2)}) copy-start(bf16[78,8,4,768]{3,1,2,0:T(8,128)(2,1)} %copy.340) | copy-start | bytes 11501572
  716.1 14.7 %copy-start.36 = (bf16[624,3072]{1,0:T(8,128)(2,1)S(1)}, bf16[624,3072]{1,0:T(8,128)(2,1)}, u32[]{:S(2)}) copy-start(bf16[624,3072]{1,0:T(8,128)(2,1)} %copy.287) | copy-start | bytes 11501572
  716.1 14.7 %copy-start.60 = (bf16[3,208,768]{2,1,0:T(8,128)(2,1)S(1)}, bf16[3,208,768]{2,1,0:T(8,128)(2,1)}, u32[]{:S(2)}) copy-start(bf16[3,208,768]{2,1,0:T(8,128)(2,1)} %copy-done.59) | copy-start | bytes 2875396
  716.1 14.7 %copy-start.66 = (bf16[3,208,768]{2,1,0:T(8,128)(2,1)S(1)}, bf16[3,208,768]{2,1,0:T(8,128)(2,1)}, u32[]{:S(2)}) copy-start(bf16[3,208,768]{2,1,0:T(8,128)(2,1)} %copy-done.65) | copy-start | bytes 2875396
  887.0 28.9 %copy-start.72 = (f32[2,96,768]{2,1,0:T(8,128)S(1)}, f32[2,96,768]{2,1,0:T(8,128)}, u32[]{:S(2)}) copy-start(f32[2,96,768]{2,1,0:T(8,128)} %param.40) | copy-start | bytes 1769476
  918.7 59.0 %copy-start.68 = (f32[2,96,192]{2,1,0:T(8,128)}, f32[2,96,192]{2,1,0:T(8,128)S(1)}, u32[]{:S(2)}) copy-start(f32[2,96,192]{2,1,0:T(8,128)S(1)} %multiply_add_fusion.11) | copy-start | bytes 442372
  1107.5 58.4 %copy-start.43 = (f32[2,96,768]{2,1,0:T(8,128)S(1)}, f32[2,96,768]{2,1,0:T(8,128)}, u32[]{:S(2)}) copy-start(f32[2,96,768]{2,1,0:T(8,128)} %param.34) | copy-start | bytes 1769476
  1107.5 58.4 %copy-start.45 = (f32[2,96,768]{2,1,0:T(8,128)S(1)}, f32[2,96,768]{2,1,0:T(8,128)}, u32[]{:S(2)}) copy-start(f32[2,96,768]{2,1,0:T(8,128)} %param.33) | copy-start | bytes 1769476
  (136 other events, 599.7 us)
Sparse Core Ops, SparseCore 0:
  984.8 56.7 all-reduce.14

commit v3 on v2

--- a/solution.py
+++ b/solution.py
@@ -284,53 +284,105 @@
     return blocks.transpose(0, 2, 1, 3).reshape(-1, lax.axis_size("head") * columns)
 
 
-def reduce_kernel(groups, pieces, *refs):
-    part_refs = refs[:groups]
-    out_ref = refs[groups]
-    (own, near, send_a, send_b, got_a, got_b, keep_a, keep_b, own_sem, near_send, near_recv,
-     hop_send, hop_recv) = refs[groups + 1 :]
-    per_group = 768 // PIECE_COLS
+def reduce_kernel(layers, *refs):
+    first_refs = refs[:layers]
+    left_refs = refs[layers : 3 * layers]
+    right_refs = refs[3 * layers : 5 * layers]
+    extra_ref, out_ref, total_ref, edge_ref = refs[5 * layers : 5 * layers + 4]
+    (own, near, made, left, left_t, right, send_a, send_b, got_a, got_b, keep_a, keep_b,
+     mine, head_got, data_got, own_sem, near_send, near_recv, hop_send, hop_recv, left_sem,
+     right_sem, edge_send, edge_recv, sum_send, sum_recv) = refs[5 * layers + 4 :]
+    per_group = D // PIECE_COLS
+    pieces = 3 * layers * per_group
     d = lax.axis_index("dp")
     h = lax.axis_index("head")
     peers = link_peers(d, h)
-    greet(list(peers.values()))
+    across = [(d, h ^ other) for other in (1, 2, 3)] + [(d ^ other, h) for other in range(1, 8)]
+    greet(across)
     y, c = h // 2, h % 2
     zh, zl, x = d // 4, (d // 2) % 2, d % 2
     order = (("y", "x"), ("x", "zl"), ("zl", "zh"), ("zh", "y"))
-    bottom_rows = own.shape[-2] - ROWS_A
-    top, bottom = pl.ds(0, ROWS_A), pl.ds(ROWS_A, bottom_rows)
+    rows_own = own.shape[-2]
+    top, bottom = pl.ds(0, ROWS_A), pl.ds(ROWS_A, rows_own - ROWS_A)
     every = slice(None)
 
-    def columns_of(piece, group, head):
-        width = part_refs[group].shape[-1] // 4
-        start = head * width + (piece % per_group) * PIECE_COLS
+    def columns_of(piece, head):
+        start = head * D + (piece % per_group) * PIECE_COLS
         return pl.ds(pl.multiple_of(start, PIECE_COLS), PIECE_COLS)
 
-    def own_copy(piece, group, side):
+    def own_copy(piece, layer, side):
         return pltpu.make_async_copy(
-            part_refs[group].at[:, :, :, :, columns_of(piece, group, 2 * side + c)],
+            first_refs[layer].at[:, :, :, :, columns_of(piece, 2 * side + c)],
             own.at[piece % SLOTS, side],
             own_sem.at[piece % SLOTS, side],
         )
 
-    def near_copy(piece, group, side):
+    def near_copy(piece, layer, side):
+        slot = piece % SLOTS
+        source = made.at[slot, side]
+        if layer is not None:
+            source = first_refs[layer].at[:, :, :, :, columns_of(piece, 2 * side + 1 - c)]
         return pltpu.make_async_remote_copy(
-            src_ref=part_refs[group].at[:, :, :, :, columns_of(piece, group, 2 * side + 1 - c)],
-            dst_ref=near.at[piece % SLOTS, side],
-            send_sem=near_send.at[piece % SLOTS, side],
-            recv_sem=near_recv.at[piece % SLOTS, side],
+            src_ref=source,
+            dst_ref=near.at[slot, side],
+            send_sem=near_send.at[slot, side],
+            recv_sem=near_recv.at[slot, side],
             device_id=peers["core"],
             device_id_type=MESH,
         )
 
+    def left_copy(pair):
+        return pltpu.make_async_copy(left_refs[pair], left.at[pair], left_sem.at[pair])
+
+    def right_copy(piece, pair, head):
+        return pltpu.make_async_copy(
+            right_refs[pair].at[:, columns_of(piece, head)],
+            right.at[piece % 2, head],
+            right_sem.at[piece % 2, head],
+        )
+
+    def is_made(piece):
+        return (piece // per_group) % 3 != 0
+
+    def fetch(piece):
+        for layer in range(layers):
+            for member in range(2):
+
+                @pl.when(piece // per_group == 3 * layer + 1 + member)
+                def _():
+                    for head in range(4):
+                        right_copy(piece, 2 * layer + member, head).start()
+
     def bring(piece):
-        for group in range(groups):
-
-            @pl.when(piece // per_group == group)
+        slot = piece % SLOTS
+        for layer in range(layers):
+
+            @pl.when(piece // per_group == 3 * layer)
             def _():
                 for side in range(2):
-                    near_copy(piece, group, side).start()
-                    own_copy(piece, group, side).start()
+                    near_copy(piece, layer, side).start()
+                    own_copy(piece, layer, side).start()
+
+            for member in range(2):
+
+                @pl.when(piece == (3 * layer + 1 + member) * per_group)
+                def _():
+                    pair = 2 * layer + member
+                    left_copy(pair).wait()
+                    left_t[...] = left[pair].T
+
+        @pl.when(is_made(piece))
+        def _():
+            for head in range(4):
+                right_copy(piece, 0, head).wait()
+            shape = own.shape[2:]
+            for side in range(2):
+                made[slot, side] = dot_nn(left_t[...], right[piece % 2, 2 * side + 1 - c]).reshape(
+                    shape
+                )
+                near_copy(piece, None, side).start()
+            for side in range(2):
+                own[slot, side] = dot_nn(left_t[...], right[piece % 2, 2 * side + c]).reshape(shape)
 
     def hop(piece, step, stream):
         slot = piece % SLOTS
@@ -347,8 +399,12 @@
     def first(piece):
         slot = piece % SLOTS
         for side in range(2):
-            near_copy(piece, 0, side).wait()
-            own_copy(piece, 0, side).wait()
+            near_copy(piece, None, side).wait()
+
+        @pl.when(jnp.logical_not(is_made(piece)))
+        def _():
+            for side in range(2):
+                own_copy(piece, 0, side).wait()
 
         def total(*index):
             return own[(slot,) + index] + near[(slot,) + index]
@@ -387,13 +443,16 @@
                 slot
             ].astype(jnp.float32)
 
+    for pair in range(2 * layers):
+        left_copy(pair).start()
     bring(0)
+    bring(1)
 
     @pl.loop(0, pieces + 4)
     def _(turn):
-        @pl.when(turn + 1 < pieces)
+        @pl.when(turn + 3 < pieces)
         def _():
-            bring(turn + 1)
+            fetch(turn + 3)
 
         @pl.when(turn < pieces)
         def _():
@@ -409,13 +468,67 @@
         def _():
             last(turn - 4)
 
-
-def reduce_whole(parts, collective_id):
-    groups = len(parts)
-    rows = parts[0].shape[0] // 8
-    widths = [part.shape[1] // 4 for part in parts]
-    pieces = sum(widths) // PIECE_COLS
-    views = [part.reshape(2, 2, 2, rows, part.shape[1]) for part in parts]
+        @pl.when(turn + 2 < pieces)
+        def _():
+            bring(turn + 2)
+
+    edges = []
+    for layer in range(layers):
+        piece = (3 * layer + 1) * per_group - 1
+        edges.append(
+            pltpu.make_async_remote_copy(
+                src_ref=out_ref.at[piece, :, pl.ds(0, 128)],
+                dst_ref=edge_ref.at[layer],
+                send_sem=edge_send.at[layer],
+                recv_sem=edge_recv.at[layer],
+                device_id=peers["core"],
+                device_id_type=MESH,
+            )
+        )
+        edges[-1].start()
+
+    squares = jnp.zeros((rows_own, PIECE_COLS), jnp.float32)
+    for piece in range(pieces):
+        squares = squares + out_ref[piece] * out_ref[piece]
+    row = lax.broadcasted_iota(jnp.int32, (8, 128), 0)
+    column = lax.broadcasted_iota(jnp.int32, (8, 128), 1)
+    mine[0] = extra_ref[...] + jnp.where((row == 0) & (column == 0), jnp.sum(squares), 0.0)
+    for phase, (got, me, count) in enumerate(((head_got, h, 4), (data_got, d, 8))):
+        copies = []
+        for other in range(1, count):
+            place = 3 * phase + other - 1
+            copies.append(
+                pltpu.make_async_remote_copy(
+                    src_ref=mine.at[phase],
+                    dst_ref=got.at[me],
+                    send_sem=sum_send.at[place],
+                    recv_sem=sum_recv.at[place],
+                    device_id=across[place],
+                    device_id_type=MESH,
+                )
+            )
+            copies[-1].start()
+        got[me] = mine[phase]
+        for copy in copies:
+            copy.wait()
+        total = got[0]
+        for other in range(1, count):
+            total = total + got[other]
+        if phase == 0:
+            mine[1] = total
+        else:
+            total_ref[...] = total
+    for copy in edges:
+        copy.wait()
+
+
+def reduce_whole(firsts, pairs, extra, collective_id):
+    layers = len(firsts)
+    frames = pairs[0][0].shape[0]
+    rows = firsts[0].shape[0] // 8
+    per_group = D // PIECE_COLS
+    pieces = 3 * layers * per_group
+    views = [first.reshape(2, 2, 2, rows, first.shape[1]) for first in firsts]
     leads = ((2, 2, 2), (2, 2), (2,), ())
 
     def buffers(count, dtype):
@@ -423,35 +536,49 @@
 
     bottom_rows = rows - ROWS_A
     whole = (SLOTS, 2, 2, 2, 2, rows, PIECE_COLS)
-    summed = pl.pallas_call(
-        functools.partial(reduce_kernel, groups, pieces),
-        out_shape=jax.ShapeDtypeStruct((pieces, rows, PIECE_COLS), jnp.float32),
-        in_specs=[anywhere()] * groups,
-        out_specs=vmem(),
+    low = jnp.bfloat16
+    summed, totals, edges = pl.pallas_call(
+        functools.partial(reduce_kernel, layers),
+        out_shape=[
+            jax.ShapeDtypeStruct((pieces, rows, PIECE_COLS), jnp.float32),
+            jax.ShapeDtypeStruct((8, 128), jnp.float32),
+            jax.ShapeDtypeStruct((layers, rows, 128), jnp.float32),
+        ],
+        in_specs=[anywhere()] * (5 * layers) + [vmem()],
+        out_specs=[vmem()] * 3,
         scratch_shapes=[
             pltpu.VMEM(whole, jnp.float32),
             pltpu.VMEM(whole, jnp.float32),
-            buffers(ROWS_A, jnp.bfloat16),
-            buffers(bottom_rows, jnp.bfloat16),
-            buffers(ROWS_A, jnp.bfloat16),
-            buffers(bottom_rows, jnp.bfloat16),
+            pltpu.VMEM(whole, jnp.float32),
+            pltpu.VMEM((2 * layers, frames, D), low),
+            pltpu.VMEM((D, frames), low),
+            pltpu.VMEM((2, 4, frames, PIECE_COLS), low),
+            buffers(ROWS_A, low),
+            buffers(bottom_rows, low),
+            buffers(ROWS_A, low),
+            buffers(bottom_rows, low),
             buffers(ROWS_A, jnp.float32),
             buffers(bottom_rows, jnp.float32),
+            pltpu.VMEM((2, 8, 128), jnp.float32),
+            pltpu.VMEM((4, 8, 128), jnp.float32),
+            pltpu.VMEM((8, 8, 128), jnp.float32),
             pltpu.SemaphoreType.DMA((SLOTS, 2)),
             pltpu.SemaphoreType.DMA((SLOTS, 2)),
             pltpu.SemaphoreType.DMA((SLOTS, 2)),
             pltpu.SemaphoreType.DMA((4, 2, SLOTS)),
             pltpu.SemaphoreType.DMA((4, 2, SLOTS)),
+            pltpu.SemaphoreType.DMA((2 * layers,)),
+            pltpu.SemaphoreType.DMA((2, 4)),
+            pltpu.SemaphoreType.DMA((layers,)),
+            pltpu.SemaphoreType.DMA((layers,)),
+            pltpu.SemaphoreType.DMA((10,)),
+            pltpu.SemaphoreType.DMA((10,)),
         ],
         compiler_params=comm_params(collective_id),
         name="reduce_grads",
-    )(*views)
-    blocks, at = [], 0
-    for width in widths:
-        count = width // PIECE_COLS
-        blocks.append(summed[at : at + count].transpose(1, 0, 2).reshape(rows, width))
-        at += count
-    return blocks
+    )(*views, *[pair[0] for pair in pairs], *[pair[1] for pair in pairs], extra)
+    summed = summed.reshape(3 * layers, per_group, rows, PIECE_COLS).transpose(0, 2, 1, 3)
+    return list(summed.reshape(3 * layers, rows, D)), totals, edges
 
 
 def reduce_general(part):
@@ -461,6 +588,196 @@
     ).transpose(0, 2, 1, 3)
     blocks = blocks.reshape((-1,) + blocks.shape[2:])
     return lax.psum_scatter(blocks, ("dp", "head"), scatter_dimension=0, tiled=True)[0]
+
+
+KIND_AT = (1, 2, 3, 0)
+
+
+def owner_of(kind, layer):
+    return 4 * layer + KIND_AT.index(kind)
+
+
+def is_owner_of(me, kind):
+    return (me % 4 == KIND_AT.index(kind)) & (me < 8)
+
+
+def to_owner_kernel(count, *refs):
+    block_refs, out_ref, send_sem, recv_sem = refs[:4], refs[4], refs[5], refs[6]
+    me = lax.axis_index("dp")
+    out_ref[...] = jnp.zeros_like(out_ref)
+    greet([{"dp": lax.rem(me + shift, count)} for shift in range(1, count)])
+
+    def copy(kind, layer, source):
+        width = block_refs[kind].shape[-1]
+        return pltpu.make_async_remote_copy(
+            src_ref=block_refs[kind].at[layer],
+            dst_ref=out_ref.at[source, :, pl.ds(0, width)],
+            send_sem=send_sem.at[2 * kind + layer],
+            recv_sem=recv_sem.at[source],
+            device_id={"dp": owner_of(kind, layer)},
+            device_id_type=MESH,
+        )
+
+    for kind in range(4):
+        for layer in range(2):
+
+            @pl.when(me != owner_of(kind, layer))
+            def _():
+                copy(kind, layer, me).start()
+
+            @pl.when(me == owner_of(kind, layer))
+            def _():
+                out_ref[me, :, : block_refs[kind].shape[-1]] = block_refs[kind][layer]
+
+    for kind in range(4):
+
+        @pl.when(is_owner_of(me, kind))
+        def _():
+            @pl.loop(0, count)
+            def _(source):
+                @pl.when(source != me)
+                def _():
+                    copy(kind, 0, source).wait_recv()
+
+        for layer in range(2):
+
+            @pl.when(me != owner_of(kind, layer))
+            def _():
+                copy(kind, layer, me).wait_send()
+
+
+def to_owner(blocks, collective_id):
+    count = lax.axis_size("dp")
+    rows = blocks[0].shape[1]
+    wide = max(block.shape[2] for block in blocks)
+    return pl.pallas_call(
+        functools.partial(to_owner_kernel, count),
+        out_shape=jax.ShapeDtypeStruct((count, rows, wide), jnp.float32),
+        in_specs=[vmem()] * 4,
+        out_specs=vmem(),
+        scratch_shapes=[pltpu.SemaphoreType.DMA((8,)), pltpu.SemaphoreType.DMA((count,))],
+        compiler_params=comm_params(collective_id),
+        name="to_owner",
+    )(*blocks)
+
+
+def from_owner_kernel(count, widths, x_ref, out_ref, send_sem, recv_sem):
+    me = lax.axis_index("dp")
+    greet([{"dp": lax.rem(me + shift, count)} for shift in range(1, count)])
+
+    def copy(kind, matrix, target):
+        columns = pl.ds(0, widths[kind])
+        return pltpu.make_async_remote_copy(
+            src_ref=x_ref.at[target, :, columns],
+            dst_ref=out_ref.at[matrix, :, columns],
+            send_sem=send_sem.at[target],
+            recv_sem=recv_sem.at[matrix],
+            device_id={"dp": target},
+            device_id_type=MESH,
+        )
+
+    for kind in range(4):
+
+        @pl.when(is_owner_of(me, kind))
+        def _():
+            @pl.loop(0, count)
+            def _(target):
+                @pl.when(target != me)
+                def _():
+                    copy(kind, me, target).start()
+
+            out_ref[me] = x_ref[me]
+
+    for kind in range(4):
+        for layer in range(2):
+            matrix = owner_of(kind, layer)
+
+            @pl.when(me != matrix)
+            def _():
+                copy(kind, matrix, me).wait_recv()
+
+        @pl.when(is_owner_of(me, kind))
+        def _():
+            @pl.loop(0, count)
+            def _(target):
+                @pl.when(target != me)
+                def _():
+                    copy(kind, me, target).wait_send()
+
+
+def from_owner(x, widths, collective_id):
+    count = lax.axis_size("dp")
+    return pl.pallas_call(
+        functools.partial(from_owner_kernel, count, widths),
+        out_shape=jax.ShapeDtypeStruct((8,) + x.shape[1:], x.dtype),
+        in_specs=[vmem()],
+        out_specs=vmem(),
+        scratch_shapes=[pltpu.SemaphoreType.DMA((count,)), pltpu.SemaphoreType.DMA((8,))],
+        compiler_params=comm_params(collective_id),
+        name="from_owner",
+    )(x)
+
+
+def gram_kernel(x_ref, out_ref, high, rest, upper, chip, got, whole, send_sem, recv_sem):
+    h = lax.axis_index("head")
+    c = h % 2
+    greet([{"head": h ^ other} for other in (1, 2)])
+    third = PIECE_COLS
+    values = x_ref[...]
+    high[...] = to_bf16(values)
+    rest[...] = to_bf16(values - high[...].astype(jnp.float32))
+
+    def dots(first, second):
+        return (
+            dot_nt(high[first], high[second])
+            + dot_nt(high[first], rest[second])
+            + dot_nt(rest[first], high[second])
+        )
+
+    r0, r1, r2 = (pl.ds(third * place, third) for place in range(3))
+    upper[0] = dots(r0, pl.ds(0, 3 * third))
+    upper[1, :, : 2 * third] = dots(r1, pl.ds(third, 2 * third))
+    upper[1, :, 2 * third :] = dots(r2, r2)
+
+    def step(place, source, target, peer):
+        copy = send_to(source, target, (send_sem, recv_sem), place, peer)
+        copy.start()
+        copy.wait()
+
+    step(0, upper.at[1 - c], got.at[0], h ^ 1)
+    chip[...] = upper[c] + got[0]
+    step(1, chip, got.at[1], h ^ 2)
+    whole[c] = chip[...] + got[1]
+    step(2, whole.at[c], whole.at[c], h ^ 1)
+    out_ref[r0, :] = whole[0]
+    out_ref[r1, pl.ds(third, 2 * third)] = whole[1, :, : 2 * third]
+    out_ref[r2, r2] = whole[1, :, 2 * third :]
+    out_ref[r1, r0] = whole[0, :, third : 2 * third].T
+    out_ref[r2, r0] = whole[0, :, 2 * third :].T
+    out_ref[r2, r1] = whole[1, :, third : 2 * third].T
+
+
+def gram_sum(x, collective_id):
+    rows, columns = x.shape
+    third = PIECE_COLS
+    return pl.pallas_call(
+        gram_kernel,
+        out_shape=jax.ShapeDtypeStruct((rows, rows), jnp.float32),
+        in_specs=[vmem()],
+        out_specs=vmem(),
+        scratch_shapes=[
+            pltpu.VMEM((rows, columns), jnp.bfloat16),
+            pltpu.VMEM((rows, columns), jnp.bfloat16),
+            pltpu.VMEM((2, third, rows), jnp.float32),
+            pltpu.VMEM((third, rows), jnp.float32),
+            pltpu.VMEM((2, third, rows), jnp.float32),
+            pltpu.VMEM((2, third, rows), jnp.float32),
+            pltpu.SemaphoreType.DMA((3,)),
+            pltpu.SemaphoreType.DMA((3,)),
+        ],
+        compiler_params=comm_params(collective_id),
+        name="gram_sum",
+    )(x)
 
 
 def send_to(source, target, sems, place, peer):
@@ -474,9 +791,9 @@
     )
 
 
-def half_mask(pair_half):
+def half_mask(half):
     lane = lax.broadcasted_iota(jnp.int32, (1, 128), 1)
-    return (lane // 64) == pair_half
+    return (lane // 64) == half
 
 
 def dot_nt(left, right):
@@ -497,213 +814,272 @@
     )
 
 
-def own_exchange(h, pair_in, pair_all, quad_in, quad_all, sems, start_place):
+def lanes(start, size):
+    return pl.ds(pl.multiple_of(start, 128), size)
+
+
+def window(head):
+    return 128 * ((3 * head) // 2)
+
+
+def bring_heads(h, rows_ref, pair_all, quad_all, parts, sems):
     c = h % 2
-    pair = [send_to(pair_in.at[1 - c], pair_all.at[c], sems, start_place, h ^ 1)]
-    quad = [
-        send_to(quad_in.at[h ^ other], quad_all.at[h], sems, start_place + other, h ^ other)
-        for other in (1, 2, 3)
-    ]
+    tile = quad_all.shape[1]
+    own, shared = pl.ds(0, 2 * tile), pl.ds(2 * tile, tile)
+    pair, quad = [], []
+    for part in range(parts):
+        pair.append(
+            send_to(
+                rows_ref.at[own, lanes(part * D + (1 - c) * HALF, HALF)],
+                pair_all.at[c, :, pl.ds(part * HALF, HALF)],
+                sems, part, h ^ 1,
+            )
+        )
+        for other in (1, 2, 3):
+            quad.append(
+                send_to(
+                    rows_ref.at[shared, lanes(part * D + window(h ^ other), WIDE)],
+                    quad_all.at[h, :, pl.ds(part * WIDE, WIDE)],
+                    sems, 3 * other + part, h ^ other,
+                )
+            )
+    for copy in pair + quad:
+        copy.start()
+    for part in range(parts):
+        pair_all[c, :, part * HALF : (part + 1) * HALF] = rows_ref[
+            own, lanes(part * D + c * HALF, HALF)
+        ]
+        quad_all[h, :, part * WIDE : (part + 1) * WIDE] = rows_ref[
+            shared, lanes(part * D + window(h), WIDE)
+        ]
     return pair, quad
 
 
-def attend_kernel(pair_in, quad_in, pair_mix, quad_mix, pair_all, quad_all, log_ref,
-                  pair_out, quad_out, send_sem, recv_sem):
+def return_pair(h, pair_out, rows_ref, parts, sems):
+    c = h % 2
+    own = pl.ds(0, pair_out.shape[1])
+    copies = []
+    for part in range(parts):
+        columns = lanes(part * D + c * HALF, HALF)
+        copies.append(
+            send_to(
+                pair_out.at[1 - c, :, pl.ds(part * HALF, HALF)], rows_ref.at[own, columns],
+                sems, 12 + part, h ^ 1,
+            )
+        )
+        copies[-1].start()
+        rows_ref[own, columns] = pair_out[c, :, part * HALF : (part + 1) * HALF]
+    return copies
+
+
+def return_quad(h, quad_out, quad_got, sems):
+    copies = []
+    for other in (1, 2, 3):
+        copies.append(
+            send_to(quad_out.at[h ^ other], quad_got.at[h], sems, 14 + other, h ^ other)
+        )
+        copies[-1].start()
+    quad_got[h] = quad_out[h]
+    return copies
+
+
+def merge_quad(quad_got, rows_ref, parts):
+    tile = quad_got.shape[1]
+    shared = slice(2 * tile, 3 * tile)
+    for part in range(parts):
+        base, start = part * WIDE, part * D
+        for side in range(2):
+            left, right = quad_got.at[2 * side], quad_got.at[2 * side + 1]
+            at = start + side * HALF
+            rows_ref[shared, at : at + 128] = left[:, base : base + 128]
+            rows_ref[shared, at + 128 : at + 256] = (
+                left[:, base + 128 : base + 256] + right[:, base : base + 128]
+            )
+            rows_ref[shared, at + 256 : at + 384] = right[:, base + 128 : base + 256]
+
+
+def attend_kernel(rows_ref, mixed_ref, pair_all, quad_all, log_ref, pair_out, quad_out, quad_got,
+                  send_sem, recv_sem):
     h = lax.axis_index("head")
-    c = h % 2
     sems = (send_sem, recv_sem)
     greet([{"head": h ^ other} for other in (1, 2, 3)])
-    pair_copies, quad_copies = own_exchange(h, pair_in, pair_all, quad_in, quad_all, sems, 0)
-    for copy in pair_copies + quad_copies:
-        copy.start()
-    pair_all[c] = pair_in[c]
-    quad_all[h] = quad_in[h]
-    tile = quad_in.shape[1]
-
-    def one_pair(packed, starts, head_place, heads, out):
-        length = packed.shape[0] * packed.shape[1]
-
-        def cols(start):
-            return packed[:, :, start : start + 128].reshape(length, 128)
-
-        keys, values = cols(starts[1]), cols(starts[2])
-
-        for row in range(length // tile):
-            per = packed.shape[1] // tile
-            query = packed[row // per, (row % per) * tile : (row % per + 1) * tile,
-                           starts[0] : starts[0] + 128]
-            mixed = jnp.zeros((tile, 128), jnp.float32)
-            logs = log_ref[row * tile : (row + 1) * tile, :]
-            lane = lax.broadcasted_iota(jnp.int32, (1, 128), 1)
-            for half in range(heads):
-                mask = half_mask(half)
-                scores = dot_nt(jnp.where(mask, query, 0), keys) * 0.125
-                top = jnp.max(scores, -1, keepdims=True)
-                exponent = jnp.exp(scores - top)
-                total = jnp.sum(exponent, -1, keepdims=True)
-                probability = to_bf16(exponent / total)
-                mixed = mixed + dot_nn(probability, jnp.where(mask, values, 0))
-                logs = jnp.where(lane == head_place + half, top + jnp.log(total), logs)
-            log_ref[row * tile : (row + 1) * tile, :] = logs
-            out(row, to_bf16(mixed))
+    pair_copies, quad_copies = bring_heads(h, rows_ref, pair_all, quad_all, 3, sems)
+    tile = quad_all.shape[1]
+    length = 4 * tile
+    lane = lax.broadcasted_iota(jnp.int32, (1, 128), 1)
+
+    def one_head(query, keys, values, mask):
+        scores = dot_nt(jnp.where(mask, query, 0) * 0.125, keys)
+        top = jnp.max(scores, -1, keepdims=True)
+        exponent = jnp.exp(scores - top)
+        total = jnp.sum(exponent, -1, keepdims=True)
+        probability = to_bf16(exponent * (1.0 / total))
+        return dot_nn(probability, jnp.where(mask, values, 0)), top + jnp.log(total)
 
     log_ref[...] = jnp.zeros_like(log_ref)
+    quad_out[...] = jnp.zeros_like(quad_out)
     for copy in pair_copies:
         copy.wait()
     for pair in range(3):
-
-        def put(row, value, pair=pair):
-            pair_out[row // 2, (row % 2) * tile : (row % 2 + 1) * tile,
-                     pair * 128 : pair * 128 + 128] = value
-
-        one_pair(pair_all, (pair * 128, HALF + pair * 128, 2 * HALF + pair * 128),
-                 2 * pair, 2, put)
-    back = [send_to(pair_out.at[1 - c], pair_mix.at[c], sems, 4, h ^ 1)]
-    back[0].start()
-    pair_mix[c] = pair_out[c]
+        keys = pair_all[:, :, HALF + pair * 128 : HALF + pair * 128 + 128].reshape(length, 128)
+        values = pair_all[:, :, 2 * HALF + pair * 128 : 2 * HALF + pair * 128 + 128].reshape(
+            length, 128
+        )
+        for row in range(4):
+            rows = slice((row % 2) * tile, (row % 2 + 1) * tile)
+            out_rows = slice(row * tile, (row + 1) * tile)
+            query = pair_all[row // 2, rows, pair * 128 : pair * 128 + 128]
+            mixed = jnp.zeros((tile, 128), jnp.float32)
+            logs = log_ref[out_rows, :]
+            for half in range(2):
+                part, log_total = one_head(query, keys, values, half_mask(half))
+                mixed = mixed + part
+                logs = jnp.where(lane == 2 * pair + half, log_total, logs)
+            log_ref[out_rows, :] = logs
+            pair_out[row // 2, rows, pair * 128 : pair * 128 + 128] = to_bf16(mixed)
+    back = return_pair(h, pair_out, mixed_ref, 1, sems)
     for copy in quad_copies:
         copy.wait()
-    for pair in range(2):
-
-        def put(row, value, pair=pair):
-            quad_out[row, :, pair * 128 : pair * 128 + 128] = value
-
-        one_pair(quad_all, (pair * 128, WIDE + pair * 128, 2 * WIDE + pair * 128),
-                 6 + 2 * pair, 2 - pair, put)
-    for other in (1, 2, 3):
-        back.append(send_to(quad_out.at[h ^ other], quad_mix.at[h], sems, 4 + other, h ^ other))
-        back[-1].start()
-    quad_mix[h] = quad_out[h]
-    for copy in back:
+    for member in range(3):
+        place = h % 2 + member
+        mask = half_mask(place % 2)
+        at = (place // 2) * 128
+        keys = quad_all[:, :, lanes(WIDE + at, 128)].reshape(length, 128)
+        values = quad_all[:, :, lanes(2 * WIDE + at, 128)].reshape(length, 128)
+        for row in range(4):
+            out_rows = slice(row * tile, (row + 1) * tile)
+            mixed, log_total = one_head(quad_all[row, :, lanes(at, 128)], keys, values, mask)
+            log_ref[out_rows, :] = jnp.where(lane == 6 + member, log_total, log_ref[out_rows, :])
+            quad_out[row, :, lanes(at, 128)] += to_bf16(mixed)
+    back_quad = return_quad(h, quad_out, quad_got, sems)
+    for copy in back + back_quad:
         copy.wait()
-
-
-def attend(pair_in, quad_in, collective_id):
-    rows, tile = pair_in.shape[1], quad_in.shape[1]
+    merge_quad(quad_got, mixed_ref, 1)
+
+
+def attend(rows, collective_id):
+    frames = rows.shape[0]
+    tile = frames // 3
     low = jnp.bfloat16
     return pl.pallas_call(
         attend_kernel,
         out_shape=[
-            jax.ShapeDtypeStruct((2, rows, HALF), low),
-            jax.ShapeDtypeStruct((4, tile, WIDE), low),
-            jax.ShapeDtypeStruct(pair_in.shape, low),
-            jax.ShapeDtypeStruct(quad_in.shape, low),
+            jax.ShapeDtypeStruct((frames, D), low),
+            jax.ShapeDtypeStruct((2, 2 * tile, 3 * HALF), low),
+            jax.ShapeDtypeStruct((4, tile, 3 * WIDE), low),
             jax.ShapeDtypeStruct((4 * tile, 128), jnp.float32),
         ],
-        in_specs=[vmem()] * 2,
-        out_specs=[vmem()] * 5,
+        in_specs=[vmem()],
+        out_specs=[vmem()] * 4,
         scratch_shapes=[
-            pltpu.VMEM((2, rows, HALF), low),
+            pltpu.VMEM((2, 2 * tile, HALF), low),
             pltpu.VMEM((4, tile, WIDE), low),
-            pltpu.SemaphoreType.DMA((8,)),
-            pltpu.SemaphoreType.DMA((8,)),
+            pltpu.VMEM((4, tile, WIDE), low),
+            pltpu.SemaphoreType.DMA((18,)),
+            pltpu.SemaphoreType.DMA((18,)),
         ],
         compiler_params=comm_params(collective_id),
         name="attend",
-    )(pair_in, quad_in)
-
-
-def attend_back_kernel(pair_all, quad_all, log_ref, pair_grad_in, quad_grad_in,
-                       pair_grad, quad_grad, pair_mixed, quad_mixed, pair_out, quad_out,
-                       grad_keys, grad_values, send_sem, recv_sem):
+    )(rows)
+
+
+def attend_back_kernel(pair_all, quad_all, log_ref, grad_ref, rows_ref, pair_mixed, quad_mixed,
+                       pair_out, quad_out, quad_got, grad_keys, grad_values, send_sem, recv_sem):
     h = lax.axis_index("head")
-    c = h % 2
     sems = (send_sem, recv_sem)
     greet([{"head": h ^ other} for other in (1, 2, 3)])
-    pair_copies, quad_copies = own_exchange(
-        h, pair_grad_in, pair_mixed, quad_grad_in, quad_mixed, sems, 0
-    )
-    for copy in pair_copies + quad_copies:
-        copy.start()
-    pair_mixed[c] = pair_grad_in[c]
-    quad_mixed[h] = quad_grad_in[h]
+    pair_copies, quad_copies = bring_heads(h, grad_ref, pair_mixed, quad_mixed, 1, sems)
     tile = quad_all.shape[1]
     length = 4 * tile
-
-    def one_pair(packed, grad_mixed, grad_start, starts, head_place, heads, out, wide):
-        per = packed.shape[1] // tile
-
-        def cols(start):
-            return packed[:, :, start : start + 128].reshape(length, 128)
-
-        keys, values = cols(starts[1]), cols(starts[2])
+    lane = lax.broadcasted_iota(jnp.int32, (1, 128), 1)
+
+    def one_head(query, keys, values, grad_out, mask, out_rows, log_lane):
+        log_total = jnp.sum(
+            jnp.where(lane == log_lane, log_ref[out_rows, :], 0.0), -1, keepdims=True
+        )
+        query = jnp.where(mask, query, 0) * 0.125
+        grad_out = jnp.where(mask, grad_out, 0)
+        probability = jnp.exp(dot_nt(query, keys) - log_total)
+        grad_prob = dot_nt(grad_out, values)
+        mean = jnp.sum(probability * grad_prob, -1, keepdims=True)
+        grad_scores = to_bf16(probability * (grad_prob - mean))
+        grad_keys[...] += dot_tn(grad_scores, query)
+        grad_values[...] += dot_tn(to_bf16(probability), grad_out)
+        return dot_nn(grad_scores, jnp.where(mask, keys, 0)) * 0.125
+
+    quad_out[...] = jnp.zeros_like(quad_out)
+    for copy in pair_copies:
+        copy.wait()
+    for pair in range(3):
+        at = [part * HALF + pair * 128 for part in range(3)]
+        keys = pair_all[:, :, at[1] : at[1] + 128].reshape(length, 128)
+        values = pair_all[:, :, at[2] : at[2] + 128].reshape(length, 128)
         grad_keys[...] = jnp.zeros_like(grad_keys)
         grad_values[...] = jnp.zeros_like(grad_values)
         for row in range(4):
-            rows = slice((row % per) * tile, (row % per + 1) * tile)
-            query = packed[row // per, rows, starts[0] : starts[0] + 128]
-            grad_out = grad_mixed[row // per, rows, grad_start : grad_start + 128]
-            lane = lax.broadcasted_iota(jnp.int32, (1, 128), 1)
+            rows = slice((row % 2) * tile, (row % 2 + 1) * tile)
+            query = pair_all[row // 2, rows, at[0] : at[0] + 128]
+            grad_out = pair_mixed[row // 2, rows, at[0] : at[0] + 128]
             grad_query = jnp.zeros((tile, 128), jnp.float32)
-            for half in range(heads):
-                mask = half_mask(half)
-                log_total = jnp.sum(
-                    jnp.where(lane == head_place + half, log_ref[row * tile : (row + 1) * tile, :], 0.0),
-                    -1, keepdims=True,
+            for half in range(2):
+                grad_query = grad_query + one_head(
+                    query, keys, values, grad_out, half_mask(half),
+                    slice(row * tile, (row + 1) * tile), 2 * pair + half,
                 )
-                query_half = jnp.where(mask, query, 0)
-                grad_half = jnp.where(mask, grad_out, 0)
-                probability = jnp.exp(dot_nt(query_half, keys) * 0.125 - log_total)
-                grad_prob = dot_nt(grad_half, values)
-                mean = jnp.sum(probability * grad_prob, -1, keepdims=True)
-                grad_scores = to_bf16(probability * (grad_prob - mean))
-                grad_query = grad_query + dot_nn(grad_scores, jnp.where(mask, keys, 0))
-                grad_keys[...] += dot_tn(grad_scores, query_half)
-                grad_values[...] += dot_tn(to_bf16(probability), grad_half)
-            out[row // per, rows, starts[0] : starts[0] + 128] = to_bf16(grad_query * 0.125)
-        out[:, :, starts[1] : starts[1] + 128] = to_bf16(grad_keys[...] * 0.125).reshape(
-            packed.shape[0], packed.shape[1], 128
-        )
-        out[:, :, starts[2] : starts[2] + 128] = to_bf16(grad_values[...]).reshape(
-            packed.shape[0], packed.shape[1], 128
-        )
-
-    for copy in pair_copies:
-        copy.wait()
-    for pair in range(3):
-        one_pair(pair_all, pair_mixed, pair * 128,
-                 (pair * 128, HALF + pair * 128, 2 * HALF + pair * 128), 2 * pair, 2, pair_out, 3)
-    back = [send_to(pair_out.at[1 - c], pair_grad.at[c], sems, 4, h ^ 1)]
-    back[0].start()
-    pair_grad[c] = pair_out[c]
+            pair_out[row // 2, rows, at[0] : at[0] + 128] = to_bf16(grad_query)
+        for part, total in ((1, grad_keys), (2, grad_values)):
+            pair_out[:, :, at[part] : at[part] + 128] = to_bf16(total[...]).reshape(
+                2, 2 * tile, 128
+            )
+    back = return_pair(h, pair_out, rows_ref, 3, sems)
     for copy in quad_copies:
         copy.wait()
-    for pair in range(2):
-        one_pair(quad_all, quad_mixed, pair * 128,
-                 (pair * 128, WIDE + pair * 128, 2 * WIDE + pair * 128), 6 + 2 * pair, 2 - pair,
-                 quad_out, 2)
-    for other in (1, 2, 3):
-        back.append(send_to(quad_out.at[h ^ other], quad_grad.at[h], sems, 4 + other, h ^ other))
-        back[-1].start()
-    quad_grad[h] = quad_out[h]
-    for copy in back:
+    for member in range(3):
+        place = h % 2 + member
+        mask = half_mask(place % 2)
+        at = (place // 2) * 128
+        keys = quad_all[:, :, lanes(WIDE + at, 128)].reshape(length, 128)
+        values = quad_all[:, :, lanes(2 * WIDE + at, 128)].reshape(length, 128)
+        grad_keys[...] = jnp.zeros_like(grad_keys)
+        grad_values[...] = jnp.zeros_like(grad_values)
+        for row in range(4):
+            grad_query = one_head(
+                quad_all[row, :, lanes(at, 128)], keys, values, quad_mixed[row, :, lanes(at, 128)],
+                mask, slice(row * tile, (row + 1) * tile), 6 + member,
+            )
+            quad_out[row, :, lanes(at, 128)] += to_bf16(grad_query)
+        for part, total in ((1, grad_keys), (2, grad_values)):
+            quad_out[:, :, lanes(part * WIDE + at, 128)] += to_bf16(total[...]).reshape(
+                4, tile, 128
+            )
+    back_quad = return_quad(h, quad_out, quad_got, sems)
+    for copy in back + back_quad:
         copy.wait()
-
-
-def attend_back(pair_all, quad_all, logs, pair_grad, quad_grad, collective_id):
+    merge_quad(quad_got, rows_ref, 3)
+
+
+def attend_back(pair_all, quad_all, logs, grad_mixed, collective_id):
     rows, tile = pair_all.shape[1], quad_all.shape[1]
     low = jnp.bfloat16
     return pl.pallas_call(
         attend_back_kernel,
-        out_shape=[
-            jax.ShapeDtypeStruct(pair_all.shape, low),
-            jax.ShapeDtypeStruct(quad_all.shape, low),
-        ],
-        in_specs=[vmem()] * 5,
-        out_specs=[vmem()] * 2,
+        out_shape=jax.ShapeDtypeStruct((3 * tile, 3 * D), low),
+        in_specs=[vmem()] * 4,
+        out_specs=vmem(),
         scratch_shapes=[
             pltpu.VMEM((2, rows, HALF), low),
             pltpu.VMEM((4, tile, WIDE), low),
             pltpu.VMEM(pair_all.shape, low),
             pltpu.VMEM(quad_all.shape, low),
+            pltpu.VMEM(quad_all.shape, low),
             pltpu.VMEM((4 * tile, 128), jnp.float32),
             pltpu.VMEM((4 * tile, 128), jnp.float32),
-            pltpu.SemaphoreType.DMA((8,)),
-            pltpu.SemaphoreType.DMA((8,)),
+            pltpu.SemaphoreType.DMA((18,)),
+            pltpu.SemaphoreType.DMA((18,)),
         ],
         compiler_params=comm_params(collective_id),
         name="attend_back",
-    )(pair_all, quad_all, logs, pair_grad, quad_grad)
+    )(pair_all, quad_all, logs, grad_mixed)
 
 
 def masked_scores(query_half, keys, keep):
@@ -859,11 +1235,37 @@
             [jnp.where(own_clip == 0, own, none), jnp.where(own_clip == 1, own, none), tiles[2:3]]
         )
 
+    block = 3 * D // head_count
+    share = D // head_count
+    is_first = core == 0
+    edge = jnp.where(is_first, out_weight[..., 128:], qkv_weight[..., :64])
+    latents = jnp.concatenate([clean_latents, noise_draw], -1)
+    latents_size = latents.size
+    packed = jnp.concatenate([latents.reshape(-1), edge.reshape(-1)]).reshape(-1, 128)
+    packed = spread(packed, "head").reshape(head_count, -1)
+    latents_all = packed[:, :latents_size].reshape(head_count, clip_count, tile, 2 * channels)
+    edge = lax.dynamic_slice_in_dim(packed[:, latents_size:], h ^ 1, 1, 0).reshape(edge.shape)
+
+    def with_edge(qkv, out, edge):
+        return jnp.where(
+            is_first,
+            jnp.concatenate([qkv, edge, out[..., :128]], -1),
+            jnp.concatenate([qkv[..., 64:], edge, out], -1),
+        )
+
+    def without_edge(own, edge):
+        qkv = jnp.where(
+            is_first, own[..., :block], jnp.concatenate([edge, own[..., : block - 64]], -1)
+        )
+        out = jnp.where(
+            is_first, jnp.concatenate([own[..., block + 64 :], edge], -1), own[..., block:]
+        )
+        return qkv, out
+
+    first_groups = to_bf16(with_edge(qkv_weight, out_weight, edge))
     weight_groups = []
     for layer in range(2):
-        weight_groups.append(
-            to_bf16(jnp.concatenate([qkv_weight[layer], out_weight[layer]], 1))
-        )
+        weight_groups.append(first_groups[layer])
         weight_groups.append(to_bf16(up_weight[layer]))
         weight_groups.append(to_bf16(down_weight[layer]))
     time_cols = time_weight.shape[1]
@@ -886,7 +1288,6 @@
     else:
         gathered = [gather_general(own) for own in [small_own] + weight_groups]
     small_all = gathered[0].reshape(data_count, small_rows, head_count, WIDE)
-    qkv_out_full = [gathered[1], gathered[4]]
     up_full = [gathered[2], gathered[5]]
     down_full = [gathered[3], gathered[6]]
     time_full = small_all[:, :rows_own, :, :time_cols].reshape(D, D)
@@ -897,15 +1298,25 @@
         .reshape(2, D, channels)
     )
     table_bf = small_all[:, rows_own : rows_own + table_rows, 0].reshape(-1, D)
-    out_full = [
-        full.reshape(D, head_count, D)[:, :, 3 * D // head_count :].reshape(D, D)
-        for full in qkv_out_full
-    ]
-
-    latents = jnp.concatenate([clean_latents, noise_draw], -1)
-    latents_all = spread(latents.reshape(-1, 128), "head").reshape(
-        head_count, clip_count, tile, 2 * channels
-    )
+
+    def split_first(whole):
+        qkv, out = [], []
+        for side in range(2):
+            at = 2 * side * D
+            qkv += [whole[:, at : at + 640], whole[:, at + D : at + D + 512]]
+            out += [whole[:, at + 640 : at + D], whole[:, at + D + 512 : at + 2 * D]]
+        return jnp.concatenate(qkv, 1), jnp.concatenate(out, 1)
+
+    def join_first(qkv, out):
+        columns = []
+        for side in range(2):
+            q, o = side * 2 * block, side * 2 * share
+            columns += [qkv[:, q : q + 640], out[:, o : o + 128]]
+            columns += [qkv[:, q + 640 : q + 1152], out[:, o + 128 : o + 384]]
+        return jnp.concatenate(columns, 1)
+
+    qkv_full, out_full = zip(*[split_first(gathered[1 + 3 * layer]) for layer in range(2)])
+
     own_latents = lax.dynamic_slice(
         latents_all, (2 * core, own_clip, 0, 0), (2, 1, tile, 2 * channels)
     )[:, 0]
@@ -921,7 +1332,6 @@
         :, None
     ].astype(jnp.float32)
     cap_unit = cap_mean * lax.rsqrt(jnp.mean(cap_mean * cap_mean, -1, keepdims=True) + 1e-06)
-    cap_all = spread(cap_unit, "dp").reshape(-1, D)
     own_captions = jnp.concatenate([lax.dynamic_slice_in_dim(captions, own_clip, 1, 0), captions[2:3]])
     own_lengths = jnp.concatenate([lax.dynamic_slice_in_dim(cap_len, own_clip, 1, 0), cap_len[2:3]])
 
@@ -934,7 +1344,12 @@
     mod_part = product("fd,ldn->fln", signal_own, ada_bf).reshape(
         data_count, clip_count, 2 * ada_cols
     )
-    mod_own = jnp.sum(swap(mod_part, "dp"), 0)
+    mod_part = jnp.concatenate(
+        [mod_part, jnp.broadcast_to(cap_unit, (data_count, clip_count, D))], -1
+    )
+    mod_part = swap(mod_part, "dp")
+    cap_all = mod_part[:, :, 2 * ada_cols :].reshape(-1, D)
+    mod_own = jnp.sum(mod_part[:, :, : 2 * ada_cols], 0)
     mod_all = (
         spread(mod_own, "head")
         .reshape(head_count, clip_count, 2, ada_cols)
@@ -943,51 +1358,20 @@
     )
     tile_mods = by_tile(mod_all)
 
-    block = 3 * D // head_count
-
-    def take_qkv(wide_rows):
-        lead = wide_rows.shape[:-1]
-        return wide_rows.reshape(lead + (head_count, D))[..., :block].reshape(lead + (3 * D,))
-
-    def put_qkv(rows):
-        blocks = rows.reshape(rows.shape[0], head_count, block)
-        return jnp.pad(blocks, ((0, 0), (0, 0), (0, D - block))).reshape(rows.shape[0], -1)
-
-    def put_out(rows):
-        blocks = rows.reshape(rows.shape[0], head_count, D - block)
-        return jnp.pad(blocks, ((0, 0), (0, 0), (block, 0))).reshape(rows.shape[0], -1)
-
     frames = clip_count * tile
-    share = D // head_count
-
-    def cut_rows(rows, parts):
-        pair = rows[: 2 * tile].reshape(2 * tile, parts, 2, HALF)
-        pair = pair.transpose(2, 0, 1, 3).reshape(2, 2 * tile, parts * HALF)
-        quad = rows[2 * tile :].reshape(tile, parts, head_count, share)
-        quad = jnp.pad(quad, ((0, 0), (0, 0), (0, 0), (0, WIDE - share)))
-        return pair, quad.transpose(2, 0, 1, 3).reshape(head_count, tile, parts * WIDE)
-
-    def join_rows(pair, quad, parts):
-        pair = pair.reshape(2, 2 * tile, parts, HALF).transpose(1, 2, 0, 3)
-        quad = quad.reshape(head_count, tile, parts, WIDE)[..., :share].transpose(1, 2, 0, 3)
-        return jnp.concatenate(
-            [pair.reshape(2 * tile, parts * D), quad.reshape(tile, parts * D)]
-        )
 
     def layer_forward(layer_index, hidden):
         modulation = tile_mods[:, layer_index].reshape(clip_count, 1, 6, D)
         mod_parts = [modulation[:, :, member] for member in range(6)]
         normed = to_bf16(modulate(hidden, mod_parts[0], mod_parts[1]))
-        weight = qkv_out_full[layer_index]
+        weight = qkv_full[layer_index]
         if layer_index == 0:
-            projected = take_qkv(to_bf16(product("fld,dn->fln", normed, weight)))
-            pair, quad = cut_rows(projected.reshape(frames, 3 * D), 3)
-            pair_mix, quad_mix, *attended = attend(pair, quad, next(ids))
-            mixed = join_rows(pair_mix, quad_mix, 1).reshape(clip_count, tile, D)
+            projected = to_bf16(product("fld,dn->fln", normed, weight))
+            mixed, *attended = attend(projected.reshape(frames, 3 * D), next(ids))
+            mixed = mixed.reshape(clip_count, tile, D)
         else:
-            query = to_bf16(product("fld,dn->fln", normed, weight[:, : 2 * D]))
-            query = jnp.concatenate([query[..., :block], query[..., D : 2 * D - block]], -1)
-            pair_kv = take_qkv(to_bf16(product("ftd,dn->ftn", own_captions, weight)))[..., D:]
+            query = to_bf16(product("fld,dn->fln", normed, weight[:, :D]))
+            pair_kv = to_bf16(product("ftd,dn->ftn", own_captions, weight[:, D:]))
             attended = (query, pair_kv)
             mixed = cross(query, pair_kv, own_lengths)
         branch = product("fle,de->fld", mixed, out_full[layer_index])
@@ -1031,7 +1415,7 @@
     final_value, final_back = jax.vjp(norm_rows, hidden)
     grad_hidden = final_back(grad_final)[0]
     fin_grad = product("flc,fld->dc", grad_pred, final_bf)
-    grad_parts = [None] * 6
+    firsts, pairs = [], []
     mod_grads = [None, None]
     for layer_index in (1, 0):
         (
@@ -1047,14 +1431,16 @@
             layer_active,
             layer_down_out,
         ) = saved_layers[layer_index]
-        weight = qkv_out_full[layer_index]
+        weight = qkv_full[layer_index]
         d_gate2 = jnp.sum(layer_down_out * grad_hidden, axis=1, keepdims=True)
         grad_down = to_bf16(mod_parts[5] * grad_hidden)
         grad_active = product("fld,dn->fln", grad_down, down_full[layer_index])
         gelu_value, gelu_back = jax.vjp(soft_gelu, layer_upper)
         grad_upper = to_bf16(gelu_back(grad_active)[0])
-        grad_parts[3 * layer_index + 2] = product("fld,fln->dn", grad_down, layer_active)
-        grad_parts[3 * layer_index + 1] = product("fld,fln->dn", layer_normed2, grad_upper)
+        pairs += [
+            (layer_normed2.reshape(frames, D), grad_upper.reshape(frames, -1)),
+            (grad_down.reshape(frames, D), layer_active.reshape(frames, -1)),
+        ]
         grad_normed2 = product("fln,dn->fld", grad_upper, up_full[layer_index])
         mod_value, mod_back = jax.vjp(modulate, layer_middle, mod_parts[3], mod_parts[4])
         grad_middle, d_shift2, d_scale2 = mod_back(grad_normed2)
@@ -1062,35 +1448,24 @@
         d_gate1 = jnp.sum(layer_branch * grad_middle, axis=1, keepdims=True)
         grad_branch = to_bf16(mod_parts[2] * grad_middle)
         grad_mixed = to_bf16(product("fld,de->fle", grad_branch, out_full[layer_index]))
-        left = [layer_normed.reshape(frames, D), grad_branch.reshape(frames, D)]
-        right = [None, put_out(layer_mixed.reshape(frames, D))]
+        out_grad = product("fld,fle->de", grad_branch, layer_mixed)
         if layer_index == 0:
-            pair, quad = cut_rows(grad_mixed.reshape(frames, D), 1)
-            pair_grad, quad_grad = attend_back(*attended, pair, quad, next(ids))
-            grad_proj = put_qkv(join_rows(pair_grad, quad_grad, 3))
-            right[0] = grad_proj
+            grad_proj = attend_back(*attended, grad_mixed.reshape(frames, D), next(ids))
             grad_normed = product("fn,dn->fd", grad_proj, weight)
+            qkv_grad = product("fd,fn->dn", layer_normed.reshape(frames, D), grad_proj)
         else:
             query, pair_kv = attended
             grad_query, grad_keys, grad_values = cross_back(query, pair_kv, own_lengths, grad_mixed)
-            tokens = 2 * CAP
-            grad_kv = jnp.concatenate(
+            grad_normed = product("fln,dn->fld", grad_query, weight[:, :D])
+            qkv_grad = jnp.concatenate(
                 [
-                    jnp.zeros((tokens, D), jnp.bfloat16),
-                    grad_keys.reshape(tokens, D),
-                    grad_values.reshape(tokens, D),
+                    product("fld,fln->dn", layer_normed, grad_query),
+                    product("ftd,ftn->dn", own_captions, grad_keys),
+                    product("ftd,ftn->dn", own_captions, grad_values),
                 ],
                 1,
             )
-            grad_query = jnp.pad(grad_query.reshape(frames, D), ((0, 0), (0, 2 * D)))
-            grad_proj = put_qkv(grad_query)
-            right[0] = grad_proj
-            left.append(own_captions.reshape(tokens, D))
-            right.append(put_qkv(grad_kv))
-            grad_normed = product("fn,dn->fd", grad_proj[:, : 2 * D], weight[:, : 2 * D])
-        grad_parts[3 * layer_index] = product(
-            "kd,kn->dn", jnp.concatenate(left), jnp.concatenate(right)
-        )
+        firsts.append(join_first(qkv_grad, out_grad))
         first_value, first_back = jax.vjp(modulate, layer_hidden, mod_parts[0], mod_parts[1])
         grad_in, d_shift1, d_scale1 = first_back(grad_normed.reshape(clip_count, tile, D))
         mod_grads[layer_index] = jnp.concatenate(
@@ -1130,23 +1505,37 @@
         lax.dynamic_slice_in_dim(grad_cond, h * time_cols, time_cols, 1),
     )
 
+    square = sum((jnp.sum(grad * grad) for grad in (ada_grad, time_grad, io_grad)))
     if linked:
-        owned = reduce_whole(grad_parts, next(ids))
+        extra = jnp.pad(jnp.stack([square, loss_part])[None], ((0, 7), (0, 126)))
+        owned, totals, edge = reduce_whole(firsts, pairs, extra, next(ids))
+        totals = totals[0, :2]
+        edge = edge[::-1]
+        edge = jnp.where(is_first, edge[..., :64], edge[..., 64:])
     else:
-        owned = [reduce_general(part) for part in grad_parts]
+        parts = []
+        for place in range(2):
+            parts.append(firsts[place])
+            parts += [product("fd,fn->dn", *pair) for pair in pairs[2 * place : 2 * place + 2]]
+        owned = [reduce_general(part) for part in parts]
+        square = square + sum((jnp.sum(part * part) for part in owned))
+        totals = lax.psum(jnp.stack([square, loss_part]), ("dp", "head"))
+        edge = jnp.stack([owned[3], owned[0]])
+        edge = jnp.where(is_first, edge[..., block : block + 64], edge[..., block - 64 : block])
+        edge = spread(edge.reshape(-1, 128), "head")
+        edge = lax.dynamic_slice_in_dim(edge, h ^ 1, 1, 0).reshape(2, rows_own, 64)
+    first_own = jnp.stack([owned[3], owned[0]])
+    total_square, total_loss = totals[0], totals[1]
+    qkv_shard, out_shard = without_edge(first_own, edge)
     shards = (
-        jnp.stack([owned[0][:, :block], owned[3][:, :block]]),
-        jnp.stack([owned[0][:, block:], owned[3][:, block:]]),
-        jnp.stack([owned[1], owned[4]]),
-        jnp.stack([owned[2], owned[5]]),
+        qkv_shard,
+        out_shard,
+        jnp.stack([owned[4], owned[1]]),
+        jnp.stack([owned[5], owned[2]]),
         ada_grad,
         time_grad[None],
         io_grad,
     )
-    square = sum((jnp.sum(shard * shard) for shard in shards))
-    totals = jnp.pad(jnp.stack([square, loss_part])[None], ((0, 7), (0, 126)))
-    totals = jnp.sum(spread(jnp.sum(spread(totals, "head"), 0), "dp"), 0)
-    total_square, total_loss = totals[0, 0], totals[0, 1]
     old_moments = (qkv_moment, out_moment, up_moment, down_moment)
     grad_norm = jnp.sqrt(total_square)
     clip_scale = jnp.minimum(1.0, CLIP_NORM / (grad_norm + 1e-06))
@@ -1154,18 +1543,17 @@
         (MUON_BETA * old_moments[member] + clip_scale * shards[member] for member in range(4))
     )
     coeff_a, coeff_b, coeff_c = NEWTON_COEFFS
-    wide = max(moment.shape[2] for moment in moments)
-    sent = jnp.concatenate(
-        [jnp.pad(moment, ((0, 0), (0, 0), (0, wide - moment.shape[2]))) for moment in moments]
-    )
-    matrices = sent.shape[0]
-    sent = jnp.pad(sent, ((0, data_count - matrices), (0, 0), (0, 0)))
-    own_matrix = swap(sent, "dp").reshape(D, wide)
+    widths = [-(-moment.shape[2] // 128) * 128 for moment in moments]
+    padded = [
+        jnp.pad(moment, ((0, 0), (0, 0), (0, width - moment.shape[2])))
+        for moment, width in zip(moments, widths)
+    ]
+    own_matrix = to_owner(padded, next(ids)).reshape(D, -1)
 
     def near_product(form, left, right):
         return jnp.einsum(form, left, right, precision=lax.Precision.HIGH)
 
-    gram = lax.psum(near_product("rc,kc->rk", own_matrix, own_matrix), "head")
+    gram = gram_sum(own_matrix, next(ids))
     unit = jnp.eye(D, dtype=jnp.float32)
     size_frob = jnp.sqrt(jnp.sum(gram * unit)) + 1e-07
     gram = gram / (size_frob * size_frob)
@@ -1176,10 +1564,16 @@
         if ns_step < NS_STEPS - 1:
             gram = near_product("rk,kj->rj", near_product("rk,kj->rj", poly, gram), poly)
     ortho_matrix = near_product("rk,kc->rc", factor, own_matrix) / size_frob
-    ortho_back = swap(ortho_matrix.reshape(data_count, rows_own, wide), "dp")
+    ortho_back = to_bf16(ortho_matrix).reshape(data_count, rows_own, -1)
+    ortho_back = from_owner(ortho_back, tuple(widths), next(ids)).astype(jnp.float32)
     ortho_rows = tuple(
         (
-            ortho_back[2 * member : 2 * member + 2, :, : moments[member].shape[2]]
+            jnp.stack(
+                [
+                    ortho_back[owner_of(member, layer), :, : moments[member].shape[2]]
+                    for layer in range(2)
+                ]
+            )
             for member in range(4)
         )
     )

time: 1190 us -> 913 us (0.77)
  local copies, waits for them, and re-layouts: 214 us -> 89.6 us
  waiting for transfers between devices: 51.3 us -> 0 us
  matrix products: 232 us -> 183 us
  other arithmetic: 79.7 us -> 51.3 us
  between operations: 26.5 us -> 10.3 us
    pallas_call x13 -> x8, Pallas kernels: 200 us -> 68.6 us  [exchange(): pl.pallas_call(functools.partial(exchange_kernel, axis, count, swapped),...]
    pallas_call x3 -> x6, Pallas kernels: 211 us -> 336 us  [the longest x1 137 us: reduce_whole(): pl.pallas_call(functools.partial(reduce_kernel, layers), out_shape=[jax.S...]
    psum x1 -> x0, waiting for transfers between devices: 51.2 us -> none  [body(): gram = lax.psum(near_product('rc,kc->rk', own_matrix, own_matrix), 'head')]
    dot_general x30, matrix products: 154 us -> 112 us  [product(): return jnp.einsum(form, left, right, preferred_element_type=jnp.float32)]
    reshape x19 -> x6, local copies, waits for them, and re-layouts: 42.4 us -> 4.67 us  [the longest x1 2.7 us: reduce_whole(): summed.reshape(3 * layers, per_group, rows, PIECE_COLS)]
    another operation x13 -> x8, local copies, waits for them, and re-layouts: 23.3 us -> 1.65 us  [the longest x7 1.63 us: reduce_whole(): return (list(summed.reshape(3 * layers, rows, D)), totals, edges)]
    concatenate x8 -> x1, other arithmetic: 21.7 us -> 0.83 us  [body(): jnp.concatenate([mod_part, jnp.broadcast_to(cap_unit, (data_count, clip_c...]
    concatenate x6 -> x3, local copies, waits for them, and re-layouts: 30.3 us -> 10.6 us  [join_first(): return jnp.concatenate(columns, 1)]
  transfers between devices with their start and end apart: 1 -> 0, of which waited for: 1 -> 0; matrix products, arithmetic and copies ran while one was open for 0% -> 0% of each run, Pallas kernels for 0% -> 0%
where the time goes in v3:
time: 913 us; the launch traced here: 905 us
  Pallas kernels  570 us (62%)
  matrix products  183 us (20%)
  local copies, waits for them, and re-layouts  89.6 us (10%)
  other arithmetic  51.3 us (6%)
  between operations  10.3 us (1%)
    pallas_call x1, Pallas kernels, reduce_whole(): pl.pallas_call(functools.partial(reduce_kernel, layers), out_shape=[jax.S...  137 us
    pallas_call x1, Pallas kernels, gather_whole(): pl.pallas_call(functools.partial(gather_kernel, groups), out_shape=[jax.S...  137 us
    dot_general x30, matrix products, product(): return jnp.einsum(form, left, right, preferred_element_type=jnp.float32)  112 us
    pallas_call x8, Pallas kernels, exchange(): pl.pallas_call(functools.partial(exchange_kernel, axis, count, swapped),...  68.6 us
    dot_general x18, matrix products, near_product(): return jnp.einsum(form, left, right, precision=lax.Precision.HIGH)  60.1 us
    pallas_call x1, Pallas kernels, attend_back(): pl.pallas_call(attend_back_kernel, out_shape=jax.ShapeDtypeStruct((3 * ti...  54.6 us
    pallas_call x1, Pallas kernels, to_owner(): pl.pallas_call(functools.partial(to_owner_kernel, count), out_shape=jax.S...  43.9 us
    pallas_call x1, Pallas kernels, from_owner(): pl.pallas_call(functools.partial(from_owner_kernel, count, widths), out_s...  35.6 us

profile of v3, /device:TPU:11, one launch (start us, length us, event | category | flops | bytes accessed | tf_op | source)
XLA Modules:
  0.0 905.0 jit_solution(10500681095009675044)
XLA Ops:
  19.7 11.2 %spread.5 = f32[4,291,128]{2,1,0:T(8,128)} custom-call(f32[291,128]{1,0:T(8,128)} %maximum_bitcast_fusion.7.x_ref), custom_call_target="tpu_custom_call" | custom-call | tf_op jit(solution)/shard_map/spread/pallas_call | solution.py:139
  36.1 137.2 %gather_weights.1 = (bf16[2,2,2,112,1024]{4,3,2,1,0:T(8,128)(2,1)}, bf16[2,2,2,96,3072]{4,3,2,1,0:T(8,128)(2,1)}, bf16[2,2,2,96,3072]{4,3,2,1,0:T(8,128)(2,1)}, ...) custom-call(bf16[112,256]{1,0:T(8,128)(2,1)} %maximum_maximum_fusion, ...), custom_call_target="tpu_custom_call" | custom-call | tf_op jit(solution)/shard_map/gather_weights/pallas_call | solution.py:259
  173.4 4.0 reshape_reshape.3
  190.9 14.9 %swap.3 = f32[8,3,3072]{2,1,0:T(4,128)} custom-call(f32[8,3,3072]{2,1,0:T(4,128)} %pad_maximum_fusion.10.x_ref), custom_call_target="tpu_custom_call" | custom-call | tf_op jit(solution)/shard_map/swap/pallas_call | solution.py:139
  209.0 6.6 spread.6
  236.6 4.8 convolution_convert_fusion
  241.5 32.9 %attend.1 = (bf16[624,768]{1,0:T(8,128)(2,1)}, bf16[2,416,1152]{2,1,0:T(8,128)(2,1)}, bf16[4,208,768]{2,1,0:T(8,128)(2,1)}, f32[832,128]{1,0:T(8,128)}) custom-call(bf16[624,2304]{1,0:T(8,128)(2,1)} %bitcast.286), custom_call_target="tpu_custom_call" | custom-call | tf_op jit(solution)/shard_map/attend/pallas_call | solution.py:964
  279.0 10.1 %multiply_convert_fusion.1 = (bf16[3,208,3072]{2,1,0:T(8,128)(2,1)S(1)}, f32[3,208,3072]{2,1,0:T(8,128)}) fusion(bf16[3,208,768]{2,1,0:T(8,128)(2,1)S(1)} %add_convert_fusion.3, bf16[768,3072,1]{1,0,2:T(8,128)(2,1)} %bitcast.336), kind=kOutput, calls=%fused_computation.21 | convolution fusion | flops 2961653760 | bytes 17178624 | tf_op jit(solution)/shard_map/fld,dn->fln/dot_general | solution.py:69
  289.3 4.5 fusion.254
  297.1 10.0 %cross.1 = bf16[3,208,768]{2,1,0:T(8,128)(2,1)} custom-call(bf16[3,208,768]{2,1,0:T(8,128)(2,1)} %convolution_convert_fusion.4.query_ref, bf16[2,256,1536]{2,1,0:T(8,128)(2,1)} %convolution_convert_fusion.1.keys_ref.values_ref, bf16[2,256,1536]{2,1,0:T(8,128)(2,1)} %convolution_convert_fusion.1.keys_ref.values_ref, s32[2]{0:T(128)} %pad_add_fusion.len_ref), custom_call_target="tpu_custom_call" | custom-call | tf_op jit(solution)/shard_map/cross/pallas_call | solution.py:1111
  307.2 3.5 fusion.253
  311.8 10.0 %multiply_convert_fusion = (bf16[3,208,3072]{2,1,0:T(8,128)(2,1)S(1)}, f32[3,208,3072]{2,1,0:T(8,128)}) fusion(bf16[3,208,768]{2,1,0:T(8,128)(2,1)S(1)} %add_convert_fusion.1, bf16[768,3072,1]{1,0,2:T(8,128)(2,1)} %bitcast.346), kind=kOutput, calls=%fused_computation.20 | convolution fusion | flops 2961653760 | bytes 17178624 | tf_op jit(solution)/shard_map/fld,dn->fln/dot_general | solution.py:69
  321.9 4.5 fusion.252
  328.8 4.9 spread.7
  348.8 11.9 %fusion.7 = bf16[3,208,3072]{2,1,0:T(8,128)(2,1)S(1)} fusion(f32[3,208,3072]{2,1,0:T(8,128)} %get-tuple-element.247, bf16[3,208,768]{2,1,0:T(8,128)(2,1)S(1)} %get-tuple-element.189, bf16[768,3072,1]{1,0,2:T(8,128)(2,1)} %bitcast.350), kind=kOutput, calls=%fused_computation.15 | convolution fusion | flops 2990407680 | bytes 17178624 | tf_op jit(solution)/shard_map/fld,dn->fln/dot_general | solution.py:69
  368.9 18.7 %cross_back.1 = (bf16[3,208,768]{2,1,0:T(8,128)(2,1)}, bf16[2,256,768]{2,1,0:T(8,128)(2,1)}, bf16[2,256,768]{2,1,0:T(8,128)(2,1)}) custom-call(bf16[3,208,768]{2,1,0:T(8,128)(2,1)} %convolution_convert_fusion.4.query_ref, bf16[2,256,1536]{2,1,0:T(8,128)(2,1)} %convolution_convert_fusion.1.keys_ref.values_ref, ...), custom_call_target="tpu_custom_call" | custom-call | tf_op jit(solution)/shard_map/cross_back/pallas_call | solution.py:1163
  398.4 11.0 %fusion.3 = bf16[3,208,3072]{2,1,0:T(8,128)(2,1)S(1)} fusion(f32[3,208,3072]{2,1,0:T(8,128)} %get-tuple-element.243, bf16[3,208,768]{2,1,0:T(8,128)(2,1)S(1)} %multiply_convert_fusion.3, bf16[768,3072,1]{1,0,2:T(8,128)(2,1)S(1)} %bitcast.345), kind=kOutput, calls=%fused_computation.11 | convolution fusion | flops 2990407680 | bytes 17178624 | tf_op jit(solution)/shard_map/fld,dn->fln/dot_general | solution.py:69
  417.8 54.6 %attend_back.1 = bf16[624,2304]{1,0:T(8,128)(2,1)} custom-call(bf16[2,416,1152]{2,1,0:T(8,128)(2,1)} %get-tuple-element.48.pair_all, bf16[4,208,768]{2,1,0:T(8,128)(2,1)} %get-tuple-element.49.quad_all, f32[832,128]{1,0:T(8,128)} %get-tuple-element.50.log_ref, bf16[624,768]{1,0:T(8,128)(2,1)} %bitcast.295), custom_call_target="tpu_custom_call" | custom-call | tf_op jit(solution)/shard_map/attend_back/pallas_call | solution.py:1064
  472.4 4.2 fusion.102
  491.9 7.1 swap.4
  500.9 11.1 %swap.5 = f32[8,62,128]{2,1,0:T(8,128)} custom-call(f32[8,62,128]{2,1,0:T(8,128)} %copy.181.x_ref), custom_call_target="tpu_custom_call" | custom-call | tf_op jit(solution)/shard_map/swap/pallas_call | solution.py:139
  516.3 5.4 spread.8
  524.0 7.4 spread.9
  539.6 4.2 fusion.278
  560.1 9.6 %copy.175 = f32[768,3072]{1,0:T(8,128)} copy(f32[768,3072]{0,1:T(8,128)} %slice_dynamic-update-slice_fusion.8) | data formatting | bytes 18874368 | tf_op jit(solution)/shard_map/concatenate | solution.py:1316
  569.7 137.3 %reduce_grads.1 = (f32[18,96,256]{2,1,0:T(8,128)}, f32[8,128]{1,0:T(8,128)}, f32[2,96,128]{2,1,0:T(8,128)}) custom-call(f32[2,2,2,96,3072]{4,3,2,1,0:T(8,128)} %bitcast.259, f32[2,2,2,96,3072]{4,3,2,1,0:T(8,128)} %bitcast.263, bf16[624,768]{1,0:T(8,128)(2,1)} %bitcast.278, bf16[624,768]{1,0:T(8,128)(2,1)} %bitcast.285, bf16[624,768]{1,0:T(8,128)(2,1)} %bitcast.277, ...), custom_call_target="tpu_custom_call" | custom-call | tf_op jit(solution)/shard_map/reduce_grads/pallas_call | solution.py:540
  721.5 43.9 %to_owner.1 = f32[8,96,768]{2,1,0:T(8,128)} custom-call(f32[2,96,640]{2,1,0:T(8,128)} %pad.23.refs_0_, f32[2,96,256]{2,1,0:T(8,128)} %pad.24.refs_1_, f32[2,96,768]{2,1,0:T(8,128)} %fusion.104.refs_2_, f32[2,96,768]{2,1,0:T(8,128)} %fusion.105.refs_3_), custom_call_target="tpu_custom_call" | custom-call | tf_op jit(solution)/shard_map/to_owner/pallas_call | solution.py:653
  767.3 31.6 %gram_sum.1 = f32[768,768]{1,0:T(8,128)} custom-call(f32[768,768]{1,0:T(8,128)} %bitcast.264), custom_call_target="tpu_custom_call" | custom-call | tf_op jit(solution)/shard_map/gram_sum/pallas_call | solution.py:763
  821.4 3.4 fusion.40
  834.7 3.7 fusion.34
  858.2 4.2 divide_convert_fusion
  862.4 35.6 %from_owner.1 = bf16[8,96,768]{2,1,0:T(8,128)(2,1)} custom-call(bf16[8,96,768]{2,1,0:T(8,128)(2,1)} %bitcast.291), custom_call_target="tpu_custom_call" | custom-call | tf_op jit(solution)/shard_map/from_owner/pallas_call | solution.py:710
  (604 shorter events, 230.6 us)
Async XLA Ops:
  0.7 18.1 %copy-start.39 = (f32[2,96,768]{2,1,0:T(8,128)S(1)}, f32[2,96,768]{2,1,0:T(8,128)}, u32[]{:S(2)}) copy-start(f32[2,96,768]{2,1,0:T(8,128)} %param.33) | copy-start | bytes 1769476
  188.6 19.8 %copy-start.99 = (f32[24,768]{1,0:T(8,128)}, f32[24,768]{1,0:T(8,128)S(1)}, u32[]{:S(2)}) copy-start(f32[24,768]{1,0:T(8,128)S(1)} %get-tuple-element.237) | copy-start | bytes 221188
  190.1 40.6 %slice-start = ((s8[4718592]{0:T(1024)(128)(4,1)}), s8[524288]{0:T(1024)(128)(4,1)S(1)}, s32[]{:S(2)}) async-start(s8[4718592]{0:T(1024)(128)(4,1)} %bitcast.269), calls=%async_computation | async-start | bytes 1048576
  218.4 92.7 %copy-start.81 = (f32[3,1,1,768]{3,0,1,2:T(4,128)}, f32[3,1,1,768]{3,0,1,2:T(4,128)S(1)}, u32[]{:S(2)}) copy-start(f32[3,1,1,768]{3,0,1,2:T(4,128)S(1)} %copy.247) | copy-start | bytes 27652
  224.6 49.8 %copy-start.68 = (bf16[768,256]{1,0:T(8,128)(2,1)}, bf16[768,256]{1,0:T(8,128)(2,1)S(1)}, u32[]{:S(2)}) copy-start(bf16[768,256]{1,0:T(8,128)(2,1)S(1)} %get-tuple-element.176) | copy-start | bytes 1179652
  241.4 33.0 %copy-start.70 = (bf16[768,256]{1,0:T(8,128)(2,1)S(1)}, bf16[768,256]{1,0:T(8,128)(2,1)}, u32[]{:S(2)}) copy-start(bf16[768,256]{1,0:T(8,128)(2,1)} %get-tuple-element.177) | copy-start | bytes 1179652
  241.4 33.0 %copy-start.84 = (bf16[768,128]{1,0:T(8,128)(2,1)S(1)}, bf16[768,128]{1,0:T(8,128)(2,1)}, u32[]{:S(2)}) copy-start(bf16[768,128]{1,0:T(8,128)(2,1)} %get-tuple-element.174) | copy-start | bytes 589828
  241.4 33.0 %copy-start.86 = (bf16[768,128]{1,0:T(8,128)(2,1)S(1)}, bf16[768,128]{1,0:T(8,128)(2,1)}, u32[]{:S(2)}) copy-start(bf16[768,128]{1,0:T(8,128)(2,1)} %get-tuple-element.175) | copy-start | bytes 589828
  241.5 33.0 %copy-start.136 = (f32[3,1,1,768]{3,0,1,2:T(4,128)S(1)}, f32[3,1,1,768]{3,0,1,2:T(4,128)}, u32[]{:S(2)}) copy-start(f32[3,1,1,768]{3,0,1,2:T(4,128)} %copy.256) | copy-start | bytes 27652
  368.9 18.7 %copy-start.7 = (f32[3,208,768]{2,1,0:T(8,128)S(1)}, f32[3,208,768]{2,1,0:T(8,128)}, u32[]{:S(2)}) copy-start(f32[3,208,768]{2,1,0:T(8,128)} %copy-done.6) | copy-start | bytes 5750788
  368.9 18.7 %copy-start.35 = (bf16[768,512]{1,0:T(8,128)(2,1)S(1)}, bf16[768,512]{1,0:T(8,128)(2,1)}, u32[]{:S(2)}) copy-start(bf16[768,512]{1,0:T(8,128)(2,1)} %copy-done.33) | copy-start | bytes 2359300
  368.9 18.7 %copy-start.95 = (f32[3,1,1,768]{3,0,1,2:T(4,128)S(1)}, f32[3,1,1,768]{3,0,1,2:T(4,128)}, u32[]{:S(2)}) copy-start(f32[3,1,1,768]{3,0,1,2:T(4,128)} %copy.250) | copy-start | bytes 27652
  368.9 18.7 %copy-start.106 = (f32[3,208]{1,0:T(4,128)S(1)}, f32[3,208]{1,0:T(4,128)}, u32[]{:S(2)}) copy-start(f32[3,208]{1,0:T(4,128)} %copy-done.105) | copy-start | bytes 7492
  417.8 54.6 %copy-start.49 = (bf16[768,640]{1,0:T(8,128)(2,1)S(1)}, bf16[768,640]{1,0:T(8,128)(2,1)}, u32[]{:S(2)}) copy-start(bf16[768,640]{1,0:T(8,128)(2,1)} %copy-done.48) | copy-start | bytes 2949124
  417.8 54.6 %copy-start.51 = (bf16[768,640]{1,0:T(8,128)(2,1)S(1)}, bf16[768,640]{1,0:T(8,128)(2,1)}, u32[]{:S(2)}) copy-start(bf16[768,640]{1,0:T(8,128)(2,1)} %copy-done.50) | copy-start | bytes 2949124
  417.8 54.6 %copy-start.57 = (bf16[768,512]{1,0:T(8,128)(2,1)S(1)}, bf16[768,512]{1,0:T(8,128)(2,1)}, u32[]{:S(2)}) copy-start(bf16[768,512]{1,0:T(8,128)(2,1)} %copy-done.56) | copy-start | bytes 2359300
  417.8 54.6 %copy-start.59 = (bf16[768,512]{1,0:T(8,128)(2,1)S(1)}, bf16[768,512]{1,0:T(8,128)(2,1)}, u32[]{:S(2)}) copy-start(bf16[768,512]{1,0:T(8,128)(2,1)} %copy-done.58) | copy-start | bytes 2359300
  512.0 27.6 %copy-start.9 = (bf16[624,2304]{1,0:T(8,128)(2,1)S(1)}, bf16[624,2304]{1,0:T(8,128)(2,1)}, u32[]{:S(2)}) copy-start(bf16[624,2304]{1,0:T(8,128)(2,1)} %attend_back.1) | copy-start | bytes 8626180
  569.7 139.7 %copy-start.134 = (f32[2,96,5]{1,0,2:T(2,128)S(1)}, f32[2,96,5]{1,0,2:T(2,128)}, u32[]{:S(2)}) copy-start(f32[2,96,5]{1,0,2:T(2,128)} %param.37) | copy-start | bytes 11524
  569.7 139.7 %copy-start.140 = (f32[2,96,5]{1,0,2:T(2,128)S(1)}, f32[2,96,5]{1,0,2:T(2,128)}, u32[]{:S(2)}) copy-start(f32[2,96,5]{1,0,2:T(2,128)} %param.47) | copy-start | bytes 11524
  569.7 139.7 %copy-start.141 = (f32[2,96,5]{1,0,2:T(2,128)S(1)}, f32[2,96,5]{1,0,2:T(2,128)}, u32[]{:S(2)}) copy-start(f32[2,96,5]{1,0,2:T(2,128)} %param.46) | copy-start | bytes 11524
  569.7 140.3 %copy-start.62 = (f32[96,192]{1,0:T(8,128)S(1)}, f32[96,192]{1,0:T(8,128)}, u32[]{:S(2)}) copy-start(f32[96,192]{1,0:T(8,128)} %param.36) | copy-start | bytes 221188
  569.7 140.3 %copy-start.107 = (f32[96,192]{1,0:T(8,128)S(1)}, f32[96,192]{1,0:T(8,128)}, u32[]{:S(2)}) copy-start(f32[96,192]{1,0:T(8,128)} %param.45) | copy-start | bytes 221188
  569.7 140.3 %copy-start.108 = (f32[96,192]{1,0:T(8,128)S(1)}, f32[96,192]{1,0:T(8,128)}, u32[]{:S(2)}) copy-start(f32[96,192]{1,0:T(8,128)} %param.44) | copy-start | bytes 221188
  719.6 45.8 %copy-start.55 = (f32[2,96,192]{2,1,0:T(8,128)}, f32[2,96,192]{2,1,0:T(8,128)S(1)}, u32[]{:S(2)}) copy-start(f32[2,96,192]{2,1,0:T(8,128)S(1)} %fusion.127) | copy-start | bytes 442372
  720.6 44.8 %copy-start.41 = (f32[2,96,576]{2,1,0:T(8,128)}, f32[2,96,576]{2,1,0:T(8,128)S(1)}, u32[]{:S(2)}) copy-start(f32[2,96,576]{2,1,0:T(8,128)S(1)} %fusion.109) | copy-start | bytes 1327108
  721.5 43.9 %copy-start.15 = (f32[2,96,1152]{2,1,0:T(8,128)S(1)}, f32[2,96,1152]{2,1,0:T(8,128)}, u32[]{:S(2)}) copy-start(f32[2,96,1152]{2,1,0:T(8,128)} %param.35) | copy-start | bytes 2654212
  721.5 43.9 %copy-start.29 = (f32[2,1152,96]{1,2,0:T(8,128)S(1)}, f32[2,1152,96]{1,2,0:T(8,128)}, u32[]{:S(2)}) copy-start(f32[2,1152,96]{1,2,0:T(8,128)} %get-tuple-element.264) | copy-start | bytes 2654212
  721.5 43.9 %copy-start.53 = (f32[2,96,1152]{2,1,0:T(8,128)S(1)}, f32[2,96,1152]{2,1,0:T(8,128)}, u32[]{:S(2)}) copy-start(f32[2,96,1152]{2,1,0:T(8,128)} %param.43) | copy-start | bytes 2654212
  721.5 43.9 %copy-start.54 = (f32[2,96,1152]{2,1,0:T(8,128)S(1)}, f32[2,96,1152]{2,1,0:T(8,128)}, u32[]{:S(2)}) copy-start(f32[2,96,1152]{2,1,0:T(8,128)} %param.42) | copy-start | bytes 2654212
  862.4 36.6 %copy-start.47 = (f32[2,96,192]{2,1,0:T(8,128)S(1)}, f32[2,96,192]{2,1,0:T(8,128)}, u32[]{:S(2)}) copy-start(f32[2,96,192]{2,1,0:T(8,128)} %param.32) | copy-start | bytes 442372
  862.4 38.4 %copy-start.31 = (f32[2,96,576]{2,1,0:T(8,128)S(1)}, f32[2,96,576]{2,1,0:T(8,128)}, u32[]{:S(2)}) copy-start(f32[2,96,576]{2,1,0:T(8,128)} %param.31) | copy-start | bytes 1327108
  (124 other events, 707.7 us)

commit v4 on v3

--- a/solution.py
+++ b/solution.py
@@ -160,51 +160,83 @@
     }
 
 
-def gather_kernel(groups, *refs):
-    own_refs, out_refs = refs[:groups], refs[groups : 2 * groups]
-    send_sem, recv_sem, core_send, core_recv, local_sem = refs[2 * groups :]
+def first_column(side, core, start):
+    if start < 512:
+        return side * 1152 + core * 640 + start
+    if start == 512:
+        return (1 - core) * (side * 1152 + 512) + core * (3 * D + side * HALF + 128)
+    return 3 * D + side * HALF + core * 256
+
+
+def gather_pieces(widths, firsts):
+    pieces = []
+    for group, width in enumerate(widths):
+        for start in range(0, width, PIECE_COLS):
+            if group in firsts and start == 512:
+                pieces += [(group, 512, 128), (group, 640, 128)]
+            else:
+                pieces.append((group, start, PIECE_COLS))
+    return pieces
+
+
+def gather_kernel(groups, firsts, *refs):
+    own_refs = refs[:groups]
+    edge_ref, latents_ref, shared_ref, table_ref, ada_ref = refs[groups : groups + 5]
+    out_refs = refs[groups + 5 : 2 * groups + 5]
+    latents_out, shared_out, mods_out = refs[2 * groups + 5 : 2 * groups + 8]
+    (tail, edge_got, times, parts, parts_got, mine, send_sem, recv_sem, core_send, core_recv,
+     local_sem, tail_sem, small_send, small_recv) = refs[2 * groups + 8 :]
     d = lax.axis_index("dp")
     h = lax.axis_index("head")
     peers = link_peers(d, h)
-    greet(list(peers.values()))
+    heads = [(d, h ^ other) for other in (1, 2, 3)]
+    datas = [(d ^ other, h) for other in range(1, 8)]
+    greet(heads + datas)
     y, c = h // 2, h % 2
     zh, zl, x = d // 4, (d // 2) % 2, d % 2
     every = slice(None)
-    pieces = [
-        (group, start)
-        for group in range(groups)
-        for start in range(0, own_refs[group].shape[1], PIECE_COLS)
-    ]
+    pieces = gather_pieces([own.shape[1] for own in own_refs], firsts)
     order_a = (("zh", (zh, zl, x)), ("zl", (every, zl, x)), ("x", (every, every, x)),
                ("y", (every, every, every)))
     order_b = (("y", (zh, zl, x)), ("zh", (zh, zl, x)), ("zl", (every, zl, x)),
                ("x", (every, every, x)))
 
+    def tail_of(piece):
+        group, start, size = pieces[piece]
+        if group in firsts and start == 2 * PIECE_COLS:
+            return firsts.index(group)
+        return None
+
+    def source_of(piece, rows):
+        group, start, size = pieces[piece]
+        place = tail_of(piece)
+        if place is not None:
+            return tail.at[place, rows]
+        return own_refs[group].at[rows, pl.ds(start, size)]
+
     def columns_of(piece, head):
-        group, start = pieces[piece]
-        width = own_refs[group].shape[1]
-        return pl.ds(pl.multiple_of(head * width + start, 128), PIECE_COLS)
+        group, start, size = pieces[piece]
+        if group in firsts:
+            return pl.ds(pl.multiple_of(first_column(head // 2, head % 2, start), 128), size)
+        return pl.ds(pl.multiple_of(head * own_refs[group].shape[1] + start, 128), size)
 
     def own_copy(piece):
-        group, start = pieces[piece]
+        group = pieces[piece][0]
         return pltpu.make_async_copy(
-            own_refs[group].at[:, pl.ds(start, PIECE_COLS)],
+            source_of(piece, pl.ds(0, own_refs[group].shape[0])),
             out_refs[group].at[zh, zl, x, :, columns_of(piece, h)],
             local_sem.at[piece],
         )
 
     def hop(piece, step, stream):
-        group, start = pieces[piece]
+        group = pieces[piece][0]
         rows_all = own_refs[group].shape[0]
         rows = pl.ds(0, ROWS_A) if stream == 0 else pl.ds(ROWS_A, rows_all - ROWS_A)
         head = h if stream < 2 else h ^ 2
         peer, index = (order_a if stream == 0 else order_b)[step]
         view = out_refs[group].at[index + (rows, columns_of(piece, head))]
-        source = view
-        if step == 0:
-            source = own_refs[group].at[rows, pl.ds(start, PIECE_COLS)]
         return pltpu.make_async_remote_copy(
-            src_ref=source,
+            src_ref=source_of(piece, rows) if step == 0 else view,
             dst_ref=view,
             send_sem=send_sem.at[piece, step, stream],
             recv_sem=recv_sem.at[piece, step, stream],
@@ -216,7 +248,7 @@
         return range(2) if step == 0 else range(3)
 
     def across(piece, side):
-        group, start = pieces[piece]
+        group = pieces[piece][0]
         view = out_refs[group].at[:, :, :, :, columns_of(piece, h ^ (2 * side))]
         return pltpu.make_async_remote_copy(
             src_ref=view,
@@ -227,8 +259,100 @@
             device_id_type=MESH,
         )
 
+    def small(place, source, target, peer):
+        return pltpu.make_async_remote_copy(
+            src_ref=source,
+            dst_ref=target,
+            send_sem=small_send.at[place],
+            recv_sem=small_recv.at[place],
+            device_id=peer,
+            device_id_type=MESH,
+        )
+
+    edge = small(0, edge_ref, edge_got, peers["core"])
+    edge.start()
+    tails = [
+        pltpu.make_async_copy(
+            own_refs[group].at[:, pl.ds(2 * PIECE_COLS, 128)], tail.at[place],
+            tail_sem.at[place],
+        )
+        for place, group in enumerate(firsts)
+    ]
+    for copy in tails:
+        copy.start()
+    latents = [
+        small(1 + place, latents_ref, latents_out.at[h], peer) for place, peer in enumerate(heads)
+    ]
+    for copy in latents:
+        copy.start()
+    latents_out[h] = latents_ref[...]
+    bring_times = pltpu.make_async_copy(out_refs[0], times, tail_sem.at[len(firsts)])
+    shares = [
+        small(4 + place, mine, shared_out.at[d], peer) for place, peer in enumerate(datas)
+    ]
+    swaps = [
+        small(11 + place, parts.at[d ^ (1 + place)], parts_got.at[d], peer)
+        for place, peer in enumerate(datas)
+    ]
+    spreads = [
+        small(18 + place, mods_out.at[h], mods_out.at[h], peer) for place, peer in enumerate(heads)
+    ]
+
+    def condition(turn):
+        if turn == 2:
+            edge.wait()
+            for copy in tails:
+                copy.wait()
+            tail[...] = tail[...] + edge_got[...]
+            for piece in range(len(pieces)):
+                if tail_of(piece) is not None:
+                    own_copy(piece).start()
+        if turn == 6:
+            for side in range(2):
+                across(0, side).wait_recv()
+            bring_times.start()
+        if turn == 7:
+            bring_times.wait()
+            rows = times.shape[-2]
+            mine[...] = shared_ref[...] + dot_nn(
+                table_ref[...], times[...].reshape(8 * rows, times.shape[-1])
+            )
+            for copy in shares:
+                copy.start()
+            shared_out[d] = mine[...]
+        if turn == 9:
+            for copy in shares:
+                copy.wait()
+            count, lines, width = shared_out.shape
+            signal = to_bf16(double_silu(shared_out[...])).reshape(count * lines, width)
+            first = (d // 2) * WIDE + (d % 2) * ada_ref.shape[1]
+            at = lax.broadcasted_iota(jnp.int32, (width, 128), 0)
+            to = lax.broadcasted_iota(jnp.int32, (width, 128), 1)
+            chosen = jnp.where((at == first + to) & (to < ada_ref.shape[1]), 1.0, 0.0)
+            own = to_bf16(dot_nn(signal, to_bf16(chosen)))[:, : ada_ref.shape[1]]
+            columns = ada_ref.shape[2]
+            for layer in range(2):
+                part = dot_nn(own, ada_ref[layer]).reshape(count, lines, columns)
+                parts[:, :, layer * columns : (layer + 1) * columns] = part[:, :8]
+            for copy in swaps:
+                copy.start()
+            parts_got[d] = parts[d]
+        if turn == 11:
+            for copy in swaps:
+                copy.wait()
+            total = parts_got[0]
+            for place in range(1, 8):
+                total = total + parts_got[place]
+            mods_out[h] = total
+            for copy in spreads:
+                copy.start()
+        if turn == 13:
+            for copy in spreads + latents:
+                copy.wait()
+
     for piece in range(len(pieces)):
-        own_copy(piece).start()
+        if tail_of(piece) is None:
+            own_copy(piece).start()
     for turn in range(len(pieces) + 4):
         for step in range(5):
             piece = turn - step
@@ -245,36 +369,57 @@
             else:
                 for side in range(2):
                     across(piece, side).start()
+        condition(turn)
     for piece in range(len(pieces)):
         for step in range(4):
             for stream in streams(step):
                 hop(piece, step, stream).wait_send()
         for side in range(2):
-            across(piece, side).wait()
-
-
-def gather_whole(owns, collective_id):
+            if piece > 0:
+                across(piece, side).wait_recv()
+            across(piece, side).wait_send()
+
+
+def gather_whole(owns, firsts, edge, latents, shared, table, ada, collective_id):
     groups = len(owns)
-    pieces = sum(own.shape[1] // PIECE_COLS for own in owns)
-    wholes = pl.pallas_call(
-        functools.partial(gather_kernel, groups),
+    pieces = len(gather_pieces([own.shape[1] for own in owns], firsts))
+    rows = owns[0].shape[0]
+    low = jnp.bfloat16
+    mod_cols = 2 * ada.shape[2]
+    *wholes, latents_all, shared_all, mods = pl.pallas_call(
+        functools.partial(gather_kernel, groups, firsts),
         out_shape=[
             jax.ShapeDtypeStruct((2, 2, 2, own.shape[0], 4 * own.shape[1]), own.dtype)
             for own in owns
+        ]
+        + [
+            jax.ShapeDtypeStruct((4,) + latents.shape, jnp.float32),
+            jax.ShapeDtypeStruct((8,) + shared.shape, jnp.float32),
+            jax.ShapeDtypeStruct((4, 8, mod_cols), jnp.float32),
         ],
-        in_specs=[anywhere()] * groups,
-        out_specs=[anywhere()] * groups,
+        in_specs=[anywhere()] * groups + [vmem()] * 5,
+        out_specs=[anywhere()] * groups + [vmem()] * 3,
         scratch_shapes=[
+            pltpu.VMEM(edge.shape, low),
+            pltpu.VMEM(edge.shape, low),
+            pltpu.VMEM((2, 2, 2, rows, 4 * owns[0].shape[1]), low),
+            pltpu.VMEM((8, 8, mod_cols), jnp.float32),
+            pltpu.VMEM((8, 8, mod_cols), jnp.float32),
+            pltpu.VMEM(shared.shape, jnp.float32),
             pltpu.SemaphoreType.DMA((pieces, 4, 3)),
             pltpu.SemaphoreType.DMA((pieces, 4, 3)),
             pltpu.SemaphoreType.DMA((pieces, 2)),
             pltpu.SemaphoreType.DMA((pieces, 2)),
             pltpu.SemaphoreType.DMA((pieces,)),
+            pltpu.SemaphoreType.DMA((len(firsts) + 1,)),
+            pltpu.SemaphoreType.DMA((21,)),
+            pltpu.SemaphoreType.DMA((21,)),
         ],
-        compiler_params=pltpu.CompilerParams(collective_id=collective_id, has_side_effects=True),
+        compiler_params=comm_params(collective_id),
         name="gather_weights",
-    )(*owns)
-    return [whole.reshape(8 * own.shape[0], -1) for whole, own in zip(wholes, owns)]
+    )(*owns, edge, latents, shared, table, ada)
+    wholes = [whole.reshape(8 * own.shape[0], -1) for whole, own in zip(wholes, owns)]
+    return wholes, latents_all, shared_all, mods
 
 
 def gather_general(own):
@@ -284,14 +429,13 @@
     return blocks.transpose(0, 2, 1, 3).reshape(-1, lax.axis_size("head") * columns)
 
 
-def reduce_kernel(layers, *refs):
-    first_refs = refs[:layers]
-    left_refs = refs[layers : 3 * layers]
-    right_refs = refs[3 * layers : 5 * layers]
-    extra_ref, out_ref, total_ref, edge_ref = refs[5 * layers : 5 * layers + 4]
-    (own, near, made, left, left_t, right, send_a, send_b, got_a, got_b, keep_a, keep_b,
-     mine, head_got, data_got, own_sem, near_send, near_recv, hop_send, hop_recv, left_sem,
-     right_sem, edge_send, edge_recv, sum_send, sum_recv) = refs[5 * layers + 4 :]
+def reduce_kernel(plan, lefts, rights, *refs):
+    left_refs, right_refs = refs[:lefts], refs[lefts : lefts + rights]
+    extra_ref, out_ref, total_ref, edge_ref = refs[lefts + rights : lefts + rights + 4]
+    (made, near, left, left_t, right, send_a, send_b, got_a, got_b, keep_a, keep_b,
+     mine, head_got, data_got, near_send, near_recv, hop_send, hop_recv, left_sem,
+     right_sem, edge_send, edge_recv, sum_send, sum_recv) = refs[lefts + rights + 4 :]
+    layers = len(plan)
     per_group = D // PIECE_COLS
     pieces = 3 * layers * per_group
     d = lax.axis_index("dp")
@@ -302,28 +446,15 @@
     y, c = h // 2, h % 2
     zh, zl, x = d // 4, (d // 2) % 2, d % 2
     order = (("y", "x"), ("x", "zl"), ("zl", "zh"), ("zh", "y"))
-    rows_own = own.shape[-2]
+    shape = made.shape[3:]
+    rows_own = shape[-2]
     top, bottom = pl.ds(0, ROWS_A), pl.ds(ROWS_A, rows_own - ROWS_A)
     every = slice(None)
 
-    def columns_of(piece, head):
-        start = head * D + (piece % per_group) * PIECE_COLS
-        return pl.ds(pl.multiple_of(start, PIECE_COLS), PIECE_COLS)
-
-    def own_copy(piece, layer, side):
-        return pltpu.make_async_copy(
-            first_refs[layer].at[:, :, :, :, columns_of(piece, 2 * side + c)],
-            own.at[piece % SLOTS, side],
-            own_sem.at[piece % SLOTS, side],
-        )
-
-    def near_copy(piece, layer, side):
+    def near_copy(piece, side):
         slot = piece % SLOTS
-        source = made.at[slot, side]
-        if layer is not None:
-            source = first_refs[layer].at[:, :, :, :, columns_of(piece, 2 * side + 1 - c)]
         return pltpu.make_async_remote_copy(
-            src_ref=source,
+            src_ref=made.at[slot, side, 1 - c],
             dst_ref=near.at[slot, side],
             send_sem=near_send.at[slot, side],
             recv_sem=near_recv.at[slot, side],
@@ -331,58 +462,112 @@
             device_id_type=MESH,
         )
 
-    def left_copy(pair):
-        return pltpu.make_async_copy(left_refs[pair], left.at[pair], left_sem.at[pair])
-
-    def right_copy(piece, pair, head):
+    def left_copy(place):
+        rows = left_refs[place].shape[0]
         return pltpu.make_async_copy(
-            right_refs[pair].at[:, columns_of(piece, head)],
+            left_refs[place], left.at[place, pl.ds(0, rows)], left_sem.at[place]
+        )
+
+    def turn_left(place, at):
+        rows = left_refs[place].shape[0]
+        left_copy(place).wait()
+        left_t[at, :, :rows] = left[place, :rows].T
+
+    def sources(layer, part, head, half):
+        column = first_column(head // 2, head % 2, part * PIECE_COLS + (128 * half if part == 2 else 0))
+        if part < 2:
+            column += 128 * half
+        for at, (left_place, right_place, start, stop) in enumerate(plan[layer][0]):
+            if start <= column < stop:
+                return left_place, right_place, column - start
+
+    def right_copies(piece, layer, part):
+        copies = []
+        for head in range(4):
+            for half in range(2):
+                left_place, right_place, column = sources(layer, part, head, half)
+                rows = right_refs[right_place].shape[0]
+                copies.append(
+                    pltpu.make_async_copy(
+                        right_refs[right_place].at[:, pl.ds(column, 128)],
+                        right.at[piece % 2, head, pl.ds(0, rows), pl.ds(128 * half, 128)],
+                        right_sem.at[piece % 2, head, half],
+                    )
+                )
+        return copies
+
+    def right_copy(piece, right_place, head):
+        start = head * D + (piece % per_group) * PIECE_COLS
+        return pltpu.make_async_copy(
+            right_refs[right_place].at[:, pl.ds(pl.multiple_of(start, PIECE_COLS), PIECE_COLS)],
             right.at[piece % 2, head],
-            right_sem.at[piece % 2, head],
-        )
-
-    def is_made(piece):
-        return (piece // per_group) % 3 != 0
+            right_sem.at[piece % 2, head, 0],
+        )
 
     def fetch(piece):
         for layer in range(layers):
+            for part in range(per_group):
+
+                @pl.when(piece == 3 * layer * per_group + part)
+                def _():
+                    for copy in right_copies(piece, layer, part):
+                        copy.start()
+
             for member in range(2):
 
                 @pl.when(piece // per_group == 3 * layer + 1 + member)
                 def _():
                     for head in range(4):
-                        right_copy(piece, 2 * layer + member, head).start()
+                        right_copy(piece, plan[layer][1 + member][1], head).start()
 
     def bring(piece):
         slot = piece % SLOTS
         for layer in range(layers):
-
-            @pl.when(piece // per_group == 3 * layer)
+            used = []
+            for left_place, _, _, _ in plan[layer][0]:
+                if left_place not in used:
+                    used.append(left_place)
+
+            @pl.when(piece == 3 * layer * per_group)
             def _():
-                for side in range(2):
-                    near_copy(piece, layer, side).start()
-                    own_copy(piece, layer, side).start()
+                for at, left_place in enumerate(used):
+                    turn_left(left_place, at)
+
+            for part in range(per_group):
+
+                @pl.when(piece == 3 * layer * per_group + part)
+                def _():
+                    for copy in right_copies(piece, layer, part):
+                        copy.wait()
+                    for head in range(4):
+                        pair = [sources(layer, part, head, half) for half in range(2)]
+                        spans = [(0, 2)] if pair[0][0] == pair[1][0] else [(0, 1), (1, 2)]
+                        for first, stop in spans:
+                            left_place, right_place, _ = pair[first]
+                            rows = right_refs[right_place].shape[0]
+                            columns = slice(128 * first, 128 * stop)
+                            made[slot, head // 2, head % 2, :, :, :, :, columns] = dot_nn(
+                                left_t[used.index(left_place), :, :rows],
+                                right[piece % 2, head, :rows, columns],
+                            ).reshape(shape[:-1] + (128 * (stop - first),))
 
             for member in range(2):
 
                 @pl.when(piece == (3 * layer + 1 + member) * per_group)
                 def _():
-                    pair = 2 * layer + member
-                    left_copy(pair).wait()
-                    left_t[...] = left[pair].T
-
-        @pl.when(is_made(piece))
+                    turn_left(plan[layer][1 + member][0], 0)
+
+        @pl.when((piece // per_group) % 3 != 0)
         def _():
             for head in range(4):
-                right_copy(piece, 0, head).wait()
-            shape = own.shape[2:]
-            for side in range(2):
-                made[slot, side] = dot_nn(left_t[...], right[piece % 2, 2 * side + 1 - c]).reshape(
-                    shape
-                )
-                near_copy(piece, None, side).start()
-            for side in range(2):
-                own[slot, side] = dot_nn(left_t[...], right[piece % 2, 2 * side + c]).reshape(shape)
+                right_copy(piece, plan[0][1][1], head).wait()
+            for head in range(4):
+                made[slot, head // 2, head % 2] = dot_nn(
+                    left_t[0], right[piece % 2, head]
+                ).reshape(shape)
+
+        for side in range(2):
+            near_copy(piece, side).start()
 
     def hop(piece, step, stream):
         slot = piece % SLOTS
@@ -399,15 +584,10 @@
     def first(piece):
         slot = piece % SLOTS
         for side in range(2):
-            near_copy(piece, None, side).wait()
-
-        @pl.when(jnp.logical_not(is_made(piece)))
-        def _():
-            for side in range(2):
-                own_copy(piece, 0, side).wait()
-
-        def total(*index):
-            return own[(slot,) + index] + near[(slot,) + index]
+            near_copy(piece, side).wait()
+
+        def total(side, *index):
+            return made[(slot, side, c) + index] + near[(slot, side) + index]
 
         send_a[0][slot] = to_bf16(total(1 - y, every, every, every, top))
         hop(piece, 0, 0).start()
@@ -443,9 +623,12 @@
                 slot
             ].astype(jnp.float32)
 
-    for pair in range(2 * layers):
-        left_copy(pair).start()
+    for place in range(lefts):
+        left_copy(place).start()
+    fetch(0)
+    fetch(1)
     bring(0)
+    fetch(2)
     bring(1)
 
     @pl.loop(0, pieces + 4)
@@ -522,36 +705,34 @@
         copy.wait()
 
 
-def reduce_whole(firsts, pairs, extra, collective_id):
-    layers = len(firsts)
-    frames = pairs[0][0].shape[0]
-    rows = firsts[0].shape[0] // 8
+def reduce_whole(plan, lefts, rights, extra, collective_id):
+    layers = len(plan)
+    frames = lefts[0].shape[0]
+    rows = D // 8
     per_group = D // PIECE_COLS
     pieces = 3 * layers * per_group
-    views = [first.reshape(2, 2, 2, rows, first.shape[1]) for first in firsts]
     leads = ((2, 2, 2), (2, 2), (2,), ())
 
     def buffers(count, dtype):
         return [pltpu.VMEM((SLOTS,) + lead + (count, PIECE_COLS), dtype) for lead in leads]
 
     bottom_rows = rows - ROWS_A
-    whole = (SLOTS, 2, 2, 2, 2, rows, PIECE_COLS)
+    blocks = (2, 2, 2, rows, PIECE_COLS)
     low = jnp.bfloat16
     summed, totals, edges = pl.pallas_call(
-        functools.partial(reduce_kernel, layers),
+        functools.partial(reduce_kernel, plan, len(lefts), len(rights)),
         out_shape=[
             jax.ShapeDtypeStruct((pieces, rows, PIECE_COLS), jnp.float32),
             jax.ShapeDtypeStruct((8, 128), jnp.float32),
             jax.ShapeDtypeStruct((layers, rows, 128), jnp.float32),
         ],
-        in_specs=[anywhere()] * (5 * layers) + [vmem()],
+        in_specs=[anywhere()] * (len(lefts) + len(rights)) + [vmem()],
         out_specs=[vmem()] * 3,
         scratch_shapes=[
-            pltpu.VMEM(whole, jnp.float32),
-            pltpu.VMEM(whole, jnp.float32),
-            pltpu.VMEM(whole, jnp.float32),
-            pltpu.VMEM((2 * layers, frames, D), low),
-            pltpu.VMEM((D, frames), low),
+            pltpu.VMEM((SLOTS, 2, 2) + blocks, jnp.float32),
+            pltpu.VMEM((SLOTS, 2) + blocks, jnp.float32),
+            pltpu.VMEM((len(lefts), frames, D), low),
+            pltpu.VMEM((3, D, frames), low),
             pltpu.VMEM((2, 4, frames, PIECE_COLS), low),
             buffers(ROWS_A, low),
             buffers(bottom_rows, low),
@@ -564,11 +745,10 @@
             pltpu.VMEM((8, 8, 128), jnp.float32),
             pltpu.SemaphoreType.DMA((SLOTS, 2)),
             pltpu.SemaphoreType.DMA((SLOTS, 2)),
-            pltpu.SemaphoreType.DMA((SLOTS, 2)),
             pltpu.SemaphoreType.DMA((4, 2, SLOTS)),
             pltpu.SemaphoreType.DMA((4, 2, SLOTS)),
-            pltpu.SemaphoreType.DMA((2 * layers,)),
-            pltpu.SemaphoreType.DMA((2, 4)),
+            pltpu.SemaphoreType.DMA((len(lefts),)),
+            pltpu.SemaphoreType.DMA((2, 4, 2)),
             pltpu.SemaphoreType.DMA((layers,)),
             pltpu.SemaphoreType.DMA((layers,)),
             pltpu.SemaphoreType.DMA((10,)),
@@ -576,7 +756,7 @@
         ],
         compiler_params=comm_params(collective_id),
         name="reduce_grads",
-    )(*views, *[pair[0] for pair in pairs], *[pair[1] for pair in pairs], extra)
+    )(*lefts, *rights, extra)
     summed = summed.reshape(3 * layers, per_group, rows, PIECE_COLS).transpose(0, 2, 1, 3)
     return list(summed.reshape(3 * layers, rows, D)), totals, edges
 
@@ -1238,13 +1418,8 @@
     block = 3 * D // head_count
     share = D // head_count
     is_first = core == 0
-    edge = jnp.where(is_first, out_weight[..., 128:], qkv_weight[..., :64])
-    latents = jnp.concatenate([clean_latents, noise_draw], -1)
-    latents_size = latents.size
-    packed = jnp.concatenate([latents.reshape(-1), edge.reshape(-1)]).reshape(-1, 128)
-    packed = spread(packed, "head").reshape(head_count, -1)
-    latents_all = packed[:, :latents_size].reshape(head_count, clip_count, tile, 2 * channels)
-    edge = lax.dynamic_slice_in_dim(packed[:, latents_size:], h ^ 1, 1, 0).reshape(edge.shape)
+    latents = jnp.concatenate([clean_latents, noise_draw], -1).transpose(0, 2, 1)
+    latents = latents.reshape(-1, tile)
 
     def with_edge(qkv, out, edge):
         return jnp.where(
@@ -1262,42 +1437,98 @@
         )
         return qkv, out
 
-    first_groups = to_bf16(with_edge(qkv_weight, out_weight, edge))
-    weight_groups = []
-    for layer in range(2):
-        weight_groups.append(first_groups[layer])
-        weight_groups.append(to_bf16(up_weight[layer]))
-        weight_groups.append(to_bf16(down_weight[layer]))
+    keep_mask = jnp.arange(CAP)[None, :] < cap_len[:, None]
+    cap_mean = product("ft,ftd->fd", keep_mask.astype(jnp.bfloat16), captions) / cap_len[
+        :, None
+    ].astype(jnp.float32)
+    cap_unit = cap_mean * lax.rsqrt(jnp.mean(cap_mean * cap_mean, -1, keepdims=True) + 1e-06)
+    own_captions = jnp.concatenate([lax.dynamic_slice_in_dim(captions, own_clip, 1, 0), captions[2:3]])
+    own_lengths = jnp.concatenate([lax.dynamic_slice_in_dim(cap_len, own_clip, 1, 0), cap_len[2:3]])
+
+    qkv_low, out_low = to_bf16(qkv_weight), to_bf16(out_weight)
+    edge = jnp.where(is_first, out_low[..., 128:], qkv_low[..., :64])
     time_cols = time_weight.shape[1]
     io_cols = io_weight.shape[2]
+    ada_cols = ada_weight.shape[2]
+    ada_bf = to_bf16(ada_weight)
     io_flat = io_weight.transpose(1, 0, 2).reshape(rows_own, 2 * io_cols)
-    table_rows = clip_count * D // WIDE
-    small_rows = -(-(rows_own + table_rows) // 16) * 16
-    small_own = jnp.concatenate(
-        [
-            jnp.pad(
-                to_bf16(jnp.concatenate([time_weight, io_flat], 1)),
-                ((0, 0), (0, WIDE - time_cols - 2 * io_cols)),
-            ),
-            to_bf16(time_table(timesteps, D)).reshape(table_rows, WIDE),
-            jnp.zeros((small_rows - rows_own - table_rows, WIDE), jnp.bfloat16),
-        ]
-    )
+    small_own = jnp.pad(
+        to_bf16(jnp.concatenate([time_weight, io_flat], 1)),
+        ((0, 0), (0, WIDE - time_cols - 2 * io_cols)),
+    )
+    table_bf = to_bf16(time_table(timesteps, D))
+
+    def listed(first_groups):
+        listed_groups = [small_own]
+        for layer in range(2):
+            listed_groups.append(first_groups[layer])
+            listed_groups.append(to_bf16(up_weight[layer]))
+            listed_groups.append(to_bf16(down_weight[layer]))
+        return listed_groups
+
     if linked:
-        gathered = gather_whole([small_own] + weight_groups, next(ids))
+        none = jnp.zeros_like(edge)
+        edge = jnp.where(
+            is_first, jnp.concatenate([edge, none], -1), jnp.concatenate([none, edge], -1)
+        )
+        shared = jnp.concatenate(
+            [
+                jnp.zeros((clip_count, D)),
+                table_bf.astype(jnp.float32),
+                cap_unit,
+                jnp.zeros((16 - 3 * clip_count, D)),
+            ]
+        )
+        gathered, latents_all, shared_all, mods = gather_whole(
+            listed(with_edge(qkv_low, out_low, none)),
+            (1, 4),
+            edge,
+            latents,
+            jnp.pad(shared, ((0, 0), (0, head_count * WIDE - D))),
+            jnp.pad(table_bf, ((0, 16 - clip_count), (0, 0))),
+            ada_bf,
+            next(ids),
+        )
+        start = (d // 2) * WIDE + (d % 2) * rows_own
+        hidden_own = lax.dynamic_slice(
+            shared_all, (0, 0, start), (data_count, clip_count, rows_own)
+        ).reshape(-1, rows_own)
+        table_own = lax.dynamic_slice(
+            shared_all, (0, clip_count, own_row), (data_count, clip_count, rows_own)
+        ).reshape(-1, rows_own)
+        cap_all = shared_all[:, 2 * clip_count : 3 * clip_count, :D].reshape(-1, D)
+        signal_own = to_bf16(double_silu(hidden_own))
+        mods = mods[:, :clip_count]
     else:
-        gathered = [gather_general(own) for own in [small_own] + weight_groups]
-    small_all = gathered[0].reshape(data_count, small_rows, head_count, WIDE)
+        edge = lax.ppermute(edge, "head", [(place, place ^ 1) for place in range(head_count)])
+        gathered = [gather_general(own) for own in listed(with_edge(qkv_low, out_low, edge))]
+        latents_all = spread(latents, "head")
+        time_full = gathered[0].reshape(D, head_count, WIDE)[:, :, :time_cols].reshape(D, D)
+        time_hidden = jnp.dot(table_bf, time_full, preferred_element_type=jnp.float32)
+        shared = jnp.concatenate([time_hidden, table_bf.astype(jnp.float32), cap_unit], 1)
+        shared_all = spread(shared, "dp").reshape(-1, 3 * D)
+        hidden_own = lax.dynamic_slice_in_dim(shared_all, own_row, rows_own, 1)
+        table_own = lax.dynamic_slice_in_dim(shared_all, D + own_row, rows_own, 1)
+        cap_all = shared_all[:, 2 * D :]
+        signal_own = to_bf16(double_silu(hidden_own))
+        mod_part = product("fd,ldn->fln", signal_own, ada_bf)
+        mod_part = mod_part.reshape(data_count, clip_count, 2 * ada_cols)
+        mods = spread(jnp.sum(swap(mod_part, "dp"), 0), "head")
     up_full = [gathered[2], gathered[5]]
     down_full = [gathered[3], gathered[6]]
-    time_full = small_all[:, :rows_own, :, :time_cols].reshape(D, D)
     io_full = (
-        small_all[:, :rows_own, :, time_cols : time_cols + 2 * io_cols]
+        gathered[0]
+        .reshape(D, head_count, WIDE)[:, :, time_cols : time_cols + 2 * io_cols]
         .reshape(D, head_count, 2, io_cols)
         .transpose(2, 0, 1, 3)
         .reshape(2, D, channels)
     )
-    table_bf = small_all[:, rows_own : rows_own + table_rows, 0].reshape(-1, D)
+    mod_all = (
+        mods.reshape(head_count, clip_count, 2, ada_cols)
+        .transpose(1, 2, 0, 3)
+        .reshape(clip_count, 2, 6 * D)
+    )
+    tile_mods = by_tile(mod_all)
 
     def split_first(whole):
         qkv, out = [], []
@@ -1315,48 +1546,24 @@
             columns += [qkv[:, q + 640 : q + 1152], out[:, o + 128 : o + 384]]
         return jnp.concatenate(columns, 1)
 
-    qkv_full, out_full = zip(*[split_first(gathered[1 + 3 * layer]) for layer in range(2)])
-
+    if linked:
+        qkv_full = [gathered[1 + 3 * layer][:, : 3 * D] for layer in range(2)]
+        out_full = [gathered[1 + 3 * layer][:, 3 * D :] for layer in range(2)]
+    else:
+        qkv_full, out_full = zip(*[split_first(gathered[1 + 3 * layer]) for layer in range(2)])
+
+    latents_all = latents_all.reshape(head_count, clip_count, 2 * channels, tile)
     own_latents = lax.dynamic_slice(
-        latents_all, (2 * core, own_clip, 0, 0), (2, 1, tile, 2 * channels)
+        latents_all, (2 * core, own_clip, 0, 0), (2, 1, 2 * channels, tile)
     )[:, 0]
-    latents = jnp.concatenate([own_latents, latents[2:3]])
-    clean_rows, noise_rows = latents[..., :channels], latents[..., channels:]
+    latents = jnp.concatenate(
+        [own_latents, lax.dynamic_slice_in_dim(latents_all, h, 1, 0)[0, 2:3]]
+    )
+    clean_rows, noise_rows = latents[:, :channels], latents[:, channels:]
     tile_times = by_tile(timesteps)[:, None, None]
     input_bf = to_bf16((1.0 - tile_times) * clean_rows + tile_times * noise_rows)
     target = noise_rows - clean_rows
-    hidden = product("flc,dc->fld", input_bf, io_full[0])
-
-    keep_mask = jnp.arange(CAP)[None, :] < cap_len[:, None]
-    cap_mean = product("ft,ftd->fd", keep_mask.astype(jnp.bfloat16), captions) / cap_len[
-        :, None
-    ].astype(jnp.float32)
-    cap_unit = cap_mean * lax.rsqrt(jnp.mean(cap_mean * cap_mean, -1, keepdims=True) + 1e-06)
-    own_captions = jnp.concatenate([lax.dynamic_slice_in_dim(captions, own_clip, 1, 0), captions[2:3]])
-    own_lengths = jnp.concatenate([lax.dynamic_slice_in_dim(cap_len, own_clip, 1, 0), cap_len[2:3]])
-
-    time_hidden = jnp.dot(table_bf, time_full, preferred_element_type=jnp.float32)
-    signal_bf = to_bf16(double_silu(time_hidden))
-    signal_own = lax.dynamic_slice_in_dim(signal_bf, own_row, rows_own, 1)
-    table_own = lax.dynamic_slice_in_dim(table_bf, own_row, rows_own, 1)
-    ada_bf = to_bf16(ada_weight)
-    ada_cols = ada_weight.shape[2]
-    mod_part = product("fd,ldn->fln", signal_own, ada_bf).reshape(
-        data_count, clip_count, 2 * ada_cols
-    )
-    mod_part = jnp.concatenate(
-        [mod_part, jnp.broadcast_to(cap_unit, (data_count, clip_count, D))], -1
-    )
-    mod_part = swap(mod_part, "dp")
-    cap_all = mod_part[:, :, 2 * ada_cols :].reshape(-1, D)
-    mod_own = jnp.sum(mod_part[:, :, : 2 * ada_cols], 0)
-    mod_all = (
-        spread(mod_own, "head")
-        .reshape(head_count, clip_count, 2, ada_cols)
-        .transpose(1, 2, 0, 3)
-        .reshape(clip_count, 2, 6 * D)
-    )
-    tile_mods = by_tile(mod_all)
+    hidden = product("fcl,dc->fld", input_bf, io_full[0])
 
     frames = clip_count * tile
 
@@ -1390,10 +1597,10 @@
         saved_layers.append(kept)
     final = norm_rows(hidden)
     final_bf = to_bf16(final)
-    predicted = product("fld,dc->flc", final_bf, io_full[1])
+    predicted = product("fld,dc->fcl", final_bf, io_full[1])
     errors = predicted - target
-    flow_part = jnp.sum(jnp.mean(errors * errors, -1))
-    grad_pred = to_bf16(2.0 * errors / errors.shape[-1])
+    flow_part = jnp.sum(jnp.mean(errors * errors, 1))
+    grad_pred = to_bf16(2.0 * errors / channels)
     pool_sum = jnp.sum(spread(by_clip(jnp.sum(final, 1)), "head"), 0)
     pooled_out = pool_sum / length
 
@@ -1411,11 +1618,16 @@
     contrast_value, contrast_back = jax.vjp(contrast_of, pool_sum)
     grad_pool = by_tile(contrast_back(jnp.ones_like(contrast_value))[0])
     loss_part = flow_part + contrast_value / head_count
-    grad_final = product("flc,dc->fld", grad_pred, io_full[1]) + grad_pool[:, None, :]
+    grad_final = product("fcl,dc->fld", grad_pred, io_full[1]) + grad_pool[:, None, :]
     final_value, final_back = jax.vjp(norm_rows, hidden)
     grad_hidden = final_back(grad_final)[0]
-    fin_grad = product("flc,fld->dc", grad_pred, final_bf)
-    firsts, pairs = [], []
+    fin_grad = product("fcl,fld->dc", grad_pred, final_bf)
+    plan, lefts, rights = [], [], []
+
+    def listed_factors(factors, factor):
+        factors.append(factor.reshape(-1, factor.shape[-1]))
+        return len(factors) - 1
+
     mod_grads = [None, None]
     for layer_index in (1, 0):
         (
@@ -1437,10 +1649,6 @@
         grad_active = product("fld,dn->fln", grad_down, down_full[layer_index])
         gelu_value, gelu_back = jax.vjp(soft_gelu, layer_upper)
         grad_upper = to_bf16(gelu_back(grad_active)[0])
-        pairs += [
-            (layer_normed2.reshape(frames, D), grad_upper.reshape(frames, -1)),
-            (grad_down.reshape(frames, D), layer_active.reshape(frames, -1)),
-        ]
         grad_normed2 = product("fln,dn->fld", grad_upper, up_full[layer_index])
         mod_value, mod_back = jax.vjp(modulate, layer_middle, mod_parts[3], mod_parts[4])
         grad_middle, d_shift2, d_scale2 = mod_back(grad_normed2)
@@ -1448,31 +1656,37 @@
         d_gate1 = jnp.sum(layer_branch * grad_middle, axis=1, keepdims=True)
         grad_branch = to_bf16(mod_parts[2] * grad_middle)
         grad_mixed = to_bf16(product("fld,de->fle", grad_branch, out_full[layer_index]))
-        out_grad = product("fld,fle->de", grad_branch, layer_mixed)
+        branch_place, branch_right = listed_factors(lefts, grad_branch), listed_factors(rights, layer_mixed)
+        normed_place = listed_factors(lefts, layer_normed)
         if layer_index == 0:
             grad_proj = attend_back(*attended, grad_mixed.reshape(frames, D), next(ids))
             grad_normed = product("fn,dn->fd", grad_proj, weight)
-            qkv_grad = product("fd,fn->dn", layer_normed.reshape(frames, D), grad_proj)
+            first = [(normed_place, listed_factors(rights, grad_proj), 0, 3 * D)]
         else:
             query, pair_kv = attended
             grad_query, grad_keys, grad_values = cross_back(query, pair_kv, own_lengths, grad_mixed)
             grad_normed = product("fln,dn->fld", grad_query, weight[:, :D])
-            qkv_grad = jnp.concatenate(
-                [
-                    product("fld,fln->dn", layer_normed, grad_query),
-                    product("ftd,ftn->dn", own_captions, grad_keys),
-                    product("ftd,ftn->dn", own_captions, grad_values),
-                ],
-                1,
+            caption_place = listed_factors(lefts, own_captions)
+            first = [
+                (normed_place, listed_factors(rights, grad_query), 0, D),
+                (caption_place, listed_factors(rights, grad_keys), D, 2 * D),
+                (caption_place, listed_factors(rights, grad_values), 2 * D, 3 * D),
+            ]
+        first.append((branch_place, branch_right, 3 * D, 4 * D))
+        plan.append(
+            (
+                tuple(first),
+                (listed_factors(lefts, layer_normed2), listed_factors(rights, grad_upper)),
+                (listed_factors(lefts, grad_down), listed_factors(rights, layer_active)),
             )
-        firsts.append(join_first(qkv_grad, out_grad))
+        )
         first_value, first_back = jax.vjp(modulate, layer_hidden, mod_parts[0], mod_parts[1])
         grad_in, d_shift1, d_scale1 = first_back(grad_normed.reshape(clip_count, tile, D))
         mod_grads[layer_index] = jnp.concatenate(
             [d_shift1, d_scale1, d_gate1, d_shift2, d_scale2, d_gate2], -1
         )[:, 0]
         grad_hidden = grad_in + grad_middle
-    in_grad = product("fld,flc->dc", to_bf16(grad_hidden), input_bf)
+    in_grad = product("fld,fcl->dc", to_bf16(grad_hidden), input_bf)
 
     mod_size = clip_count * 2 * ada_cols
     io_size = rows_own * 2 * io_cols
@@ -1496,28 +1710,32 @@
     ada_grad = exact_product("fd,fln->ldn", signal_own.astype(jnp.float32), mod_grad)
     grad_signal = exact_product("fln,ldn->fd", mod_grad, ada_bf.astype(jnp.float32))
     grad_signal = jnp.sum(spread(grad_signal, "head"), 0)
-    hidden_own = lax.dynamic_slice_in_dim(time_hidden, own_row, rows_own, 1)
     signal_own_value, signal_back = jax.vjp(double_silu, hidden_own)
     grad_cond = spread(signal_back(grad_signal)[0], "dp").transpose(1, 0, 2).reshape(-1, D)
     time_grad = exact_product(
         "fd,fn->dn",
-        table_own.astype(jnp.float32),
+        table_own,
         lax.dynamic_slice_in_dim(grad_cond, h * time_cols, time_cols, 1),
     )
 
     square = sum((jnp.sum(grad * grad) for grad in (ada_grad, time_grad, io_grad)))
     if linked:
         extra = jnp.pad(jnp.stack([square, loss_part])[None], ((0, 7), (0, 126)))
-        owned, totals, edge = reduce_whole(firsts, pairs, extra, next(ids))
+        owned, totals, edge = reduce_whole(tuple(plan), lefts, rights, extra, next(ids))
         totals = totals[0, :2]
         edge = edge[::-1]
         edge = jnp.where(is_first, edge[..., :64], edge[..., 64:])
     else:
-        parts = []
-        for place in range(2):
-            parts.append(firsts[place])
-            parts += [product("fd,fn->dn", *pair) for pair in pairs[2 * place : 2 * place + 2]]
-        owned = [reduce_general(part) for part in parts]
+
+        def made(left_place, right_place):
+            return product("fd,fn->dn", lefts[left_place], rights[right_place])
+
+        owned = []
+        for first, *pairs in plan:
+            columns = jnp.concatenate([made(*source[:2]) for source in first], 1)
+            owned.append(join_first(columns[:, : 3 * D], columns[:, 3 * D :]))
+            owned += [made(*pair) for pair in pairs]
+        owned = [reduce_general(part) for part in owned]
         square = square + sum((jnp.sum(part * part) for part in owned))
         totals = lax.psum(jnp.stack([square, loss_part]), ("dp", "head"))
         edge = jnp.stack([owned[3], owned[0]])

time: 913 us -> 824 us (0.903)
  local copies, waits for them, and re-layouts: 89.6 us -> 35.8 us
  matrix products: 183 us -> 164 us
  Pallas kernels: 570 us -> 557 us
    pallas_call x8 -> x5, Pallas kernels: 68.6 us -> 35.1 us  [exchange(): pl.pallas_call(functools.partial(exchange_kernel, axis, count, swapped),...]
    unnamed x350 -> x163, local copies, waits for them, and re-layouts: 28 us -> 6.15 us
    pallas_call x2, Pallas kernels: 274 us -> 296 us  [the longest x1 155 us: gather_whole(): pl.pallas_call(functools.partial(gather_kernel, groups, firsts), out_shap...]
    dot_general x30 -> x23, matrix products: 112 us -> 99.8 us  [product(): return jnp.einsum(form, left, right, preferred_element_type=jnp.float32)]
    slice x17 -> x6, local copies, waits for them, and re-layouts: 14 us -> 2.55 us  [the longest x1 1.03 us: body(): cap_all = shared_all[:, 2 * clip_count:3 * clip_count, :D].reshape(-1, D)]
    concatenate x5 -> x2, local copies, waits for them, and re-layouts: 10.9 us -> 0.08 us  [body(): jnp.concatenate([jnp.zeros((clip_count, D)), table_bf.astype(jnp.float32)...]
where the time goes in v4:
time: 824 us; the launch traced here: 815 us
  Pallas kernels  557 us (68%)
  matrix products  164 us (20%)
  other arithmetic  48.2 us (6%)
  local copies, waits for them, and re-layouts  35.8 us (4%)
  between operations  9.35 us (1%)
    pallas_call x1, Pallas kernels, gather_whole(): pl.pallas_call(functools.partial(gather_kernel, groups, firsts), out_shap...  155 us
    pallas_call x1, Pallas kernels, reduce_whole(): pl.pallas_call(functools.partial(reduce_kernel, plan, len(lefts), len(rig...  140 us
    dot_general x23, matrix products, product(): return jnp.einsum(form, left, right, preferred_element_type=jnp.float32)  99.8 us
    dot_general x18, matrix products, near_product(): return jnp.einsum(form, left, right, precision=lax.Precision.HIGH)  60.1 us
    pallas_call x1, Pallas kernels, attend_back(): pl.pallas_call(attend_back_kernel, out_shape=jax.ShapeDtypeStruct((3 * ti...  54.2 us
    pallas_call x1, Pallas kernels, to_owner(): pl.pallas_call(functools.partial(to_owner_kernel, count), out_shape=jax.S...  44.1 us
    pallas_call x1, Pallas kernels, from_owner(): pl.pallas_call(functools.partial(from_owner_kernel, count, widths), out_s...  35.2 us
    pallas_call x5, Pallas kernels, exchange(): pl.pallas_call(functools.partial(exchange_kernel, axis, count, swapped),...  35.1 us

profile of v4, /device:TPU:11, one launch (start us, length us, event | category | flops | bytes accessed | tf_op | source)
XLA Modules:
  0.0 814.6 jit_solution(7729750334212481979)
XLA Ops:
  21.6 155.2 %gather_weights.1 = (bf16[2,2,2,96,1024]{4,3,2,1,0:T(8,128)(2,1)}, bf16[2,2,2,96,3072]{4,3,2,1,0:T(8,128)(2,1)}, bf16[2,2,2,96,3072]{4,3,2,1,0:T(8,128)(2,1)}, b...) custom-call(bf16[96,256]{1,0:T(8,128)(2,1)} %fusion.126.refs_0_, ...), custom_call_target="tpu_custom_call" | custom-call | tf_op jit(solution)/shard_map/gather_weights/pallas_call | solution.py:389
  183.2 4.3 convolution_convert_fusion.1.keys_ref.values_ref
  191.5 6.3 convolution_convert_fusion
  197.8 33.7 %attend.1 = (bf16[624,768]{1,0:T(8,128)(2,1)}, bf16[2,416,1152]{2,1,0:T(8,128)(2,1)}, bf16[4,208,768]{2,1,0:T(8,128)(2,1)}, f32[832,128]{1,0:T(8,128)}) custom-call(bf16[624,2304]{1,0:T(8,128)(2,1)} %bitcast.266), custom_call_target="tpu_custom_call" | custom-call | tf_op jit(solution)/shard_map/attend/pallas_call | solution.py:1144
  231.5 3.9 fusion.233
  236.4 7.0 multiply_convert_fusion.1
  243.5 4.5 fusion.232
  249.0 3.5 convolution_convert_fusion.4.query_ref
  252.5 9.6 %cross.1 = bf16[3,208,768]{2,1,0:T(8,128)(2,1)} custom-call(bf16[3,208,768]{2,1,0:T(8,128)(2,1)} %convolution_convert_fusion.4.query_ref, bf16[2,256,1536]{2,1,0:T(8,128)(2,1)} %convolution_convert_fusion.1.keys_ref.values_ref, bf16[2,256,1536]{2,1,0:T(8,128)(2,1)} %convolution_convert_fusion.1.keys_ref.values_ref, s32[2]{0:T(128)} %pad_add_fusion.len_ref), custom_call_target="tpu_custom_call" | custom-call | tf_op jit(solution)/shard_map/cross/pallas_call | solution.py:1291
  262.0 3.8 fusion.231
  266.7 10.1 %multiply_convert_fusion = (bf16[3,208,3072]{2,1,0:T(8,128)(2,1)S(1)}, f32[3,208,3072]{2,1,0:T(8,128)}) fusion(bf16[3,208,768]{2,1,0:T(8,128)(2,1)S(1)} %add_convert_fusion.1, bf16[768,3072,1]{1,0,2:T(8,128)(2,1)} %bitcast.333), kind=kOutput, calls=%fused_computation.20 | convolution fusion | flops 2961653760 | bytes 17178624 | tf_op jit(solution)/shard_map/fld,dn->fln/dot_general | solution.py:69
  276.9 4.5 fusion.230
  283.8 5.1 spread.3
  299.4 11.9 %fusion.7 = bf16[3,208,3072]{2,1,0:T(8,128)(2,1)S(1)} fusion(f32[3,208,3072]{2,1,0:T(8,128)} %get-tuple-element.240, bf16[3,208,768]{2,1,0:T(8,128)(2,1)S(1)} %get-tuple-element.181, bf16[768,3072,1]{1,0,2:T(8,128)(2,1)} %bitcast.337), kind=kOutput, calls=%fused_computation.15 | convolution fusion | flops 2990407680 | bytes 17178624 | tf_op jit(solution)/shard_map/fld,dn->fln/dot_general | solution.py:69
  311.3 3.4 multiply_reduce_fusion.11
  321.5 18.4 %cross_back.1 = (bf16[3,208,768]{2,1,0:T(8,128)(2,1)}, bf16[2,256,768]{2,1,0:T(8,128)(2,1)}, bf16[2,256,768]{2,1,0:T(8,128)(2,1)}) custom-call(bf16[3,208,768]{2,1,0:T(8,128)(2,1)} %convolution_convert_fusion.4.query_ref, bf16[2,256,1536]{2,1,0:T(8,128)(2,1)} %convolution_convert_fusion.1.keys_ref.values_ref, ...), custom_call_target="tpu_custom_call" | custom-call | tf_op jit(solution)/shard_map/cross_back/pallas_call | solution.py:1343
  345.7 11.0 %fusion.3 = bf16[3,208,3072]{2,1,0:T(8,128)(2,1)S(1)} fusion(f32[3,208,3072]{2,1,0:T(8,128)} %get-tuple-element.236, bf16[3,208,768]{2,1,0:T(8,128)(2,1)S(1)} %multiply_convert_fusion.3, bf16[768,3072,1]{1,0,2:T(8,128)(2,1)S(1)} %bitcast.332), kind=kOutput, calls=%fused_computation.11 | convolution fusion | flops 2990407680 | bytes 17178624 | tf_op jit(solution)/shard_map/fld,dn->fln/dot_general | solution.py:69
  362.7 3.5 convolution_convert_fusion.2
  366.2 54.2 %attend_back.1.refs_16_ = bf16[624,2304]{1,0:T(8,128)(2,1)} custom-call(bf16[2,416,1152]{2,1,0:T(8,128)(2,1)} %get-tuple-element.54.pair_all, bf16[4,208,768]{2,1,0:T(8,128)(2,1)} %get-tuple-element.55.quad_all, f32[832,128]{1,0:T(8,128)} %get-tuple-element.56.log_ref, bf16[624,768]{1,0:T(8,128)(2,1)} %bitcast.277), custom_call_target="tpu_custom_call" | custom-call | tf_op jit(solution)/shard_map/attend_back/pallas_call | solution.py:1244
  420.4 5.3 fusion.13
  432.5 6.9 swap.2
  441.3 11.5 %swap.3 = f32[8,62,128]{2,1,0:T(8,128)} custom-call(f32[8,62,128]{2,1,0:T(8,128)} %copy.128.x_ref), custom_call_target="tpu_custom_call" | custom-call | tf_op jit(solution)/shard_map/swap/pallas_call | solution.py:139
  455.7 5.4 spread.4
  462.5 6.3 spread.5
  474.7 140.4 %reduce_grads.1 = (f32[18,96,256]{2,1,0:T(8,128)}, f32[8,128]{1,0:T(8,128)}, f32[2,96,128]{2,1,0:T(8,128)}) custom-call(bf16[624,768]{1,0:T(8,128)(2,1)} %bitcast.256, bf16[624,768]{1,0:T(8,128)(2,1)} %bitcast.254, bf16[512,768]{1,0:T(8,128)(2,1)} %bitcast.265, bf16[624,768]{1,0:T(8,128)(2,1)} %bitcast.255, bf16[624,768]{1,0:T(8,128)(2,1)} %bitcast.264, ...), custom_call_target="tpu_custom_call" | custom-call | tf_op jit(solution)/shard_map/reduce_grads/pallas_call | solution.py:722
  631.5 44.1 %to_owner.1 = f32[8,96,768]{2,1,0:T(8,128)} custom-call(f32[2,96,640]{2,1,0:T(8,128)} %pad.35.refs_0_, f32[2,96,256]{2,1,0:T(8,128)} %pad.36.refs_1_, f32[2,96,768]{2,1,0:T(8,128)} %fusion.103.refs_2_, f32[2,96,768]{2,1,0:T(8,128)} %fusion.104.refs_3_), custom_call_target="tpu_custom_call" | custom-call | tf_op jit(solution)/shard_map/to_owner/pallas_call | solution.py:833
  677.5 31.5 %gram_sum.1 = f32[768,768]{1,0:T(8,128)} custom-call(f32[768,768]{1,0:T(8,128)} %bitcast.247), custom_call_target="tpu_custom_call" | custom-call | tf_op jit(solution)/shard_map/gram_sum/pallas_call | solution.py:943
  731.6 3.4 fusion.39
  744.8 3.7 fusion.33
  758.4 3.4 fusion.27
  768.3 4.1 divide_convert_fusion
  772.5 35.2 %from_owner.1 = bf16[8,96,768]{2,1,0:T(8,128)(2,1)} custom-call(bf16[8,96,768]{2,1,0:T(8,128)(2,1)} %bitcast.273), custom_call_target="tpu_custom_call" | custom-call | tf_op jit(solution)/shard_map/from_owner/pallas_call | solution.py:890
  (390 shorter events, 150.1 us)
Async XLA Ops:
  0.7 16.4 %copy-start.34 = (f32[2,96,576]{2,1,0:T(8,128)S(1)}, f32[2,96,576]{2,1,0:T(8,128)}, u32[]{:S(2)}) copy-start(f32[2,96,576]{2,1,0:T(8,128)} %param.31) | copy-start | bytes 1327108
  0.7 15.7 %copy-start.49 = (f32[3,208,20]{1,2,0:T(8,128)S(1)}, f32[3,208,20]{1,2,0:T(8,128)}, u32[]{:S(2)}) copy-start(f32[3,208,20]{1,2,0:T(8,128)} %param.25) | copy-start | bytes 149764
  0.7 15.7 %copy-start.50 = (f32[3,208,20]{1,2,0:T(8,128)S(1)}, f32[3,208,20]{1,2,0:T(8,128)}, u32[]{:S(2)}) copy-start(f32[3,208,20]{1,2,0:T(8,128)} %param.24) | copy-start | bytes 149764
  197.8 38.6 %slice-start = ((s8[4718592]{0:T(1024)(128)(4,1)}), s8[524288]{0:T(1024)(128)(4,1)S(1)}, s32[]{:S(2)}) async-start(s8[4718592]{0:T(1024)(128)(4,1)} %bitcast.321), calls=%async_computation | async-start | bytes 1048576
  248.1 14.0 %copy-start = (f32[3,208,768]{2,1,0:T(8,128)}, f32[3,208,768]{2,1,0:T(8,128)S(1)}, u32[]{:S(2)}) copy-start(f32[3,208,768]{2,1,0:T(8,128)S(1)} %get-tuple-element.167) | copy-start | bytes 5750788
  249.0 13.1 %copy-start.16 = (bf16[3,208,768]{2,1,0:T(8,128)(2,1)}, bf16[3,208,768]{2,1,0:T(8,128)(2,1)S(1)}, u32[]{:S(2)}) copy-start(bf16[3,208,768]{2,1,0:T(8,128)(2,1)S(1)} %add_convert_fusion.2) | copy-start | bytes 2875396
  265.8 11.0 %copy-start.4 = (f32[3,208,768]{2,1,0:T(8,128)}, f32[3,208,768]{2,1,0:T(8,128)S(1)}, u32[]{:S(2)}) copy-start(f32[3,208,768]{2,1,0:T(8,128)S(1)} %get-tuple-element.165) | copy-start | bytes 5750788
  299.0 12.3 %slice-start.8 = ((s8[4718592]{0:T(1024)(128)(4,1)}), s8[4194304]{0:T(1024)(128)(4,1)S(1)}, s32[]{:S(2)}) async-start(s8[4718592]{0:T(1024)(128)(4,1)} %bitcast.334), calls=%async_computation.8 | async-start | bytes 8388608
  299.4 11.9 %copy-start.25 = (bf16[3,208,768]{2,1,0:T(8,128)(2,1)}, bf16[3,208,768]{2,1,0:T(8,128)(2,1)S(1)}, u32[]{:S(2)}) copy-start(bf16[3,208,768]{2,1,0:T(8,128)(2,1)S(1)} %get-tuple-element.181) | copy-start | bytes 2875396
  299.4 11.9 %copy-start.5 = (f32[3,208,768]{2,1,0:T(8,128)S(1)}, f32[3,208,768]{2,1,0:T(8,128)}, u32[]{:S(2)}) copy-start(f32[3,208,768]{2,1,0:T(8,128)} %copy-done.4) | copy-start | bytes 5750788
  299.4 11.9 %slice-start.9 = ((s8[4718592]{0:T(1024)(128)(4,1)}), s8[524288]{0:T(1024)(128)(4,1)S(1)}, s32[]{:S(2)}) async-start(s8[4718592]{0:T(1024)(128)(4,1)} %bitcast.334), calls=%async_computation.9 | async-start | bytes 1048576
  321.5 18.4 %copy-start.1 = (f32[3,208,768]{2,1,0:T(8,128)S(1)}, f32[3,208,768]{2,1,0:T(8,128)}, u32[]{:S(2)}) copy-start(f32[3,208,768]{2,1,0:T(8,128)} %copy-done) | copy-start | bytes 5750788
  344.1 12.6 %slice-start.2 = ((s8[4718592]{0:T(1024)(128)(4,1)}), s8[4194304]{0:T(1024)(128)(4,1)S(1)}, s32[]{:S(2)}) async-start(s8[4718592]{0:T(1024)(128)(4,1)} %bitcast.324), calls=%async_computation.2 | async-start | bytes 8388608
  345.7 11.1 %copy-start.19 = (bf16[3,208,768]{2,1,0:T(8,128)(2,1)}, bf16[3,208,768]{2,1,0:T(8,128)(2,1)S(1)}, u32[]{:S(2)}) copy-start(bf16[3,208,768]{2,1,0:T(8,128)(2,1)S(1)} %multiply_convert_fusion.3) | copy-start | bytes 2875396
  345.7 11.1 %copy-start.7 = (f32[3,208,768]{2,1,0:T(8,128)S(1)}, f32[3,208,768]{2,1,0:T(8,128)}, u32[]{:S(2)}) copy-start(f32[3,208,768]{2,1,0:T(8,128)} %copy-done.6) | copy-start | bytes 5750788
  345.7 11.1 %slice-start.3 = ((s8[4718592]{0:T(1024)(128)(4,1)}), s8[524288]{0:T(1024)(128)(4,1)S(1)}, s32[]{:S(2)}) async-start(s8[4718592]{0:T(1024)(128)(4,1)} %bitcast.324), calls=%async_computation.3 | async-start | bytes 1048576
  362.7 57.7 %copy-start.20 = (bf16[3,208,768]{2,1,0:T(8,128)(2,1)}, bf16[3,208,768]{2,1,0:T(8,128)(2,1)S(1)}, u32[]{:S(2)}) copy-start(bf16[3,208,768]{2,1,0:T(8,128)(2,1)S(1)} %multiply_convert_fusion.2) | copy-start | bytes 2875396
  431.7 23.0 %copy-start.13 = (bf16[2,96,1152]{2,1,0:T(8,128)(2,1)S(1)}, bf16[2,96,1152]{2,1,0:T(8,128)(2,1)}, u32[]{:S(2)}) copy-start(bf16[2,96,1152]{2,1,0:T(8,128)(2,1)} %convert_element_type.146.refs_11_) | copy-start | bytes 1327108
  440.4 30.4 %copy-start.51 = (bf16[24,96,1]{1,0,2:T(8,128)(2,1)S(1)}, bf16[24,96,1]{1,0,2:T(8,128)(2,1)}, u32[]{:S(2)}) copy-start(bf16[24,96,1]{1,0,2:T(8,128)(2,1)} %reshape.555) | copy-start | bytes 13828
  474.7 142.8 %copy-start.52 = (f32[2,96,5]{1,0,2:T(2,128)S(1)}, f32[2,96,5]{1,0,2:T(2,128)}, u32[]{:S(2)}) copy-start(f32[2,96,5]{1,0,2:T(2,128)} %param.37) | copy-start | bytes 11524
  474.7 142.8 %copy-start.54 = (f32[2,96,5]{1,0,2:T(2,128)S(1)}, f32[2,96,5]{1,0,2:T(2,128)}, u32[]{:S(2)}) copy-start(f32[2,96,5]{1,0,2:T(2,128)} %param.47) | copy-start | bytes 11524
  474.7 142.8 %copy-start.55 = (f32[2,96,5]{1,0,2:T(2,128)S(1)}, f32[2,96,5]{1,0,2:T(2,128)}, u32[]{:S(2)}) copy-start(f32[2,96,5]{1,0,2:T(2,128)} %param.46) | copy-start | bytes 11524
  474.7 143.5 %copy-start.45 = (f32[96,192]{1,0:T(8,128)S(1)}, f32[96,192]{1,0:T(8,128)}, u32[]{:S(2)}) copy-start(f32[96,192]{1,0:T(8,128)} %param.36) | copy-start | bytes 221188
  474.7 143.5 %copy-start.47 = (f32[96,192]{1,0:T(8,128)S(1)}, f32[96,192]{1,0:T(8,128)}, u32[]{:S(2)}) copy-start(f32[96,192]{1,0:T(8,128)} %param.45) | copy-start | bytes 221188
  474.7 143.4 %copy-start.48 = (f32[96,192]{1,0:T(8,128)S(1)}, f32[96,192]{1,0:T(8,128)}, u32[]{:S(2)}) copy-start(f32[96,192]{1,0:T(8,128)} %param.44) | copy-start | bytes 221188
  629.6 46.0 %copy-start.43 = (f32[2,96,192]{2,1,0:T(8,128)}, f32[2,96,192]{2,1,0:T(8,128)S(1)}, u32[]{:S(2)}) copy-start(f32[2,96,192]{2,1,0:T(8,128)S(1)} %fusion.118) | copy-start | bytes 442372
  630.6 45.0 %copy-start.33 = (f32[2,96,576]{2,1,0:T(8,128)}, f32[2,96,576]{2,1,0:T(8,128)S(1)}, u32[]{:S(2)}) copy-start(f32[2,96,576]{2,1,0:T(8,128)S(1)} %fusion.108) | copy-start | bytes 1327108
  631.5 44.1 %copy-start.27 = (f32[2,96,1152]{2,1,0:T(8,128)S(1)}, f32[2,96,1152]{2,1,0:T(8,128)}, u32[]{:S(2)}) copy-start(f32[2,96,1152]{2,1,0:T(8,128)} %param.35) | copy-start | bytes 2654212
  631.5 44.1 %copy-start.40 = (f32[2,96,1152]{2,1,0:T(8,128)S(1)}, f32[2,96,1152]{2,1,0:T(8,128)}, u32[]{:S(2)}) copy-start(f32[2,96,1152]{2,1,0:T(8,128)} %param.43) | copy-start | bytes 2654212
  631.5 44.1 %copy-start.41 = (f32[2,96,1152]{2,1,0:T(8,128)S(1)}, f32[2,96,1152]{2,1,0:T(8,128)}, u32[]{:S(2)}) copy-start(f32[2,96,1152]{2,1,0:T(8,128)} %param.42) | copy-start | bytes 2654212
  772.5 36.1 %copy-start.42 = (f32[2,96,192]{2,1,0:T(8,128)S(1)}, f32[2,96,192]{2,1,0:T(8,128)}, u32[]{:S(2)}) copy-start(f32[2,96,192]{2,1,0:T(8,128)} %param.32) | copy-start | bytes 442372
  772.5 37.9 %copy-start.35 = (f32[2,96,576]{2,1,0:T(8,128)S(1)}, f32[2,96,576]{2,1,0:T(8,128)}, u32[]{:S(2)}) copy-start(f32[2,96,576]{2,1,0:T(8,128)} %param.31) | copy-start | bytes 1327108
  (37 other events, 156.4 us)

commit v5 on v4

--- a/solution.py
+++ b/solution.py
@@ -320,7 +320,7 @@
             for copy in shares:
                 copy.start()
             shared_out[d] = mine[...]
-        if turn == 9:
+        if turn == 11:
             for copy in shares:
                 copy.wait()
             count, lines, width = shared_out.shape
@@ -337,7 +337,7 @@
             for copy in swaps:
                 copy.start()
             parts_got[d] = parts[d]
-        if turn == 11:
+        if turn == 15:
             for copy in swaps:
                 copy.wait()
             total = parts_got[0]
@@ -346,7 +346,7 @@
             mods_out[h] = total
             for copy in spreads:
                 copy.start()
-        if turn == 13:
+        if turn == 19:
             for copy in spreads + latents:
                 copy.wait()
 
@@ -431,10 +431,14 @@
 
 def reduce_kernel(plan, lefts, rights, *refs):
     left_refs, right_refs = refs[:lefts], refs[lefts : lefts + rights]
-    extra_ref, out_ref, total_ref, edge_ref = refs[lefts + rights : lefts + rights + 4]
+    (extra_ref, mod_ref, io_ref, signal_ref, slope_ref, table_ref, ada_ref, out_ref, total_ref,
+     edge_ref, ada_out, time_out, io_out) = refs[lefts + rights : lefts + rights + 13]
     (made, near, left, left_t, right, send_a, send_b, got_a, got_b, keep_a, keep_b,
-     mine, head_got, data_got, near_send, near_recv, hop_send, hop_recv, left_sem,
-     right_sem, edge_send, edge_recv, sum_send, sum_recv) = refs[lefts + rights + 4 :]
+     mine, head_got, data_got, mod_got, io_got, mod_sum, io_sum, mod_all, io_all, part, part_got,
+     inner, inner_all, near_send, near_recv, hop_send, hop_recv, left_sem,
+     right_sem, edge_send, edge_recv, sum_send, sum_recv, small_send, small_recv) = refs[
+        lefts + rights + 13 :
+    ]
     layers = len(plan)
     per_group = D // PIECE_COLS
     pieces = 3 * layers * per_group
@@ -623,6 +627,87 @@
                 slot
             ].astype(jnp.float32)
 
+    def small(place, source, target, peer):
+        return pltpu.make_async_remote_copy(
+            src_ref=source,
+            dst_ref=target,
+            send_sem=small_send.at[place],
+            recv_sem=small_recv.at[place],
+            device_id=peer,
+            device_id_type=MESH,
+        )
+
+    heads = [(across[other - 1], h ^ other, other - 1) for other in (1, 2, 3)]
+    datas = [(across[2 + other], d ^ other, other - 1) for other in range(1, 8)]
+    mod_swaps = [small(at, mod_ref.at[place], mod_got.at[h], peer) for peer, place, at in heads]
+    io_swaps = [small(3 + at, io_ref.at[place], io_got.at[h], peer) for peer, place, at in heads]
+    mod_spreads = [small(6 + at, mod_sum, mod_all.at[d], peer) for peer, _, at in datas]
+    io_moves = [small(13 + at, io_sum.at[place], io_all.at[d], peer) for peer, place, at in datas]
+    part_spreads = [small(20 + at, part, part_got.at[h], peer) for peer, _, at in heads]
+    inner_spreads = [small(23 + at, inner, inner_all.at[d], peer) for peer, _, at in datas]
+
+    def total_of(ref):
+        total = ref[0]
+        for place in range(1, ref.shape[0]):
+            total = total + ref[place]
+        return total
+
+    def exact(left, right, contract):
+        return lax.dot_general(
+            left, right, (contract, ((), ())), precision=HIGHEST_PRECISION,
+            preferred_element_type=jnp.float32,
+        )
+
+    def condition(turn):
+        @pl.when(turn == 2)
+        def _():
+            for copy in mod_swaps + io_swaps:
+                copy.wait()
+            mod_sum[...] = total_of(mod_got)
+            io_sum[...] = total_of(io_got)
+            for copy in mod_spreads + io_moves:
+                copy.start()
+            mod_all[d] = mod_sum[...]
+            io_all[d] = io_sum[d]
+
+        @pl.when(turn == 6)
+        def _():
+            for copy in mod_spreads + io_moves:
+                copy.wait()
+            io_out[...] = total_of(io_all)
+            columns = ada_ref.shape[2]
+            total = jnp.zeros(part.shape, jnp.float32)
+            for layer in range(2):
+                grads = mod_all[:, :, layer * columns : (layer + 1) * columns].reshape(
+                    part.shape[0], columns
+                )
+                ada_out[layer] = exact(signal_ref[...], grads, ((0,), (0,)))
+                total = total + exact(grads, ada_ref[layer].astype(jnp.float32), ((1,), (1,)))
+            part[...] = total
+            for copy in part_spreads:
+                copy.start()
+            part_got[h] = total
+
+        @pl.when(turn == 10)
+        def _():
+            for copy in part_spreads:
+                copy.wait()
+            inner[...] = total_of(part_got) * slope_ref[...]
+            for copy in inner_spreads:
+                copy.start()
+            inner_all[d] = inner[...]
+
+        @pl.when(turn == 14)
+        def _():
+            for copy in inner_spreads:
+                copy.wait()
+            for place in range(2):
+                time_out[place] = exact(table_ref[...], inner_all[2 * h + place], ((0,), (0,)))
+
+    for copy in mod_swaps + io_swaps:
+        copy.start()
+    mod_got[h] = mod_ref[h]
+    io_got[h] = io_ref[h]
     for place in range(lefts):
         left_copy(place).start()
     fetch(0)
@@ -654,6 +739,8 @@
         @pl.when(turn + 2 < pieces)
         def _():
             bring(turn + 2)
+
+        condition(turn)
 
     edges = []
     for layer in range(layers):
@@ -675,7 +762,10 @@
         squares = squares + out_ref[piece] * out_ref[piece]
     row = lax.broadcasted_iota(jnp.int32, (8, 128), 0)
     column = lax.broadcasted_iota(jnp.int32, (8, 128), 1)
-    mine[0] = extra_ref[...] + jnp.where((row == 0) & (column == 0), jnp.sum(squares), 0.0)
+    square = jnp.sum(squares)
+    for ref in (ada_out, time_out, io_out):
+        square = square + jnp.sum(ref[...] * ref[...])
+    mine[0] = extra_ref[...] + jnp.where((row == 0) & (column == 0), square, 0.0)
     for phase, (got, me, count) in enumerate(((head_got, h, 4), (data_got, d, 8))):
         copies = []
         for other in range(1, count):
@@ -705,7 +795,7 @@
         copy.wait()
 
 
-def reduce_whole(plan, lefts, rights, extra, collective_id):
+def reduce_whole(plan, lefts, rights, smalls, collective_id):
     layers = len(plan)
     frames = lefts[0].shape[0]
     rows = D // 8
@@ -719,15 +809,19 @@
     bottom_rows = rows - ROWS_A
     blocks = (2, 2, 2, rows, PIECE_COLS)
     low = jnp.bfloat16
-    summed, totals, edges = pl.pallas_call(
+    mod, io, signal, ada = smalls[1], smalls[2], smalls[3], smalls[6]
+    summed, *others = pl.pallas_call(
         functools.partial(reduce_kernel, plan, len(lefts), len(rights)),
         out_shape=[
             jax.ShapeDtypeStruct((pieces, rows, PIECE_COLS), jnp.float32),
             jax.ShapeDtypeStruct((8, 128), jnp.float32),
             jax.ShapeDtypeStruct((layers, rows, 128), jnp.float32),
+            jax.ShapeDtypeStruct(ada.shape, jnp.float32),
+            jax.ShapeDtypeStruct((2, rows, rows), jnp.float32),
+            jax.ShapeDtypeStruct(io.shape[2:], jnp.float32),
         ],
-        in_specs=[anywhere()] * (len(lefts) + len(rights)) + [vmem()],
-        out_specs=[vmem()] * 3,
+        in_specs=[anywhere()] * (len(lefts) + len(rights)) + [vmem()] * 7,
+        out_specs=[vmem()] * 6,
         scratch_shapes=[
             pltpu.VMEM((SLOTS, 2, 2) + blocks, jnp.float32),
             pltpu.VMEM((SLOTS, 2) + blocks, jnp.float32),
@@ -743,6 +837,16 @@
             pltpu.VMEM((2, 8, 128), jnp.float32),
             pltpu.VMEM((4, 8, 128), jnp.float32),
             pltpu.VMEM((8, 8, 128), jnp.float32),
+            pltpu.VMEM(mod.shape, jnp.float32),
+            pltpu.VMEM(io.shape, jnp.float32),
+            pltpu.VMEM(mod.shape[1:], jnp.float32),
+            pltpu.VMEM(io.shape[1:], jnp.float32),
+            pltpu.VMEM((8,) + mod.shape[1:], jnp.float32),
+            pltpu.VMEM(io.shape[1:], jnp.float32),
+            pltpu.VMEM(signal.shape, jnp.float32),
+            pltpu.VMEM((4,) + signal.shape, jnp.float32),
+            pltpu.VMEM(signal.shape, jnp.float32),
+            pltpu.VMEM((8,) + signal.shape, jnp.float32),
             pltpu.SemaphoreType.DMA((SLOTS, 2)),
             pltpu.SemaphoreType.DMA((SLOTS, 2)),
             pltpu.SemaphoreType.DMA((4, 2, SLOTS)),
@@ -753,12 +857,14 @@
             pltpu.SemaphoreType.DMA((layers,)),
             pltpu.SemaphoreType.DMA((10,)),
             pltpu.SemaphoreType.DMA((10,)),
+            pltpu.SemaphoreType.DMA((30,)),
+            pltpu.SemaphoreType.DMA((30,)),
         ],
         compiler_params=comm_params(collective_id),
         name="reduce_grads",
-    )(*lefts, *rights, extra)
+    )(*lefts, *rights, *smalls)
     summed = summed.reshape(3 * layers, per_group, rows, PIECE_COLS).transpose(0, 2, 1, 3)
-    return list(summed.reshape(3 * layers, rows, D)), totals, edges
+    return list(summed.reshape(3 * layers, rows, D)), *others
 
 
 def reduce_general(part):
@@ -1078,59 +1184,67 @@
             rows_ref[shared, at + 256 : at + 384] = right[:, base + 128 : base + 256]
 
 
+def row_half(half):
+    row = lax.broadcasted_iota(jnp.int32, (128, 1), 0)
+    return (row // 64) == half
+
+
+CHUNKS = ((0, 384), (384, 832))
+
+
+def probabilities(scores):
+    top = jnp.max(scores, 0, keepdims=True)
+    exponent = jnp.exp(scores - top)
+    total = jnp.sum(exponent, 0, keepdims=True)
+    return exponent * (1.0 / total), top + jnp.log(total)
+
+
 def attend_kernel(rows_ref, mixed_ref, pair_all, quad_all, log_ref, pair_out, quad_out, quad_got,
-                  send_sem, recv_sem):
+                  joined, send_sem, recv_sem):
     h = lax.axis_index("head")
     sems = (send_sem, recv_sem)
     greet([{"head": h ^ other} for other in (1, 2, 3)])
     pair_copies, quad_copies = bring_heads(h, rows_ref, pair_all, quad_all, 3, sems)
     tile = quad_all.shape[1]
     length = 4 * tile
-    lane = lax.broadcasted_iota(jnp.int32, (1, 128), 1)
-
-    def one_head(query, keys, values, mask):
-        scores = dot_nt(jnp.where(mask, query, 0) * 0.125, keys)
-        top = jnp.max(scores, -1, keepdims=True)
-        exponent = jnp.exp(scores - top)
-        total = jnp.sum(exponent, -1, keepdims=True)
-        probability = to_bf16(exponent * (1.0 / total))
-        return dot_nn(probability, jnp.where(mask, values, 0)), top + jnp.log(total)
+
+    def heads(query, keys, values, members):
+        values_t = values.T
+        for start, stop in CHUNKS:
+            mixed = jnp.zeros((128, stop - start), jnp.float32)
+            for half, log_row in members:
+                chunk = jnp.where(half_mask(half), query[start:stop], 0) * 0.125
+                probability, logs = probabilities(dot_nt(keys, chunk))
+                mixed = mixed + dot_nn(
+                    jnp.where(row_half(half), values_t, 0), to_bf16(probability)
+                )
+                log_ref[log_row : log_row + 1, start:stop] = logs
+            joined[start:stop, :] = to_bf16(mixed.T)
 
     log_ref[...] = jnp.zeros_like(log_ref)
     quad_out[...] = jnp.zeros_like(quad_out)
     for copy in pair_copies:
         copy.wait()
     for pair in range(3):
-        keys = pair_all[:, :, HALF + pair * 128 : HALF + pair * 128 + 128].reshape(length, 128)
-        values = pair_all[:, :, 2 * HALF + pair * 128 : 2 * HALF + pair * 128 + 128].reshape(
-            length, 128
-        )
-        for row in range(4):
-            rows = slice((row % 2) * tile, (row % 2 + 1) * tile)
-            out_rows = slice(row * tile, (row + 1) * tile)
-            query = pair_all[row // 2, rows, pair * 128 : pair * 128 + 128]
-            mixed = jnp.zeros((tile, 128), jnp.float32)
-            logs = log_ref[out_rows, :]
-            for half in range(2):
-                part, log_total = one_head(query, keys, values, half_mask(half))
-                mixed = mixed + part
-                logs = jnp.where(lane == 2 * pair + half, log_total, logs)
-            log_ref[out_rows, :] = logs
-            pair_out[row // 2, rows, pair * 128 : pair * 128 + 128] = to_bf16(mixed)
+        query, keys, values = (
+            pair_all[:, :, part * HALF + pair * 128 : part * HALF + pair * 128 + 128].reshape(
+                length, 128
+            )
+            for part in range(3)
+        )
+        heads(query, keys, values, ((0, 2 * pair), (1, 2 * pair + 1)))
+        pair_out[:, :, pair * 128 : pair * 128 + 128] = joined[...].reshape(2, 2 * tile, 128)
     back = return_pair(h, pair_out, mixed_ref, 1, sems)
     for copy in quad_copies:
         copy.wait()
     for member in range(3):
         place = h % 2 + member
-        mask = half_mask(place % 2)
         at = (place // 2) * 128
-        keys = quad_all[:, :, lanes(WIDE + at, 128)].reshape(length, 128)
-        values = quad_all[:, :, lanes(2 * WIDE + at, 128)].reshape(length, 128)
-        for row in range(4):
-            out_rows = slice(row * tile, (row + 1) * tile)
-            mixed, log_total = one_head(quad_all[row, :, lanes(at, 128)], keys, values, mask)
-            log_ref[out_rows, :] = jnp.where(lane == 6 + member, log_total, log_ref[out_rows, :])
-            quad_out[row, :, lanes(at, 128)] += to_bf16(mixed)
+        query, keys, values = (
+            quad_all[:, :, lanes(part * WIDE + at, 128)].reshape(length, 128) for part in range(3)
+        )
+        heads(query, keys, values, ((place % 2, 6 + member),))
+        quad_out[:, :, lanes(at, 128)] += joined[...].reshape(4, tile, 128)
     back_quad = return_quad(h, quad_out, quad_got, sems)
     for copy in back + back_quad:
         copy.wait()
@@ -1147,7 +1261,7 @@
             jax.ShapeDtypeStruct((frames, D), low),
             jax.ShapeDtypeStruct((2, 2 * tile, 3 * HALF), low),
             jax.ShapeDtypeStruct((4, tile, 3 * WIDE), low),
-            jax.ShapeDtypeStruct((4 * tile, 128), jnp.float32),
+            jax.ShapeDtypeStruct((16, 4 * tile), jnp.float32),
         ],
         in_specs=[vmem()],
         out_specs=[vmem()] * 4,
@@ -1155,6 +1269,7 @@
             pltpu.VMEM((2, 2 * tile, HALF), low),
             pltpu.VMEM((4, tile, WIDE), low),
             pltpu.VMEM((4, tile, WIDE), low),
+            pltpu.VMEM((4 * tile, 128), low),
             pltpu.SemaphoreType.DMA((18,)),
             pltpu.SemaphoreType.DMA((18,)),
         ],
@@ -1164,74 +1279,65 @@
 
 
 def attend_back_kernel(pair_all, quad_all, log_ref, grad_ref, rows_ref, pair_mixed, quad_mixed,
-                       pair_out, quad_out, quad_got, grad_keys, grad_values, send_sem, recv_sem):
+                       pair_out, quad_out, quad_got, grad_keys, grad_values, grads, send_sem,
+                       recv_sem):
     h = lax.axis_index("head")
     sems = (send_sem, recv_sem)
     greet([{"head": h ^ other} for other in (1, 2, 3)])
     pair_copies, quad_copies = bring_heads(h, grad_ref, pair_mixed, quad_mixed, 1, sems)
     tile = quad_all.shape[1]
     length = 4 * tile
-    lane = lax.broadcasted_iota(jnp.int32, (1, 128), 1)
-
-    def one_head(query, keys, values, grad_out, mask, out_rows, log_lane):
-        log_total = jnp.sum(
-            jnp.where(lane == log_lane, log_ref[out_rows, :], 0.0), -1, keepdims=True
-        )
-        query = jnp.where(mask, query, 0) * 0.125
-        grad_out = jnp.where(mask, grad_out, 0)
-        probability = jnp.exp(dot_nt(query, keys) - log_total)
-        grad_prob = dot_nt(grad_out, values)
-        mean = jnp.sum(probability * grad_prob, -1, keepdims=True)
-        grad_scores = to_bf16(probability * (grad_prob - mean))
-        grad_keys[...] += dot_tn(grad_scores, query)
-        grad_values[...] += dot_tn(to_bf16(probability), grad_out)
-        return dot_nn(grad_scores, jnp.where(mask, keys, 0)) * 0.125
+
+    def heads(query, keys, values, grad_out, members):
+        keys_t = keys.T
+        grad_keys[...] = jnp.zeros_like(grad_keys)
+        grad_values[...] = jnp.zeros_like(grad_values)
+        for start, stop in CHUNKS:
+            grad_query = jnp.zeros((128, stop - start), jnp.float32)
+            for half, log_row in members:
+                mask = half_mask(half)
+                chunk = jnp.where(mask, query[start:stop], 0) * 0.125
+                grad_chunk = jnp.where(mask, grad_out[start:stop], 0)
+                probability = jnp.exp(
+                    dot_nt(keys, chunk) - log_ref[log_row : log_row + 1, start:stop]
+                )
+                grad_prob = dot_nt(values, grad_chunk)
+                mean = jnp.sum(probability * grad_prob, 0, keepdims=True)
+                grad_scores = to_bf16(probability * (grad_prob - mean))
+                grad_keys[...] += dot_nn(grad_scores, chunk)
+                grad_values[...] += dot_nn(to_bf16(probability), grad_chunk)
+                grad_query = grad_query + dot_nn(
+                    jnp.where(row_half(half), keys_t, 0), grad_scores
+                )
+            grads[0, start:stop, :] = to_bf16(grad_query.T * 0.125)
+        grads[1] = to_bf16(grad_keys[...])
+        grads[2] = to_bf16(grad_values[...])
 
     quad_out[...] = jnp.zeros_like(quad_out)
     for copy in pair_copies:
         copy.wait()
     for pair in range(3):
         at = [part * HALF + pair * 128 for part in range(3)]
-        keys = pair_all[:, :, at[1] : at[1] + 128].reshape(length, 128)
-        values = pair_all[:, :, at[2] : at[2] + 128].reshape(length, 128)
-        grad_keys[...] = jnp.zeros_like(grad_keys)
-        grad_values[...] = jnp.zeros_like(grad_values)
-        for row in range(4):
-            rows = slice((row % 2) * tile, (row % 2 + 1) * tile)
-            query = pair_all[row // 2, rows, at[0] : at[0] + 128]
-            grad_out = pair_mixed[row // 2, rows, at[0] : at[0] + 128]
-            grad_query = jnp.zeros((tile, 128), jnp.float32)
-            for half in range(2):
-                grad_query = grad_query + one_head(
-                    query, keys, values, grad_out, half_mask(half),
-                    slice(row * tile, (row + 1) * tile), 2 * pair + half,
-                )
-            pair_out[row // 2, rows, at[0] : at[0] + 128] = to_bf16(grad_query)
-        for part, total in ((1, grad_keys), (2, grad_values)):
-            pair_out[:, :, at[part] : at[part] + 128] = to_bf16(total[...]).reshape(
-                2, 2 * tile, 128
-            )
+        query, keys, values = (
+            pair_all[:, :, start : start + 128].reshape(length, 128) for start in at
+        )
+        grad_out = pair_mixed[:, :, at[0] : at[0] + 128].reshape(length, 128)
+        heads(query, keys, values, grad_out, ((0, 2 * pair), (1, 2 * pair + 1)))
+        for part in range(3):
+            pair_out[:, :, at[part] : at[part] + 128] = grads[part].reshape(2, 2 * tile, 128)
     back = return_pair(h, pair_out, rows_ref, 3, sems)
     for copy in quad_copies:
         copy.wait()
     for member in range(3):
         place = h % 2 + member
-        mask = half_mask(place % 2)
         at = (place // 2) * 128
-        keys = quad_all[:, :, lanes(WIDE + at, 128)].reshape(length, 128)
-        values = quad_all[:, :, lanes(2 * WIDE + at, 128)].reshape(length, 128)
-        grad_keys[...] = jnp.zeros_like(grad_keys)
-        grad_values[...] = jnp.zeros_like(grad_values)
-        for row in range(4):
-            grad_query = one_head(
-                quad_all[row, :, lanes(at, 128)], keys, values, quad_mixed[row, :, lanes(at, 128)],
-                mask, slice(row * tile, (row + 1) * tile), 6 + member,
-            )
-            quad_out[row, :, lanes(at, 128)] += to_bf16(grad_query)
-        for part, total in ((1, grad_keys), (2, grad_values)):
-            quad_out[:, :, lanes(part * WIDE + at, 128)] += to_bf16(total[...]).reshape(
-                4, tile, 128
-            )
+        query, keys, values = (
+            quad_all[:, :, lanes(part * WIDE + at, 128)].reshape(length, 128) for part in range(3)
+        )
+        grad_out = quad_mixed[:, :, lanes(at, 128)].reshape(length, 128)
+        heads(query, keys, values, grad_out, ((place % 2, 6 + member),))
+        for part in range(3):
+            quad_out[:, :, lanes(part * WIDE + at, 128)] += grads[part].reshape(4, tile, 128)
     back_quad = return_quad(h, quad_out, quad_got, sems)
     for copy in back + back_quad:
         copy.wait()
@@ -1254,6 +1360,7 @@
             pltpu.VMEM(quad_all.shape, low),
             pltpu.VMEM((4 * tile, 128), jnp.float32),
             pltpu.VMEM((4 * tile, 128), jnp.float32),
+            pltpu.VMEM((3, 4 * tile, 128), low),
             pltpu.SemaphoreType.DMA((18,)),
             pltpu.SemaphoreType.DMA((18,)),
         ],
@@ -1262,26 +1369,27 @@
     )(pair_all, quad_all, logs, grad_mixed)
 
 
-def masked_scores(query_half, keys, keep):
-    return jnp.where(keep, dot_nt(query_half, keys) * 0.125, -1e30)
+def cross_frames(clip, tile):
+    return slice(2 * clip, 2 + clip), (2 - clip) * tile
+
+
+def masked_scores(keys, query_half, length):
+    token = lax.broadcasted_iota(jnp.int32, (keys.shape[0], 1), 0)
+    return jnp.where(token < length, dot_nt(keys, query_half), -1e30)
 
 
 def cross_kernel(query_ref, keys_ref, values_ref, len_ref, out_ref):
     tile = query_ref.shape[1]
-    tokens = keys_ref.shape[1]
-    token = lax.broadcasted_iota(jnp.int32, (1, tokens), 1)
-    for row in range(3):
-        clip = row // 2
-        keep = token < len_ref[clip]
-        keys, values = keys_ref[clip], values_ref[clip]
-        mixed = jnp.zeros((tile, 128), jnp.float32)
+    for clip in range(2):
+        tiles, count = cross_frames(clip, tile)
+        query = query_ref[tiles].reshape(count, 128)
+        values_t = values_ref[clip].T
+        mixed = jnp.zeros((128, count), jnp.float32)
         for half in range(2):
-            mask = half_mask(half)
-            scores = masked_scores(jnp.where(mask, query_ref[row], 0), keys, keep)
-            exponent = jnp.exp(scores - jnp.max(scores, -1, keepdims=True))
-            probability = to_bf16(exponent / jnp.sum(exponent, -1, keepdims=True))
-            mixed = mixed + dot_nn(probability, jnp.where(mask, values, 0))
-        out_ref[row] = to_bf16(mixed)
+            chunk = jnp.where(half_mask(half), query, 0) * 0.125
+            probability, _ = probabilities(masked_scores(keys_ref[clip], chunk, len_ref[clip]))
+            mixed = mixed + dot_nn(jnp.where(row_half(half), values_t, 0), to_bf16(probability))
+        out_ref[tiles] = to_bf16(mixed.T).reshape(2 - clip, tile, 128)
 
 
 def cross(query, pair_kv, lengths):
@@ -1308,29 +1416,28 @@
                       grad_keys_ref, grad_values_ref):
     tile = query_ref.shape[1]
     tokens = keys_ref.shape[1]
-    token = lax.broadcasted_iota(jnp.int32, (1, tokens), 1)
     for clip in range(2):
-        keep = token < len_ref[clip]
+        tiles, count = cross_frames(clip, tile)
         keys, values = keys_ref[clip], values_ref[clip]
+        query = query_ref[tiles].reshape(count, 128)
+        grad = grad_ref[tiles].reshape(count, 128)
+        keys_t = keys.T
         grad_keys = jnp.zeros((tokens, 128), jnp.float32)
         grad_values = jnp.zeros((tokens, 128), jnp.float32)
-        for row in range(2 * clip, 2 + clip):
-            grad_query = jnp.zeros((tile, 128), jnp.float32)
-            for half in range(2):
-                mask = half_mask(half)
-                query_half = jnp.where(mask, query_ref[row], 0)
-                grad_half = jnp.where(mask, grad_ref[row], 0)
-                scores = masked_scores(query_half, keys, keep)
-                exponent = jnp.exp(scores - jnp.max(scores, -1, keepdims=True))
-                probability = exponent / jnp.sum(exponent, -1, keepdims=True)
-                grad_prob = dot_nt(grad_half, values)
-                mean = jnp.sum(probability * grad_prob, -1, keepdims=True)
-                grad_scores = to_bf16(probability * (grad_prob - mean))
-                grad_query = grad_query + dot_nn(grad_scores, jnp.where(mask, keys, 0))
-                grad_keys = grad_keys + dot_tn(grad_scores, query_half)
-                grad_values = grad_values + dot_tn(to_bf16(probability), grad_half)
-            grad_query_ref[row] = to_bf16(grad_query * 0.125)
-        grad_keys_ref[clip] = to_bf16(grad_keys * 0.125)
+        grad_query = jnp.zeros((128, count), jnp.float32)
+        for half in range(2):
+            mask = half_mask(half)
+            chunk = jnp.where(mask, query, 0) * 0.125
+            grad_half = jnp.where(mask, grad, 0)
+            probability, _ = probabilities(masked_scores(keys, chunk, len_ref[clip]))
+            grad_prob = dot_nt(values, grad_half)
+            mean = jnp.sum(probability * grad_prob, 0, keepdims=True)
+            grad_scores = to_bf16(probability * (grad_prob - mean))
+            grad_keys = grad_keys + dot_nn(grad_scores, chunk)
+            grad_values = grad_values + dot_nn(to_bf16(probability), grad_half)
+            grad_query = grad_query + dot_nn(jnp.where(row_half(half), keys_t, 0), grad_scores)
+        grad_query_ref[tiles] = to_bf16(grad_query.T * 0.125).reshape(2 - clip, tile, 128)
+        grad_keys_ref[clip] = to_bf16(grad_keys)
         grad_values_ref[clip] = to_bf16(grad_values)
 
 
@@ -1691,41 +1798,55 @@
     mod_size = clip_count * 2 * ada_cols
     io_size = rows_own * 2 * io_cols
     mod_grad = by_clip(jnp.stack(mod_grads, 1)).reshape(clip_count, 2, head_count, ada_cols)
-    mod_grad = mod_grad.transpose(2, 0, 1, 3).reshape(head_count, mod_size)
+    mod_grad = mod_grad.transpose(2, 0, 1, 3).reshape(head_count, clip_count, 2 * ada_cols)
     io_part = (
         jnp.stack([in_grad, fin_grad])
         .reshape(2, data_count, rows_own, head_count, io_cols)
         .transpose(3, 1, 0, 2, 4)
-        .reshape(head_count, data_count * io_size)
-    )
-    packed = jnp.concatenate([mod_grad, io_part], 1).reshape(head_count, -1, 128)
-    packed = jnp.sum(swap(packed, "head"), 0).reshape(-1)
-    mod_grad = jnp.broadcast_to(packed[:mod_size], (data_count, mod_size))
-    lines = -(-(mod_size + io_size) // 128)
-    packed = jnp.concatenate([mod_grad, packed[mod_size:].reshape(data_count, io_size)], 1)
-    packed = jnp.pad(packed, ((0, 0), (0, lines * 128 - mod_size - io_size)))
-    packed = swap(packed.reshape(data_count, lines, 128), "dp").reshape(data_count, -1)
-    mod_grad = packed[:, :mod_size].reshape(-1, 2, ada_cols)
-    io_grad = jnp.sum(packed[:, mod_size : mod_size + io_size], 0).reshape(2, rows_own, io_cols)
-    ada_grad = exact_product("fd,fln->ldn", signal_own.astype(jnp.float32), mod_grad)
-    grad_signal = exact_product("fln,ldn->fd", mod_grad, ada_bf.astype(jnp.float32))
-    grad_signal = jnp.sum(spread(grad_signal, "head"), 0)
+        .reshape(head_count, data_count, io_size)
+    )
     signal_own_value, signal_back = jax.vjp(double_silu, hidden_own)
-    grad_cond = spread(signal_back(grad_signal)[0], "dp").transpose(1, 0, 2).reshape(-1, D)
-    time_grad = exact_product(
-        "fd,fn->dn",
-        table_own,
-        lax.dynamic_slice_in_dim(grad_cond, h * time_cols, time_cols, 1),
-    )
-
-    square = sum((jnp.sum(grad * grad) for grad in (ada_grad, time_grad, io_grad)))
     if linked:
-        extra = jnp.pad(jnp.stack([square, loss_part])[None], ((0, 7), (0, 126)))
-        owned, totals, edge = reduce_whole(tuple(plan), lefts, rights, extra, next(ids))
+
+        def padded_clips(values):
+            values = values.reshape(data_count, clip_count, rows_own)
+            values = jnp.pad(values, ((0, 0), (0, 8 - clip_count), (0, 0)))
+            return values.reshape(-1, rows_own)
+
+        io_lines = -(-io_size // 1024) * 8
+        io_part = jnp.pad(io_part, ((0, 0), (0, 0), (0, io_lines * 128 - io_size)))
+        smalls = (
+            jnp.pad(loss_part.reshape(1, 1), ((0, 7), (1, 126))),
+            jnp.pad(mod_grad, ((0, 0), (0, 8 - clip_count), (0, 0))),
+            io_part.reshape(head_count, data_count, io_lines, 128),
+            padded_clips(signal_own.astype(jnp.float32)),
+            padded_clips(signal_back(jnp.ones_like(hidden_own))[0]),
+            padded_clips(table_own),
+            ada_bf,
+        )
+        owned, totals, edge, ada_grad, time_grad, io_grad = reduce_whole(
+            tuple(plan), lefts, rights, smalls, next(ids)
+        )
         totals = totals[0, :2]
         edge = edge[::-1]
         edge = jnp.where(is_first, edge[..., :64], edge[..., 64:])
+        time_grad = jnp.concatenate([time_grad[0], time_grad[1]], 1)
+        io_grad = io_grad.reshape(-1)[:io_size].reshape(2, rows_own, io_cols)
     else:
+        io_grad = lax.psum(io_part, ("dp", "head"))
+        io_grad = lax.dynamic_slice(io_grad, (h, d, 0), (1, 1, io_size))
+        io_grad = io_grad.reshape(2, rows_own, io_cols)
+        mod_grad = jnp.sum(swap(mod_grad, "head"), 0)
+        mod_grad = spread(mod_grad, "dp").reshape(-1, 2, ada_cols)
+        ada_grad = exact_product("fd,fln->ldn", signal_own.astype(jnp.float32), mod_grad)
+        grad_signal = exact_product("fln,ldn->fd", mod_grad, ada_bf.astype(jnp.float32))
+        grad_signal = jnp.sum(spread(grad_signal, "head"), 0)
+        grad_cond = spread(signal_back(grad_signal)[0], "dp").transpose(1, 0, 2).reshape(-1, D)
+        time_grad = exact_product(
+            "fd,fn->dn",
+            table_own,
+            lax.dynamic_slice_in_dim(grad_cond, h * time_cols, time_cols, 1),
+        )
 
         def made(left_place, right_place):
             return product("fd,fn->dn", lefts[left_place], rights[right_place])
@@ -1736,7 +1857,7 @@
             owned.append(join_first(columns[:, : 3 * D], columns[:, 3 * D :]))
             owned += [made(*pair) for pair in pairs]
         owned = [reduce_general(part) for part in owned]
-        square = square + sum((jnp.sum(part * part) for part in owned))
+        square = sum((jnp.sum(part * part) for part in owned + [ada_grad, time_grad, io_grad]))
         totals = lax.psum(jnp.stack([square, loss_part]), ("dp", "head"))
         edge = jnp.stack([owned[3], owned[0]])
         edge = jnp.where(is_first, edge[..., block : block + 64], edge[..., block - 64 : block])

time: 824 us -> 774 us (0.939)
  Pallas kernels: 557 us -> 520 us
    pallas_call x5 -> x1, Pallas kernels: 35.1 us -> 5.07 us  [exchange(): pl.pallas_call(functools.partial(exchange_kernel, axis, count, swapped),...]
    pallas_call x1, Pallas kernels: 54.2 us -> 45.1 us  [attend_back(): pl.pallas_call(attend_back_kernel, out_shape=jax.ShapeDtypeStruct((3 * ti...]
where the time goes in v5:
time: 774 us; the launch traced here: 766 us
  Pallas kernels  520 us (67%)
  matrix products  160 us (21%)
  other arithmetic  44.3 us (6%)
  local copies, waits for them, and re-layouts  33.5 us (4%)
    pallas_call x1, Pallas kernels, gather_whole(): pl.pallas_call(functools.partial(gather_kernel, groups, firsts), out_shap...  156 us
    pallas_call x1, Pallas kernels, reduce_whole(): pl.pallas_call(functools.partial(reduce_kernel, plan, len(lefts), len(rig...  147 us
    dot_general x23, matrix products, product(): return jnp.einsum(form, left, right, preferred_element_type=jnp.float32)  99.4 us
    dot_general x18, matrix products, near_product(): return jnp.einsum(form, left, right, precision=lax.Precision.HIGH)  60.1 us
    pallas_call x1, Pallas kernels, attend_back(): pl.pallas_call(attend_back_kernel, out_shape=jax.ShapeDtypeStruct((3 * ti...  45.1 us
    pallas_call x1, Pallas kernels, to_owner(): pl.pallas_call(functools.partial(to_owner_kernel, count), out_shape=jax.S...  44.6 us
    pallas_call x1, Pallas kernels, from_owner(): pl.pallas_call(functools.partial(from_owner_kernel, count, widths), out_s...  35.9 us
    pallas_call x1, Pallas kernels, attend(): pl.pallas_call(attend_kernel, out_shape=[jax.ShapeDtypeStruct((frames, D)...  31.8 us

profile of v5, /device:TPU:11, one launch (start us, length us, event | category | flops | bytes accessed | tf_op | source)
XLA Modules:
  0.0 765.6 jit_solution(14499816472122476166)
XLA Ops:
  21.6 156.4 %gather_weights.1 = (bf16[2,2,2,96,1024]{4,3,2,1,0:T(8,128)(2,1)}, bf16[2,2,2,96,3072]{4,3,2,1,0:T(8,128)(2,1)}, bf16[2,2,2,96,3072]{4,3,2,1,0:T(8,128)(2,1)}, b...) custom-call(bf16[96,256]{1,0:T(8,128)(2,1)} %fusion.122.refs_0_, ...), custom_call_target="tpu_custom_call" | custom-call | tf_op jit(solution)/shard_map/gather_weights/pallas_call | solution.py:389
  185.6 4.3 convolution_convert_fusion.1.keys_ref.values_ref
  194.2 6.3 convolution_convert_fusion
  200.5 31.8 %attend.1 = (bf16[624,768]{1,0:T(8,128)(2,1)}, bf16[2,416,1152]{2,1,0:T(8,128)(2,1)}, bf16[4,208,768]{2,1,0:T(8,128)(2,1)}, f32[16,832]{1,0:T(8,128)}) custom-call(bf16[624,2304]{1,0:T(8,128)(2,1)} %bitcast.261), custom_call_target="tpu_custom_call" | custom-call | tf_op jit(solution)/shard_map/attend/pallas_call | solution.py:1258
  232.3 3.9 fusion.224
  237.2 6.6 multiply_convert_fusion.1
  243.9 4.5 fusion.223
  249.4 3.5 convolution_convert_fusion.4.query_ref
  252.9 9.8 %cross.1 = bf16[3,208,768]{2,1,0:T(8,128)(2,1)} custom-call(bf16[3,208,768]{2,1,0:T(8,128)(2,1)} %convolution_convert_fusion.4.query_ref, bf16[2,256,1536]{2,1,0:T(8,128)(2,1)} %convolution_convert_fusion.1.keys_ref.values_ref, bf16[2,256,1536]{2,1,0:T(8,128)(2,1)} %convolution_convert_fusion.1.keys_ref.values_ref, s32[2]{0:T(128)} %pad_add_fusion.len_ref), custom_call_target="tpu_custom_call" | custom-call | tf_op jit(solution)/shard_map/cross/pallas_call | solution.py:1399
  262.6 3.8 fusion.222
  267.3 9.9 %multiply_convert_fusion = (bf16[3,208,3072]{2,1,0:T(8,128)(2,1)S(1)}, f32[3,208,3072]{2,1,0:T(8,128)}) fusion(bf16[3,208,768]{2,1,0:T(8,128)(2,1)S(1)} %add_convert_fusion.1, bf16[768,3072,1]{1,0,2:T(8,128)(2,1)} %bitcast.325), kind=kOutput, calls=%fused_computation.20 | convolution fusion | flops 2961653760 | bytes 17178624 | tf_op jit(solution)/shard_map/fld,dn->fln/dot_general | solution.py:69
  277.3 4.5 fusion.221
  284.2 5.1 spread.1
  300.4 11.9 %fusion.7 = bf16[3,208,3072]{2,1,0:T(8,128)(2,1)S(1)} fusion(f32[3,208,3072]{2,1,0:T(8,128)} %get-tuple-element.248, bf16[3,208,768]{2,1,0:T(8,128)(2,1)S(1)} %get-tuple-element.185, bf16[768,3072,1]{1,0,2:T(8,128)(2,1)} %bitcast.329), kind=kOutput, calls=%fused_computation.15 | convolution fusion | flops 2990407680 | bytes 17178624 | tf_op jit(solution)/shard_map/fld,dn->fln/dot_general | solution.py:69
  312.4 3.4 multiply_reduce_fusion.11
  322.6 13.7 %cross_back.1 = (bf16[3,208,768]{2,1,0:T(8,128)(2,1)}, bf16[2,256,768]{2,1,0:T(8,128)(2,1)}, bf16[2,256,768]{2,1,0:T(8,128)(2,1)}) custom-call(bf16[3,208,768]{2,1,0:T(8,128)(2,1)} %convolution_convert_fusion.4.query_ref, bf16[2,256,1536]{2,1,0:T(8,128)(2,1)} %convolution_convert_fusion.1.keys_ref.values_ref, ...), custom_call_target="tpu_custom_call" | custom-call | tf_op jit(solution)/shard_map/cross_back/pallas_call | solution.py:1450
  342.0 11.0 %fusion.3 = bf16[3,208,3072]{2,1,0:T(8,128)(2,1)S(1)} fusion(f32[3,208,3072]{2,1,0:T(8,128)} %get-tuple-element.244, bf16[3,208,768]{2,1,0:T(8,128)(2,1)S(1)} %multiply_convert_fusion.3, bf16[768,3072,1]{1,0,2:T(8,128)(2,1)S(1)} %bitcast.324), kind=kOutput, calls=%fused_computation.11 | convolution fusion | flops 2990407680 | bytes 17178624 | tf_op jit(solution)/shard_map/fld,dn->fln/dot_general | solution.py:69
  353.1 3.4 multiply_reduce_fusion.9
  359.1 3.5 convolution_convert_fusion.2
  362.6 45.1 %attend_back.1.refs_16_ = bf16[624,2304]{1,0:T(8,128)(2,1)} custom-call(bf16[2,416,1152]{2,1,0:T(8,128)(2,1)} %get-tuple-element.57.pair_all, bf16[4,208,768]{2,1,0:T(8,128)(2,1)} %get-tuple-element.58.quad_all, f32[16,832]{1,0:T(8,128)} %get-tuple-element.59.log_ref, bf16[624,768]{1,0:T(8,128)(2,1)} %bitcast.269), custom_call_target="tpu_custom_call" | custom-call | tf_op jit(solution)/shard_map/attend_back/pallas_call | solution.py:1350
  407.7 5.3 fusion.13
  420.0 146.9 %reduce_grads.1 = (f32[18,96,256]{2,1,0:T(8,128)}, f32[8,128]{1,0:T(8,128)}, f32[2,96,128]{2,1,0:T(8,128)}, f32[2,96,1152]{2,1,0:T(8,128)}, f32[2,96,96]{2,1,0:T(8,128)}, /*index=5*/f32[8,128]{1,0:T(8,128)}) custom-call(bf16[624,768]{1,0:T(8,128)(2,1)} %bitcast.255, bf16[624,768]{1,0:T(8,128)(2,1)} %bitcast.253, bf16[512,768]{1,0:T(8,128)(2,1)} %bitcast.260, ...), custom_call_target="tpu_custom_call" | custom-call | tf_op jit(solution)/shard_map/reduce_grads/pallas_call | solution.py:813
  581.6 44.6 %to_owner.1 = f32[8,96,768]{2,1,0:T(8,128)} custom-call(f32[2,96,640]{2,1,0:T(8,128)} %pad.54.refs_0_, f32[2,96,256]{2,1,0:T(8,128)} %pad.55.refs_1_, f32[2,96,768]{2,1,0:T(8,128)} %fusion.102.refs_2_, f32[2,96,768]{2,1,0:T(8,128)} %fusion.103.refs_3_), custom_call_target="tpu_custom_call" | custom-call | tf_op jit(solution)/shard_map/to_owner/pallas_call | solution.py:939
  628.1 31.3 %gram_sum.1 = f32[768,768]{1,0:T(8,128)} custom-call(f32[768,768]{1,0:T(8,128)} %bitcast.242), custom_call_target="tpu_custom_call" | custom-call | tf_op jit(solution)/shard_map/gram_sum/pallas_call | solution.py:1049
  675.3 3.4 fusion.37
  681.9 3.4 fusion.39
  691.8 3.4 fusion.35
  695.1 3.7 fusion.33
  702.0 3.4 fusion.25
  708.7 3.4 fusion.27
  718.7 4.1 divide_convert_fusion
  722.8 35.9 %from_owner.1 = bf16[8,96,768]{2,1,0:T(8,128)(2,1)} custom-call(bf16[8,96,768]{2,1,0:T(8,128)(2,1)} %bitcast.268), custom_call_target="tpu_custom_call" | custom-call | tf_op jit(solution)/shard_map/from_owner/pallas_call | solution.py:996
  (368 shorter events, 127.1 us)
Async XLA Ops:
  0.7 16.4 %copy-start.33 = (f32[2,96,576]{2,1,0:T(8,128)S(1)}, f32[2,96,576]{2,1,0:T(8,128)}, u32[]{:S(2)}) copy-start(f32[2,96,576]{2,1,0:T(8,128)} %param.31) | copy-start | bytes 1327108
  0.7 15.7 %copy-start.50 = (f32[3,208,20]{1,2,0:T(8,128)S(1)}, f32[3,208,20]{1,2,0:T(8,128)}, u32[]{:S(2)}) copy-start(f32[3,208,20]{1,2,0:T(8,128)} %param.25) | copy-start | bytes 149764
  0.7 15.7 %copy-start.51 = (f32[3,208,20]{1,2,0:T(8,128)S(1)}, f32[3,208,20]{1,2,0:T(8,128)}, u32[]{:S(2)}) copy-start(f32[3,208,20]{1,2,0:T(8,128)} %param.24) | copy-start | bytes 149764
  200.5 36.7 %slice-start = ((s8[4718592]{0:T(1024)(128)(4,1)}), s8[524288]{0:T(1024)(128)(4,1)S(1)}, s32[]{:S(2)}) async-start(s8[4718592]{0:T(1024)(128)(4,1)} %bitcast.313), calls=%async_computation | async-start | bytes 1048576
  248.4 14.2 %copy-start = (f32[3,208,768]{2,1,0:T(8,128)}, f32[3,208,768]{2,1,0:T(8,128)S(1)}, u32[]{:S(2)}) copy-start(f32[3,208,768]{2,1,0:T(8,128)S(1)} %get-tuple-element.171) | copy-start | bytes 5750788
  249.4 13.2 %copy-start.19 = (bf16[3,208,768]{2,1,0:T(8,128)(2,1)}, bf16[3,208,768]{2,1,0:T(8,128)(2,1)S(1)}, u32[]{:S(2)}) copy-start(bf16[3,208,768]{2,1,0:T(8,128)(2,1)S(1)} %add_convert_fusion.2) | copy-start | bytes 2875396
  266.4 10.9 %copy-start.4 = (f32[3,208,768]{2,1,0:T(8,128)}, f32[3,208,768]{2,1,0:T(8,128)S(1)}, u32[]{:S(2)}) copy-start(f32[3,208,768]{2,1,0:T(8,128)S(1)} %get-tuple-element.169) | copy-start | bytes 5750788
  266.8 10.5 %slice-start.10 = ((s8[4718592]{0:T(1024)(128)(4,1)}), s8[4194304]{0:T(1024)(128)(4,1)S(1)}, s32[]{:S(2)}) async-start(s8[4718592]{0:T(1024)(128)(4,1)} %bitcast.330), calls=%async_computation.10 | async-start | bytes 8388608
  300.0 12.4 %slice-start.8 = ((s8[4718592]{0:T(1024)(128)(4,1)}), s8[4194304]{0:T(1024)(128)(4,1)S(1)}, s32[]{:S(2)}) async-start(s8[4718592]{0:T(1024)(128)(4,1)} %bitcast.326), calls=%async_computation.8 | async-start | bytes 8388608
  300.4 12.0 %copy-start.24 = (bf16[3,208,768]{2,1,0:T(8,128)(2,1)}, bf16[3,208,768]{2,1,0:T(8,128)(2,1)S(1)}, u32[]{:S(2)}) copy-start(bf16[3,208,768]{2,1,0:T(8,128)(2,1)S(1)} %get-tuple-element.185) | copy-start | bytes 2875396
  300.4 12.0 %copy-start.5 = (f32[3,208,768]{2,1,0:T(8,128)S(1)}, f32[3,208,768]{2,1,0:T(8,128)}, u32[]{:S(2)}) copy-start(f32[3,208,768]{2,1,0:T(8,128)} %copy-done.4) | copy-start | bytes 5750788
  300.4 12.0 %slice-start.9 = ((s8[4718592]{0:T(1024)(128)(4,1)}), s8[524288]{0:T(1024)(128)(4,1)S(1)}, s32[]{:S(2)}) async-start(s8[4718592]{0:T(1024)(128)(4,1)} %bitcast.326), calls=%async_computation.9 | async-start | bytes 1048576
  322.6 13.7 %copy-start.1 = (f32[3,208,768]{2,1,0:T(8,128)S(1)}, f32[3,208,768]{2,1,0:T(8,128)}, u32[]{:S(2)}) copy-start(f32[3,208,768]{2,1,0:T(8,128)} %copy-done) | copy-start | bytes 5750788
  340.5 12.6 %slice-start.2 = ((s8[4718592]{0:T(1024)(128)(4,1)}), s8[4194304]{0:T(1024)(128)(4,1)S(1)}, s32[]{:S(2)}) async-start(s8[4718592]{0:T(1024)(128)(4,1)} %bitcast.316), calls=%async_computation.2 | async-start | bytes 8388608
  342.0 11.1 %copy-start.22 = (bf16[3,208,768]{2,1,0:T(8,128)(2,1)}, bf16[3,208,768]{2,1,0:T(8,128)(2,1)S(1)}, u32[]{:S(2)}) copy-start(bf16[3,208,768]{2,1,0:T(8,128)(2,1)S(1)} %multiply_convert_fusion.3) | copy-start | bytes 2875396
  342.0 11.1 %copy-start.7 = (f32[3,208,768]{2,1,0:T(8,128)S(1)}, f32[3,208,768]{2,1,0:T(8,128)}, u32[]{:S(2)}) copy-start(f32[3,208,768]{2,1,0:T(8,128)} %copy-done.6) | copy-start | bytes 5750788
  342.0 11.1 %slice-start.3 = ((s8[4718592]{0:T(1024)(128)(4,1)}), s8[524288]{0:T(1024)(128)(4,1)S(1)}, s32[]{:S(2)}) async-start(s8[4718592]{0:T(1024)(128)(4,1)} %bitcast.316), calls=%async_computation.3 | async-start | bytes 1048576
  359.1 48.6 %copy-start.23 = (bf16[3,208,768]{2,1,0:T(8,128)(2,1)}, bf16[3,208,768]{2,1,0:T(8,128)(2,1)S(1)}, u32[]{:S(2)}) copy-start(bf16[3,208,768]{2,1,0:T(8,128)(2,1)S(1)} %multiply_convert_fusion.2) | copy-start | bytes 2875396
  420.0 150.0 %copy-start.52 = (f32[2,96,5]{1,0,2:T(2,128)S(1)}, f32[2,96,5]{1,0,2:T(2,128)}, u32[]{:S(2)}) copy-start(f32[2,96,5]{1,0,2:T(2,128)} %param.37) | copy-start | bytes 11524
  420.0 150.0 %copy-start.54 = (f32[2,96,5]{1,0,2:T(2,128)S(1)}, f32[2,96,5]{1,0,2:T(2,128)}, u32[]{:S(2)}) copy-start(f32[2,96,5]{1,0,2:T(2,128)} %param.47) | copy-start | bytes 11524
  420.0 150.0 %copy-start.55 = (f32[2,96,5]{1,0,2:T(2,128)S(1)}, f32[2,96,5]{1,0,2:T(2,128)}, u32[]{:S(2)}) copy-start(f32[2,96,5]{1,0,2:T(2,128)} %param.46) | copy-start | bytes 11524
  420.0 151.5 %copy-start.46 = (f32[96,192]{1,0:T(8,128)S(1)}, f32[96,192]{1,0:T(8,128)}, u32[]{:S(2)}) copy-start(f32[96,192]{1,0:T(8,128)} %param.36) | copy-start | bytes 221188
  420.0 151.5 %copy-start.48 = (f32[96,192]{1,0:T(8,128)S(1)}, f32[96,192]{1,0:T(8,128)}, u32[]{:S(2)}) copy-start(f32[96,192]{1,0:T(8,128)} %param.45) | copy-start | bytes 221188
  420.0 151.5 %copy-start.49 = (f32[96,192]{1,0:T(8,128)S(1)}, f32[96,192]{1,0:T(8,128)}, u32[]{:S(2)}) copy-start(f32[96,192]{1,0:T(8,128)} %param.44) | copy-start | bytes 221188
  579.7 46.5 %copy-start.43 = (f32[2,96,192]{2,1,0:T(8,128)}, f32[2,96,192]{2,1,0:T(8,128)S(1)}, u32[]{:S(2)}) copy-start(f32[2,96,192]{2,1,0:T(8,128)S(1)} %fusion.114) | copy-start | bytes 442372
  580.7 45.5 %copy-start.32 = (f32[2,96,576]{2,1,0:T(8,128)}, f32[2,96,576]{2,1,0:T(8,128)S(1)}, u32[]{:S(2)}) copy-start(f32[2,96,576]{2,1,0:T(8,128)S(1)} %fusion.107) | copy-start | bytes 1327108
  581.5 44.6 %copy-start.26 = (f32[2,96,1152]{2,1,0:T(8,128)S(1)}, f32[2,96,1152]{2,1,0:T(8,128)}, u32[]{:S(2)}) copy-start(f32[2,96,1152]{2,1,0:T(8,128)} %param.35) | copy-start | bytes 2654212
  581.5 44.6 %copy-start.39 = (f32[2,96,1152]{2,1,0:T(8,128)S(1)}, f32[2,96,1152]{2,1,0:T(8,128)}, u32[]{:S(2)}) copy-start(f32[2,96,1152]{2,1,0:T(8,128)} %param.43) | copy-start | bytes 2654212
  581.5 44.6 %copy-start.40 = (f32[2,96,1152]{2,1,0:T(8,128)S(1)}, f32[2,96,1152]{2,1,0:T(8,128)}, u32[]{:S(2)}) copy-start(f32[2,96,1152]{2,1,0:T(8,128)} %param.42) | copy-start | bytes 2654212
  581.5 44.6 %copy-start.41 = (f32[2,96,1152]{2,1,0:T(8,128)S(1)}, f32[2,96,1152]{2,1,0:T(8,128)}, u32[]{:S(2)}) copy-start(f32[2,96,1152]{2,1,0:T(8,128)} %get-tuple-element.63) | copy-start | bytes 2654212
  722.8 36.8 %copy-start.42 = (f32[2,96,192]{2,1,0:T(8,128)S(1)}, f32[2,96,192]{2,1,0:T(8,128)}, u32[]{:S(2)}) copy-start(f32[2,96,192]{2,1,0:T(8,128)} %param.32) | copy-start | bytes 442372
  722.8 38.6 %copy-start.34 = (f32[2,96,576]{2,1,0:T(8,128)S(1)}, f32[2,96,576]{2,1,0:T(8,128)}, u32[]{:S(2)}) copy-start(f32[2,96,576]{2,1,0:T(8,128)} %param.31) | copy-start | bytes 1327108
  (37 other events, 150.7 us)

commit v6 on v5

--- a/solution.py
+++ b/solution.py
@@ -329,11 +329,15 @@
             at = lax.broadcasted_iota(jnp.int32, (width, 128), 0)
             to = lax.broadcasted_iota(jnp.int32, (width, 128), 1)
             chosen = jnp.where((at == first + to) & (to < ada_ref.shape[1]), 1.0, 0.0)
-            own = to_bf16(dot_nn(signal, to_bf16(chosen)))[:, : ada_ref.shape[1]]
-            columns = ada_ref.shape[2]
-            for layer in range(2):
-                part = dot_nn(own, ada_ref[layer]).reshape(count, lines, columns)
-                parts[:, :, layer * columns : (layer + 1) * columns] = part[:, :8]
+            own = to_bf16(dot_nn(signal, to_bf16(chosen)))
+            row = lax.broadcasted_iota(jnp.int32, (count * lines, count * lines), 0)
+            source = lax.broadcasted_iota(jnp.int32, (count * lines, count * lines), 1)
+            within = row % lines
+            repeat = (source == row) & (within < 3) | (source == row - 3) & (within >= 3) & (within < 6)
+            own = to_bf16(dot_nn(to_bf16(jnp.where(repeat, 1.0, 0.0)), own))[:, : ada_ref.shape[1]]
+            within = lax.broadcasted_iota(jnp.int32, (count * lines, 1), 0) % lines
+            part = jnp.where(within < 3, dot_nn(own, ada_ref[0]), dot_nn(own, ada_ref[1]))
+            parts[...] = part.reshape(parts.shape)
             for copy in swaps:
                 copy.start()
             parts_got[d] = parts[d]
@@ -385,7 +389,7 @@
     pieces = len(gather_pieces([own.shape[1] for own in owns], firsts))
     rows = owns[0].shape[0]
     low = jnp.bfloat16
-    mod_cols = 2 * ada.shape[2]
+    mod_cols = ada.shape[2]
     *wholes, latents_all, shared_all, mods = pl.pallas_call(
         functools.partial(gather_kernel, groups, firsts),
         out_shape=[
@@ -1223,9 +1227,7 @@
 
     log_ref[...] = jnp.zeros_like(log_ref)
     quad_out[...] = jnp.zeros_like(quad_out)
-    for copy in pair_copies:
-        copy.wait()
-    for pair in range(3):
+    def pair_heads(pair):
         query, keys, values = (
             pair_all[:, :, part * HALF + pair * 128 : part * HALF + pair * 128 + 128].reshape(
                 length, 128
@@ -1234,7 +1236,11 @@
         )
         heads(query, keys, values, ((0, 2 * pair), (1, 2 * pair + 1)))
         pair_out[:, :, pair * 128 : pair * 128 + 128] = joined[...].reshape(2, 2 * tile, 128)
-    back = return_pair(h, pair_out, mixed_ref, 1, sems)
+
+    for copy in pair_copies:
+        copy.wait()
+    pair_heads(0)
+    pair_heads(1)
     for copy in quad_copies:
         copy.wait()
     for member in range(3):
@@ -1246,6 +1252,8 @@
         heads(query, keys, values, ((place % 2, 6 + member),))
         quad_out[:, :, lanes(at, 128)] += joined[...].reshape(4, tile, 128)
     back_quad = return_quad(h, quad_out, quad_got, sems)
+    pair_heads(2)
+    back = return_pair(h, pair_out, mixed_ref, 1, sems)
     for copy in back + back_quad:
         copy.wait()
     merge_quad(quad_got, mixed_ref, 1)
@@ -1314,9 +1322,7 @@
         grads[2] = to_bf16(grad_values[...])
 
     quad_out[...] = jnp.zeros_like(quad_out)
-    for copy in pair_copies:
-        copy.wait()
-    for pair in range(3):
+    def pair_heads(pair):
         at = [part * HALF + pair * 128 for part in range(3)]
         query, keys, values = (
             pair_all[:, :, start : start + 128].reshape(length, 128) for start in at
@@ -1325,7 +1331,10 @@
         heads(query, keys, values, grad_out, ((0, 2 * pair), (1, 2 * pair + 1)))
         for part in range(3):
             pair_out[:, :, at[part] : at[part] + 128] = grads[part].reshape(2, 2 * tile, 128)
-    back = return_pair(h, pair_out, rows_ref, 3, sems)
+
+    for copy in pair_copies:
+        copy.wait()
+    pair_heads(0)
     for copy in quad_copies:
         copy.wait()
     for member in range(3):
@@ -1339,6 +1348,9 @@
         for part in range(3):
             quad_out[:, :, lanes(part * WIDE + at, 128)] += grads[part].reshape(4, tile, 128)
     back_quad = return_quad(h, quad_out, quad_got, sems)
+    pair_heads(1)
+    pair_heads(2)
+    back = return_pair(h, pair_out, rows_ref, 3, sems)
     for copy in back + back_quad:
         copy.wait()
     merge_quad(quad_got, rows_ref, 3)
@@ -1581,18 +1593,18 @@
         shared = jnp.concatenate(
             [
                 jnp.zeros((clip_count, D)),
-                table_bf.astype(jnp.float32),
                 cap_unit,
-                jnp.zeros((16 - 3 * clip_count, D)),
+                jnp.pad(timesteps[None], ((0, 7 - 2 * clip_count), (0, D - clip_count))),
             ]
         )
+        shared = jnp.pad(shared, ((0, 8 - shared.shape[0]), (0, head_count * WIDE - D)))
         gathered, latents_all, shared_all, mods = gather_whole(
             listed(with_edge(qkv_low, out_low, none)),
             (1, 4),
             edge,
             latents,
-            jnp.pad(shared, ((0, 0), (0, head_count * WIDE - D))),
-            jnp.pad(table_bf, ((0, 16 - clip_count), (0, 0))),
+            shared,
+            jnp.pad(table_bf, ((0, 8 - clip_count), (0, 0))),
             ada_bf,
             next(ids),
         )
@@ -1600,12 +1612,13 @@
         hidden_own = lax.dynamic_slice(
             shared_all, (0, 0, start), (data_count, clip_count, rows_own)
         ).reshape(-1, rows_own)
-        table_own = lax.dynamic_slice(
-            shared_all, (0, clip_count, own_row), (data_count, clip_count, rows_own)
-        ).reshape(-1, rows_own)
-        cap_all = shared_all[:, 2 * clip_count : 3 * clip_count, :D].reshape(-1, D)
+        times_all = shared_all[:, 2 * clip_count, :clip_count].reshape(-1)
+        table_own = to_bf16(time_table(times_all, D)).astype(jnp.float32)
+        table_own = lax.dynamic_slice_in_dim(table_own, own_row, rows_own, 1)
+        cap_all = shared_all[:, clip_count : 2 * clip_count, :D].reshape(-1, D)
         signal_own = to_bf16(double_silu(hidden_own))
-        mods = mods[:, :clip_count]
+        mods = mods[:, : 2 * clip_count].reshape(head_count, 2, clip_count, ada_cols)
+        mods = mods.transpose(0, 2, 1, 3)
     else:
         edge = lax.ppermute(edge, "head", [(place, place ^ 1) for place in range(head_count)])
         gathered = [gather_general(own) for own in listed(with_edge(qkv_low, out_low, edge))]

time: 774 us -> 758 us (0.979)
  Pallas kernels: 520 us -> 501 us
    pallas_call x1, Pallas kernels: 45.1 us -> 35.1 us  [attend_back(): pl.pallas_call(attend_back_kernel, out_shape=jax.ShapeDtypeStruct((3 * ti...]
    pallas_call x1, Pallas kernels: 156 us -> 147 us  [gather_whole(): pl.pallas_call(functools.partial(gather_kernel, groups, firsts), out_shap...]
where the time goes in v6:
time: 758 us; the launch traced here: 749 us
  Pallas kernels  501 us (66%)
  matrix products  160 us (21%)
  other arithmetic  47.5 us (6%)
  local copies, waits for them, and re-layouts  32.8 us (4%)
    pallas_call x1, Pallas kernels, gather_whole(): pl.pallas_call(functools.partial(gather_kernel, groups, firsts), out_shap...  147 us
    pallas_call x1, Pallas kernels, reduce_whole(): pl.pallas_call(functools.partial(reduce_kernel, plan, len(lefts), len(rig...  147 us
    dot_general x23, matrix products, product(): return jnp.einsum(form, left, right, preferred_element_type=jnp.float32)  99.4 us
    dot_general x18, matrix products, near_product(): return jnp.einsum(form, left, right, precision=lax.Precision.HIGH)  60.1 us
    pallas_call x1, Pallas kernels, to_owner(): pl.pallas_call(functools.partial(to_owner_kernel, count), out_shape=jax.S...  45.2 us
    pallas_call x1, Pallas kernels, attend_back(): pl.pallas_call(attend_back_kernel, out_shape=jax.ShapeDtypeStruct((3 * ti...  35.1 us
    pallas_call x1, Pallas kernels, from_owner(): pl.pallas_call(functools.partial(from_owner_kernel, count, widths), out_s...  35.1 us
    pallas_call x1, Pallas kernels, attend(): pl.pallas_call(attend_kernel, out_shape=[jax.ShapeDtypeStruct((frames, D)...  31.8 us

profile of v6, /device:TPU:11, one launch (start us, length us, event | category | flops | bytes accessed | tf_op | source)
XLA Modules:
  0.0 748.8 jit_solution(6728948533110467390)
XLA Ops:
  23.0 147.5 %gather_weights.1 = (bf16[2,2,2,96,1024]{4,3,2,1,0:T(8,128)(2,1)}, bf16[2,2,2,96,3072]{4,3,2,1,0:T(8,128)(2,1)}, bf16[2,2,2,96,3072]{4,3,2,1,0:T(8,128)(2,1)}, b...) custom-call(bf16[96,256]{1,0:T(8,128)(2,1)} %fusion.122.refs_0_, ...), custom_call_target="tpu_custom_call" | custom-call | tf_op jit(solution)/shard_map/gather_weights/pallas_call | solution.py:393
  179.2 4.3 convolution_convert_fusion.1.keys_ref.values_ref
  187.8 6.3 convolution_convert_fusion
  194.1 31.8 %attend.1 = (bf16[624,768]{1,0:T(8,128)(2,1)}, bf16[2,416,1152]{2,1,0:T(8,128)(2,1)}, bf16[4,208,768]{2,1,0:T(8,128)(2,1)}, f32[16,832]{1,0:T(8,128)}) custom-call(bf16[624,2304]{1,0:T(8,128)(2,1)} %bitcast.263), custom_call_target="tpu_custom_call" | custom-call | tf_op jit(solution)/shard_map/attend/pallas_call | solution.py:1266
  225.9 3.9 fusion.230
  230.8 6.6 multiply_convert_fusion.1
  237.5 4.5 fusion.229
  242.9 3.5 convolution_convert_fusion.4.query_ref
  246.4 9.8 %cross.1 = bf16[3,208,768]{2,1,0:T(8,128)(2,1)} custom-call(bf16[3,208,768]{2,1,0:T(8,128)(2,1)} %convolution_convert_fusion.4.query_ref, bf16[2,256,1536]{2,1,0:T(8,128)(2,1)} %convolution_convert_fusion.1.keys_ref.values_ref, bf16[2,256,1536]{2,1,0:T(8,128)(2,1)} %convolution_convert_fusion.1.keys_ref.values_ref, s32[2]{0:T(128)} %pad_add_fusion.len_ref), custom_call_target="tpu_custom_call" | custom-call | tf_op jit(solution)/shard_map/cross/pallas_call | solution.py:1411
  256.2 3.8 fusion.228
  260.9 9.9 %multiply_convert_fusion = (bf16[3,208,3072]{2,1,0:T(8,128)(2,1)S(1)}, f32[3,208,3072]{2,1,0:T(8,128)}) fusion(bf16[3,208,768]{2,1,0:T(8,128)(2,1)S(1)} %add_convert_fusion.1, bf16[768,3072,1]{1,0,2:T(8,128)(2,1)} %bitcast.328), kind=kOutput, calls=%fused_computation.20 | convolution fusion | flops 2961653760 | bytes 17178624 | tf_op jit(solution)/shard_map/fld,dn->fln/dot_general | solution.py:69
  270.8 4.5 fusion.227
  277.8 5.1 spread.1
  294.0 11.9 %fusion.7 = bf16[3,208,3072]{2,1,0:T(8,128)(2,1)S(1)} fusion(f32[3,208,3072]{2,1,0:T(8,128)} %get-tuple-element.245, bf16[3,208,768]{2,1,0:T(8,128)(2,1)S(1)} %get-tuple-element.185, bf16[768,3072,1]{1,0,2:T(8,128)(2,1)} %bitcast.332), kind=kOutput, calls=%fused_computation.15 | convolution fusion | flops 2990407680 | bytes 17178624 | tf_op jit(solution)/shard_map/fld,dn->fln/dot_general | solution.py:69
  306.0 3.4 multiply_reduce_fusion.11
  316.1 13.7 %cross_back.1 = (bf16[3,208,768]{2,1,0:T(8,128)(2,1)}, bf16[2,256,768]{2,1,0:T(8,128)(2,1)}, bf16[2,256,768]{2,1,0:T(8,128)(2,1)}) custom-call(bf16[3,208,768]{2,1,0:T(8,128)(2,1)} %convolution_convert_fusion.4.query_ref, bf16[2,256,1536]{2,1,0:T(8,128)(2,1)} %convolution_convert_fusion.1.keys_ref.values_ref, ...), custom_call_target="tpu_custom_call" | custom-call | tf_op jit(solution)/shard_map/cross_back/pallas_call | solution.py:1462
  335.6 11.0 %fusion.3 = bf16[3,208,3072]{2,1,0:T(8,128)(2,1)S(1)} fusion(f32[3,208,3072]{2,1,0:T(8,128)} %get-tuple-element.241, bf16[3,208,768]{2,1,0:T(8,128)(2,1)S(1)} %multiply_convert_fusion.3, bf16[768,3072,1]{1,0,2:T(8,128)(2,1)S(1)} %bitcast.327), kind=kOutput, calls=%fused_computation.11 | convolution fusion | flops 2990407680 | bytes 17178624 | tf_op jit(solution)/shard_map/fld,dn->fln/dot_general | solution.py:69
  346.7 3.4 multiply_reduce_fusion.9
  352.7 3.5 convolution_convert_fusion.2
  356.1 35.1 %attend_back.1.refs_16_ = bf16[624,2304]{1,0:T(8,128)(2,1)} custom-call(bf16[2,416,1152]{2,1,0:T(8,128)(2,1)} %get-tuple-element.57.pair_all, bf16[4,208,768]{2,1,0:T(8,128)(2,1)} %get-tuple-element.58.quad_all, f32[16,832]{1,0:T(8,128)} %get-tuple-element.59.log_ref, bf16[624,768]{1,0:T(8,128)(2,1)} %bitcast.271), custom_call_target="tpu_custom_call" | custom-call | tf_op jit(solution)/shard_map/attend_back/pallas_call | solution.py:1362
  391.3 5.3 fusion.13
  403.5 146.9 %reduce_grads.1 = (f32[18,96,256]{2,1,0:T(8,128)}, f32[8,128]{1,0:T(8,128)}, f32[2,96,128]{2,1,0:T(8,128)}, f32[2,96,1152]{2,1,0:T(8,128)}, f32[2,96,96]{2,1,0:T(8,128)}, /*index=5*/f32[8,128]{1,0:T(8,128)}) custom-call(bf16[624,768]{1,0:T(8,128)(2,1)} %bitcast.257, bf16[624,768]{1,0:T(8,128)(2,1)} %bitcast.255, bf16[512,768]{1,0:T(8,128)(2,1)} %bitcast.262, ...), custom_call_target="tpu_custom_call" | custom-call | tf_op jit(solution)/shard_map/reduce_grads/pallas_call | solution.py:817
  565.1 45.2 %to_owner.1 = f32[8,96,768]{2,1,0:T(8,128)} custom-call(f32[2,96,640]{2,1,0:T(8,128)} %pad.59.refs_0_, f32[2,96,256]{2,1,0:T(8,128)} %pad.60.refs_1_, f32[2,96,768]{2,1,0:T(8,128)} %fusion.102.refs_2_, f32[2,96,768]{2,1,0:T(8,128)} %fusion.103.refs_3_), custom_call_target="tpu_custom_call" | custom-call | tf_op jit(solution)/shard_map/to_owner/pallas_call | solution.py:943
  612.3 31.0 %gram_sum.1 = f32[768,768]{1,0:T(8,128)} custom-call(f32[768,768]{1,0:T(8,128)} %bitcast.244), custom_call_target="tpu_custom_call" | custom-call | tf_op jit(solution)/shard_map/gram_sum/pallas_call | solution.py:1053
  659.2 3.4 fusion.37
  665.8 3.4 fusion.39
  675.7 3.4 fusion.35
  679.1 3.7 fusion.33
  685.9 3.4 fusion.25
  692.7 3.4 fusion.27
  702.6 4.1 divide_convert_fusion
  706.8 35.1 %from_owner.1 = bf16[8,96,768]{2,1,0:T(8,128)(2,1)} custom-call(bf16[8,96,768]{2,1,0:T(8,128)(2,1)} %bitcast.270), custom_call_target="tpu_custom_call" | custom-call | tf_op jit(solution)/shard_map/from_owner/pallas_call | solution.py:1000
  (367 shorter events, 129.7 us)
Async XLA Ops:
  0.7 17.8 %copy-start.33 = (f32[2,96,576]{2,1,0:T(8,128)S(1)}, f32[2,96,576]{2,1,0:T(8,128)}, u32[]{:S(2)}) copy-start(f32[2,96,576]{2,1,0:T(8,128)} %param.31) | copy-start | bytes 1327108
  194.1 36.7 %slice-start = ((s8[4718592]{0:T(1024)(128)(4,1)}), s8[524288]{0:T(1024)(128)(4,1)S(1)}, s32[]{:S(2)}) async-start(s8[4718592]{0:T(1024)(128)(4,1)} %bitcast.316), calls=%async_computation | async-start | bytes 1048576
  242.0 14.2 %copy-start = (f32[3,208,768]{2,1,0:T(8,128)}, f32[3,208,768]{2,1,0:T(8,128)S(1)}, u32[]{:S(2)}) copy-start(f32[3,208,768]{2,1,0:T(8,128)S(1)} %get-tuple-element.171) | copy-start | bytes 5750788
  242.9 13.2 %copy-start.19 = (bf16[3,208,768]{2,1,0:T(8,128)(2,1)}, bf16[3,208,768]{2,1,0:T(8,128)(2,1)S(1)}, u32[]{:S(2)}) copy-start(bf16[3,208,768]{2,1,0:T(8,128)(2,1)S(1)} %add_convert_fusion.2) | copy-start | bytes 2875396
  259.9 10.9 %copy-start.4 = (f32[3,208,768]{2,1,0:T(8,128)}, f32[3,208,768]{2,1,0:T(8,128)S(1)}, u32[]{:S(2)}) copy-start(f32[3,208,768]{2,1,0:T(8,128)S(1)} %get-tuple-element.169) | copy-start | bytes 5750788
  260.3 10.5 %slice-start.10 = ((s8[4718592]{0:T(1024)(128)(4,1)}), s8[4194304]{0:T(1024)(128)(4,1)S(1)}, s32[]{:S(2)}) async-start(s8[4718592]{0:T(1024)(128)(4,1)} %bitcast.333), calls=%async_computation.10 | async-start | bytes 8388608
  260.9 9.9 %copy-start.20 = (bf16[3,208,768]{2,1,0:T(8,128)(2,1)}, bf16[3,208,768]{2,1,0:T(8,128)(2,1)S(1)}, u32[]{:S(2)}) copy-start(bf16[3,208,768]{2,1,0:T(8,128)(2,1)S(1)} %add_convert_fusion.1) | copy-start | bytes 2875396
  260.9 10.0 %slice-start.11 = ((s8[4718592]{0:T(1024)(128)(4,1)}), s8[524288]{0:T(1024)(128)(4,1)S(1)}, s32[]{:S(2)}) async-start(s8[4718592]{0:T(1024)(128)(4,1)} %bitcast.333), calls=%async_computation.11 | async-start | bytes 1048576
  293.6 12.4 %slice-start.8 = ((s8[4718592]{0:T(1024)(128)(4,1)}), s8[4194304]{0:T(1024)(128)(4,1)S(1)}, s32[]{:S(2)}) async-start(s8[4718592]{0:T(1024)(128)(4,1)} %bitcast.329), calls=%async_computation.8 | async-start | bytes 8388608
  294.0 12.0 %copy-start.24 = (bf16[3,208,768]{2,1,0:T(8,128)(2,1)}, bf16[3,208,768]{2,1,0:T(8,128)(2,1)S(1)}, u32[]{:S(2)}) copy-start(bf16[3,208,768]{2,1,0:T(8,128)(2,1)S(1)} %get-tuple-element.185) | copy-start | bytes 2875396
  294.0 12.0 %copy-start.5 = (f32[3,208,768]{2,1,0:T(8,128)S(1)}, f32[3,208,768]{2,1,0:T(8,128)}, u32[]{:S(2)}) copy-start(f32[3,208,768]{2,1,0:T(8,128)} %copy-done.4) | copy-start | bytes 5750788
  294.0 12.0 %slice-start.9 = ((s8[4718592]{0:T(1024)(128)(4,1)}), s8[524288]{0:T(1024)(128)(4,1)S(1)}, s32[]{:S(2)}) async-start(s8[4718592]{0:T(1024)(128)(4,1)} %bitcast.329), calls=%async_computation.9 | async-start | bytes 1048576
  316.1 13.7 %copy-start.1 = (f32[3,208,768]{2,1,0:T(8,128)S(1)}, f32[3,208,768]{2,1,0:T(8,128)}, u32[]{:S(2)}) copy-start(f32[3,208,768]{2,1,0:T(8,128)} %copy-done) | copy-start | bytes 5750788
  334.1 12.6 %slice-start.2 = ((s8[4718592]{0:T(1024)(128)(4,1)}), s8[4194304]{0:T(1024)(128)(4,1)S(1)}, s32[]{:S(2)}) async-start(s8[4718592]{0:T(1024)(128)(4,1)} %bitcast.319), calls=%async_computation.2 | async-start | bytes 8388608
  335.6 11.1 %copy-start.22 = (bf16[3,208,768]{2,1,0:T(8,128)(2,1)}, bf16[3,208,768]{2,1,0:T(8,128)(2,1)S(1)}, u32[]{:S(2)}) copy-start(bf16[3,208,768]{2,1,0:T(8,128)(2,1)S(1)} %multiply_convert_fusion.3) | copy-start | bytes 2875396
  335.6 11.1 %copy-start.7 = (f32[3,208,768]{2,1,0:T(8,128)S(1)}, f32[3,208,768]{2,1,0:T(8,128)}, u32[]{:S(2)}) copy-start(f32[3,208,768]{2,1,0:T(8,128)} %copy-done.6) | copy-start | bytes 5750788
  335.6 11.1 %slice-start.3 = ((s8[4718592]{0:T(1024)(128)(4,1)}), s8[524288]{0:T(1024)(128)(4,1)S(1)}, s32[]{:S(2)}) async-start(s8[4718592]{0:T(1024)(128)(4,1)} %bitcast.319), calls=%async_computation.3 | async-start | bytes 1048576
  352.7 38.6 %copy-start.23 = (bf16[3,208,768]{2,1,0:T(8,128)(2,1)}, bf16[3,208,768]{2,1,0:T(8,128)(2,1)S(1)}, u32[]{:S(2)}) copy-start(bf16[3,208,768]{2,1,0:T(8,128)(2,1)S(1)} %multiply_convert_fusion.2) | copy-start | bytes 2875396
  403.5 150.0 %copy-start.50 = (f32[2,96,5]{1,0,2:T(2,128)S(1)}, f32[2,96,5]{1,0,2:T(2,128)}, u32[]{:S(2)}) copy-start(f32[2,96,5]{1,0,2:T(2,128)} %param.37) | copy-start | bytes 11524
  403.5 150.0 %copy-start.52 = (f32[2,96,5]{1,0,2:T(2,128)S(1)}, f32[2,96,5]{1,0,2:T(2,128)}, u32[]{:S(2)}) copy-start(f32[2,96,5]{1,0,2:T(2,128)} %param.47) | copy-start | bytes 11524
  403.5 150.0 %copy-start.53 = (f32[2,96,5]{1,0,2:T(2,128)S(1)}, f32[2,96,5]{1,0,2:T(2,128)}, u32[]{:S(2)}) copy-start(f32[2,96,5]{1,0,2:T(2,128)} %param.46) | copy-start | bytes 11524
  403.5 151.5 %copy-start.46 = (f32[96,192]{1,0:T(8,128)S(1)}, f32[96,192]{1,0:T(8,128)}, u32[]{:S(2)}) copy-start(f32[96,192]{1,0:T(8,128)} %param.36) | copy-start | bytes 221188
  403.5 151.5 %copy-start.48 = (f32[96,192]{1,0:T(8,128)S(1)}, f32[96,192]{1,0:T(8,128)}, u32[]{:S(2)}) copy-start(f32[96,192]{1,0:T(8,128)} %param.45) | copy-start | bytes 221188
  403.5 151.5 %copy-start.49 = (f32[96,192]{1,0:T(8,128)S(1)}, f32[96,192]{1,0:T(8,128)}, u32[]{:S(2)}) copy-start(f32[96,192]{1,0:T(8,128)} %param.44) | copy-start | bytes 221188
  563.2 47.1 %copy-start.43 = (f32[2,96,192]{2,1,0:T(8,128)}, f32[2,96,192]{2,1,0:T(8,128)S(1)}, u32[]{:S(2)}) copy-start(f32[2,96,192]{2,1,0:T(8,128)S(1)} %fusion.114) | copy-start | bytes 442372
  564.2 46.1 %copy-start.32 = (f32[2,96,576]{2,1,0:T(8,128)}, f32[2,96,576]{2,1,0:T(8,128)S(1)}, u32[]{:S(2)}) copy-start(f32[2,96,576]{2,1,0:T(8,128)S(1)} %fusion.107) | copy-start | bytes 1327108
  565.1 45.3 %copy-start.26 = (f32[2,96,1152]{2,1,0:T(8,128)S(1)}, f32[2,96,1152]{2,1,0:T(8,128)}, u32[]{:S(2)}) copy-start(f32[2,96,1152]{2,1,0:T(8,128)} %param.35) | copy-start | bytes 2654212
  565.1 45.3 %copy-start.39 = (f32[2,96,1152]{2,1,0:T(8,128)S(1)}, f32[2,96,1152]{2,1,0:T(8,128)}, u32[]{:S(2)}) copy-start(f32[2,96,1152]{2,1,0:T(8,128)} %param.43) | copy-start | bytes 2654212
  565.1 45.3 %copy-start.40 = (f32[2,96,1152]{2,1,0:T(8,128)S(1)}, f32[2,96,1152]{2,1,0:T(8,128)}, u32[]{:S(2)}) copy-start(f32[2,96,1152]{2,1,0:T(8,128)} %param.42) | copy-start | bytes 2654212
  565.1 45.3 %copy-start.41 = (f32[2,96,1152]{2,1,0:T(8,128)S(1)}, f32[2,96,1152]{2,1,0:T(8,128)}, u32[]{:S(2)}) copy-start(f32[2,96,1152]{2,1,0:T(8,128)} %get-tuple-element.63) | copy-start | bytes 2654212
  706.8 36.0 %copy-start.42 = (f32[2,96,192]{2,1,0:T(8,128)S(1)}, f32[2,96,192]{2,1,0:T(8,128)}, u32[]{:S(2)}) copy-start(f32[2,96,192]{2,1,0:T(8,128)} %param.32) | copy-start | bytes 442372
  706.8 37.8 %copy-start.34 = (f32[2,96,576]{2,1,0:T(8,128)S(1)}, f32[2,96,576]{2,1,0:T(8,128)}, u32[]{:S(2)}) copy-start(f32[2,96,576]{2,1,0:T(8,128)} %param.31) | copy-start | bytes 1327108
  (35 other events, 134.2 us)

commit v7 on v6

--- a/solution.py
+++ b/solution.py
@@ -39,12 +39,19 @@
     return sigmoid_unit(sigmoid_unit(values))
 
 
+GELU_RATE = 0.7978845608
+GELU_CUBE = 0.7978845608 * 0.044715
+
+
 def soft_gelu(values):
-    return (
-        0.5
-        * values
-        * (1.0 + jnp.tanh(0.7978845608 * (values + 0.044715 * values * values * values)))
-    )
+    return 0.5 * values * (1.0 + jnp.tanh(values * (GELU_RATE + GELU_CUBE * (values * values))))
+
+
+def soft_gelu_slope(values):
+    square = values * values
+    bend = jnp.tanh(values * (GELU_RATE + GELU_CUBE * square))
+    steep = values * (GELU_RATE + (3.0 * GELU_CUBE) * square)
+    return 0.5 * ((1.0 + bend) + (1.0 - bend * bend) * steep)
 
 
 def norm_rows(values):
@@ -516,14 +523,14 @@
         for layer in range(layers):
             for part in range(per_group):
 
-                @pl.when(piece == 3 * layer * per_group + part)
+                @pl.when(piece == (3 * layer + 2) * per_group + part)
                 def _():
                     for copy in right_copies(piece, layer, part):
                         copy.start()
 
             for member in range(2):
 
-                @pl.when(piece // per_group == 3 * layer + 1 + member)
+                @pl.when(piece // per_group == 3 * layer + member)
                 def _():
                     for head in range(4):
                         right_copy(piece, plan[layer][1 + member][1], head).start()
@@ -536,14 +543,14 @@
                 if left_place not in used:
                     used.append(left_place)
 
-            @pl.when(piece == 3 * layer * per_group)
+            @pl.when(piece == (3 * layer + 2) * per_group)
             def _():
                 for at, left_place in enumerate(used):
                     turn_left(left_place, at)
 
             for part in range(per_group):
 
-                @pl.when(piece == 3 * layer * per_group + part)
+                @pl.when(piece == (3 * layer + 2) * per_group + part)
                 def _():
                     for copy in right_copies(piece, layer, part):
                         copy.wait()
@@ -561,11 +568,11 @@
 
             for member in range(2):
 
-                @pl.when(piece == (3 * layer + 1 + member) * per_group)
+                @pl.when(piece == (3 * layer + member) * per_group)
                 def _():
                     turn_left(plan[layer][1 + member][0], 0)
 
-        @pl.when((piece // per_group) % 3 != 0)
+        @pl.when((piece // per_group) % 3 != 2)
         def _():
             for head in range(4):
                 right_copy(piece, plan[0][1][1], head).wait()
@@ -712,10 +719,13 @@
         copy.start()
     mod_got[h] = mod_ref[h]
     io_got[h] = io_ref[h]
-    for place in range(lefts):
-        left_copy(place).start()
+    soonest = plan[0][1][0]
+    left_copy(soonest).start()
     fetch(0)
     fetch(1)
+    for place in range(lefts):
+        if place != soonest:
+            left_copy(place).start()
     bring(0)
     fetch(2)
     bring(1)
@@ -748,7 +758,7 @@
 
     edges = []
     for layer in range(layers):
-        piece = (3 * layer + 1) * per_group - 1
+        piece = 3 * (layer + 1) * per_group - 1
         edges.append(
             pltpu.make_async_remote_copy(
                 src_ref=out_ref.at[piece, :, pl.ds(0, 128)],
@@ -1025,16 +1035,28 @@
         )
 
     r0, r1, r2 = (pl.ds(third * place, third) for place in range(3))
-    upper[0] = dots(r0, pl.ds(0, 3 * third))
-    upper[1, :, : 2 * third] = dots(r1, pl.ds(third, 2 * third))
-    upper[1, :, 2 * third :] = dots(r2, r2)
+
+    def blocks(core):
+        @pl.when(core == 0)
+        def _():
+            upper[0] = dots(r0, pl.ds(0, 3 * third))
+
+        @pl.when(core == 1)
+        def _():
+            upper[1, :, : 2 * third] = dots(r1, pl.ds(third, 2 * third))
+            upper[1, :, 2 * third :] = dots(r2, r2)
+
+    near = send_to(upper.at[1 - c], got.at[0], (send_sem, recv_sem), 0, h ^ 1)
+    blocks(1 - c)
+    near.start()
+    blocks(c)
+    near.wait()
 
     def step(place, source, target, peer):
         copy = send_to(source, target, (send_sem, recv_sem), place, peer)
         copy.start()
         copy.wait()
 
-    step(0, upper.at[1 - c], got.at[0], h ^ 1)
     chip[...] = upper[c] + got[0]
     step(1, chip, got.at[1], h ^ 2)
     whole[c] = chip[...] + got[1]
@@ -1767,8 +1789,7 @@
         d_gate2 = jnp.sum(layer_down_out * grad_hidden, axis=1, keepdims=True)
         grad_down = to_bf16(mod_parts[5] * grad_hidden)
         grad_active = product("fld,dn->fln", grad_down, down_full[layer_index])
-        gelu_value, gelu_back = jax.vjp(soft_gelu, layer_upper)
-        grad_upper = to_bf16(gelu_back(grad_active)[0])
+        grad_upper = to_bf16(grad_active * soft_gelu_slope(layer_upper))
         grad_normed2 = product("fln,dn->fld", grad_upper, up_full[layer_index])
         mod_value, mod_back = jax.vjp(modulate, layer_middle, mod_parts[3], mod_parts[4])
         grad_middle, d_shift2, d_scale2 = mod_back(grad_normed2)
@@ -1867,23 +1888,23 @@
         owned = []
         for first, *pairs in plan:
             columns = jnp.concatenate([made(*source[:2]) for source in first], 1)
+            owned += [made(*pair) for pair in pairs]
             owned.append(join_first(columns[:, : 3 * D], columns[:, 3 * D :]))
-            owned += [made(*pair) for pair in pairs]
         owned = [reduce_general(part) for part in owned]
         square = sum((jnp.sum(part * part) for part in owned + [ada_grad, time_grad, io_grad]))
         totals = lax.psum(jnp.stack([square, loss_part]), ("dp", "head"))
-        edge = jnp.stack([owned[3], owned[0]])
+        edge = jnp.stack([owned[5], owned[2]])
         edge = jnp.where(is_first, edge[..., block : block + 64], edge[..., block - 64 : block])
         edge = spread(edge.reshape(-1, 128), "head")
         edge = lax.dynamic_slice_in_dim(edge, h ^ 1, 1, 0).reshape(2, rows_own, 64)
-    first_own = jnp.stack([owned[3], owned[0]])
+    first_own = jnp.stack([owned[5], owned[2]])
     total_square, total_loss = totals[0], totals[1]
     qkv_shard, out_shard = without_edge(first_own, edge)
     shards = (
         qkv_shard,
         out_shard,
+        jnp.stack([owned[3], owned[0]]),
         jnp.stack([owned[4], owned[1]]),
-        jnp.stack([owned[5], owned[2]]),
         ada_grad,
         time_grad[None],
         io_grad,

time: 758 us -> 752 us (level)
  no operation moved by 1% of the time
where the time goes in v7:
time: 752 us; the launch traced here: 743 us
  Pallas kernels  501 us (67%)
  matrix products  155 us (21%)
  other arithmetic  47.5 us (6%)
  local copies, waits for them, and re-layouts  32.5 us (4%)
    pallas_call x1, Pallas kernels, gather_whole(): pl.pallas_call(functools.partial(gather_kernel, groups, firsts), out_shap...  147 us
    pallas_call x1, Pallas kernels, reduce_whole(): pl.pallas_call(functools.partial(reduce_kernel, plan, len(lefts), len(rig...  147 us
    dot_general x23, matrix products, product(): return jnp.einsum(form, left, right, preferred_element_type=jnp.float32)  94.7 us
    dot_general x18, matrix products, near_product(): return jnp.einsum(form, left, right, precision=lax.Precision.HIGH)  60 us
    pallas_call x1, Pallas kernels, to_owner(): pl.pallas_call(functools.partial(to_owner_kernel, count), out_shape=jax.S...  45 us
    pallas_call x1, Pallas kernels, attend_back(): pl.pallas_call(attend_back_kernel, out_shape=jax.ShapeDtypeStruct((3 * ti...  35.1 us
    pallas_call x1, Pallas kernels, from_owner(): pl.pallas_call(functools.partial(from_owner_kernel, count, widths), out_s...  34.8 us
    pallas_call x1, Pallas kernels, attend(): pl.pallas_call(attend_kernel, out_shape=[jax.ShapeDtypeStruct((frames, D)...  32 us

profile of v7, /device:TPU:11, one launch (start us, length us, event | category | flops | bytes accessed | tf_op | source)
XLA Modules:
  0.0 743.3 jit_solution(16553726142710896179)
XLA Ops:
  23.0 147.5 %gather_weights.1 = (bf16[2,2,2,96,1024]{4,3,2,1,0:T(8,128)(2,1)}, bf16[2,2,2,96,3072]{4,3,2,1,0:T(8,128)(2,1)}, bf16[2,2,2,96,3072]{4,3,2,1,0:T(8,128)(2,1)}, b...) custom-call(bf16[96,256]{1,0:T(8,128)(2,1)} %fusion.112.refs_0_, ...), custom_call_target="tpu_custom_call" | custom-call | tf_op jit(solution)/shard_map/gather_weights/pallas_call | solution.py:400
  179.2 4.3 convolution_convert_fusion.1.keys_ref.values_ref
  187.5 6.3 convolution_convert_fusion
  193.9 32.0 %attend.1 = (bf16[624,768]{1,0:T(8,128)(2,1)}, bf16[2,416,1152]{2,1,0:T(8,128)(2,1)}, bf16[4,208,768]{2,1,0:T(8,128)(2,1)}, f32[16,832]{1,0:T(8,128)}) custom-call(bf16[624,2304]{1,0:T(8,128)(2,1)} %bitcast.263), custom_call_target="tpu_custom_call" | custom-call | tf_op jit(solution)/shard_map/attend/pallas_call | solution.py:1288
  225.9 3.9 fusion.220
  230.8 6.4 multiply_convert_fusion.3
  237.2 4.5 fusion.219
  242.7 3.5 convolution_convert_fusion.4.query_ref
  246.2 9.5 %cross.1 = bf16[3,208,768]{2,1,0:T(8,128)(2,1)} custom-call(bf16[3,208,768]{2,1,0:T(8,128)(2,1)} %convolution_convert_fusion.4.query_ref, bf16[2,256,1536]{2,1,0:T(8,128)(2,1)} %convolution_convert_fusion.1.keys_ref.values_ref, bf16[2,256,1536]{2,1,0:T(8,128)(2,1)} %convolution_convert_fusion.1.keys_ref.values_ref, s32[2]{0:T(128)} %pad_add_fusion.len_ref), custom_call_target="tpu_custom_call" | custom-call | tf_op jit(solution)/shard_map/cross/pallas_call | solution.py:1433
  255.7 3.8 fusion.218
  260.4 9.6 %multiply_convert_fusion.2 = (bf16[3,208,3072]{2,1,0:T(8,128)(2,1)S(1)}, f32[3,208,3072]{2,1,0:T(8,128)}) fusion(bf16[3,208,768]{2,1,0:T(8,128)(2,1)S(1)} %add_convert_fusion.1, bf16[768,3072,1]{1,0,2:T(8,128)(2,1)} %bitcast.328), kind=kOutput, calls=%fused_computation.2 | convolution fusion | flops 2959736832 | bytes 17178624 | tf_op jit(solution)/shard_map/fld,dn->fln/dot_general | solution.py:76
  270.0 4.5 fusion.217
  277.0 5.1 spread.1
  293.2 10.3 %multiply_convert_fusion.1 = bf16[3,208,3072]{2,1,0:T(8,128)(2,1)S(1)} fusion(f32[3,208,3072]{2,1,0:T(8,128)} %get-tuple-element.245, bf16[3,208,768]{2,1,0:T(8,128)(2,1)S(1)} %get-tuple-element.185, bf16[768,3072,1]{1,0,2:T(8,128)(2,1)} %bitcast.332), kind=kOutput, calls=%fused_computation.1 | convolution fusion | flops 2973155328 | bytes 17178624 | tf_op jit(solution)/shard_map/fld,dn->fln/dot_general | solution.py:76
  303.5 3.4 multiply_reduce_fusion.11
  313.6 13.7 %cross_back.1 = (bf16[3,208,768]{2,1,0:T(8,128)(2,1)}, bf16[2,256,768]{2,1,0:T(8,128)(2,1)}, bf16[2,256,768]{2,1,0:T(8,128)(2,1)}) custom-call(bf16[3,208,768]{2,1,0:T(8,128)(2,1)} %convolution_convert_fusion.4.query_ref, bf16[2,256,1536]{2,1,0:T(8,128)(2,1)} %convolution_convert_fusion.1.keys_ref.values_ref, ...), custom_call_target="tpu_custom_call" | custom-call | tf_op jit(solution)/shard_map/cross_back/pallas_call | solution.py:1484
  333.1 8.6 %multiply_convert_fusion = bf16[3,208,3072]{2,1,0:T(8,128)(2,1)S(1)} fusion(f32[3,208,3072]{2,1,0:T(8,128)} %get-tuple-element.241, bf16[3,208,768]{2,1,0:T(8,128)(2,1)S(1)} %multiply_convert_fusion.5, bf16[768,3072,1]{1,0,2:T(8,128)(2,1)S(1)} %bitcast.327), kind=kOutput, calls=%fused_computation | convolution fusion | flops 2973155328 | bytes 17178624 | tf_op jit(solution)/shard_map/fld,dn->fln/dot_general | solution.py:76
  341.8 3.4 multiply_reduce_fusion.9
  347.7 3.5 convolution_convert_fusion.2
  351.2 35.1 %attend_back.1.refs_16_ = bf16[624,2304]{1,0:T(8,128)(2,1)} custom-call(bf16[2,416,1152]{2,1,0:T(8,128)(2,1)} %get-tuple-element.57.pair_all, bf16[4,208,768]{2,1,0:T(8,128)(2,1)} %get-tuple-element.58.quad_all, f32[16,832]{1,0:T(8,128)} %get-tuple-element.59.log_ref, bf16[624,768]{1,0:T(8,128)(2,1)} %bitcast.271), custom_call_target="tpu_custom_call" | custom-call | tf_op jit(solution)/shard_map/attend_back/pallas_call | solution.py:1384
  386.4 5.3 fusion.3
  398.7 147.1 %reduce_grads.1 = (f32[18,96,256]{2,1,0:T(8,128)}, f32[8,128]{1,0:T(8,128)}, f32[2,96,128]{2,1,0:T(8,128)}, f32[2,96,1152]{2,1,0:T(8,128)}, f32[2,96,96]{2,1,0:T(8,128)}, /*index=5*/f32[8,128]{1,0:T(8,128)}) custom-call(bf16[624,768]{1,0:T(8,128)(2,1)} %bitcast.257, bf16[624,768]{1,0:T(8,128)(2,1)} %bitcast.255, bf16[512,768]{1,0:T(8,128)(2,1)} %bitcast.262, ...), custom_call_target="tpu_custom_call" | custom-call | tf_op jit(solution)/shard_map/reduce_grads/pallas_call | solution.py:827
  560.4 45.0 %to_owner.1 = f32[8,96,768]{2,1,0:T(8,128)} custom-call(f32[2,96,640]{2,1,0:T(8,128)} %pad.59.refs_0_, f32[2,96,256]{2,1,0:T(8,128)} %pad.60.refs_1_, f32[2,96,768]{2,1,0:T(8,128)} %fusion.92.refs_2_, f32[2,96,768]{2,1,0:T(8,128)} %fusion.93.refs_3_), custom_call_target="tpu_custom_call" | custom-call | tf_op jit(solution)/shard_map/to_owner/pallas_call | solution.py:953
  607.4 30.8 %gram_sum.1 = f32[768,768]{1,0:T(8,128)} custom-call(f32[768,768]{1,0:T(8,128)} %bitcast.244), custom_call_target="tpu_custom_call" | custom-call | tf_op jit(solution)/shard_map/gram_sum/pallas_call | solution.py:1075
  654.1 3.4 fusion.27
  663.9 3.4 fusion.235
  670.6 3.4 fusion.25
  677.2 3.6 fusion.236
  680.8 3.3 fusion.15
  684.1 3.4 fusion.19
  697.4 4.1 divide_convert_fusion
  701.6 34.8 %from_owner.1 = bf16[8,96,768]{2,1,0:T(8,128)(2,1)} custom-call(bf16[8,96,768]{2,1,0:T(8,128)(2,1)} %bitcast.270), custom_call_target="tpu_custom_call" | custom-call | tf_op jit(solution)/shard_map/from_owner/pallas_call | solution.py:1010
  (367 shorter events, 129.6 us)
Async XLA Ops:
  0.7 17.8 %copy-start.33 = (f32[2,96,576]{2,1,0:T(8,128)S(1)}, f32[2,96,576]{2,1,0:T(8,128)}, u32[]{:S(2)}) copy-start(f32[2,96,576]{2,1,0:T(8,128)} %param.31) | copy-start | bytes 1327108
  10.9 9.4 %copy-start.30 = (f32[2,96,768]{2,1,0:T(8,128)S(1)}, f32[2,96,768]{2,1,0:T(8,128)}, u32[]{:S(2)}) copy-start(f32[2,96,768]{2,1,0:T(8,128)} %param.33) | copy-start | bytes 1769476
  193.9 36.9 %slice-start = ((s8[4718592]{0:T(1024)(128)(4,1)}), s8[524288]{0:T(1024)(128)(4,1)S(1)}, s32[]{:S(2)}) async-start(s8[4718592]{0:T(1024)(128)(4,1)} %bitcast.316), calls=%async_computation | async-start | bytes 1048576
  241.7 13.9 %copy-start = (f32[3,208,768]{2,1,0:T(8,128)}, f32[3,208,768]{2,1,0:T(8,128)S(1)}, u32[]{:S(2)}) copy-start(f32[3,208,768]{2,1,0:T(8,128)S(1)} %get-tuple-element.171) | copy-start | bytes 5750788
  242.7 13.0 %copy-start.19 = (bf16[3,208,768]{2,1,0:T(8,128)(2,1)}, bf16[3,208,768]{2,1,0:T(8,128)(2,1)S(1)}, u32[]{:S(2)}) copy-start(bf16[3,208,768]{2,1,0:T(8,128)(2,1)S(1)} %add_convert_fusion.2) | copy-start | bytes 2875396
  259.5 10.5 %copy-start.4 = (f32[3,208,768]{2,1,0:T(8,128)}, f32[3,208,768]{2,1,0:T(8,128)S(1)}, u32[]{:S(2)}) copy-start(f32[3,208,768]{2,1,0:T(8,128)S(1)} %get-tuple-element.169) | copy-start | bytes 5750788
  259.8 10.2 %slice-start.10 = ((s8[4718592]{0:T(1024)(128)(4,1)}), s8[4194304]{0:T(1024)(128)(4,1)S(1)}, s32[]{:S(2)}) async-start(s8[4718592]{0:T(1024)(128)(4,1)} %bitcast.333), calls=%async_computation.10 | async-start | bytes 8388608
  260.4 9.6 %copy-start.20 = (bf16[3,208,768]{2,1,0:T(8,128)(2,1)}, bf16[3,208,768]{2,1,0:T(8,128)(2,1)S(1)}, u32[]{:S(2)}) copy-start(bf16[3,208,768]{2,1,0:T(8,128)(2,1)S(1)} %add_convert_fusion.1) | copy-start | bytes 2875396
  260.4 9.6 %slice-start.11 = ((s8[4718592]{0:T(1024)(128)(4,1)}), s8[524288]{0:T(1024)(128)(4,1)S(1)}, s32[]{:S(2)}) async-start(s8[4718592]{0:T(1024)(128)(4,1)} %bitcast.333), calls=%async_computation.11 | async-start | bytes 1048576
  274.9 8.7 %copy-start.54 = (s32[3]{0:T(128)S(1)}, s32[3]{0:T(128)}, u32[]{:S(2)}) copy-start(s32[3]{0:T(128)} %param.29) | copy-start | bytes 40
  292.8 10.7 %slice-start.8 = ((s8[4718592]{0:T(1024)(128)(4,1)}), s8[4194304]{0:T(1024)(128)(4,1)S(1)}, s32[]{:S(2)}) async-start(s8[4718592]{0:T(1024)(128)(4,1)} %bitcast.329), calls=%async_computation.8 | async-start | bytes 8388608
  293.1 10.3 %copy-start.24 = (bf16[3,208,768]{2,1,0:T(8,128)(2,1)}, bf16[3,208,768]{2,1,0:T(8,128)(2,1)S(1)}, u32[]{:S(2)}) copy-start(bf16[3,208,768]{2,1,0:T(8,128)(2,1)S(1)} %get-tuple-element.185) | copy-start | bytes 2875396
  293.2 10.3 %copy-start.5 = (f32[3,208,768]{2,1,0:T(8,128)S(1)}, f32[3,208,768]{2,1,0:T(8,128)}, u32[]{:S(2)}) copy-start(f32[3,208,768]{2,1,0:T(8,128)} %copy-done.4) | copy-start | bytes 5750788
  293.2 10.3 %slice-start.9 = ((s8[4718592]{0:T(1024)(128)(4,1)}), s8[524288]{0:T(1024)(128)(4,1)S(1)}, s32[]{:S(2)}) async-start(s8[4718592]{0:T(1024)(128)(4,1)} %bitcast.329), calls=%async_computation.9 | async-start | bytes 1048576
  313.6 13.7 %copy-start.1 = (f32[3,208,768]{2,1,0:T(8,128)S(1)}, f32[3,208,768]{2,1,0:T(8,128)}, u32[]{:S(2)}) copy-start(f32[3,208,768]{2,1,0:T(8,128)} %copy-done) | copy-start | bytes 5750788
  331.6 10.2 %slice-start.2 = ((s8[4718592]{0:T(1024)(128)(4,1)}), s8[4194304]{0:T(1024)(128)(4,1)S(1)}, s32[]{:S(2)}) async-start(s8[4718592]{0:T(1024)(128)(4,1)} %bitcast.319), calls=%async_computation.2 | async-start | bytes 8388608
  333.1 8.7 %slice-start.3 = ((s8[4718592]{0:T(1024)(128)(4,1)}), s8[524288]{0:T(1024)(128)(4,1)S(1)}, s32[]{:S(2)}) async-start(s8[4718592]{0:T(1024)(128)(4,1)} %bitcast.319), calls=%async_computation.3 | async-start | bytes 1048576
  347.7 38.6 %copy-start.23 = (bf16[3,208,768]{2,1,0:T(8,128)(2,1)}, bf16[3,208,768]{2,1,0:T(8,128)(2,1)S(1)}, u32[]{:S(2)}) copy-start(bf16[3,208,768]{2,1,0:T(8,128)(2,1)S(1)} %multiply_convert_fusion.4) | copy-start | bytes 2875396
  398.6 150.3 %copy-start.50 = (f32[2,96,5]{1,0,2:T(2,128)S(1)}, f32[2,96,5]{1,0,2:T(2,128)}, u32[]{:S(2)}) copy-start(f32[2,96,5]{1,0,2:T(2,128)} %param.37) | copy-start | bytes 11524
  398.6 150.3 %copy-start.52 = (f32[2,96,5]{1,0,2:T(2,128)S(1)}, f32[2,96,5]{1,0,2:T(2,128)}, u32[]{:S(2)}) copy-start(f32[2,96,5]{1,0,2:T(2,128)} %param.47) | copy-start | bytes 11524
  398.6 150.3 %copy-start.53 = (f32[2,96,5]{1,0,2:T(2,128)S(1)}, f32[2,96,5]{1,0,2:T(2,128)}, u32[]{:S(2)}) copy-start(f32[2,96,5]{1,0,2:T(2,128)} %param.46) | copy-start | bytes 11524
  398.6 151.7 %copy-start.46 = (f32[96,192]{1,0:T(8,128)S(1)}, f32[96,192]{1,0:T(8,128)}, u32[]{:S(2)}) copy-start(f32[96,192]{1,0:T(8,128)} %param.36) | copy-start | bytes 221188
  398.6 151.7 %copy-start.48 = (f32[96,192]{1,0:T(8,128)S(1)}, f32[96,192]{1,0:T(8,128)}, u32[]{:S(2)}) copy-start(f32[96,192]{1,0:T(8,128)} %param.45) | copy-start | bytes 221188
  398.6 151.7 %copy-start.49 = (f32[96,192]{1,0:T(8,128)S(1)}, f32[96,192]{1,0:T(8,128)}, u32[]{:S(2)}) copy-start(f32[96,192]{1,0:T(8,128)} %param.44) | copy-start | bytes 221188
  558.6 46.9 %copy-start.43 = (f32[2,96,192]{2,1,0:T(8,128)}, f32[2,96,192]{2,1,0:T(8,128)S(1)}, u32[]{:S(2)}) copy-start(f32[2,96,192]{2,1,0:T(8,128)S(1)} %fusion.104) | copy-start | bytes 442372
  559.6 45.9 %copy-start.32 = (f32[2,96,576]{2,1,0:T(8,128)}, f32[2,96,576]{2,1,0:T(8,128)S(1)}, u32[]{:S(2)}) copy-start(f32[2,96,576]{2,1,0:T(8,128)S(1)} %fusion.97) | copy-start | bytes 1327108
  560.4 45.0 %copy-start.26 = (f32[2,96,1152]{2,1,0:T(8,128)S(1)}, f32[2,96,1152]{2,1,0:T(8,128)}, u32[]{:S(2)}) copy-start(f32[2,96,1152]{2,1,0:T(8,128)} %param.35) | copy-start | bytes 2654212
  560.4 45.0 %copy-start.39 = (f32[2,96,1152]{2,1,0:T(8,128)S(1)}, f32[2,96,1152]{2,1,0:T(8,128)}, u32[]{:S(2)}) copy-start(f32[2,96,1152]{2,1,0:T(8,128)} %param.43) | copy-start | bytes 2654212
  560.4 45.0 %copy-start.40 = (f32[2,96,1152]{2,1,0:T(8,128)S(1)}, f32[2,96,1152]{2,1,0:T(8,128)}, u32[]{:S(2)}) copy-start(f32[2,96,1152]{2,1,0:T(8,128)} %param.42) | copy-start | bytes 2654212
  560.4 45.0 %copy-start.41 = (f32[2,96,1152]{2,1,0:T(8,128)S(1)}, f32[2,96,1152]{2,1,0:T(8,128)}, u32[]{:S(2)}) copy-start(f32[2,96,1152]{2,1,0:T(8,128)} %get-tuple-element.63) | copy-start | bytes 2654212
  701.6 35.7 %copy-start.42 = (f32[2,96,192]{2,1,0:T(8,128)S(1)}, f32[2,96,192]{2,1,0:T(8,128)}, u32[]{:S(2)}) copy-start(f32[2,96,192]{2,1,0:T(8,128)} %param.32) | copy-start | bytes 442372
  701.6 37.5 %copy-start.34 = (f32[2,96,576]{2,1,0:T(8,128)S(1)}, f32[2,96,576]{2,1,0:T(8,128)}, u32[]{:S(2)}) copy-start(f32[2,96,576]{2,1,0:T(8,128)} %param.31) | copy-start | bytes 1327108
  (35 other events, 134.9 us)
